TPU v7x, 32 devices: a whole 2x2x4 slice. The times are simulated.
32 devices in a mesh: wide: 8 (over z, x), narrow: 4 (over y, core).
Axes of the slice: x: 2, y: 2, z: 4, core: 2. Of those that a mesh axis runs over, the one named last changes fastest.
Arguments:
- block: float32 [4, 1024, 512], P(None, 'wide', 'narrow'), may hold values from -6 to 6
- east_weight: float32 [1024, 512], P('wide', 'narrow'), may hold values from 0.2 to 5
- north_weight: float32 [1024, 512], P('wide', 'narrow'), may hold values from 0.2 to 5
- fine_groups: int32 [1024, 512], P('wide', 'narrow'), may hold values from 0 to 2047
- tiles_one: float32 [512, 4, 128, 128], P(('wide', 'narrow')), as said below
- columns_one: int32 [512, 3], P(('wide', 'narrow')), may hold values from 0 to 79
- live_one: int32 [512, 3], P(('wide', 'narrow')), may hold values 0 or 1
- coarse_groups: int32 [65536], P(('wide', 'narrow')), may hold values from 0 to 255
- tiles_two: float32 [128, 4, 64, 64], P(('wide', 'narrow')), as said below
- columns_two: int32 [128, 3], P(('wide', 'narrow')), may hold values from 0 to 19
- live_two: int32 [128, 3], P(('wide', 'narrow')), may hold values 0 or 1
- coarser_groups: int32 [8192], P(('wide', 'narrow')), may hold values from 0 to 31
- chain_forward: float32 [8, 128, 128], P('wide')
- chain_gain: float32 [8, 128, 128], P('wide')
- chain_backward: float32 [8, 128, 128], P('wide')
Outputs:
- corrected: float32 [4, 1024, 512], P(None, 'wide', 'narrow')
Inputs may be any that keep to these rules, and one draw needn't show every extreme that they name: `tiles_one`: in every row tile, slot 0 is the tile of that row tile with itself, and its diagonal entries lie in 1 to 2. `tiles_two`: in every row tile, slot 0 is the tile of that row tile with itself, and its diagonal entries lie in 1 to 2.
All inputs are finite; a program needn't handle non-finite values. No bound on the sum of `live_one` or of `live_two` on one device may be relied on, other than what follows from the above.
Results may differ from a plain program's by a relative error of at most 0.0001.
Values sent between devices are 32-bit elements; how exact they have to be, the bound alone decides.
No kernel may reach another device: no remote copies, remote signals or barrier semaphores. Data moves between devices by JAX's collectives and lax.ppermute only.
A program may use at most 128 MiB of HBM per device.

v0:
```python
import jax
import jax.numpy as jnp
from jax import lax
from jax.sharding import PartitionSpec as P

COLS = 4
C1 = 2048
C2 = 256
C3L = 32


shift_value = 0.1
jacobi_weight = 0.6
smooth_weight = 0.5


def extended(shard, sides, width):
    for axis, dim in sides:
        peers, length = (lax.axis_size(axis), shard.shape[dim])
        up = [(i, (i + 1) % peers) for i in range(peers - 1)]
        down = [(j, i) for i, j in up]
        last = lax.slice_in_dim(shard, length - width, length, axis=dim)
        leading = lax.slice_in_dim(shard, 0, width, axis=dim)
        before = lax.ppermute(last, axis, up)
        after = lax.ppermute(leading, axis, down)
        shard = jnp.concatenate([before, shard, after], axis=dim)
    return shard


def shifted(block, axis, distance):
    devices = range(lax.axis_size(axis))
    route = [(i - distance, i) for i in devices if i - distance in devices]
    return lax.ppermute(block, axis, route)


def carried_in(value, axis, join, neutral, backward):
    count, mine = (lax.axis_size(axis), lax.axis_index(axis))
    pieces = jax.tree.map(lambda part: lax.all_gather(part, axis), value)
    if backward:
        pieces = jax.tree.map(lambda part: part[::-1], pieces)
        mine = count - 1 - mine
    so_far = jax.tree.map(
        lambda part, zero: jnp.full_like(part, 0) + jnp.asarray(zero, part.dtype), value, neutral
    )

    def turn(position, so_far):
        longer = join(so_far, jax.tree.map(lambda part: part[position], pieces))
        return jax.tree.map(lambda new, old: jnp.where(position < mine, new, old), longer, so_far)

    return lax.fori_loop(0, count - 1, turn, so_far)


def combine_fine(field, padded, east_live, west_live, north_live, south_live):
    east_side = padded[:, 2:, 1:-1]
    west_side = padded[:, :-2, 1:-1]
    north_side = padded[:, 1:-1, 2:]
    south_side = padded[:, 1:-1, :-2]
    result = shift_value * field + east_live * (field - east_side) + west_live * (field - west_side)
    return result + north_live * (field - north_side) + south_live * (field - south_side)


def tile_product(tiles, blocks, picked):
    own_part = jnp.einsum("rab,crb->cra", tiles[:, 0], blocks, precision=lax.Precision.HIGHEST)
    other_part = jnp.einsum("rkab,crkb->cra", tiles[:, 1:], picked, precision=lax.Precision.HIGHEST)
    return (own_part + other_part).reshape(blocks.shape[0], -1)


def neighbours(field):
    padded = extended(field.reshape(COLS, 1, 1, -1), (("wide", 1), ("narrow", 2)), 1)
    return jnp.stack(
        [padded[:, 1, 1], padded[:, 0, 1], padded[:, 2, 1], padded[:, 1, 0], padded[:, 1, 2]],
        axis=1,
    )


def coarse_apply(field, tiles, columns, live):
    tile_count = tiles.shape[0]
    tile_size = tiles.shape[2]
    beside_all = neighbours(field).reshape(COLS, 5 * tile_count, tile_size)
    blocks = field.reshape(COLS, tile_count, tile_size)
    picked = jnp.take(beside_all, columns.reshape(-1), axis=1)
    picked = picked.reshape(COLS, tile_count, columns.shape[1], tile_size)
    picked = picked * (live == 1).astype(jnp.float32)[None, :, :, None]
    return tile_product(tiles, blocks, picked)


def segment_total(values, indices, segment_count):
    return jax.ops.segment_sum(values.T, indices, num_segments=segment_count).T


def smooth_cycle(level, right, levels, coarsest):
    if level == len(levels):
        return coarsest(right)
    apply_op, diagonal, restrict_op, prolong_op = levels[level]
    first_iter = jacobi_weight * right / diagonal
    second_iter = first_iter + jacobi_weight * (right - apply_op(first_iter)) / diagonal
    leftover = right - apply_op(second_iter)
    scaled = leftover / diagonal
    coarse_right = restrict_op(leftover - smooth_weight * apply_op(scaled))
    coarse_answer = smooth_cycle(level + 1, coarse_right, levels, coarsest)
    spread = prolong_op(coarse_answer)
    third_iter = second_iter + (spread - smooth_weight * apply_op(spread) / diagonal)
    fourth_iter = third_iter + jacobi_weight * (right - apply_op(third_iter)) / diagonal
    return fourth_iter + jacobi_weight * (right - apply_op(fourth_iter)) / diagonal


def compose(earlier, later):
    joined = jnp.dot(later[0], earlier[0], precision=lax.Precision.HIGHEST)
    offset = jnp.dot(later[0], earlier[1], precision=lax.Precision.HIGHEST) + later[1]
    return (joined, offset)


def body(
    block,
    east_weight,
    north_weight,
    fine_groups,
    tiles_one,
    columns_one,
    live_one,
    coarse_groups,
    tiles_two,
    columns_two,
    live_two,
    coarser_groups,
    chain_forward,
    chain_gain,
    chain_backward,
):
    rows_local = east_weight.shape[0]
    columns_local = east_weight.shape[1]
    row_global = lax.axis_index("wide") * rows_local + lax.broadcasted_iota(
        jnp.int32, east_weight.shape, 0
    )
    column_global = lax.axis_index("narrow") * columns_local + lax.broadcasted_iota(
        jnp.int32, east_weight.shape, 1
    )
    east_live = jnp.where(row_global < rows_local * lax.axis_size("wide") - 1, east_weight, 0.0)
    north_live = jnp.where(
        column_global < columns_local * lax.axis_size("narrow") - 1, north_weight, 0.0
    )
    west_edge = shifted(east_live[-1:, :], "wide", 1)
    west_live = jnp.concatenate([west_edge, east_live[:-1]], axis=0)
    south_edge = shifted(north_live[:, -1:], "narrow", 1)
    south_live = jnp.concatenate([south_edge, north_live[:, :-1]], axis=1)
    fine_diagonal = shift_value + east_live + west_live + north_live + south_live
    fine_ids = fine_groups.reshape(-1)

    def apply_fine(field):
        padded = extended(field, (("wide", 1), ("narrow", 2)), 1)
        return combine_fine(field, padded, east_live, west_live, north_live, south_live)

    def restrict_fine(field):
        return segment_total(field.reshape(COLS, -1), fine_ids, C1)

    def prolong_fine(coarse):
        return jnp.take(coarse, fine_ids, axis=1).reshape(block.shape)

    def apply_one(field):
        return coarse_apply(field, tiles_one, columns_one, live_one)

    def restrict_one(field):
        return segment_total(field, coarse_groups, C2)

    def prolong_one(coarse):
        return jnp.take(coarse, coarse_groups, axis=1)

    def apply_two(field):
        return coarse_apply(field, tiles_two, columns_two, live_two)

    def restrict_two(field):
        return segment_total(field, coarser_groups, C3L)

    def prolong_two(coarse):
        return jnp.take(coarse, coarser_groups, axis=1)

    def chain_solve(right):
        grouped = lax.all_gather(right, "narrow", axis=1, tiled=True)
        piece_now = grouped.T
        forward_map = chain_forward[0]
        back_map = chain_backward[0]
        start_term = jnp.dot(chain_gain[0], piece_now, precision=lax.Precision.HIGHEST)
        identity = (jnp.eye(piece_now.shape[0], dtype=jnp.float32), jnp.zeros_like(piece_now))
        before = carried_in((forward_map, start_term), "wide", compose, identity, False)
        ahead_value = jnp.dot(forward_map, before[1], precision=lax.Precision.HIGHEST) + start_term
        beyond = carried_in((back_map, ahead_value), "wide", compose, identity, True)
        behind_value = jnp.dot(back_map, beyond[1], precision=lax.Precision.HIGHEST) + ahead_value
        own_rows = right.shape[1]
        mine = lax.dynamic_slice_in_dim(
            behind_value, lax.axis_index("narrow") * own_rows, own_rows, 0
        )
        return mine.T

    diag_one = jnp.diagonal(tiles_one[:, 0], axis1=1, axis2=2).reshape(-1)
    diag_two = jnp.diagonal(tiles_two[:, 0], axis1=1, axis2=2).reshape(-1)
    levels = (
        (apply_fine, fine_diagonal, restrict_fine, prolong_fine),
        (apply_one, diag_one, restrict_one, prolong_one),
        (apply_two, diag_two, restrict_two, prolong_two),
    )
    return smooth_cycle(0, block, levels, chain_solve)


def solution(mesh):
    in_specs = (
        P(None, "wide", "narrow"),
        P("wide", "narrow"),
        P("wide", "narrow"),
        P("wide", "narrow"),
        P(("wide", "narrow"), None, None, None),
        P(("wide", "narrow"), None),
        P(("wide", "narrow"), None),
        P(("wide", "narrow")),
        P(("wide", "narrow"), None, None, None),
        P(("wide", "narrow"), None),
        P(("wide", "narrow"), None),
        P(("wide", "narrow")),
        P("wide", None, None),
        P("wide", None, None),
        P("wide", None, None),
    )
    out_specs = P(None, "wide", "narrow")
    return jax.shard_map(body, mesh=mesh, in_specs=in_specs, out_specs=out_specs, check_vma=False)
```

profile of v0, /device:TPU:17, one launch (start us, length us, event | category | flops | bytes accessed | tf_op | source)
XLA Modules:
  0.0 900.4 jit_solution(13654762516147919722)
XLA Ops:
  12.7 23.7 %all_gather.22 = f32[8,128,128]{2,1,0:T(8,128)} all-gather(f32[1,128,128]{2,1,0:T(8,128)} %param.35), channel_id=1, replica_groups=mesh['wide'=8,'narrow'=4] {'wide'}, dimensions={0}, use_global_device_ids=true | all-gather | bytes 589824 | tf_op jit(solution)/shard_map/all_gather | solution.py:38
  36.4 27.6 %all_gather.21 = f32[8,128,128]{2,1,0:T(8,128)} all-gather(f32[1,128,128]{2,1,0:T(8,128)} %param.37), channel_id=1, replica_groups=mesh['wide'=8,'narrow'=4] {'wide'}, dimensions={0}, use_global_device_ids=true | all-gather | bytes 589824 | tf_op jit(solution)/shard_map/all_gather | solution.py:38
  78.3 15.0 %collective-permute-start.5 = (f32[4,130,1]{2,1,0:T(8,128)S(1)}, f32[4,130,1]{2,1,0:T(8,128)S(1)}, u32[]{:S(2)}, u32[]{:S(2)}) collective-permute-start(f32[4,130,1]{2,1,0:T(8,128)S(1)} %get-tuple-element.309), channel_id=1, source_target_pairs={{0,1},{1,2},{2,3},{4,5},{5,6},{6,7},{8,9},{9,10},{10,11},{12,13},{... | collective-permute-start | bytes 6248 | tf_op jit(solution)/shard_map/ppermute | solution.py:24
  96.8 4.4 collective-permute-done.4
  117.1 4.4 collective-permute-done.8
  136.8 4.7 copy.485
  143.7 4.7 copy.616
  148.4 87.8 %scatter_custom_fusion = f32[2048,4]{1,0:T(8,128)S(1)} fusion(s32[16384]{0:T(1024)} %bitcast.568, f32[16384,4]{1,0:T(8,128)} %bitcast.522, f32[]{:T(128)} %constant.142.clone.1), kind=kCustom, calls=%fused_computation.150 | custom fusion | flops 65536 | bytes 33280 | tf_op jit(solution)/shard_map/scatter-add | solution.py:88
  246.5 4.7 collective-permute-start.16
  271.3 5.3 fusion.28
  285.1 4.6 collective-permute-start.19
  316.0 5.4 fusion.31
  330.2 4.6 collective-permute-start.23
  363.8 5.3 fusion.34
  373.9 12.0 %scatter_custom_fusion.1 = f32[256,4]{1,0:T(8,128)S(1)} fusion(s32[2048]{0:T(1024)} %param.30, f32[4,2048]{0,1:T(8,128)} %copy.521, f32[4,2048]{0,1:T(8,128)S(1)} %copy.510, f32[2048,4]{1,0:T(8,128)S(1)} %scatter_custom_fusion, f32[]{:T(128)} %constant.142.clone.1), kind=kCustom, calls=%fused_computation.115 | custom fusion | flops 24576 | bytes 1118720 | tf_op jit(solution)/shard_map/scatter-add | solution.py:88
  417.2 4.4 collective-permute-start.31
  443.6 4.6 collective-permute-start.35
  474.0 22.9 %all-gather = f32[1024,4]{0,1:T(4,128)S(1)} all-gather(f32[128,4]{0,1:T(4,128)S(1)} %convolution_bitcast_fusion.8), channel_id=2, replica_groups=mesh['wide'=8,'narrow'=4] {'wide'}, dimensions={0}, use_global_device_ids=true | all-gather | bytes 18432 | tf_op jit(solution)/shard_map/all_gather | solution.py:38
  496.9 16.1 %while.28 = (s32[]{:T(128)}, f32[128,4]{0,1:T(4,128)}, s32[]{:T(128)}, f32[8,128,128]{2,1,0:T(8,128)}, f32[8,128,4]{1,2,0:T(4,128)S(1)}, /*index=5*/s32[]{:T(128)}, s32[]{:T(128)}) while((s32[]{:T(128)}, f32[128,4]{0,1:T(4,128)}, s32[]{:T(128)}, f32[8,128,128]{2,1,0:T(8,128)}, f32[8,128,4]{1,2,0:T(4,128)S(1)}, ...), condition=%wide.region_4.7_spmd.clone, body=%wide.region_3.6_spmd.clone.sunk | while | flops 788484 | bytes 80487 | solution.py:50
  514.1 21.4 %all-gather.1 = f32[1024,4]{0,1:T(4,128)S(1)} all-gather(f32[128,4]{0,1:T(4,128)S(1)} %fusion.63), channel_id=3, replica_groups=mesh['wide'=8,'narrow'=4] {'wide'}, dimensions={0}, use_global_device_ids=true | all-gather | bytes 18432 | tf_op jit(solution)/shard_map/all_gather | solution.py:38
  535.5 10.5 %while.29 = (s32[]{:T(128)}, f32[128,4]{0,1:T(4,128)}, s32[]{:T(128)}, f32[8,128,128]{2,1,0:T(8,128)S(1)}, f32[8,128,4]{1,2,0:T(4,128)S(1)}, /*index=5*/s32[]{:T(128)}, s32[]{:T(128)}) while((s32[]{:T(128)}, f32[128,4]{0,1:T(4,128)}, s32[]{:T(128)}, f32[8,128,128]{2,1,0:T(8,128)S(1)}, f32[8,128,4]{1,2,0:T(4,128)S(1)}, ...), condition=%wide.region_6.9_spmd.clone, body=%wide.region_5.8_spmd.clone.sunk | while | flops 788484 | bytes 80487 | solution.py:50
  557.3 14.2 %collective-permute-start.40 = (f32[4,3,1,256]{0,3,2,1:T(8,128)S(1)}, f32[4,3,1,256]{0,3,2,1:T(8,128)S(1)}, u32[]{:S(2)}, u32[]{:S(2)}) collective-permute-start(f32[4,3,1,256]{0,3,2,1:T(8,128)S(1)} %pad_maximum_fusion.3), channel_id=1, source_target_pairs={{0,1},{1,2},{2,3},{4,5},{5,6},{6,7},{8,9},{9,10},{10,11},{12,13},{... | collective-permute-start | bytes 36872 | tf_op jit(solution)/shard_map/ppermute | solution.py:24
  636.0 6.4 gather_fusion.3
  674.3 5.3 fusion.37
  718.8 5.3 fusion.40
  764.8 5.3 fusion.43
  776.1 54.8 %gather_fusion.4 = f32[16384,4]{1,0:T(8,128)} fusion(f32[4,2048]{0,1:T(8,128)S(1)} %fusion.78, s32[16384]{0:T(1024)S(1)} %broadcast_clamp_fusion), kind=kCustom, calls=%fused_computation.16 | custom fusion | bytes 589824 | tf_op jit(solution)/shard_map/jit(_take)/gather | solution.py:157
  830.9 5.3 copy.593
  836.3 4.5 collective-permute-start.62
  846.2 5.1 collective-permute-start.65
  854.8 4.4 collective-permute-done.64
  894.5 4.4 collective-permute-done.72
  (511 shorter events, 515.2 us)
Async XLA Ops:
  1.1 67.1 %collective-permute-start = (f32[1,128]{1,0:T(1,128)S(1)}, f32[1,128]{1,0:T(1,128)S(1)}, u32[]{:S(2)}, u32[]{:S(2)}) collective-permute-start(f32[1,128]{1,0:T(1,128)S(1)} %slice.400), channel_id=1, source_target_pairs={{0,4},{4,8},{8,12},{12,16},{16,20},{20,24},{24,28},{1,5},{5,9},{9,... | collective-permute-start | bytes 1544 | tf_op jit(solution)/shard_map/ppermute | solution.py:33
  5.1 63.0 %collective-permute-start.1 = (f32[128,1]{1,0:T(8,128)S(1)}, f32[128,1]{1,0:T(8,128)S(1)}, u32[]{:S(2)}, u32[]{:S(2)}) collective-permute-start(f32[128,1]{1,0:T(8,128)S(1)} %slice.402), channel_id=1, source_target_pairs={{0,1},{1,2},{2,3},{4,5},{5,6},{6,7},{8,9},{9,10},{10,11},{12,13},{... | collective-permute-start | bytes 1544 | tf_op jit(solution)/shard_map/ppermute | solution.py:33
  78.3 18.5 %collective-permute-start.5 = (f32[4,130,1]{2,1,0:T(8,128)S(1)}, f32[4,130,1]{2,1,0:T(8,128)S(1)}, u32[]{:S(2)}, u32[]{:S(2)}) collective-permute-start(f32[4,130,1]{2,1,0:T(8,128)S(1)} %get-tuple-element.309), channel_id=1, source_target_pairs={{0,1},{1,2},{2,3},{4,5},{5,6},{6,7},{8,9},{9,10},{10,11},{12,13},{... | collective-permute-start | bytes 6248 | tf_op jit(solution)/shard_map/ppermute | solution.py:24
  131.6 11.7 %collective-permute-start.13 = (f32[4,130,1]{2,1,0:T(8,128)}, f32[4,130,1]{2,1,0:T(8,128)S(1)}, u32[]{:S(2)}, u32[]{:S(2)}) collective-permute-start(f32[4,130,1]{2,1,0:T(8,128)} %get-tuple-element.305), channel_id=1, source_target_pairs={{0,1},{1,2},{2,3},{4,5},{5,6},{6,7},{8,9},{9,10},{10,11},{12,13},{... | collective-permute-start | bytes 6248 | tf_op jit(solution)/shard_map/ppermute | solution.py:24
  134.8 8.5 collective-permute-start.12
  246.5 11.2 %collective-permute-start.16 = (f32[4,3,1,2048]{3,0,2,1:T(4,128)}, f32[4,3,1,2048]{3,0,2,1:T(4,128)}, u32[]{:S(2)}, u32[]{:S(2)}) collective-permute-start(f32[4,3,1,2048]{3,0,2,1:T(4,128)} %pad_maximum_fusion.60), channel_id=1, source_target_pairs={{0,1},{1,2},{2,3},{4,5},{5,6},{6,7},{8,9},{9,10},{10,11},{12,13},{... | collective-permute-start | bytes 294920 | tf_op jit(solution)/shard_map/ppermute | solution.py:24
  251.3 9.0 collective-permute-start.17
  291.6 10.9 %collective-permute-start.20 = (f32[4,3,1,2048]{3,0,2,1:T(4,128)}, f32[4,3,1,2048]{3,0,2,1:T(4,128)}, u32[]{:S(2)}, u32[]{:S(2)}) collective-permute-start(f32[4,3,1,2048]{3,0,2,1:T(4,128)} %pad_maximum_fusion.61), channel_id=1, source_target_pairs={{0,1},{1,2},{2,3},{4,5},{5,6},{6,7},{8,9},{9,10},{10,11},{12,13},{... | collective-permute-start | bytes 294920 | tf_op jit(solution)/shard_map/ppermute | solution.py:24
  295.9 9.0 %collective-permute-start.21 = (f32[4,3,1,2048]{3,0,2,1:T(4,128)}, f32[4,3,1,2048]{3,0,2,1:T(4,128)}, u32[]{:S(2)}, u32[]{:S(2)}) collective-permute-start(f32[4,3,1,2048]{3,0,2,1:T(4,128)} %pad_maximum_fusion.61), channel_id=1, source_target_pairs={{1,0},{2,1},{3,2},{5,4},{6,5},{7,6},{9,8},{10,9},{11,10},{13,12},{... | collective-permute-start | bytes 294920 | tf_op jit(solution)/shard_map/ppermute | solution.py:25
  328.0 10.6 %collective-permute-start.22 = (f32[4,1,1,2048]{3,0,2,1:T(4,128)S(1)}, f32[4,1,1,2048]{3,0,2,1:T(4,128)S(1)}, u32[]{:S(2)}, u32[]{:S(2)}) collective-permute-start(f32[4,1,1,2048]{3,0,2,1:T(4,128)S(1)} %copy.512), channel_id=1, source_target_pairs={{0,4},{4,8},{8,12},{12,16},{16,20},{20,24},{24,28},{1,5},{5,9},{9,... | collective-permute-start | bytes 98312 | tf_op jit(solution)/shard_map/ppermute | solution.py:24
  330.2 8.4 collective-permute-start.23
  338.6 13.6 %collective-permute-start.24 = (f32[4,3,1,2048]{3,0,2,1:T(4,128)S(1)}, f32[4,3,1,2048]{3,0,2,1:T(4,128)S(1)}, u32[]{:S(2)}, u32[]{:S(2)}) collective-permute-start(f32[4,3,1,2048]{3,0,2,1:T(4,128)S(1)} %pad_maximum_fusion.62), channel_id=1, source_target_pairs={{0,1},{1,2},{2,3},{4,5},{5,6},{6,7},{8,9},{9,10},{10,11},{12,13},{... | collective-permute-start | bytes 294920 | tf_op jit(solution)/shard_map/ppermute | solution.py:24
  342.5 11.1 %collective-permute-start.25 = (f32[4,3,1,2048]{3,0,2,1:T(4,128)S(1)}, f32[4,3,1,2048]{3,0,2,1:T(4,128)S(1)}, u32[]{:S(2)}, u32[]{:S(2)}) collective-permute-start(f32[4,3,1,2048]{3,0,2,1:T(4,128)S(1)} %pad_maximum_fusion.62), channel_id=1, source_target_pairs={{1,0},{2,1},{3,2},{5,4},{6,5},{7,6},{9,8},{10,9},{11,10},{13,12},{... | collective-permute-start | bytes 294920 | tf_op jit(solution)/shard_map/ppermute | solution.py:25
  395.3 9.0 collective-permute-start.28
  399.6 9.1 %collective-permute-start.29 = (f32[4,3,1,256]{0,3,2,1:T(8,128)S(1)}, f32[4,3,1,256]{0,3,2,1:T(8,128)S(1)}, u32[]{:S(2)}, u32[]{:S(2)}) collective-permute-start(f32[4,3,1,256]{0,3,2,1:T(8,128)S(1)} %pad_maximum_fusion), channel_id=1, source_target_pairs={{1,0},{2,1},{3,2},{5,4},{6,5},{7,6},{9,8},{10,9},{11,10},{13,12},{... | collective-permute-start | bytes 36872 | tf_op jit(solution)/shard_map/ppermute | solution.py:25
  426.3 9.1 %collective-permute-start.33 = (f32[4,3,1,256]{0,3,2,1:T(8,128)S(1)}, f32[4,3,1,256]{0,3,2,1:T(8,128)S(1)}, u32[]{:S(2)}, u32[]{:S(2)}) collective-permute-start(f32[4,3,1,256]{0,3,2,1:T(8,128)S(1)} %pad_maximum_fusion.1), channel_id=1, source_target_pairs={{1,0},{2,1},{3,2},{5,4},{6,5},{7,6},{9,8},{10,9},{11,10},{13,12},{... | collective-permute-start | bytes 36872 | tf_op jit(solution)/shard_map/ppermute | solution.py:25
  441.3 9.5 %collective-permute-start.34 = (f32[4,1,1,256]{0,3,2,1:T(8,128)S(1)}, f32[4,1,1,256]{0,3,2,1:T(8,128)}, u32[]{:S(2)}, u32[]{:S(2)}) collective-permute-start(f32[4,1,1,256]{0,3,2,1:T(8,128)S(1)} %bitcast.545), channel_id=1, source_target_pairs={{0,4},{4,8},{8,12},{12,16},{16,20},{20,24},{24,28},{1,5},{5,9},{9,... | collective-permute-start | bytes 12296 | tf_op jit(solution)/shard_map/ppermute | solution.py:24
  453.9 9.1 %collective-permute-start.37 = (f32[4,3,1,256]{0,3,2,1:T(8,128)S(1)}, f32[4,3,1,256]{0,3,2,1:T(8,128)S(1)}, u32[]{:S(2)}, u32[]{:S(2)}) collective-permute-start(f32[4,3,1,256]{0,3,2,1:T(8,128)S(1)} %pad_maximum_fusion.2), channel_id=1, source_target_pairs={{1,0},{2,1},{3,2},{5,4},{6,5},{7,6},{9,8},{10,9},{11,10},{13,12},{... | collective-permute-start | bytes 36872 | tf_op jit(solution)/shard_map/ppermute | solution.py:25
  557.3 18.9 %collective-permute-start.40 = (f32[4,3,1,256]{0,3,2,1:T(8,128)S(1)}, f32[4,3,1,256]{0,3,2,1:T(8,128)S(1)}, u32[]{:S(2)}, u32[]{:S(2)}) collective-permute-start(f32[4,3,1,256]{0,3,2,1:T(8,128)S(1)} %pad_maximum_fusion.3), channel_id=1, source_target_pairs={{0,1},{1,2},{2,3},{4,5},{5,6},{6,7},{8,9},{9,10},{10,11},{12,13},{... | collective-permute-start | bytes 36872 | tf_op jit(solution)/shard_map/ppermute | solution.py:24
  571.5 9.1 %collective-permute-start.41 = (f32[4,3,1,256]{0,3,2,1:T(8,128)S(1)}, f32[4,3,1,256]{0,3,2,1:T(8,128)S(1)}, u32[]{:S(2)}, u32[]{:S(2)}) collective-permute-start(f32[4,3,1,256]{0,3,2,1:T(8,128)S(1)} %pad_maximum_fusion.3), channel_id=1, source_target_pairs={{1,0},{2,1},{3,2},{5,4},{6,5},{7,6},{9,8},{10,9},{11,10},{13,12},{... | collective-permute-start | bytes 36872 | tf_op jit(solution)/shard_map/ppermute | solution.py:25
  585.4 8.2 collective-permute-start.42
  594.9 7.9 collective-permute-start.44
  598.0 9.1 %collective-permute-start.45 = (f32[4,3,1,256]{0,3,2,1:T(8,128)S(1)}, f32[4,3,1,256]{0,3,2,1:T(8,128)S(1)}, u32[]{:S(2)}, u32[]{:S(2)}) collective-permute-start(f32[4,3,1,256]{0,3,2,1:T(8,128)S(1)} %pad_maximum_fusion.4), channel_id=1, source_target_pairs={{1,0},{2,1},{3,2},{5,4},{6,5},{7,6},{9,8},{10,9},{11,10},{13,12},{... | collective-permute-start | bytes 36872 | tf_op jit(solution)/shard_map/ppermute | solution.py:25
  622.8 9.1 %collective-permute-start.49 = (f32[4,3,1,256]{0,3,2,1:T(8,128)S(1)}, f32[4,3,1,256]{0,3,2,1:T(8,128)S(1)}, u32[]{:S(2)}, u32[]{:S(2)}) collective-permute-start(f32[4,3,1,256]{0,3,2,1:T(8,128)S(1)} %pad_maximum_fusion.5), channel_id=1, source_target_pairs={{1,0},{2,1},{3,2},{5,4},{6,5},{7,6},{9,8},{10,9},{11,10},{13,12},{... | collective-permute-start | bytes 36872 | tf_op jit(solution)/shard_map/ppermute | solution.py:25
  644.5 8.8 collective-permute-start.50
  654.7 8.8 collective-permute-start.52
  695.0 10.3 %collective-permute-start.56 = (f32[4,3,1,2048]{3,0,2,1:T(4,128)}, f32[4,3,1,2048]{3,0,2,1:T(4,128)}, u32[]{:S(2)}, u32[]{:S(2)}) collective-permute-start(f32[4,3,1,2048]{3,0,2,1:T(4,128)} %pad_maximum_fusion.64), channel_id=1, source_target_pairs={{0,1},{1,2},{2,3},{4,5},{5,6},{6,7},{8,9},{9,10},{10,11},{12,13},{... | collective-permute-start | bytes 294920 | tf_op jit(solution)/shard_map/ppermute | solution.py:24
  698.7 9.0 %collective-permute-start.57 = (f32[4,3,1,2048]{3,0,2,1:T(4,128)}, f32[4,3,1,2048]{3,0,2,1:T(4,128)}, u32[]{:S(2)}, u32[]{:S(2)}) collective-permute-start(f32[4,3,1,2048]{3,0,2,1:T(4,128)} %pad_maximum_fusion.64), channel_id=1, source_target_pairs={{1,0},{2,1},{3,2},{5,4},{6,5},{7,6},{9,8},{10,9},{11,10},{13,12},{... | collective-permute-start | bytes 294920 | tf_op jit(solution)/shard_map/ppermute | solution.py:25
  731.4 8.2 collective-permute-start.58
  740.3 10.9 %collective-permute-start.60 = (f32[4,3,1,2048]{3,0,2,1:T(4,128)}, f32[4,3,1,2048]{3,0,2,1:T(4,128)}, u32[]{:S(2)}, u32[]{:S(2)}) collective-permute-start(f32[4,3,1,2048]{3,0,2,1:T(4,128)} %pad_maximum_fusion.65), channel_id=1, source_target_pairs={{0,1},{1,2},{2,3},{4,5},{5,6},{6,7},{8,9},{9,10},{10,11},{12,13},{... | collective-permute-start | bytes 294920 | tf_op jit(solution)/shard_map/ppermute | solution.py:24
  744.7 9.1 %collective-permute-start.61 = (f32[4,3,1,2048]{3,0,2,1:T(4,128)}, f32[4,3,1,2048]{3,0,2,1:T(4,128)}, u32[]{:S(2)}, u32[]{:S(2)}) collective-permute-start(f32[4,3,1,2048]{3,0,2,1:T(4,128)} %pad_maximum_fusion.65), channel_id=1, source_target_pairs={{1,0},{2,1},{3,2},{5,4},{6,5},{7,6},{9,8},{10,9},{11,10},{13,12},{... | collective-permute-start | bytes 294920 | tf_op jit(solution)/shard_map/ppermute | solution.py:25
  846.2 8.5 collective-permute-start.65
  (82 other events, 2236.0 us)
where the time goes:
time: 914 us; the launch traced here: 900 us
  starting transfers between devices  241 us (26%)
  local copies, waits for them, and re-layouts  234 us (26%)
  other arithmetic  156 us (17%)
  blocking collectives  99.7 us (11%)
  waiting for transfers between devices  87.2 us (10%)
  matrix products  80.5 us (9%)
    ppermute x36, starting transfers between devices, extended(): before = lax.ppermute(last, axis, up)  126 us
    ppermute x36, starting transfers between devices, extended(): after = lax.ppermute(leading, axis, down)  108 us
    scatter-add x3, other arithmetic, segment_total(): return jax.ops.segment_sum(values.T, indices, num_segments=segment_count).T  101 us
    all_gather x4, blocking collectives, carried_in(): pieces = jax.tree.map(lambda part: lax.all_gather(part, axis), value)  95.7 us
    gather x2, local copies, waits for them, and re-layouts, prolong_fine(): return jnp.take(coarse, fine_ids, axis=1).reshape(block.shape)  60.1 us
    ppermute x36, waiting for transfers between devices, extended(): after = lax.ppermute(leading, axis, down)  51.6 us
    unnamed x130, local copies, waits for them, and re-layouts  48.4 us
    dot_general x12, matrix products, tile_product(): jnp.einsum('rkab,crkb->cra', tiles[:, 1:], picked, precision=lax.Precisio...  39.4 us
  transfers between devices with their start and end apart: 74, of which 33 were waited for; matrix products, arithmetic and copies ran while one was open for 9% of the time, Pallas kernels for 0%

commit v1 on v0

v1 whole, which is shorter than its diff:
```python
import functools

import jax
import jax.numpy as jnp
from jax import lax
from jax.experimental import pallas as pl
from jax.experimental.pallas import tpu as pltpu
from jax.sharding import PartitionSpec as P

F32 = jnp.float32
BF16 = jnp.bfloat16
SHIFT = 0.1
JACOBI = 0.6
LANES = 128
RIM = 4
PAD = 16
VMEM = pl.BlockSpec(memory_space=pltpu.VMEM)
SMEM = pl.BlockSpec(memory_space=pltpu.SMEM)
W_ODD, N_ODD, HAS_WEST, HAS_EAST, HAS_SOUTH, HAS_NORTH, W_AT, N_AT = range(8)


def sds(shape, dtype=F32):
    return jax.ShapeDtypeStruct(shape, dtype)


def call(kernel, outs, ins, scratch=(), specs=None, name=None):
    specs = specs or [VMEM] * len(ins)
    return pl.pallas_call(
        kernel,
        out_shape=outs,
        in_specs=specs,
        out_specs=jax.tree.map(lambda _: VMEM, outs),
        scratch_shapes=list(scratch),
        compiler_params=pltpu.CompilerParams(vmem_limit_bytes=48 * 1024 * 1024),
        name=name,
    )(*ins)


def parts_of(x):
    hi = x.astype(BF16).astype(F32)
    rest = x - hi
    mid = rest.astype(BF16).astype(F32)
    return hi, mid, rest - mid


def rows_of(x):
    return jnp.concatenate([*parts_of(x), jnp.zeros_like(x)], axis=0)


def rows_sum(s, cols):
    return s[0:cols] + s[cols : 2 * cols] + s[2 * cols : 3 * cols]


def dot_nt(a, b):
    return lax.dot_general(a, b, (((1,), (1,)), ((), ())), preferred_element_type=F32)


def store_parts(xs, base, x):
    count, cols, _ = x.shape
    for i, part in enumerate(parts_of(x)):
        xs[pl.ds(base, count), i * cols : (i + 1) * cols, :] = part


def tiles_kernel(tiles_ref, t_ref, d_ref):
    slots, size = tiles_ref.shape[1], tiles_ref.shape[2]
    if size < LANES:
        t_ref[...] = jnp.zeros_like(t_ref)
    for r in range(tiles_ref.shape[0]):
        for k in range(slots):
            tile = tiles_ref[r, k]
            if size < LANES:
                tile = jnp.concatenate([tile, jnp.zeros((size, LANES - size), F32)], axis=1)
            hi = tile.astype(BF16)
            lo = (tile - hi.astype(F32)).astype(BF16)
            t_ref[r, 0:size, k * LANES : (k + 1) * LANES] = hi
            t_ref[r, LANES : LANES + size, k * LANES : (k + 1) * LANES] = lo
            if k == 0:
                row = lax.broadcasted_iota(jnp.int32, tile.shape, 0)
                col = lax.broadcasted_iota(jnp.int32, tile.shape, 1)
                diag = jnp.sum(jnp.where(row == col, tile, 0.0), axis=0, keepdims=True)
                lane = lax.broadcasted_iota(jnp.int32, diag.shape, 1)
                d_ref[r] = jnp.where(lane < size, diag, 1.0)


def split_tiles(tiles):
    count, slots, size, _ = tiles.shape
    step = min(count, 4)
    return pl.pallas_call(
        tiles_kernel,
        grid=(count // step,),
        in_specs=[pl.BlockSpec((step, slots, size, size), lambda i: (i, 0, 0, 0))],
        out_specs=[
            pl.BlockSpec((step, 2 * LANES, slots * LANES), lambda i: (i, 0, 0)),
            pl.BlockSpec((step, 1, LANES), lambda i: (i, 0, 0)),
        ],
        out_shape=[sds((count, 2 * LANES, slots * LANES), BF16), sds((count, 1, LANES))],
        compiler_params=pltpu.CompilerParams(vmem_limit_bytes=32 * 1024 * 1024),
        name="split_tiles",
    )(tiles)


def index_kernel(flags, *refs):
    half = len(refs) // 2
    w_odd, n_odd = flags[W_ODD], flags[N_ODD]
    region = (0, 3 + (1 - w_odd), 3 + w_odd, 1 + (1 - n_odd), 1 + n_odd)
    there = (1, flags[HAS_WEST], flags[HAS_EAST], flags[HAS_SOUTH], flags[HAS_NORTH])
    for level in range(2):
        columns, live, out = refs[2 * level], refs[2 * level + 1], refs[4 + level]
        count, slots = out.shape
        code = columns[...]
        place = jnp.full(code.shape, 5 * count, jnp.int32)
        for s in range(5):
            at = code - s * count
            ok = (at >= 0) & (at < count) & (live[...] == 1) & (there[s] == 1)
            place = jnp.where(ok, at + region[s] * count, place)
        out[:, 1:] = place
        out[:, 0:1] = lax.broadcasted_iota(jnp.int32, (count, 1), 0)


def apply_tiles(t_ref, xs, idx):
    count, slots = idx.shape
    cols = 4
    out = []
    for r in range(count):
        lhs = jnp.concatenate([xs[idx[r, k]] for k in range(slots)], axis=1).astype(BF16)
        both = dot_nt(lhs, t_ref[r])
        out.append(rows_sum(both[:, :LANES] + both[:, LANES:], cols))
    return out


def fill_blocks(xs, own, others, count):
    xs[:, 12:16, :] = jnp.zeros((xs.shape[0], 4, LANES), F32)
    xs[5 * count] = jnp.zeros((16, LANES), F32)
    store_parts(xs, 0, own[0:count])
    for i, other in enumerate(others):
        store_parts(xs, (i + 1) * count, other[0:count])


def smooth_kernel(idx, t, d, b, own, o1, o2, o3, o4, out, xs):
    count = b.shape[0]
    fill_blocks(xs, own, (o1, o2, o3, o4), count)
    for r, ax in enumerate(apply_tiles(t, xs, idx)):
        out[r] = own[r] + JACOBI * (b[r] - ax) / d[r]


def residual_kernel(idx, t, d, b, own, o1, o2, o3, o4, left, scaled, xs):
    count = b.shape[0]
    fill_blocks(xs, own, (o1, o2, o3, o4), count)
    for r, ax in enumerate(apply_tiles(t, xs, idx)):
        rest = b[r] - ax
        left[r] = rest
        scaled[r] = rest / d[r]


def restrict_one_kernel(idx, t, left, groups, d2, own, o1, o2, o3, o4, b2, first, xs):
    count = left.shape[0]
    fill_blocks(xs, own, (o1, o2, o3, o4), count)
    total = None
    coarse_tiles, _, lanes = b2.shape
    size = coarse_tiles * lanes // 2
    for r, ax in enumerate(apply_tiles(t, xs, idx)):
        rows = rows_of(left[r] - 0.5 * ax).astype(BF16)
        hot = lax.broadcasted_iota(jnp.int32, (size, LANES), 0) == groups[r : r + 1, :]
        term = dot_nt(rows, hot.astype(F32).astype(BF16))
        total = term if total is None else total + term
    total = rows_sum(total, 4)
    half = LANES // 2
    lane = lax.broadcasted_iota(jnp.int32, (4, LANES), 1)
    for tile in range(coarse_tiles):
        pair = total[:, (tile // 2) * LANES : (tile // 2 + 1) * LANES]
        if tile % 2:
            pair = pltpu.roll(pair, half, 1)
        value = jnp.where(lane < half, pair, 0.0)
        b2[tile] = value
        first[tile] = JACOBI * value / d2[tile]


def restrict_two_kernel(flags, idx, t, left, groups, own, o1, o2, o3, o4, out, xs):
    count = left.shape[0]
    fill_blocks(xs, own, (o1, o2, o3, o4), count)
    offset = flags[N_AT] * flags[8]
    total = None
    for r, ax in enumerate(apply_tiles(t, xs, idx)):
        rows = rows_of(left[r] - 0.5 * ax).astype(BF16)
        hot = lax.broadcasted_iota(jnp.int32, (LANES, LANES), 0) == groups[r : r + 1, :] + offset
        term = dot_nt(rows, hot.astype(F32).astype(BF16))
        total = term if total is None else total + term
    total = rows_sum(total, 4)
    out[...] = jnp.broadcast_to(total[None], out.shape)


def chain_maps_kernel(flags, maps, out):
    count = maps.shape[0]
    at = flags[W_AT]
    for v in range(count):
        for i in range(3):
            piece = maps[v ^ at, i]
            hi = piece.astype(BF16)
            out[v, i, 0:LANES] = hi
            out[v, i, LANES : 2 * LANES] = (piece - hi.astype(F32)).astype(BF16)


def map_product(m, x):
    both = dot_nt(rows_of(x).astype(BF16), m)
    return rows_sum(both[:, :LANES] + both[:, LANES:], 4)


def take_lanes(table, lanes):
    return jnp.take_along_axis(table, jnp.broadcast_to(lanes, table.shape), axis=1)


def chain_kernel(flags, maps, pieces, idx, t, d, x2, groups, g1, g2, g3, g4, out, xs, ys):
    blocks = maps.shape[0]
    narrow = pieces.shape[0] // blocks
    carry = None
    for v in range(blocks):
        b = pieces[v * narrow]
        for k in range(1, narrow):
            b = b + pieces[v * narrow + k]
        now = map_product(maps[v, 1], b)
        if carry is not None:
            now = now + map_product(maps[v, 0], carry)
        ys[v] = now
        carry = now
    for v in range(blocks - 2, -1, -1):
        carry = ys[v] + map_product(maps[v, 2], carry)
        ys[v] = carry
    count = x2.shape[0]
    xs[5 * count] = jnp.zeros((16, LANES), F32)
    size = flags[8]
    w, n, w_odd, n_odd = flags[W_AT], flags[N_AT], flags[W_ODD], flags[N_ODD]
    n_first = n + 1 - 2 * n_odd
    n_second = jnp.clip(n - 1 + 2 * n_odd, 0, narrow - 1)
    w_first = w + 1 - 2 * w_odd
    w_second = jnp.clip(w - 1 + 2 * w_odd, 0, blocks - 1)
    where = ((w, n), (w, n_first), (w, n_second), (w_first, n), (w_second, n))
    lane = lax.broadcasted_iota(jnp.int32, (16, LANES), 1)
    for p, ((pw, pn), group) in enumerate(zip(where, (groups, g1, g2, g3, g4))):
        table = rows_of(ys[pw])
        for tile in range(count):
            index = (group[tile : tile + 1, :] + pn * size) & (LANES - 1)
            got = take_lanes(table, index)
            xs[p * count + tile] = jnp.where(lane < LANES // 2, got, 0.0)
    for r, ax in enumerate(apply_tiles(t, xs, idx)):
        out[r] = x2[r] + (rows_sum(xs[r], 4) - 0.5 * ax / d[r])


def prolong_one_kernel(idx, t, d, x2, groups, g1, g2, g3, g4, own, o1, o2, o3, o4, out, xs):
    count = x2.shape[0]
    xs[5 * count] = jnp.zeros((16, LANES), F32)
    half = LANES // 2
    lane = lax.broadcasted_iota(jnp.int32, (4, LANES), 1)
    for p, (u, group) in enumerate(
        zip((own, o1, o2, o3, o4), (groups, g1, g2, g3, g4))
    ):
        tables = []
        for i in range(u.shape[0] // 2):
            wide = jnp.where(lane < half, u[2 * i], pltpu.roll(u[2 * i + 1], half, 1))
            tables.append(rows_of(wide))
        for tile in range(count):
            index = group[tile : tile + 1, :]
            got = take_lanes(tables[0], index & (LANES - 1))
            for i in range(1, len(tables)):
                more = take_lanes(tables[i], index & (LANES - 1))
                got = jnp.where((index >> 7) == i, more, got)
            xs[p * count + tile] = got
    for r, ax in enumerate(apply_tiles(t, xs, idx)):
        out[r] = x2[r] + (rows_sum(xs[r], 4) - 0.5 * ax / d[r])


def live_weights(flags, east, north):
    row = lax.broadcasted_iota(jnp.int32, east.shape, 0)
    col = lax.broadcasted_iota(jnp.int32, east.shape, 1)
    east = jnp.where((flags[HAS_EAST] == 1) | (row < east.shape[0] - 1), east, 0.0)
    north = jnp.where((flags[HAS_NORTH] == 1) | (col < north.shape[1] - 1), north, 0.0)
    return east, north


def narrow_rims(flags, fields, first, second):
    odd = flags[N_ODD] == 1
    for i, field in enumerate(fields):
        turned = field.T
        low, high = turned[0:RIM], turned[-RIM:]
        first[i] = jnp.where(odd, low, high)
        second[i] = jnp.where(odd, high, low)


def narrow_sides(flags, first, second, i):
    odd = flags[N_ODD] == 1
    low = jnp.where(odd, first[i], second[i]) * flags[HAS_SOUTH].astype(F32)
    high = jnp.where(odd, second[i], first[i]) * flags[HAS_NORTH].astype(F32)
    return low, high


def with_sides(flags, field, first, second, i):
    low, high = narrow_sides(flags, first, second, i)
    side = jnp.concatenate([high, jnp.zeros((LANES - 2 * RIM, LANES), F32), low], axis=0)
    return jnp.concatenate([field, side.T], axis=1)


def wide_rims(flags, field, i, first, second):
    odd = flags[W_ODD] == 1
    low, high = field[0:RIM], field[-RIM:]
    first[i] = jnp.where(odd, low, high)
    second[i] = jnp.where(odd, high, low)


def with_rows(flags, field, first, second, i):
    odd = flags[W_ODD] == 1
    low = jnp.where(odd, first[i], second[i]) * flags[HAS_WEST].astype(F32)
    high = jnp.where(odd, second[i], first[i]) * flags[HAS_EAST].astype(F32)
    rim = jnp.concatenate([high, jnp.zeros((PAD - 2 * RIM, field.shape[1]), F32), low], axis=0)
    return jnp.concatenate([field, rim], axis=0)


def fine_first_kernel(flags, block, east, north, first, second):
    e, n = live_weights(flags, east[...], north[...])
    narrow_rims(flags, [*(block[c] for c in range(block.shape[0])), e, n], first, second)


def fine_second_kernel(flags, block, east, north, o1, o2, ext, first, second):
    e, n = live_weights(flags, east[...], north[...])
    for i, field in enumerate([*(block[c] for c in range(block.shape[0])), e, n]):
        wider = with_sides(flags, field, o1, o2, i)
        ext[i] = wider
        wide_rims(flags, wider, i, first, second)


def beside(field, e, n):
    rows, lanes = field.shape
    return (
        e * pltpu.roll(field, rows - 1, 0)
        + pltpu.roll(e * field, 1, 0)
        + n * pltpu.roll(field, lanes - 1, 1)
        + pltpu.roll(n * field, 1, 1)
    )


def fine_down_kernel(flags, ext, o1, o2, groups, d1, keep, b1, first, q_ref):
    cols = ext.shape[0] - 2
    rows = ext.shape[1]
    e = with_rows(flags, ext[cols], o1, o2, cols)
    n = with_rows(flags, ext[cols + 1], o1, o2, cols + 1)
    inv = 1.0 / (SHIFT + e + pltpu.roll(e, 1, 0) + n + pltpu.roll(n, 1, 1))
    diag = SHIFT + e + pltpu.roll(e, 1, 0) + n + pltpu.roll(n, 1, 1)
    keep[2 * cols] = e
    keep[2 * cols + 1] = n
    keep[2 * cols + 2] = inv
    for c in range(cols):
        b = with_rows(flags, ext[c], o1, o2, c)
        x1 = JACOBI * b * inv
        x2 = x1 + JACOBI * ((1.0 - JACOBI) * b + beside(x1, e, n)) * inv
        keep[c] = x2
        keep[cols + c] = b
        rest = b - diag * x2 + beside(x2, e, n)
        q = 0.5 * (rest + beside(rest * inv, e, n))
        for i, part in enumerate(parts_of(q[:rows, :LANES])):
            q_ref[i * cols + c] = part
    count = b1.shape[0]
    step = 4

    def add_rows(j, total):
        left, right = [], []
        for k in range(step):
            row = j * step + k
            group = groups[pl.ds(row, 1), :]
            high, low = group >> 7, group & (LANES - 1)
            mask = lax.broadcasted_iota(jnp.int32, (count, LANES), 0) == high
            left.append(
                jnp.concatenate(
                    [
                        jnp.where(mask, q_ref[i, pl.ds(row, 1), :], 0.0).astype(BF16)
                        for i in range(3 * cols)
                    ],
                    axis=0,
                )
            )
            hot = lax.broadcasted_iota(jnp.int32, (LANES, LANES), 0) == low
            right.append(hot.astype(F32).astype(BF16))
        return total + dot_nt(jnp.concatenate(left, axis=1), jnp.concatenate(right, axis=1))

    total = lax.fori_loop(
        0, rows // step, add_rows, jnp.zeros((3 * cols * count, LANES), F32)
    )
    size = cols * count
    total = total[0:size] + total[size : 2 * size] + total[2 * size : 3 * size]
    for c in range(cols):
        value = total[c * count : (c + 1) * count]
        b1[:, c, :] = value
        first[:, c, :] = JACOBI * value / d1[:, 0, :]


def fine_spread_kernel(flags, t, idx, d, b, groups, own, o1, o2, o3, o4, spread, first, second, xs, us):
    count, cols, _ = b.shape
    fill_blocks(xs, own, (o1, o2, o3, o4), count)
    for r, ax in enumerate(apply_tiles(t, xs, idx)):
        us[r] = own[r] + JACOBI * (b[r] - ax) / d[r]
    rows = groups.shape[0]
    for c in range(cols):
        for j in range(rows // 8):
            group = groups[8 * j : 8 * j + 8, :]
            high, low = group >> 7, group & (LANES - 1)
            value = jnp.zeros((8, LANES), F32)
            for h in range(count):
                table = jnp.broadcast_to(us[h, c : c + 1, :], (8, LANES))
                got = jnp.take_along_axis(table, low, axis=1)
                value = jnp.where(high == h, got, value)
            spread[c, 8 * j : 8 * j + 8, :] = value
    narrow_rims(flags, [spread[c] for c in range(cols)], first, second)


def fine_sides_kernel(flags, spread, o1, o2, ext, first, second):
    for c in range(spread.shape[0]):
        wider = with_sides(flags, spread[c], o1, o2, c)
        ext[c] = wider
        wide_rims(flags, wider, c, first, second)


def fine_up_kernel(flags, keep, ext, o1, o2, out):
    cols = out.shape[0]
    e, n, inv = keep[2 * cols], keep[2 * cols + 1], keep[2 * cols + 2]
    for c in range(cols):
        b = keep[cols + c]
        spread = with_rows(flags, ext[c], o1, o2, c)
        x = keep[c] + 0.5 * (spread + beside(spread, e, n) * inv)
        for _ in range(2):
            x = (1.0 - JACOBI) * x + JACOBI * (b + beside(x, e, n)) * inv
        out[c] = x[: out.shape[1], :LANES]


def pairs(start, count):
    out = []
    for i in range(start, count - 1, 2):
        out += [(i, i + 1), (i + 1, i)]
    return out


def routes(wide, narrow):
    narrow_first = pairs(0, narrow)
    narrow_second = pairs(1, narrow) + [(0, narrow - 1), (narrow - 1, 0)]
    wide_first = pairs(0, wide)
    both = [(a * narrow + k, b * narrow + k) for a, b in pairs(1, wide) for k in range(narrow)]
    for a in (0, wide - 1):
        both += [(a * narrow + k, a * narrow + (k ^ 1)) for k in range(narrow)]
    return narrow_first, narrow_second, wide_first, both


def exchange_narrow(first, second, route):
    return lax.ppermute(first, "narrow", route[0]), lax.ppermute(second, "narrow", route[1])


def exchange_wide(first, second, route):
    return (
        lax.ppermute(first, "wide", route[2]),
        lax.ppermute(second, ("wide", "narrow"), route[3]),
    )


def exchange(x, route):
    return (*exchange_narrow(x, x, route), *exchange_wide(x, x, route))


def body(
    sizes,
    block,
    east,
    north,
    fine_groups,
    tiles_one,
    columns_one,
    live_one,
    coarse_groups,
    tiles_two,
    columns_two,
    live_two,
    coarser_groups,
    chain_forward,
    chain_gain,
    chain_backward,
):
    wide, narrow = sizes
    route = routes(wide, narrow)
    w, n = lax.axis_index("wide"), lax.axis_index("narrow")
    cols = block.shape[0]
    rows = block.shape[1]
    count1, slots = tiles_one.shape[:2]
    count2, _, size2, _ = tiles_two.shape
    level3 = chain_forward.shape[-1] // narrow
    flags = jnp.stack(
        [w % 2, n % 2, w > 0, w < wide - 1, n > 0, n < narrow - 1, w, n, jnp.int32(level3)]
    ).astype(jnp.int32)

    rim = sds((cols + 2, RIM, LANES))
    first, second = call(
        fine_first_kernel, [rim, rim], (flags, block, east, north), specs=[SMEM] + [VMEM] * 3
    )
    o1, o2 = exchange_narrow(first, second, route)

    tiles1, d1 = split_tiles(tiles_one)
    tiles2, d2 = split_tiles(tiles_two)
    idx1, idx2 = call(
        index_kernel,
        [sds((count1, slots), jnp.int32), sds((count2, slots), jnp.int32)],
        (flags, columns_one, live_one, columns_two, live_two),
        specs=[SMEM] + [VMEM] * 4,
    )
    maps = jnp.stack([chain_forward, chain_gain, chain_backward], axis=1)
    step = 1
    while step < wide:
        maps = jnp.concatenate(
            [maps, lax.ppermute(maps, "wide", [(i, i ^ step) for i in range(wide)])], axis=0
        )
        step *= 2
    chain = call(
        chain_maps_kernel,
        sds((wide, 3, 2 * LANES, LANES), BF16),
        (flags, maps),
        specs=[SMEM, VMEM],
    )

    rim = sds((cols + 2, RIM, 2 * LANES))
    ext, first, second = call(
        fine_second_kernel,
        [sds((cols + 2, rows, 2 * LANES)), rim, rim],
        (flags, block, east, north, o1, o2),
        specs=[SMEM] + [VMEM] * 5,
    )
    o1, o2 = exchange_wide(first, second, route)
    field1 = sds((count1, cols, LANES))
    field2 = sds((count2, cols, LANES))
    keep, b1, x1 = call(
        fine_down_kernel,
        [sds((2 * cols + 3, rows + PAD, 2 * LANES)), field1, field1],
        (flags, ext, o1, o2, fine_groups, d1),
        scratch=[pltpu.VMEM((3 * cols, rows, LANES), F32)],
        specs=[SMEM] + [VMEM] * 5,
    )

    groups1 = coarse_groups.reshape(count1, LANES)
    groups2 = jnp.pad(coarser_groups.reshape(count2, size2), ((0, 0), (0, LANES - size2)))
    xs1 = [pltpu.VMEM((5 * count1 + 1, 16, LANES), F32)]
    xs2 = [pltpu.VMEM((5 * count2 + 1, 16, LANES), F32)]
    lead = [SMEM]
    near_groups = exchange(jnp.concatenate([groups1, groups2], axis=0), route)
    near1 = tuple(g[:count1] for g in near_groups)
    near2 = tuple(g[count1:] for g in near_groups)

    def smooth(idx, t, d, b, x, xs, like):
        return call(
            smooth_kernel, like, (idx, t, d, b, x, *exchange(x, route)), xs, lead + [VMEM] * 8
        )

    x2 = smooth(idx1, tiles1, d1, b1, x1, xs1, field1)
    left, scaled = call(
        residual_kernel,
        [field1, field1],
        (idx1, tiles1, d1, b1, x2, *exchange(x2, route)),
        xs1,
        lead + [VMEM] * 8,
    )
    b2, y1 = call(
        restrict_one_kernel,
        [field2, field2],
        (idx1, tiles1, left, groups1, d2, scaled, *exchange(scaled, route)),
        xs1,
        lead + [VMEM] * 9,
    )

    y2 = smooth(idx2, tiles2, d2, b2, y1, xs2, field2)
    left, scaled = call(
        residual_kernel,
        [field2, field2],
        (idx2, tiles2, d2, b2, y2, *exchange(y2, route)),
        xs2,
        lead + [VMEM] * 8,
    )
    out3 = call(
        restrict_two_kernel,
        sds((wide * narrow, cols, LANES)),
        (flags, idx2, tiles2, left, groups2, scaled, *exchange(scaled, route)),
        xs2,
        [SMEM, SMEM] + [VMEM] * 8,
    )
    pieces = lax.all_to_all(out3, ("wide", "narrow"), 0, 0)
    y3 = call(
        chain_kernel,
        field2,
        (flags, chain, pieces, idx2, tiles2, d2, y2, groups2, *near2),
        xs2 + [pltpu.VMEM((wide, cols, LANES), F32)],
        [SMEM, VMEM, VMEM, SMEM] + [VMEM] * 8,
    )
    y4 = smooth(idx2, tiles2, d2, b2, y3, xs2, field2)
    y5 = smooth(idx2, tiles2, d2, b2, y4, xs2, field2)

    x3 = call(
        prolong_one_kernel,
        field1,
        (idx1, tiles1, d1, x2, groups1, *near1, y5, *exchange(y5, route)),
        xs1,
        lead + [VMEM] * 13,
    )
    x4 = smooth(idx1, tiles1, d1, b1, x3, xs1, field1)
    rim = sds((cols, RIM, LANES))
    spread, first, second = call(
        fine_spread_kernel,
        [sds((cols, rows, LANES)), rim, rim],
        (flags, tiles1, idx1, d1, b1, fine_groups, x4, *exchange(x4, route)),
        xs1 + [pltpu.VMEM((count1, cols, LANES), F32)],
        [SMEM, VMEM, SMEM] + [VMEM] * 8,
    )
    o1, o2 = exchange_narrow(first, second, route)
    rim = sds((cols, RIM, 2 * LANES))
    ext, first, second = call(
        fine_sides_kernel,
        [sds((cols, rows, 2 * LANES)), rim, rim],
        (flags, spread, o1, o2),
        specs=[SMEM] + [VMEM] * 3,
    )
    o1, o2 = exchange_wide(first, second, route)
    return call(
        fine_up_kernel,
        sds((cols, rows, LANES)),
        (flags, keep, ext, o1, o2),
        specs=[SMEM] + [VMEM] * 4,
    )


def solution(mesh):
    tile = P(("wide", "narrow"), None, None, None)
    pair = P(("wide", "narrow"), None)
    line = P(("wide", "narrow"))
    grid = P("wide", "narrow")
    chain = P("wide", None, None)
    field = P(None, "wide", "narrow")
    in_specs = (
        field, grid, grid, grid, tile, pair, pair, line, tile, pair, pair, line, chain, chain, chain,
    )
    sizes = (mesh.shape["wide"], mesh.shape["narrow"])
    return jax.shard_map(
        functools.partial(body, sizes), mesh=mesh, in_specs=in_specs, out_specs=field, check_vma=False
    )
```

time: 914 us -> 181 us (0.20)
  the two profiles are of different devices: /device:TPU:17 before, /device:TPU:0 now
where the time goes in v1:
time: 181 us
  starting transfers between devices  81.6 us (45%)
  waiting for transfers between devices  46.8 us (26%)
  Pallas kernels  39.1 us (22%)
  local copies, waits for them, and re-layouts  8 us (4%)
  other arithmetic  4.99 us (3%)
    ppermute x14, starting transfers between devices, exchange_wide(): lax.ppermute(first, 'wide', route[2])  53 us
    pallas_call x19, Pallas kernels, call(): pl.pallas_call(kernel, out_shape=outs, in_specs=specs, out_specs=jax.tree...  38.1 us
    ppermute x14, waiting for transfers between devices, exchange_narrow(): lax.ppermute(second, 'narrow', route[1])  17.1 us
    ppermute x3, waiting for transfers between devices, body(): lax.ppermute(maps, 'wide', [(i, i ^ step) for i in range(wide)])  13.4 us
    ppermute x14, starting transfers between devices, exchange_narrow(): lax.ppermute(first, 'narrow', route[0])  13.2 us
    ppermute x14, waiting for transfers between devices, exchange_wide(): lax.ppermute(first, 'wide', route[2])  10.9 us
    unnamed x42, local copies, waits for them, and re-layouts  7.82 us
    ppermute x3, starting transfers between devices, body(): lax.ppermute(maps, 'wide', [(i, i ^ step) for i in range(wide)])  7.42 us
  transfers between devices with their start and end apart: 60, of which 27 were waited for; matrix products, arithmetic and copies ran while one was open for 1% of the time, Pallas kernels for 13%

profile of v1, /device:TPU:0, one launch (start us, length us, event | category | flops | bytes accessed | tf_op | source)
XLA Modules:
  0.0 181.0 jit_solution(5832412440038609655)
XLA Ops:
  1.0 3.0 %collective-permute-start.20 = (f32[1,3,128,128]{3,2,1,0:T(8,128)S(1)}, f32[1,3,128,128]{3,2,1,0:T(8,128)S(1)}, u32[]{:S(2)}, u32[]{:S(2)}) collective-permute-start(f32[1,3,128,128]{3,2,1,0:T(8,128)S(1)} %pad_maximum_fusion.3), channel_id=1, source_target_pairs={{0,4},{4,0},{8,12},{12,8},{16,20},{20,16},{24,28},{28,24},{1,5},{5... | collective-permute-start | bytes 589832 | tf_op jit(solution)/shard_map/ppermute | solution.py:511
  4.0 4.9 %collective-permute-done.20 = f32[1,3,128,128]{3,2,1,0:T(8,128)S(1)} collective-permute-done((f32[1,3,128,128]{3,2,1,0:T(8,128)S(1)}, f32[1,3,128,128]{3,2,1,0:T(8,128)S(1)}, u32[]{:S(2)}, u32[]{:S(2)}) %collective-permute-start.20) | collective-permute-done | bytes 196640 | tf_op jit(solution)/shard_map/ppermute | solution.py:511
  9.8 1.9 %collective-permute-start.21 = (f32[2,3,128,128]{3,2,1,0:T(8,128)S(1)}, f32[2,3,128,128]{3,2,1,0:T(8,128)S(1)}, u32[]{:S(2)}, u32[]{:S(2)}) collective-permute-start(f32[2,3,128,128]{3,2,1,0:T(8,128)S(1)} %pad_maximum_fusion.2), channel_id=1, source_target_pairs={{0,8},{4,12},{8,0},{12,4},{16,24},{20,28},{24,16},{28,20},{1,9},{5... | collective-permute-start | bytes 1179656 | tf_op jit(solution)/shard_map/ppermute | solution.py:511
  11.7 8.5 %collective-permute-done.21 = f32[2,3,128,128]{3,2,1,0:T(8,128)S(1)} collective-permute-done((f32[2,3,128,128]{3,2,1,0:T(8,128)S(1)}, f32[2,3,128,128]{3,2,1,0:T(8,128)S(1)}, u32[]{:S(2)}, u32[]{:S(2)}) %collective-permute-start.21) | collective-permute-done | bytes 393248 | tf_op jit(solution)/shard_map/ppermute | solution.py:511
  22.0 2.5 %collective-permute-start.22 = (f32[4,3,128,128]{3,2,1,0:T(8,128)}, f32[4,3,128,128]{3,2,1,0:T(8,128)}, u32[]{:S(2)}, u32[]{:S(2)}) collective-permute-start(f32[4,3,128,128]{3,2,1,0:T(8,128)} %pad_maximum_fusion.1), channel_id=1, source_target_pairs={{0,16},{4,20},{8,24},{12,28},{16,0},{20,4},{24,8},{28,12},{1,17},{... | collective-permute-start | bytes 2359304 | tf_op jit(solution)/shard_map/ppermute | solution.py:511
  31.1 2.2 %copy-done.3 = f32[16,4,128,128]{3,2,1,0:T(8,128)S(1)} copy-done((f32[16,4,128,128]{3,2,1,0:T(8,128)S(1)}, f32[16,4,128,128]{3,2,1,0:T(8,128)}, u32[]{:S(2)}) %copy-start.3) | copy-done | bytes 4194328
  34.1 2.0 %copy-done = bf16[16,256,512]{2,1,0:T(8,128)(2,1)} copy-done((bf16[16,256,512]{2,1,0:T(8,128)(2,1)}, bf16[16,256,512]{2,1,0:T(8,128)(2,1)S(1)}, u32[]{:S(2)}) %copy-start) | copy-done | bytes 4194328
  36.2 9.3 %shard_map.147 = (f32[11,144,256]{2,1,0:T(8,128)S(1)}, f32[16,4,128]{2,1,0:T(4,128)S(1)}, f32[16,4,128]{2,1,0:T(4,128)S(1)}) custom-call(s32[9]{0:T(128)S(1)} %stack.63.flags, f32[6,128,256]{2,1,0:T(8,128)S(1)} %get-tuple-element.33.ext, f32[6,4,256]{2,1,0:T(4,128)S(1)} %collective-permute-done.2.o1, f32[6,4,256]{2,1,0:T(4,128)S(1)} %collective-permute-done.3.o2, ...), custom_call_target="tpu_custom_call" | custom-call | tf_op jit(solution)/shard_map/pallas_call | solution.py:28
  47.0 8.7 %collective-permute-start.6 = (f32[16,4,128]{2,1,0:T(4,128)S(1)}, f32[16,4,128]{2,1,0:T(4,128)S(1)}, u32[]{:S(2)}, u32[]{:S(2)}) collective-permute-start(f32[16,4,128]{2,1,0:T(4,128)S(1)} %get-tuple-element.41.own), channel_id=1, source_target_pairs={{0,4},{4,0},{8,12},{12,8},{16,20},{20,16},{24,28},{28,24},{1,5},{5... | collective-permute-start | bytes 98312 | tf_op jit(solution)/shard_map/ppermute | solution.py:454
  59.4 2.2 %copy-done.1 = bf16[16,256,512]{2,1,0:T(8,128)(2,1)S(1)} copy-done((bf16[16,256,512]{2,1,0:T(8,128)(2,1)S(1)}, bf16[16,256,512]{2,1,0:T(8,128)(2,1)}, u32[]{:S(2)}) %copy-start.1) | copy-done | bytes 4194328
  61.5 1.9 %shard_map.149.own.x2 = f32[16,4,128]{2,1,0:T(4,128)S(1)} custom-call(s32[16,4]{1,0:T(8,128)S(1)} %get-tuple-element.39.idx, bf16[16,256,512]{2,1,0:T(8,128)(2,1)S(1)} %copy-done.1, f32[16,1,128]{2,1,0:T(1,128)S(1)} %get-tuple-element.36.d1.d, f32[16,4,128]{2,1,0:T(4,128)S(1)} %get-tuple-element.40.b, f32[16,4,128]{2,1,0:T(4,128)S(1)} %get-tuple-element.41.own, ...), custom_call_target="tpu_custom_call" | custom-call | tf_op jit(solution)/shard_map/pallas_call | solution.py:28
  63.7 19.7 %collective-permute-start.14 = (f32[16,4,128]{2,1,0:T(4,128)S(1)}, f32[16,4,128]{2,1,0:T(4,128)S(1)}, u32[]{:S(2)}, u32[]{:S(2)}) collective-permute-start(f32[16,4,128]{2,1,0:T(4,128)S(1)} %shard_map.149.own.x2), channel_id=1, source_target_pairs={{0,4},{4,0},{8,12},{12,8},{16,20},{20,16},{24,28},{28,24},{1,5},{5... | collective-permute-start | bytes 98312 | tf_op jit(solution)/shard_map/ppermute | solution.py:454
  86.8 1.9 %shard_map.150 = (f32[16,4,128]{2,1,0:T(4,128)S(1)}, f32[16,4,128]{2,1,0:T(4,128)S(1)}) custom-call(s32[16,4]{1,0:T(8,128)S(1)} %get-tuple-element.39.idx, bf16[16,256,512]{2,1,0:T(8,128)(2,1)S(1)} %copy-done.1, f32[16,1,128]{2,1,0:T(1,128)S(1)} %get-tuple-element.36.d1.d, f32[16,4,128]{2,1,0:T(4,128)S(1)} %get-tuple-element.40.b, ...), custom_call_target="tpu_custom_call" | custom-call | tf_op jit(solution)/shard_map/pallas_call | solution.py:28
  93.6 2.4 %shard_map.151 = (f32[4,4,128]{2,1,0:T(4,128)S(1)}, f32[4,4,128]{2,1,0:T(4,128)S(1)}) custom-call(s32[16,4]{1,0:T(8,128)S(1)} %get-tuple-element.39.idx, bf16[16,256,512]{2,1,0:T(8,128)(2,1)S(1)} %copy-done.1, f32[16,4,128]{2,1,0:T(4,128)S(1)} %get-tuple-element.45.left, s32[16,128]{1,0:T(8,128)S(1)} %bitcast.12, f32[4,1,128]{2,1,0:T(1,128)S(1)} %get-tuple-element.44.d2.d, ...), custom_call_target="tpu_custom_call" | custom-call | tf_op jit(solution)/shard_map/pallas_call | solution.py:28
  96.0 2.5 %collective-permute-start.25 = (f32[4,4,128]{2,1,0:T(4,128)S(1)}, f32[4,4,128]{2,1,0:T(4,128)S(1)}, u32[]{:S(2)}, u32[]{:S(2)}) collective-permute-start(f32[4,4,128]{2,1,0:T(4,128)S(1)} %get-tuple-element.48.own), channel_id=1, source_target_pairs={{0,4},{4,0},{8,12},{12,8},{16,20},{20,16},{24,28},{28,24},{1,5},{5... | collective-permute-start | bytes 24584 | tf_op jit(solution)/shard_map/ppermute | solution.py:454
  102.6 1.8 %collective-permute-start.29 = (f32[4,4,128]{2,1,0:T(4,128)S(1)}, f32[4,4,128]{2,1,0:T(4,128)S(1)}, u32[]{:S(2)}, u32[]{:S(2)}) collective-permute-start(f32[4,4,128]{2,1,0:T(4,128)S(1)} %shard_map.153.own.x2), channel_id=1, source_target_pairs={{0,4},{4,0},{8,12},{12,8},{16,20},{20,16},{24,28},{28,24},{1,5},{5... | collective-permute-start | bytes 24584 | tf_op jit(solution)/shard_map/ppermute | solution.py:454
  106.3 2.7 %collective-permute-start.10 = (s32[20,128]{1,0:T(8,128)S(1)}, s32[20,128]{1,0:T(8,128)S(1)}, u32[]{:S(2)}, u32[]{:S(2)}) collective-permute-start(s32[20,128]{1,0:T(8,128)S(1)} %pad_add_fusion), channel_id=1, source_target_pairs={{0,4},{4,0},{8,12},{12,8},{16,20},{20,16},{24,28},{28,24},{1,5},{5... | collective-permute-start | bytes 30728 | tf_op jit(solution)/shard_map/ppermute | solution.py:454
  111.4 3.1 %collective-permute-start.33 = (f32[4,4,128]{2,1,0:T(4,128)S(1)}, f32[4,4,128]{2,1,0:T(4,128)S(1)}, u32[]{:S(2)}, u32[]{:S(2)}) collective-permute-start(f32[4,4,128]{2,1,0:T(4,128)S(1)} %get-tuple-element.50.own), channel_id=1, source_target_pairs={{0,4},{4,0},{8,12},{12,8},{16,20},{20,16},{24,28},{28,24},{1,5},{5... | collective-permute-start | bytes 24584 | tf_op jit(solution)/shard_map/ppermute | solution.py:454
  119.3 3.7 %all-to-all-start = ((f32[32,4,128]{2,1,0:T(4,128)}), f32[32,4,128]{2,1,0:T(4,128)S(1)}, u32[]{:S(2)}, u32[]{:S(2)}) async-start(f32[32,4,128]{2,1,0:T(4,128)} %shard_map.155), calls=%async_computation | async-start | bytes 131072 | tf_op jit(solution)/shard_map/all_to_all | solution.py:584
  125.0 5.2 %all-to-all-done.pieces = f32[32,4,128]{2,1,0:T(4,128)S(1)} async-done(((f32[32,4,128]{2,1,0:T(4,128)}), f32[32,4,128]{2,1,0:T(4,128)S(1)}, u32[]{:S(2)}, u32[]{:S(2)}) %all-to-all-start) | async-done | bytes 65568 | tf_op jit(solution)/shard_map/all_to_all | solution.py:584
  130.3 3.0 %shard_map.156.own = f32[4,4,128]{2,1,0:T(4,128)S(1)} custom-call(s32[9]{0:T(128)S(1)} %stack.63.flags, bf16[8,3,256,128]{3,2,1,0:T(8,128)(2,1)S(1)} %shard_map.152.maps, f32[32,4,128]{2,1,0:T(4,128)S(1)} %all-to-all-done.pieces, s32[4,4]{1,0:T(4,128)S(1)} %get-tuple-element.42.idx, bf16[4,256,512]{2,1,0:T(8,128)(2,1)S(1)} %get-tuple-element.43.t, ...), custom_call_target="tpu_custom_call" | custom-call | tf_op jit(solution)/shard_map/pallas_call | solution.py:28
  133.4 2.0 %collective-permute-start.37 = (f32[4,4,128]{2,1,0:T(4,128)S(1)}, f32[4,4,128]{2,1,0:T(4,128)S(1)}, u32[]{:S(2)}, u32[]{:S(2)}) collective-permute-start(f32[4,4,128]{2,1,0:T(4,128)S(1)} %shard_map.156.own), channel_id=1, source_target_pairs={{0,4},{4,0},{8,12},{12,8},{16,20},{20,16},{24,28},{28,24},{1,5},{5... | collective-permute-start | bytes 24584 | tf_op jit(solution)/shard_map/ppermute | solution.py:454
  139.5 2.1 %collective-permute-start.41 = (f32[4,4,128]{2,1,0:T(4,128)S(1)}, f32[4,4,128]{2,1,0:T(4,128)S(1)}, u32[]{:S(2)}, u32[]{:S(2)}) collective-permute-start(f32[4,4,128]{2,1,0:T(4,128)S(1)} %shard_map.157.own), channel_id=1, source_target_pairs={{0,4},{4,0},{8,12},{12,8},{16,20},{20,16},{24,28},{28,24},{1,5},{5... | collective-permute-start | bytes 24584 | tf_op jit(solution)/shard_map/ppermute | solution.py:454
  145.7 2.2 %collective-permute-start.45 = (f32[4,4,128]{2,1,0:T(4,128)S(1)}, f32[4,4,128]{2,1,0:T(4,128)S(1)}, u32[]{:S(2)}, u32[]{:S(2)}) collective-permute-start(f32[4,4,128]{2,1,0:T(4,128)S(1)} %shard_map.158.own), channel_id=1, source_target_pairs={{0,4},{4,0},{8,12},{12,8},{16,20},{20,16},{24,28},{28,24},{1,5},{5... | collective-permute-start | bytes 24584 | tf_op jit(solution)/shard_map/ppermute | solution.py:454
  151.1 2.5 %shard_map.159.own = f32[16,4,128]{2,1,0:T(4,128)S(1)} custom-call(s32[16,4]{1,0:T(8,128)S(1)} %get-tuple-element.39.idx, bf16[16,256,512]{2,1,0:T(8,128)(2,1)S(1)} %copy-done.2, f32[16,1,128]{2,1,0:T(1,128)S(1)} %get-tuple-element.36.d1.d, f32[16,4,128]{2,1,0:T(4,128)S(1)} %shard_map.149.own.x2, s32[16,128]{1,0:T(8,128)S(1)} %bitcast.14, ...), custom_call_target="tpu_custom_call" | custom-call | tf_op jit(solution)/shard_map/pallas_call | solution.py:28
  153.6 2.6 %collective-permute-start.49 = (f32[16,4,128]{2,1,0:T(4,128)S(1)}, f32[16,4,128]{2,1,0:T(4,128)S(1)}, u32[]{:S(2)}, u32[]{:S(2)}) collective-permute-start(f32[16,4,128]{2,1,0:T(4,128)S(1)} %shard_map.159.own), channel_id=1, source_target_pairs={{0,4},{4,0},{8,12},{12,8},{16,20},{20,16},{24,28},{28,24},{1,5},{5... | collective-permute-start | bytes 98312 | tf_op jit(solution)/shard_map/ppermute | solution.py:454
  159.6 1.9 %shard_map.160.own = f32[16,4,128]{2,1,0:T(4,128)S(1)} custom-call(s32[16,4]{1,0:T(8,128)S(1)} %get-tuple-element.39.idx, bf16[16,256,512]{2,1,0:T(8,128)(2,1)S(1)} %copy-done.2, f32[16,1,128]{2,1,0:T(1,128)S(1)} %get-tuple-element.36.d1.d, f32[16,4,128]{2,1,0:T(4,128)S(1)} %get-tuple-element.40.b, f32[16,4,128]{2,1,0:T(4,128)S(1)} %shard_map.159.own, ...), custom_call_target="tpu_custom_call" | custom-call | tf_op jit(solution)/shard_map/pallas_call | solution.py:28
  161.6 2.1 %collective-permute-start.53 = (f32[16,4,128]{2,1,0:T(4,128)S(1)}, f32[16,4,128]{2,1,0:T(4,128)S(1)}, u32[]{:S(2)}, u32[]{:S(2)}) collective-permute-start(f32[16,4,128]{2,1,0:T(4,128)S(1)} %shard_map.160.own), channel_id=1, source_target_pairs={{0,4},{4,0},{8,12},{12,8},{16,20},{20,16},{24,28},{28,24},{1,5},{5... | collective-permute-start | bytes 98312 | tf_op jit(solution)/shard_map/ppermute | solution.py:454
  167.0 3.4 %shard_map.161 = (f32[4,128,128]{2,1,0:T(8,128)S(1)}, f32[4,4,128]{2,1,0:T(4,128)S(1)}, f32[4,4,128]{2,1,0:T(4,128)S(1)}) custom-call(s32[9]{0:T(128)S(1)} %stack.63.flags, bf16[16,256,512]{2,1,0:T(8,128)(2,1)S(1)} %copy-done.2, s32[16,4]{1,0:T(8,128)S(1)} %get-tuple-element.39.idx, f32[16,1,128]{2,1,0:T(1,128)S(1)} %get-tuple-element.36.d1.d, ...), custom_call_target="tpu_custom_call" | custom-call | tf_op jit(solution)/shard_map/pallas_call | solution.py:28
  171.6 2.0 %collective-permute-done.56.o2 = f32[4,4,128]{2,1,0:T(4,128)S(1)} collective-permute-done((f32[4,4,128]{2,1,0:T(4,128)S(1)}, f32[4,4,128]{2,1,0:T(4,128)S(1)}, u32[]{:S(2)}, u32[]{:S(2)}) %collective-permute-start.56) | collective-permute-done | bytes 8224 | tf_op jit(solution)/shard_map/ppermute | solution.py:449
  175.1 3.0 %collective-permute-done.57.o1 = f32[4,4,256]{2,1,0:T(4,128)S(1)} collective-permute-done((f32[4,4,256]{2,1,0:T(4,128)S(1)}, f32[4,4,256]{2,1,0:T(4,128)S(1)}, u32[]{:S(2)}, u32[]{:S(2)}) %collective-permute-start.57) | collective-permute-done | bytes 16416 | tf_op jit(solution)/shard_map/ppermute | solution.py:454
  178.1 2.9 %shard_map.163 = f32[4,128,128]{2,1,0:T(8,128)} custom-call(s32[9]{0:T(128)S(1)} %stack.63.flags, f32[11,144,256]{2,1,0:T(8,128)S(1)} %copy-done.5, f32[4,128,256]{2,1,0:T(8,128)S(1)} %get-tuple-element.54.ext, f32[4,4,256]{2,1,0:T(4,128)S(1)} %collective-permute-done.57.o1, f32[4,4,256]{2,1,0:T(4,128)S(1)} %collective-permute-done.58.o2), custom_call_target="tpu_custom_call" | custom-call | tf_op jit(solution)/shard_map/pallas_call | solution.py:28
  (167 shorter events, 60.9 us)
Async XLA Ops:
  1.0 7.9 %collective-permute-start.20 = (f32[1,3,128,128]{3,2,1,0:T(8,128)S(1)}, f32[1,3,128,128]{3,2,1,0:T(8,128)S(1)}, u32[]{:S(2)}, u32[]{:S(2)}) collective-permute-start(f32[1,3,128,128]{3,2,1,0:T(8,128)S(1)} %pad_maximum_fusion.3), channel_id=1, source_target_pairs={{0,4},{4,0},{8,12},{12,8},{16,20},{20,16},{24,28},{28,24},{1,5},{5... | collective-permute-start | bytes 589832 | tf_op jit(solution)/shard_map/ppermute | solution.py:511
  9.8 10.4 %collective-permute-start.21 = (f32[2,3,128,128]{3,2,1,0:T(8,128)S(1)}, f32[2,3,128,128]{3,2,1,0:T(8,128)S(1)}, u32[]{:S(2)}, u32[]{:S(2)}) collective-permute-start(f32[2,3,128,128]{3,2,1,0:T(8,128)S(1)} %pad_maximum_fusion.2), channel_id=1, source_target_pairs={{0,8},{4,12},{8,0},{12,4},{16,24},{20,28},{24,16},{28,20},{1,9},{5... | collective-permute-start | bytes 1179656 | tf_op jit(solution)/shard_map/ppermute | solution.py:511
  22.0 101.0 %collective-permute-start.22 = (f32[4,3,128,128]{3,2,1,0:T(8,128)}, f32[4,3,128,128]{3,2,1,0:T(8,128)}, u32[]{:S(2)}, u32[]{:S(2)}) collective-permute-start(f32[4,3,128,128]{3,2,1,0:T(8,128)} %pad_maximum_fusion.1), channel_id=1, source_target_pairs={{0,16},{4,20},{8,24},{12,28},{16,0},{20,4},{24,8},{28,12},{1,17},{... | collective-permute-start | bytes 2359304 | tf_op jit(solution)/shard_map/ppermute | solution.py:511
  29.3 6.8 %collective-permute-start.2 = (f32[6,4,256]{2,1,0:T(4,128)S(1)}, f32[6,4,256]{2,1,0:T(4,128)S(1)}, u32[]{:S(2)}, u32[]{:S(2)}) collective-permute-start(f32[6,4,256]{2,1,0:T(4,128)S(1)} %get-tuple-element.34), channel_id=1, source_target_pairs={{0,4},{4,0},{8,12},{12,8},{16,20},{20,16},{24,28},{28,24},{1,5},{5... | collective-permute-start | bytes 73736 | tf_op jit(solution)/shard_map/ppermute | solution.py:454
  30.9 5.3 %collective-permute-start.3 = (f32[6,4,256]{2,1,0:T(4,128)S(1)}, f32[6,4,256]{2,1,0:T(4,128)S(1)}, u32[]{:S(2)}, u32[]{:S(2)}) collective-permute-start(f32[6,4,256]{2,1,0:T(4,128)S(1)} %get-tuple-element.35), channel_id=1, source_target_pairs={{4,8},{5,9},{6,10},{7,11},{8,4},{9,5},{10,6},{11,7},{12,16},{13,17... | collective-permute-start | bytes 73736 | tf_op jit(solution)/shard_map/ppermute | solution.py:455
  46.7 11.5 %collective-permute-start.7 = (f32[16,4,128]{2,1,0:T(4,128)S(1)}, f32[16,4,128]{2,1,0:T(4,128)S(1)}, u32[]{:S(2)}, u32[]{:S(2)}) collective-permute-start(f32[16,4,128]{2,1,0:T(4,128)S(1)} %get-tuple-element.41.own), channel_id=1, source_target_pairs={{4,8},{5,9},{6,10},{7,11},{8,4},{9,5},{10,6},{11,7},{12,16},{13,17... | collective-permute-start | bytes 98312 | tf_op jit(solution)/shard_map/ppermute | solution.py:455
  47.0 11.1 %collective-permute-start.6 = (f32[16,4,128]{2,1,0:T(4,128)S(1)}, f32[16,4,128]{2,1,0:T(4,128)S(1)}, u32[]{:S(2)}, u32[]{:S(2)}) collective-permute-start(f32[16,4,128]{2,1,0:T(4,128)S(1)} %get-tuple-element.41.own), channel_id=1, source_target_pairs={{0,4},{4,0},{8,12},{12,8},{16,20},{20,16},{24,28},{28,24},{1,5},{5... | collective-permute-start | bytes 98312 | tf_op jit(solution)/shard_map/ppermute | solution.py:454
  55.7 3.6 %collective-permute-start.5 = (f32[16,4,128]{2,1,0:T(4,128)S(1)}, f32[16,4,128]{2,1,0:T(4,128)S(1)}, u32[]{:S(2)}, u32[]{:S(2)}) collective-permute-start(f32[16,4,128]{2,1,0:T(4,128)S(1)} %get-tuple-element.41.own), channel_id=1, source_target_pairs={{1,2},{2,1},{0,3},{3,0},{5,6},{6,5},{4,7},{7,4},{9,10},{10,9},{8,1... | collective-permute-start | bytes 98312 | tf_op jit(solution)/shard_map/ppermute | solution.py:449
  55.7 3.6 %collective-permute-start.4 = (f32[16,4,128]{2,1,0:T(4,128)S(1)}, f32[16,4,128]{2,1,0:T(4,128)S(1)}, u32[]{:S(2)}, u32[]{:S(2)}) collective-permute-start(f32[16,4,128]{2,1,0:T(4,128)S(1)} %get-tuple-element.41.own), channel_id=1, source_target_pairs={{0,1},{1,0},{2,3},{3,2},{4,5},{5,4},{6,7},{7,6},{8,9},{9,8},{10,11... | collective-permute-start | bytes 98312 | tf_op jit(solution)/shard_map/ppermute | solution.py:449
  63.5 21.2 %collective-permute-start.15 = (f32[16,4,128]{2,1,0:T(4,128)S(1)}, f32[16,4,128]{2,1,0:T(4,128)S(1)}, u32[]{:S(2)}, u32[]{:S(2)}) collective-permute-start(f32[16,4,128]{2,1,0:T(4,128)S(1)} %shard_map.149.own.x2), channel_id=1, source_target_pairs={{4,8},{5,9},{6,10},{7,11},{8,4},{9,5},{10,6},{11,7},{12,16},{13,17... | collective-permute-start | bytes 98312 | tf_op jit(solution)/shard_map/ppermute | solution.py:455
  63.7 21.6 %collective-permute-start.14 = (f32[16,4,128]{2,1,0:T(4,128)S(1)}, f32[16,4,128]{2,1,0:T(4,128)S(1)}, u32[]{:S(2)}, u32[]{:S(2)}) collective-permute-start(f32[16,4,128]{2,1,0:T(4,128)S(1)} %shard_map.149.own.x2), channel_id=1, source_target_pairs={{0,4},{4,0},{8,12},{12,8},{16,20},{20,16},{24,28},{28,24},{1,5},{5... | collective-permute-start | bytes 98312 | tf_op jit(solution)/shard_map/ppermute | solution.py:454
  83.3 3.5 %collective-permute-start.13 = (f32[16,4,128]{2,1,0:T(4,128)S(1)}, f32[16,4,128]{2,1,0:T(4,128)S(1)}, u32[]{:S(2)}, u32[]{:S(2)}) collective-permute-start(f32[16,4,128]{2,1,0:T(4,128)S(1)} %shard_map.149.own.x2), channel_id=1, source_target_pairs={{1,2},{2,1},{0,3},{3,0},{5,6},{6,5},{4,7},{7,4},{9,10},{10,9},{8,1... | collective-permute-start | bytes 98312 | tf_op jit(solution)/shard_map/ppermute | solution.py:449
  88.8 4.0 %collective-permute-start.18 = (f32[16,4,128]{2,1,0:T(4,128)S(1)}, f32[16,4,128]{2,1,0:T(4,128)S(1)}, u32[]{:S(2)}, u32[]{:S(2)}) collective-permute-start(f32[16,4,128]{2,1,0:T(4,128)S(1)} %get-tuple-element.46.own), channel_id=1, source_target_pairs={{0,4},{4,0},{8,12},{12,8},{16,20},{20,16},{24,28},{28,24},{1,5},{5... | collective-permute-start | bytes 98312 | tf_op jit(solution)/shard_map/ppermute | solution.py:454
  96.0 3.9 %collective-permute-start.26 = (f32[4,4,128]{2,1,0:T(4,128)S(1)}, f32[4,4,128]{2,1,0:T(4,128)S(1)}, u32[]{:S(2)}, u32[]{:S(2)}) collective-permute-start(f32[4,4,128]{2,1,0:T(4,128)S(1)} %get-tuple-element.48.own), channel_id=1, source_target_pairs={{4,8},{5,9},{6,10},{7,11},{8,4},{9,5},{10,6},{11,7},{12,16},{13,17... | collective-permute-start | bytes 24584 | tf_op jit(solution)/shard_map/ppermute | solution.py:455
  96.0 4.1 %collective-permute-start.25 = (f32[4,4,128]{2,1,0:T(4,128)S(1)}, f32[4,4,128]{2,1,0:T(4,128)S(1)}, u32[]{:S(2)}, u32[]{:S(2)}) collective-permute-start(f32[4,4,128]{2,1,0:T(4,128)S(1)} %get-tuple-element.48.own), channel_id=1, source_target_pairs={{0,4},{4,0},{8,12},{12,8},{16,20},{20,16},{24,28},{28,24},{1,5},{5... | collective-permute-start | bytes 24584 | tf_op jit(solution)/shard_map/ppermute | solution.py:454
  102.6 3.7 %collective-permute-start.29 = (f32[4,4,128]{2,1,0:T(4,128)S(1)}, f32[4,4,128]{2,1,0:T(4,128)S(1)}, u32[]{:S(2)}, u32[]{:S(2)}) collective-permute-start(f32[4,4,128]{2,1,0:T(4,128)S(1)} %shard_map.153.own.x2), channel_id=1, source_target_pairs={{0,4},{4,0},{8,12},{12,8},{16,20},{20,16},{24,28},{28,24},{1,5},{5... | collective-permute-start | bytes 24584 | tf_op jit(solution)/shard_map/ppermute | solution.py:454
  104.4 4.6 %collective-permute-start.28 = (f32[4,4,128]{2,1,0:T(4,128)S(1)}, f32[4,4,128]{2,1,0:T(4,128)S(1)}, u32[]{:S(2)}, u32[]{:S(2)}) collective-permute-start(f32[4,4,128]{2,1,0:T(4,128)S(1)} %shard_map.153.own.x2), channel_id=1, source_target_pairs={{1,2},{2,1},{0,3},{3,0},{5,6},{6,5},{4,7},{7,4},{9,10},{10,9},{8,1... | collective-permute-start | bytes 24584 | tf_op jit(solution)/shard_map/ppermute | solution.py:449
  104.4 4.6 %collective-permute-start.27 = (f32[4,4,128]{2,1,0:T(4,128)S(1)}, f32[4,4,128]{2,1,0:T(4,128)S(1)}, u32[]{:S(2)}, u32[]{:S(2)}) collective-permute-start(f32[4,4,128]{2,1,0:T(4,128)S(1)} %shard_map.153.own.x2), channel_id=1, source_target_pairs={{0,1},{1,0},{2,3},{3,2},{4,5},{5,4},{6,7},{7,6},{8,9},{9,8},{10,11... | collective-permute-start | bytes 24584 | tf_op jit(solution)/shard_map/ppermute | solution.py:449
  105.8 5.5 %collective-permute-start.11 = (s32[20,128]{1,0:T(8,128)S(1)}, s32[20,128]{1,0:T(8,128)S(1)}, u32[]{:S(2)}, u32[]{:S(2)}) collective-permute-start(s32[20,128]{1,0:T(8,128)S(1)} %pad_add_fusion), channel_id=1, source_target_pairs={{4,8},{5,9},{6,10},{7,11},{8,4},{9,5},{10,6},{11,7},{12,16},{13,17... | collective-permute-start | bytes 30728 | tf_op jit(solution)/shard_map/ppermute | solution.py:455
  106.3 5.1 %collective-permute-start.10 = (s32[20,128]{1,0:T(8,128)S(1)}, s32[20,128]{1,0:T(8,128)S(1)}, u32[]{:S(2)}, u32[]{:S(2)}) collective-permute-start(s32[20,128]{1,0:T(8,128)S(1)} %pad_add_fusion), channel_id=1, source_target_pairs={{0,4},{4,0},{8,12},{12,8},{16,20},{20,16},{24,28},{28,24},{1,5},{5... | collective-permute-start | bytes 30728 | tf_op jit(solution)/shard_map/ppermute | solution.py:454
  109.0 5.5 %collective-permute-start.9 = (s32[20,128]{1,0:T(8,128)S(1)}, s32[20,128]{1,0:T(8,128)S(1)}, u32[]{:S(2)}, u32[]{:S(2)}) collective-permute-start(s32[20,128]{1,0:T(8,128)S(1)} %pad_add_fusion), channel_id=1, source_target_pairs={{1,2},{2,1},{0,3},{3,0},{5,6},{6,5},{4,7},{7,4},{9,10},{10,9},{8,1... | collective-permute-start | bytes 30728 | tf_op jit(solution)/shard_map/ppermute | solution.py:449
  109.0 5.5 %collective-permute-start.8 = (s32[20,128]{1,0:T(8,128)S(1)}, s32[20,128]{1,0:T(8,128)S(1)}, u32[]{:S(2)}, u32[]{:S(2)}) collective-permute-start(s32[20,128]{1,0:T(8,128)S(1)} %pad_add_fusion), channel_id=1, source_target_pairs={{0,1},{1,0},{2,3},{3,2},{4,5},{5,4},{6,7},{7,6},{8,9},{9,8},{10,11... | collective-permute-start | bytes 30728 | tf_op jit(solution)/shard_map/ppermute | solution.py:449
  111.3 4.2 %collective-permute-start.34 = (f32[4,4,128]{2,1,0:T(4,128)S(1)}, f32[4,4,128]{2,1,0:T(4,128)S(1)}, u32[]{:S(2)}, u32[]{:S(2)}) collective-permute-start(f32[4,4,128]{2,1,0:T(4,128)S(1)} %get-tuple-element.50.own), channel_id=1, source_target_pairs={{4,8},{5,9},{6,10},{7,11},{8,4},{9,5},{10,6},{11,7},{12,16},{13,17... | collective-permute-start | bytes 24584 | tf_op jit(solution)/shard_map/ppermute | solution.py:455
  111.4 4.7 %collective-permute-start.33 = (f32[4,4,128]{2,1,0:T(4,128)S(1)}, f32[4,4,128]{2,1,0:T(4,128)S(1)}, u32[]{:S(2)}, u32[]{:S(2)}) collective-permute-start(f32[4,4,128]{2,1,0:T(4,128)S(1)} %get-tuple-element.50.own), channel_id=1, source_target_pairs={{0,4},{4,0},{8,12},{12,8},{16,20},{20,16},{24,28},{28,24},{1,5},{5... | collective-permute-start | bytes 24584 | tf_op jit(solution)/shard_map/ppermute | solution.py:454
  119.3 11.0 %all-to-all-start = ((f32[32,4,128]{2,1,0:T(4,128)}), f32[32,4,128]{2,1,0:T(4,128)S(1)}, u32[]{:S(2)}, u32[]{:S(2)}) async-start(f32[32,4,128]{2,1,0:T(4,128)} %shard_map.155), calls=%async_computation | async-start | bytes 131072 | tf_op jit(solution)/shard_map/all_to_all | solution.py:584
  133.4 3.7 %collective-permute-start.37 = (f32[4,4,128]{2,1,0:T(4,128)S(1)}, f32[4,4,128]{2,1,0:T(4,128)S(1)}, u32[]{:S(2)}, u32[]{:S(2)}) collective-permute-start(f32[4,4,128]{2,1,0:T(4,128)S(1)} %shard_map.156.own), channel_id=1, source_target_pairs={{0,4},{4,0},{8,12},{12,8},{16,20},{20,16},{24,28},{28,24},{1,5},{5... | collective-permute-start | bytes 24584 | tf_op jit(solution)/shard_map/ppermute | solution.py:454
  139.5 3.7 %collective-permute-start.41 = (f32[4,4,128]{2,1,0:T(4,128)S(1)}, f32[4,4,128]{2,1,0:T(4,128)S(1)}, u32[]{:S(2)}, u32[]{:S(2)}) collective-permute-start(f32[4,4,128]{2,1,0:T(4,128)S(1)} %shard_map.157.own), channel_id=1, source_target_pairs={{0,4},{4,0},{8,12},{12,8},{16,20},{20,16},{24,28},{28,24},{1,5},{5... | collective-permute-start | bytes 24584 | tf_op jit(solution)/shard_map/ppermute | solution.py:454
  145.7 3.9 %collective-permute-start.45 = (f32[4,4,128]{2,1,0:T(4,128)S(1)}, f32[4,4,128]{2,1,0:T(4,128)S(1)}, u32[]{:S(2)}, u32[]{:S(2)}) collective-permute-start(f32[4,4,128]{2,1,0:T(4,128)S(1)} %shard_map.158.own), channel_id=1, source_target_pairs={{0,4},{4,0},{8,12},{12,8},{16,20},{20,16},{24,28},{28,24},{1,5},{5... | collective-permute-start | bytes 24584 | tf_op jit(solution)/shard_map/ppermute | solution.py:454
  153.5 3.5 %collective-permute-start.50 = (f32[16,4,128]{2,1,0:T(4,128)S(1)}, f32[16,4,128]{2,1,0:T(4,128)S(1)}, u32[]{:S(2)}, u32[]{:S(2)}) collective-permute-start(f32[16,4,128]{2,1,0:T(4,128)S(1)} %shard_map.159.own), channel_id=1, source_target_pairs={{4,8},{5,9},{6,10},{7,11},{8,4},{9,5},{10,6},{11,7},{12,16},{13,17... | collective-permute-start | bytes 98312 | tf_op jit(solution)/shard_map/ppermute | solution.py:455
  153.6 4.5 %collective-permute-start.49 = (f32[16,4,128]{2,1,0:T(4,128)S(1)}, f32[16,4,128]{2,1,0:T(4,128)S(1)}, u32[]{:S(2)}, u32[]{:S(2)}) collective-permute-start(f32[16,4,128]{2,1,0:T(4,128)S(1)} %shard_map.159.own), channel_id=1, source_target_pairs={{0,4},{4,0},{8,12},{12,8},{16,20},{20,16},{24,28},{28,24},{1,5},{5... | collective-permute-start | bytes 98312 | tf_op jit(solution)/shard_map/ppermute | solution.py:454
  161.6 4.0 %collective-permute-start.53 = (f32[16,4,128]{2,1,0:T(4,128)S(1)}, f32[16,4,128]{2,1,0:T(4,128)S(1)}, u32[]{:S(2)}, u32[]{:S(2)}) collective-permute-start(f32[16,4,128]{2,1,0:T(4,128)S(1)} %shard_map.160.own), channel_id=1, source_target_pairs={{0,4},{4,0},{8,12},{12,8},{16,20},{20,16},{24,28},{28,24},{1,5},{5... | collective-permute-start | bytes 98312 | tf_op jit(solution)/shard_map/ppermute | solution.py:454
  174.3 3.8 %collective-permute-start.57 = (f32[4,4,256]{2,1,0:T(4,128)S(1)}, f32[4,4,256]{2,1,0:T(4,128)S(1)}, u32[]{:S(2)}, u32[]{:S(2)}) collective-permute-start(f32[4,4,256]{2,1,0:T(4,128)S(1)} %get-tuple-element.55), channel_id=1, source_target_pairs={{0,4},{4,0},{8,12},{12,8},{16,20},{20,16},{24,28},{28,24},{1,5},{5... | collective-permute-start | bytes 49160 | tf_op jit(solution)/shard_map/ppermute | solution.py:454
  (48 other events, 432.4 us)

commit v2 on v1

--- a/solution.py
+++ b/solution.py
@@ -15,6 +15,8 @@
 RIM = 4
 PAD = 16
 VMEM = pl.BlockSpec(memory_space=pltpu.VMEM)
+PLAIN = pl.BlockSpec(memory_space=pltpu.VMEM)
+HBM = pl.BlockSpec(memory_space=pl.ANY)
 SMEM = pl.BlockSpec(memory_space=pltpu.SMEM)
 W_ODD, N_ODD, HAS_WEST, HAS_EAST, HAS_SOUTH, HAS_NORTH, W_AT, N_AT = range(8)
 
@@ -23,17 +25,51 @@
     return jax.ShapeDtypeStruct(shape, dtype)
 
 
-def call(kernel, outs, ins, scratch=(), specs=None, name=None):
+def constrain(x, spec):
+    if spec is VMEM:
+        return pltpu.with_memory_space_constraint(x, pltpu.VMEM)
+    if spec is HBM or spec is SMEM:
+        return pltpu.with_memory_space_constraint(x, pltpu.HBM)
+    return x
+
+
+def call(kernel, outs, ins, scratch=(), specs=None, mib=12, us=2, hold=None, far=(), loose=()):
+    hold = {} if hold is None else hold
+    outs, tree = jax.tree.flatten(outs)
     specs = specs or [VMEM] * len(ins)
-    return pl.pallas_call(
-        kernel,
-        out_shape=outs,
+    places = {x: i for i, x in enumerate(ins) if isinstance(x, str)}
+    rest = [name for name in hold if name not in places]
+    places |= {name: len(ins) + i for i, name in enumerate(rest)}
+    inputs = [hold[x] if isinstance(x, str) else x for x in ins] + [hold[name] for name in rest]
+    specs = list(specs) + [VMEM] * len(rest)
+    inputs = [constrain(x, spec) for x, spec in zip(inputs, specs)]
+    count_in, count_out = len(ins), len(outs)
+    shapes = [
+        o if o in loose else (pltpu.HBM if o in far else pltpu.VMEM)(o.shape, o.dtype) for o in outs
+    ]
+    shapes += [pltpu.VMEM(hold[name].shape, hold[name].dtype) for name in hold]
+
+    def inner(*refs):
+        first = len(inputs)
+        kernel(
+            *refs[:count_in],
+            *refs[first : first + count_out],
+            *refs[first + count_out + len(hold) :],
+        )
+
+    results = pl.pallas_call(
+        inner,
+        out_shape=shapes,
         in_specs=specs,
-        out_specs=jax.tree.map(lambda _: VMEM, outs),
+        out_specs=[HBM if o in far else VMEM for o in outs] + [VMEM] * len(hold),
         scratch_shapes=list(scratch),
-        compiler_params=pltpu.CompilerParams(vmem_limit_bytes=48 * 1024 * 1024),
-        name=name,
-    )(*ins)
+        input_output_aliases={places[name]: count_out + i for i, name in enumerate(hold)},
+        compiler_params=pltpu.CompilerParams(vmem_limit_bytes=mib * 1024 * 1024),
+        cost_estimate=pl.CostEstimate(flops=0, bytes_accessed=int(us * 3.5e6), transcendentals=0),
+    )(*inputs)
+    for name, value in zip(list(hold), results[count_out:]):
+        hold[name] = value
+    return jax.tree.unflatten(tree, results[:count_out])
 
 
 def parts_of(x):
@@ -61,7 +97,7 @@
         xs[pl.ds(base, count), i * cols : (i + 1) * cols, :] = part
 
 
-def tiles_kernel(tiles_ref, t_ref, d_ref):
+def tiles_kernel(tiles_ref, t_ref, d_ref, *again):
     slots, size = tiles_ref.shape[1], tiles_ref.shape[2]
     if size < LANES:
         t_ref[...] = jnp.zeros_like(t_ref)
@@ -80,23 +116,26 @@
                 diag = jnp.sum(jnp.where(row == col, tile, 0.0), axis=0, keepdims=True)
                 lane = lax.broadcasted_iota(jnp.int32, diag.shape, 1)
                 d_ref[r] = jnp.where(lane < size, diag, 1.0)
-
-
-def split_tiles(tiles):
+    for ref in again:
+        ref[...] = t_ref[...]
+
+
+def split_tiles(tiles, again):
     count, slots, size, _ = tiles.shape
     step = min(count, 4)
+    spec = pl.BlockSpec((step, 2 * LANES, slots * LANES), lambda i: (i, 0, 0))
+    shape = (count, 2 * LANES, slots * LANES)
     return pl.pallas_call(
         tiles_kernel,
         grid=(count // step,),
         in_specs=[pl.BlockSpec((step, slots, size, size), lambda i: (i, 0, 0, 0))],
-        out_specs=[
-            pl.BlockSpec((step, 2 * LANES, slots * LANES), lambda i: (i, 0, 0)),
-            pl.BlockSpec((step, 1, LANES), lambda i: (i, 0, 0)),
-        ],
-        out_shape=[sds((count, 2 * LANES, slots * LANES), BF16), sds((count, 1, LANES))],
-        compiler_params=pltpu.CompilerParams(vmem_limit_bytes=32 * 1024 * 1024),
+        out_specs=[spec, pl.BlockSpec((step, 1, LANES), lambda i: (i, 0, 0))] + [spec] * again,
+        out_shape=[pltpu.VMEM(shape, BF16), pltpu.VMEM((count, 1, LANES), F32)]
+        + [pltpu.HBM(shape, BF16)] * again,
+        compiler_params=pltpu.CompilerParams(vmem_limit_bytes=16 * 1024 * 1024),
+        cost_estimate=pl.CostEstimate(flops=0, bytes_accessed=2 * 4 * tiles.size, transcendentals=0),
         name="split_tiles",
-    )(tiles)
+    )(pltpu.with_memory_space_constraint(tiles, pltpu.HBM))
 
 
 def index_kernel(flags, *refs):
@@ -189,15 +228,24 @@
     out[...] = jnp.broadcast_to(total[None], out.shape)
 
 
-def chain_maps_kernel(flags, maps, out):
-    count = maps.shape[0]
-    at = flags[W_AT]
-    for v in range(count):
-        for i in range(3):
-            piece = maps[v ^ at, i]
-            hi = piece.astype(BF16)
-            out[v, i, 0:LANES] = hi
-            out[v, i, LANES : 2 * LANES] = (piece - hi.astype(F32)).astype(BF16)
+def chain_maps_kernel(order, flags, *refs):
+    *pieces, out = refs
+    position = -1
+    for piece in pieces:
+        rows = piece.shape[2]
+        for k in range(piece.shape[0]):
+            position += 1
+            v, q = flags[W_AT], flags[N_AT]
+            for bit, (axis, step) in enumerate(order):
+                if position >> bit & 1:
+                    v, q = (v ^ step, q) if axis == "wide" else (v, q ^ step)
+            for i in range(3):
+                value = piece[k, i]
+                hi = value.astype(BF16)
+                at = pl.multiple_of(q * rows, rows)
+                out[v, i, pl.ds(at, rows), :] = hi
+                at = pl.multiple_of(LANES + q * rows, rows)
+                out[v, i, pl.ds(at, rows), :] = (value - hi.astype(F32)).astype(BF16)
 
 
 def map_product(m, x):
@@ -209,7 +257,18 @@
     return jnp.take_along_axis(table, jnp.broadcast_to(lanes, table.shape), axis=1)
 
 
-def chain_kernel(flags, maps, pieces, idx, t, d, x2, groups, g1, g2, g3, g4, out, xs, ys):
+def groups_kernel(own1, own2, o1, o2, o3, o4, out):
+    count1, count2 = own1.shape[0], own2.shape[0]
+    out[0, 0:count1] = own1[...]
+    out[0, count1:] = own2[...]
+    for p, ref in enumerate((o1, o2, o3, o4)):
+        cols = ref.shape[1]
+        for i in range(count1 + count2):
+            row = ref[count1 + i // cols, i % cols : i % cols + 1, :]
+            out[p + 1, i : i + 1] = row.astype(jnp.int32)
+
+
+def chain_kernel(flags, maps, pieces, idx, t, d, x2, groups, out, xs, ys):
     blocks = maps.shape[0]
     narrow = pieces.shape[0] // blocks
     carry = None
@@ -235,30 +294,30 @@
     w_second = jnp.clip(w - 1 + 2 * w_odd, 0, blocks - 1)
     where = ((w, n), (w, n_first), (w, n_second), (w_first, n), (w_second, n))
     lane = lax.broadcasted_iota(jnp.int32, (16, LANES), 1)
-    for p, ((pw, pn), group) in enumerate(zip(where, (groups, g1, g2, g3, g4))):
+    first = groups.shape[1] - count
+    for p, (pw, pn) in enumerate(where):
         table = rows_of(ys[pw])
         for tile in range(count):
-            index = (group[tile : tile + 1, :] + pn * size) & (LANES - 1)
+            index = groups[p, first + tile : first + tile + 1, :]
+            index = (index + pn * size) & (LANES - 1)
             got = take_lanes(table, index)
             xs[p * count + tile] = jnp.where(lane < LANES // 2, got, 0.0)
     for r, ax in enumerate(apply_tiles(t, xs, idx)):
         out[r] = x2[r] + (rows_sum(xs[r], 4) - 0.5 * ax / d[r])
 
 
-def prolong_one_kernel(idx, t, d, x2, groups, g1, g2, g3, g4, own, o1, o2, o3, o4, out, xs):
+def prolong_one_kernel(idx, t, d, x2, groups, own, o1, o2, o3, o4, out, xs):
     count = x2.shape[0]
     xs[5 * count] = jnp.zeros((16, LANES), F32)
     half = LANES // 2
     lane = lax.broadcasted_iota(jnp.int32, (4, LANES), 1)
-    for p, (u, group) in enumerate(
-        zip((own, o1, o2, o3, o4), (groups, g1, g2, g3, g4))
-    ):
+    for p, u in enumerate((own, o1, o2, o3, o4)):
         tables = []
         for i in range(u.shape[0] // 2):
             wide = jnp.where(lane < half, u[2 * i], pltpu.roll(u[2 * i + 1], half, 1))
             tables.append(rows_of(wide))
         for tile in range(count):
-            index = group[tile : tile + 1, :]
+            index = groups[p, tile : tile + 1, :]
             got = take_lanes(tables[0], index & (LANES - 1))
             for i in range(1, len(tables)):
                 more = take_lanes(tables[i], index & (LANES - 1))
@@ -313,15 +372,30 @@
     return jnp.concatenate([field, rim], axis=0)
 
 
-def fine_first_kernel(flags, block, east, north, first, second):
-    e, n = live_weights(flags, east[...], north[...])
-    narrow_rims(flags, [*(block[c] for c in range(block.shape[0])), e, n], first, second)
-
-
-def fine_second_kernel(flags, block, east, north, o1, o2, ext, first, second):
-    e, n = live_weights(flags, east[...], north[...])
-    for i, field in enumerate([*(block[c] for c in range(block.shape[0])), e, n]):
-        wider = with_sides(flags, field, o1, o2, i)
+def fine_first_kernel(
+    flags, block, east, north, forward, gain, backward, fields, first, second, piece, edges, sems
+):
+    cols = block.shape[0]
+    rows = piece.shape[2]
+    at = pl.multiple_of(flags[N_AT] * rows, rows)
+    copies = [
+        (block, fields.at[0:cols]),
+        (east, edges.at[0]),
+        (north, edges.at[1]),
+        *((m.at[0, pl.ds(at, rows)], piece.at[0, i]) for i, m in enumerate((forward, gain, backward))),
+    ]
+    copies = [pltpu.make_async_copy(a, b, sems.at[i]) for i, (a, b) in enumerate(copies)]
+    for copy in copies:
+        copy.start()
+    for copy in copies:
+        copy.wait()
+    fields[cols], fields[cols + 1] = live_weights(flags, edges[0], edges[1])
+    narrow_rims(flags, [fields[c] for c in range(cols + 2)], first, second)
+
+
+def fine_second_kernel(flags, fields, o1, o2, ext, first, second):
+    for i in range(fields.shape[0]):
+        wider = with_sides(flags, fields[i], o1, o2, i)
         ext[i] = wider
         wide_rims(flags, wider, i, first, second)
 
@@ -336,7 +410,7 @@
     )
 
 
-def fine_down_kernel(flags, ext, o1, o2, groups, d1, keep, b1, first, q_ref):
+def fine_down_kernel(flags, ext, o1, o2, groups, d1, near1, near2, far, b1, first, q_ref, keep, sem):
     cols = ext.shape[0] - 2
     rows = ext.shape[1]
     e = with_rows(flags, ext[cols], o1, o2, cols)
@@ -356,6 +430,8 @@
         q = 0.5 * (rest + beside(rest * inv, e, n))
         for i, part in enumerate(parts_of(q[:rows, :LANES])):
             q_ref[i * cols + c] = part
+    copy = pltpu.make_async_copy(keep, far, sem.at[0])
+    copy.start()
     count = b1.shape[0]
     step = 4
 
@@ -387,7 +463,13 @@
     for c in range(cols):
         value = total[c * count : (c + 1) * count]
         b1[:, c, :] = value
-        first[:, c, :] = JACOBI * value / d1[:, 0, :]
+        first[0:count, c, :] = JACOBI * value / d1[:, 0, :]
+    groups = [near1[i : i + 1, :] for i in range(count)] + [
+        near2[i : i + 1, :] for i in range(near2.shape[0])
+    ]
+    for i, group in enumerate(groups):
+        first[count + i // cols, i % cols : i % cols + 1, :] = group.astype(F32)
+    copy.wait()
 
 
 def fine_spread_kernel(flags, t, idx, d, b, groups, own, o1, o2, o3, o4, spread, first, second, xs, us):
@@ -409,15 +491,9 @@
     narrow_rims(flags, [spread[c] for c in range(cols)], first, second)
 
 
-def fine_sides_kernel(flags, spread, o1, o2, ext, first, second):
-    for c in range(spread.shape[0]):
-        wider = with_sides(flags, spread[c], o1, o2, c)
-        ext[c] = wider
-        wide_rims(flags, wider, c, first, second)
-
-
-def fine_up_kernel(flags, keep, ext, o1, o2, out):
+def fine_up_kernel(flags, keep, ext, o1, o2, far, out, sems):
     cols = out.shape[0]
+    copies = []
     e, n, inv = keep[2 * cols], keep[2 * cols + 1], keep[2 * cols + 2]
     for c in range(cols):
         b = keep[cols + c]
@@ -426,6 +502,10 @@
         for _ in range(2):
             x = (1.0 - JACOBI) * x + JACOBI * (b + beside(x, e, n)) * inv
         out[c] = x[: out.shape[1], :LANES]
+        copies.append(pltpu.make_async_copy(out.at[c], far.at[c], sems.at[c]))
+        copies[-1].start()
+    for copy in copies:
+        copy.wait()
 
 
 def pairs(start, count):
@@ -490,138 +570,217 @@
         [w % 2, n % 2, w > 0, w < wide - 1, n > 0, n < narrow - 1, w, n, jnp.int32(level3)]
     ).astype(jnp.int32)
 
+    order = [("wide", 1 << i) for i in reversed(range((wide - 1).bit_length()))]
+    order += [("narrow", 1 << i) for i in reversed(range((narrow - 1).bit_length()))]
+    share = chain_forward.shape[1] // narrow
+    held = []
+    done = []
+
+    def swap(x, axis, step):
+        return lax.ppermute(x, axis, [(i, i ^ step) for i in range(lax.axis_size(axis))])
+
+    def gather_step(*anchor):
+        step = order[len(done)]
+        merged = held if len(done) == len(order) - 1 or len(held) == 1 else [jnp.concatenate(held, axis=0)]
+        merged, anchor = lax.optimization_barrier((merged, anchor))
+        held[:] = merged + [swap(m, *step) for m in merged]
+        done.append(step)
+        return anchor
+
     rim = sds((cols + 2, RIM, LANES))
-    first, second = call(
-        fine_first_kernel, [rim, rim], (flags, block, east, north), specs=[SMEM] + [VMEM] * 3
-    )
+    fields, first, second, piece = call(
+        fine_first_kernel,
+        [sds((cols + 2, rows, LANES)), rim, rim, sds((1, 3, share, LANES))],
+        (flags, block, east, north, chain_forward, chain_gain, chain_backward),
+        scratch=[pltpu.VMEM((2, rows, LANES), F32), pltpu.SemaphoreType.DMA((6,))],
+        specs=[SMEM] + [HBM] * 6,
+    )
+    held.append(piece)
+    first, second = gather_step(first, second)
     o1, o2 = exchange_narrow(first, second, route)
 
-    tiles1, d1 = split_tiles(tiles_one)
-    tiles2, d2 = split_tiles(tiles_two)
     idx1, idx2 = call(
         index_kernel,
         [sds((count1, slots), jnp.int32), sds((count2, slots), jnp.int32)],
         (flags, columns_one, live_one, columns_two, live_two),
         specs=[SMEM] + [VMEM] * 4,
-    )
-    maps = jnp.stack([chain_forward, chain_gain, chain_backward], axis=1)
-    step = 1
-    while step < wide:
-        maps = jnp.concatenate(
-            [maps, lax.ppermute(maps, "wide", [(i, i ^ step) for i in range(wide)])], axis=0
-        )
-        step *= 2
-    chain = call(
-        chain_maps_kernel,
-        sds((wide, 3, 2 * LANES, LANES), BF16),
-        (flags, maps),
-        specs=[SMEM, VMEM],
+        us=0.5,
+    )
+    tiles2, d2 = split_tiles(tiles_two, 0)
+    groups1 = coarse_groups.reshape(count1, LANES)
+    groups2 = jnp.pad(coarser_groups.reshape(count2, size2), ((0, 0), (0, LANES - size2)))
+    o1, idx1, idx2, tiles2, d2, groups1, groups2 = lax.optimization_barrier(
+        (o1, idx1, idx2, tiles2, d2, groups1, groups2)
     )
 
     rim = sds((cols + 2, RIM, 2 * LANES))
     ext, first, second = call(
         fine_second_kernel,
         [sds((cols + 2, rows, 2 * LANES)), rim, rim],
-        (flags, block, east, north, o1, o2),
-        specs=[SMEM] + [VMEM] * 5,
-    )
+        (flags, fields, o1, o2),
+        specs=[SMEM] + [VMEM] * 3,
+    )
+    first, second = gather_step(first, second)
     o1, o2 = exchange_wide(first, second, route)
     field1 = sds((count1, cols, LANES))
     field2 = sds((count2, cols, LANES))
+    tiles1, d1, tiles1_far = split_tiles(tiles_one, 1)
+    more = -(-(count1 + count2) // cols)
+    hold = {"t1": tiles1, "d1": d1}
+    kept = sds((2 * cols + 3, rows + PAD, 2 * LANES))
     keep, b1, x1 = call(
         fine_down_kernel,
-        [sds((2 * cols + 3, rows + PAD, 2 * LANES)), field1, field1],
-        (flags, ext, o1, o2, fine_groups, d1),
-        scratch=[pltpu.VMEM((3 * cols, rows, LANES), F32)],
-        specs=[SMEM] + [VMEM] * 5,
-    )
-
-    groups1 = coarse_groups.reshape(count1, LANES)
-    groups2 = jnp.pad(coarser_groups.reshape(count2, size2), ((0, 0), (0, LANES - size2)))
+        [kept, field1, sds((count1 + more, cols, LANES))],
+        (flags, ext, o1, o2, fine_groups, "d1", groups1, groups2),
+        scratch=[
+            pltpu.VMEM((3 * cols, rows, LANES), F32),
+            pltpu.VMEM(kept.shape, F32),
+            pltpu.SemaphoreType.DMA((1,)),
+        ],
+        specs=[SMEM] + [VMEM] * 7,
+        mib=16,
+        us=7,
+        hold=hold,
+        far=(kept,),
+    )
+    hold["b1"] = b1
+
     xs1 = [pltpu.VMEM((5 * count1 + 1, 16, LANES), F32)]
     xs2 = [pltpu.VMEM((5 * count2 + 1, 16, LANES), F32)]
     lead = [SMEM]
-    near_groups = exchange(jnp.concatenate([groups1, groups2], axis=0), route)
-    near1 = tuple(g[:count1] for g in near_groups)
-    near2 = tuple(g[count1:] for g in near_groups)
-
-    def smooth(idx, t, d, b, x, xs, like):
-        return call(
-            smooth_kernel, like, (idx, t, d, b, x, *exchange(x, route)), xs, lead + [VMEM] * 8
-        )
-
-    x2 = smooth(idx1, tiles1, d1, b1, x1, xs1, field1)
+
+    def smooth(level, x):
+        idx, like, xs = (idx1, field1, xs1) if level == 1 else (idx2, field2, xs2)
+        near = exchange(x, route)
+        ins = (idx, f"t{level}", f"d{level}", f"b{level}", x, *near)
+        return call(smooth_kernel, like, ins, xs, lead + [VMEM] * 8, hold=hold), near
+
+    (x1,) = gather_step(x1)
+    x2, near = smooth(1, x1)
+    groups = call(
+        groups_kernel,
+        sds((5, count1 + count2, LANES), jnp.int32),
+        (groups1, groups2, *near),
+        specs=[VMEM] * 6,
+        us=1,
+    )
+    (x2,) = gather_step(x2)
+    near = exchange(x2, route)
+    hold |= {"x2": x2, "groups": groups, "d2": d2}
     left, scaled = call(
         residual_kernel,
         [field1, field1],
-        (idx1, tiles1, d1, b1, x2, *exchange(x2, route)),
+        (idx1, "t1", "d1", "b1", "x2", *near),
         xs1,
         lead + [VMEM] * 8,
-    )
+        hold=hold,
+    )
+    while len(done) < len(order):
+        (scaled,) = gather_step(scaled)
     b2, y1 = call(
         restrict_one_kernel,
         [field2, field2],
-        (idx1, tiles1, left, groups1, d2, scaled, *exchange(scaled, route)),
+        (idx1, "t1", left, groups1, "d2", scaled, *exchange(scaled, route)),
         xs1,
         lead + [VMEM] * 9,
-    )
-
-    y2 = smooth(idx2, tiles2, d2, b2, y1, xs2, field2)
+        hold=hold,
+    )
+
+    del hold["t1"]
+    hold |= {"b2": b2, "t2": tiles2}
+    y2, _ = smooth(2, y1)
+    maps, y2 = lax.optimization_barrier((held, y2))
+    near = exchange(y2, route)
+    chain_shape = sds((wide, 3, 2 * LANES, LANES), BF16)
+    big = wide > 16
+    chain = call(
+        functools.partial(chain_maps_kernel, order),
+        chain_shape,
+        (flags, *maps),
+        specs=[SMEM] + [PLAIN if big else VMEM] * len(maps),
+        mib=48 if big else 12,
+        us=0.7,
+        loose=(chain_shape,) if big else (),
+    )
+    if not big:
+        hold["chain"] = chain
+    hold["y2"] = y2
     left, scaled = call(
         residual_kernel,
         [field2, field2],
-        (idx2, tiles2, d2, b2, y2, *exchange(y2, route)),
+        (idx2, "t2", "d2", "b2", "y2", *near),
         xs2,
         lead + [VMEM] * 8,
+        us=1,
+        hold=hold,
     )
     out3 = call(
         restrict_two_kernel,
         sds((wide * narrow, cols, LANES)),
-        (flags, idx2, tiles2, left, groups2, scaled, *exchange(scaled, route)),
+        (flags, idx2, "t2", left, groups2, scaled, *exchange(scaled, route)),
         xs2,
         [SMEM, SMEM] + [VMEM] * 8,
+        hold=hold,
     )
     pieces = lax.all_to_all(out3, ("wide", "narrow"), 0, 0)
     y3 = call(
         chain_kernel,
         field2,
-        (flags, chain, pieces, idx2, tiles2, d2, y2, groups2, *near2),
+        (flags, chain if big else "chain", pieces, idx2, "t2", "d2", "y2", "groups"),
         xs2 + [pltpu.VMEM((wide, cols, LANES), F32)],
-        [SMEM, VMEM, VMEM, SMEM] + [VMEM] * 8,
-    )
-    y4 = smooth(idx2, tiles2, d2, b2, y3, xs2, field2)
-    y5 = smooth(idx2, tiles2, d2, b2, y4, xs2, field2)
-
+        [SMEM, PLAIN if big else VMEM, VMEM, SMEM] + [VMEM] * 4,
+        mib=32 if big else 12,
+        us=3,
+        hold=hold,
+    )
+    hold.pop("chain", None)
+    y4, _ = smooth(2, y3)
+    y5, _ = smooth(2, y4)
+
+    for name in ("t2", "d2", "b2", "y2"):
+        del hold[name]
+    hold["t1"] = tiles1_far
     x3 = call(
         prolong_one_kernel,
         field1,
-        (idx1, tiles1, d1, x2, groups1, *near1, y5, *exchange(y5, route)),
+        (idx1, "t1", "d1", "x2", "groups", y5, *exchange(y5, route)),
         xs1,
-        lead + [VMEM] * 13,
-    )
-    x4 = smooth(idx1, tiles1, d1, b1, x3, xs1, field1)
+        lead + [VMEM] * 9,
+        hold=hold,
+    )
+    del hold["x2"], hold["groups"]
+    x4, _ = smooth(1, x3)
     rim = sds((cols, RIM, LANES))
     spread, first, second = call(
         fine_spread_kernel,
         [sds((cols, rows, LANES)), rim, rim],
-        (flags, tiles1, idx1, d1, b1, fine_groups, x4, *exchange(x4, route)),
+        (flags, "t1", idx1, "d1", "b1", fine_groups, x4, *exchange(x4, route)),
         xs1 + [pltpu.VMEM((count1, cols, LANES), F32)],
         [SMEM, VMEM, SMEM] + [VMEM] * 8,
+        us=3,
+        hold=hold,
     )
     o1, o2 = exchange_narrow(first, second, route)
     rim = sds((cols, RIM, 2 * LANES))
+    for name in ("t1", "d1", "b1"):
+        del hold[name]
     ext, first, second = call(
-        fine_sides_kernel,
+        fine_second_kernel,
         [sds((cols, rows, 2 * LANES)), rim, rim],
         (flags, spread, o1, o2),
         specs=[SMEM] + [VMEM] * 3,
+        us=1,
+        hold=hold,
     )
     o1, o2 = exchange_wide(first, second, route)
+    whole = sds((cols, rows, LANES))
     return call(
         fine_up_kernel,
-        sds((cols, rows, LANES)),
+        whole,
         (flags, keep, ext, o1, o2),
+        scratch=[pltpu.VMEM(whole.shape, F32), pltpu.SemaphoreType.DMA((cols,))],
         specs=[SMEM] + [VMEM] * 4,
+        far=(whole,),
     )
 
 

time: 181 us -> 147 us (0.81)
  starting transfers between devices: 81.6 us -> 49.4 us
  waiting for transfers between devices: 46.8 us -> 34.8 us
  blocking collectives: 0 us -> 10.5 us
  Pallas kernels: 39.1 us -> 47 us
  other arithmetic: 4.99 us -> 0.06 us
  local copies, waits for them, and re-layouts: 8 us -> 4.34 us
    ppermute x14 -> x13, starting transfers between devices: 53 us -> 26.5 us  [exchange_wide(): lax.ppermute(first, 'wide', route[2])]
    ppermute x3 -> x6, waiting for transfers between devices: 13.4 us -> 0.03 us  [swap(): lax.ppermute(x, axis, [(i, i ^ step) for i in range(lax.axis_size(axis))])]
    all_to_all x0 -> x1, blocking collectives: none -> 10.5 us  [body(): pieces = lax.all_to_all(out3, ('wide', 'narrow'), 0, 0)]
    pallas_call x2, Pallas kernels: 1 us -> 6.32 us  [split_tiles(): pl.pallas_call(tiles_kernel, grid=(count // step,), in_specs=[pl.BlockSpe...]
    all_to_all x1 -> x0, waiting for transfers between devices: 5.21 us -> none  [body(): pieces = lax.all_to_all(out3, ('wide', 'narrow'), 0, 0)]
    unnamed x42 -> x18, local copies, waits for them, and re-layouts: 7.82 us -> 2.91 us
    ppermute x14 -> x13, waiting for transfers between devices: 10.9 us -> 15.3 us  [exchange_wide(): lax.ppermute(first, 'wide', route[2])]
    concatenate x4 -> x3, other arithmetic: 4.03 us -> 0.06 us  [gather_step(): jnp.concatenate(held, axis=0)]
  transfers between devices with their start and end apart: 60 -> 58, of which waited for: 27 -> 23; matrix products, arithmetic and copies ran while one was open for 1% -> 2% of each run, Pallas kernels for 13% -> 18%
where the time goes in v2:
time: 147 us
  starting transfers between devices  49.4 us (34%)
  Pallas kernels  47 us (32%)
  waiting for transfers between devices  34.8 us (24%)
  blocking collectives  10.5 us (7%)
  local copies, waits for them, and re-layouts  4.34 us (3%)
    pallas_call x20, Pallas kernels, call(): pl.pallas_call(inner, out_shape=shapes, in_specs=specs, out_specs=[HBM if...  40.7 us
    ppermute x13, starting transfers between devices, exchange_wide(): lax.ppermute(first, 'wide', route[2])  26.5 us
    ppermute x13, waiting for transfers between devices, exchange_narrow(): lax.ppermute(second, 'narrow', route[1])  19.2 us
    ppermute x13, waiting for transfers between devices, exchange_wide(): lax.ppermute(first, 'wide', route[2])  15.3 us
    all_to_all x1, blocking collectives, body(): pieces = lax.all_to_all(out3, ('wide', 'narrow'), 0, 0)  10.5 us
    ppermute x6, starting transfers between devices, swap(): lax.ppermute(x, axis, [(i, i ^ step) for i in range(lax.axis_size(axis))])  9.53 us
    ppermute x13, starting transfers between devices, exchange_narrow(): lax.ppermute(first, 'narrow', route[0])  9.31 us
    pallas_call x2, Pallas kernels, split_tiles(): pl.pallas_call(tiles_kernel, grid=(count // step,), in_specs=[pl.BlockSpe...  6.32 us
  transfers between devices with their start and end apart: 58, of which 23 were waited for; matrix products, arithmetic and copies ran while one was open for 2% of the time, Pallas kernels for 18%

profile of v2, /device:TPU:0, one launch (start us, length us, event | category | flops | bytes accessed | tf_op | source)
XLA Modules:
  0.0 146.6 jit_solution(9068095331370195070)
XLA Ops:
  0.7 1.8 %shard_map.145 = (f32[6,128,128]{2,1,0:T(8,128)S(1)}, f32[6,4,128]{2,1,0:T(4,128)S(1)}, f32[6,4,128]{2,1,0:T(4,128)S(1)}, f32[1,3,32,128]{3,2,1,0:T(8,128)S(1)}) custom-call(s32[9]{0:T(128)} %stack.51.refs_0_, f32[4,128,128]{2,1,0:T(8,128)} %refs_1_.2, f32[128,128]{1,0:T(8,128)} %refs_2_.2, f32[128,128]{1,0:T(8,128)} %refs_3_.2, f32[1,128,128]{2,1,0:T(8,128)} %refs_4_.3, ...), custom_call_target="tpu_custom_call" | custom-call | bytes 7000000 | tf_op jit(solution)/shard_map/pallas_call | solution.py:60
  2.5 4.1 %collective-permute-start.2 = (f32[1,3,32,128]{3,2,1,0:T(8,128)S(1)}, f32[1,3,32,128]{3,2,1,0:T(8,128)S(1)}, u32[]{:S(2)}, u32[]{:S(2)}) collective-permute-start(f32[1,3,32,128]{3,2,1,0:T(8,128)S(1)} %get-tuple-element.146), channel_id=1, source_target_pairs={{0,16},{4,20},{8,24},{12,28},{16,0},{20,4},{24,8},{28,12},{1,17},{... | collective-permute-start | bytes 147464 | tf_op jit(solution)/shard_map/ppermute | solution.py:580
  6.6 1.6 %collective-permute-start.1 = (f32[6,4,128]{2,1,0:T(4,128)S(1)}, f32[6,4,128]{2,1,0:T(4,128)S(1)}, u32[]{:S(2)}, u32[]{:S(2)}) collective-permute-start(f32[6,4,128]{2,1,0:T(4,128)S(1)} %get-tuple-element.144), channel_id=1, source_target_pairs={{1,2},{2,1},{0,3},{3,0},{5,6},{6,5},{4,7},{7,4},{9,10},{10,9},{8,1... | collective-permute-start | bytes 36872 | tf_op jit(solution)/shard_map/ppermute | solution.py:529
  14.8 1.6 %collective-permute-start.5 = (f32[2,3,32,128]{3,2,1,0:T(8,128)S(1)}, f32[2,3,32,128]{3,2,1,0:T(8,128)S(1)}, u32[]{:S(2)}, u32[]{:S(2)}) collective-permute-start(f32[2,3,32,128]{3,2,1,0:T(8,128)S(1)} %pad_maximum_fusion.2), channel_id=1, source_target_pairs={{0,8},{4,12},{8,0},{12,4},{16,24},{20,28},{24,16},{28,20},{1,9},{5... | collective-permute-start | bytes 294920 | tf_op jit(solution)/shard_map/ppermute | solution.py:580
  17.9 5.1 %split_tiles.3 = (bf16[16,256,512]{2,1,0:T(8,128)(2,1)S(1)}, f32[16,1,128]{2,1,0:T(1,128)S(1)}, bf16[16,256,512]{2,1,0:T(8,128)(2,1)}) custom-call(f32[16,4,128,128]{3,2,1,0:T(8,128)} %tiles_ref.3), custom_call_target="tpu_custom_call" | custom-call | bytes 8388608 | tf_op jit(solution)/shard_map/split_tiles/pallas_call | solution.py:128
  23.0 9.3 %shard_map.148 = (f32[11,144,256]{2,1,0:T(8,128)}, f32[16,4,128]{2,1,0:T(4,128)S(1)}, f32[21,4,128]{2,1,0:T(4,128)S(1)}, bf16[16,256,512]{2,1,0:T(8,128)(2,1)S(1)}, f32[16,1,128]{2,1,0:T(1,128)S(1)}) custom-call(s32[9]{0:T(128)} %stack.51.refs_0_, f32[6,128,256]{2,1,0:T(8,128)S(1)} %get-tuple-element.145.refs_1_, ...), custom_call_target="tpu_custom_call", output_to_operand_aliasing={{3}: (8, {}), {4}: (5, {})} | custom-call | bytes 24500000 | tf_op jit(solution)/shard_map/pallas_call | solution.py:60
  32.4 2.0 %collective-permute-start.10 = (f32[4,3,32,128]{3,2,1,0:T(8,128)S(1)}, f32[4,3,32,128]{3,2,1,0:T(8,128)S(1)}, u32[]{:S(2)}, u32[]{:S(2)}) collective-permute-start(f32[4,3,32,128]{3,2,1,0:T(8,128)S(1)} %pad_maximum_fusion.1), channel_id=1, source_target_pairs={{0,4},{4,0},{8,12},{12,8},{16,20},{20,16},{24,28},{28,24},{1,5},{5... | collective-permute-start | bytes 589832 | tf_op jit(solution)/shard_map/ppermute | solution.py:580
  34.4 1.9 %collective-permute-start.8 = (f32[21,4,128]{2,1,0:T(4,128)S(1)}, f32[21,4,128]{2,1,0:T(4,128)S(1)}, u32[]{:S(2)}, u32[]{:S(2)}) collective-permute-start(f32[21,4,128]{2,1,0:T(4,128)S(1)} %get-tuple-element.165.refs_4_), channel_id=1, source_target_pairs={{0,4},{4,0},{8,12},{12,8},{16,20},{20,16},{24,28},{28,24},{1,5},{5... | collective-permute-start | bytes 129032 | tf_op jit(solution)/shard_map/ppermute | solution.py:534
  36.9 3.8 %collective-permute-done.8.refs_7_.refs_4_ = f32[21,4,128]{2,1,0:T(4,128)S(1)} collective-permute-done((f32[21,4,128]{2,1,0:T(4,128)S(1)}, f32[21,4,128]{2,1,0:T(4,128)S(1)}, u32[]{:S(2)}, u32[]{:S(2)}) %collective-permute-start.8) | collective-permute-done | bytes 43040 | tf_op jit(solution)/shard_map/ppermute | solution.py:534
  40.7 2.0 %shard_map.149 = (f32[16,4,128]{2,1,0:T(4,128)S(1)}, bf16[16,256,512]{2,1,0:T(8,128)(2,1)S(1)}, f32[16,1,128]{2,1,0:T(1,128)S(1)}, f32[16,4,128]{2,1,0:T(4,128)S(1)}) custom-call(s32[16,4]{1,0:T(8,128)} %copy-done.2, bf16[16,256,512]{2,1,0:T(8,128)(2,1)S(1)} %get-tuple-element.160.refs_1_, ...), custom_call_target="tpu_custom_call", output_to_operand_aliasing={{1}: (1, {}), {2}: (2, {}), {3}: (3, {})} | custom-call | bytes 7000000 | tf_op jit(solution)/shard_map/pallas_call | solution.py:60
  43.4 3.0 %collective-permute-start.13 = (f32[16,4,128]{2,1,0:T(4,128)S(1)}, f32[16,4,128]{2,1,0:T(4,128)S(1)}, u32[]{:S(2)}, u32[]{:S(2)}) collective-permute-start(f32[16,4,128]{2,1,0:T(4,128)S(1)} %get-tuple-element.171.refs_4_), channel_id=1, source_target_pairs={{0,4},{4,0},{8,12},{12,8},{16,20},{20,16},{24,28},{28,24},{1,5},{5... | collective-permute-start | bytes 98312 | tf_op jit(solution)/shard_map/ppermute | solution.py:534
  46.4 1.6 %collective-permute-start.11 = (f32[16,4,128]{2,1,0:T(4,128)S(1)}, f32[16,4,128]{2,1,0:T(4,128)S(1)}, u32[]{:S(2)}, u32[]{:S(2)}) collective-permute-start(f32[16,4,128]{2,1,0:T(4,128)S(1)} %get-tuple-element.171.refs_4_), channel_id=1, source_target_pairs={{0,1},{1,0},{2,3},{3,2},{4,5},{5,4},{6,7},{7,6},{8,9},{9,8},{10,11... | collective-permute-start | bytes 98312 | tf_op jit(solution)/shard_map/ppermute | solution.py:529
  48.3 4.7 %collective-permute-done.12.refs_6_ = f32[16,4,128]{2,1,0:T(4,128)S(1)} collective-permute-done((f32[16,4,128]{2,1,0:T(4,128)S(1)}, f32[16,4,128]{2,1,0:T(4,128)S(1)}, u32[]{:S(2)}, u32[]{:S(2)}) %collective-permute-start.12) | collective-permute-done | bytes 32800 | tf_op jit(solution)/shard_map/ppermute | solution.py:529
  53.0 2.0 %shard_map.151 = (f32[16,4,128]{2,1,0:T(4,128)S(1)}, f32[16,4,128]{2,1,0:T(4,128)S(1)}, bf16[16,256,512]{2,1,0:T(8,128)(2,1)S(1)}, f32[16,1,128]{2,1,0:T(1,128)S...) custom-call(s32[16,4]{1,0:T(8,128)} %copy-done.2, ...), custom_call_target="tpu_custom_call", output_to_operand_aliasing={{2}: (1, {}), {3}: (2, {}), {4}: (3, {}), {5}: (4, {}), {6}... | custom-call | bytes 7000000 | tf_op jit(solution)/shard_map/pallas_call | solution.py:60
  59.0 1.7 %collective-permute-done.18.refs_8_ = f32[16,4,128]{2,1,0:T(4,128)S(1)} collective-permute-done((f32[16,4,128]{2,1,0:T(4,128)S(1)}, f32[16,4,128]{2,1,0:T(4,128)S(1)}, u32[]{:S(2)}, u32[]{:S(2)}) %collective-permute-start.18) | collective-permute-done | bytes 32800 | tf_op jit(solution)/shard_map/ppermute | solution.py:534
  62.0 2.5 %shard_map.152 = (f32[4,4,128]{2,1,0:T(4,128)S(1)}, f32[4,4,128]{2,1,0:T(4,128)S(1)}, bf16[16,256,512]{2,1,0:T(8,128)(2,1)S(1)}, f32[16,1,128]{2,1,0:T(1,128)S(1...) custom-call(s32[16,4]{1,0:T(8,128)} %copy-done.2, ...), custom_call_target="tpu_custom_call", output_to_operand_aliasing={{2}: (1, {}), {3}: (10, {}), {4}: (11, {}), {5}: (12, {}), ... | custom-call | bytes 7000000 | tf_op jit(solution)/shard_map/pallas_call | solution.py:60
  64.6 2.3 %collective-permute-start.22 = (f32[4,4,128]{2,1,0:T(4,128)S(1)}, f32[4,4,128]{2,1,0:T(4,128)S(1)}, u32[]{:S(2)}, u32[]{:S(2)}) collective-permute-start(f32[4,4,128]{2,1,0:T(4,128)S(1)} %get-tuple-element.185.refs_4_), channel_id=1, source_target_pairs={{0,4},{4,0},{8,12},{12,8},{16,20},{20,16},{24,28},{28,24},{1,5},{5... | collective-permute-start | bytes 24584 | tf_op jit(solution)/shard_map/ppermute | solution.py:534
  71.2 2.6 %collective-permute-start.28 = (f32[4,4,128]{2,1,0:T(4,128)S(1)}, f32[4,4,128]{2,1,0:T(4,128)S(1)}, u32[]{:S(2)}, u32[]{:S(2)}) collective-permute-start(f32[4,4,128]{2,1,0:T(4,128)S(1)} %get-tuple-element.196.refs_4_), channel_id=1, source_target_pairs={{0,4},{4,0},{8,12},{12,8},{16,20},{20,16},{24,28},{28,24},{1,5},{5... | collective-permute-start | bytes 24584 | tf_op jit(solution)/shard_map/ppermute | solution.py:534
  78.0 1.9 %collective-permute-start.32 = (f32[4,4,128]{2,1,0:T(4,128)S(1)}, f32[4,4,128]{2,1,0:T(4,128)S(1)}, u32[]{:S(2)}, u32[]{:S(2)}) collective-permute-start(f32[4,4,128]{2,1,0:T(4,128)S(1)} %get-tuple-element.207.refs_5_), channel_id=1, source_target_pairs={{0,4},{4,0},{8,12},{12,8},{16,20},{20,16},{24,28},{28,24},{1,5},{5... | collective-permute-start | bytes 24584 | tf_op jit(solution)/shard_map/ppermute | solution.py:534
  84.3 10.5 %all_to_all.5.refs_2_ = f32[32,4,128]{2,1,0:T(4,128)S(1)} all-to-all(f32[32,4,128]{2,1,0:T(4,128)S(1)} %get-tuple-element.217), channel_id=1, replica_groups=mesh['wide'=8,'narrow'=4] {'wide','narrow'}, dimensions={0} | all-to-all | bytes 131072 | tf_op jit(solution)/shard_map/all_to_all | solution.py:725
  94.7 3.1 %shard_map.157 = (f32[4,4,128]{2,1,0:T(4,128)S(1)}, f32[16,1,128]{2,1,0:T(1,128)S(1)}, f32[16,4,128]{2,1,0:T(4,128)S(1)}, f32[16,4,128]{2,1,0:T(4,128)S(1)}, s32...) custom-call(s32[9]{0:T(128)} %stack.51.refs_0_, ...), custom_call_target="tpu_custom_call", output_to_operand_aliasing={{1}: (8, {}), {2}: (9, {}), {3}: (10, {}), {4}: (7, {}), {5... | custom-call | bytes 10500000 | tf_op jit(solution)/shard_map/pallas_call | solution.py:60
  98.1 2.0 %collective-permute-start.36 = (f32[4,4,128]{2,1,0:T(4,128)S(1)}, f32[4,4,128]{2,1,0:T(4,128)S(1)}, u32[]{:S(2)}, u32[]{:S(2)}) collective-permute-start(f32[4,4,128]{2,1,0:T(4,128)S(1)} %get-tuple-element.229.refs_4_), channel_id=1, source_target_pairs={{0,4},{4,0},{8,12},{12,8},{16,20},{20,16},{24,28},{28,24},{1,5},{5... | collective-permute-start | bytes 24584 | tf_op jit(solution)/shard_map/ppermute | solution.py:534
  104.3 2.1 %collective-permute-start.40 = (f32[4,4,128]{2,1,0:T(4,128)S(1)}, f32[4,4,128]{2,1,0:T(4,128)S(1)}, u32[]{:S(2)}, u32[]{:S(2)}) collective-permute-start(f32[4,4,128]{2,1,0:T(4,128)S(1)} %get-tuple-element.238.refs_4_), channel_id=1, source_target_pairs={{0,4},{4,0},{8,12},{12,8},{16,20},{20,16},{24,28},{28,24},{1,5},{5... | collective-permute-start | bytes 24584 | tf_op jit(solution)/shard_map/ppermute | solution.py:534
  110.6 2.2 %collective-permute-start.44 = (f32[4,4,128]{2,1,0:T(4,128)S(1)}, f32[4,4,128]{2,1,0:T(4,128)S(1)}, u32[]{:S(2)}, u32[]{:S(2)}) collective-permute-start(f32[4,4,128]{2,1,0:T(4,128)S(1)} %get-tuple-element.247.refs_5_), channel_id=1, source_target_pairs={{0,4},{4,0},{8,12},{12,8},{16,20},{20,16},{24,28},{28,24},{1,5},{5... | collective-permute-start | bytes 24584 | tf_op jit(solution)/shard_map/ppermute | solution.py:534
  115.9 2.6 %shard_map.160 = (f32[16,4,128]{2,1,0:T(4,128)S(1)}, f32[16,1,128]{2,1,0:T(1,128)S(1)}, f32[16,4,128]{2,1,0:T(4,128)S(1)}, f32[16,4,128]{2,1,0:T(4,128)S(1)}, s3...) custom-call(s32[16,4]{1,0:T(8,128)} %copy-done.2, ...), custom_call_target="tpu_custom_call", output_to_operand_aliasing={{1}: (2, {}), {2}: (10, {}), {3}: (3, {}), {4}: (4, {}), {5... | custom-call | bytes 7000000 | tf_op jit(solution)/shard_map/pallas_call | solution.py:60
  118.6 2.6 %collective-permute-start.48 = (f32[16,4,128]{2,1,0:T(4,128)S(1)}, f32[16,4,128]{2,1,0:T(4,128)S(1)}, u32[]{:S(2)}, u32[]{:S(2)}) collective-permute-start(f32[16,4,128]{2,1,0:T(4,128)S(1)} %get-tuple-element.252.refs_4_), channel_id=1, source_target_pairs={{0,4},{4,0},{8,12},{12,8},{16,20},{20,16},{24,28},{28,24},{1,5},{5... | collective-permute-start | bytes 98312 | tf_op jit(solution)/shard_map/ppermute | solution.py:534
  124.6 2.2 %shard_map.161 = (f32[16,4,128]{2,1,0:T(4,128)S(1)}, f32[16,1,128]{2,1,0:T(1,128)S(1)}, f32[16,4,128]{2,1,0:T(4,128)S(1)}, bf16[16,256,512]{2,1,0:T(8,128)(2,1)S(1)}) custom-call(s32[16,4]{1,0:T(8,128)} %copy-done.2, bf16[16,256,512]{2,1,0:T(8,128)(2,1)S(1)} %get-tuple-element.249.refs_1_, ...), custom_call_target="tpu_custom_call", output_to_operand_aliasing={{1}: (2, {}), {2}: (3, {}), {3}: (1, {})} | custom-call | bytes 7000000 | tf_op jit(solution)/shard_map/pallas_call | solution.py:60
  126.8 2.1 %collective-permute-start.52 = (f32[16,4,128]{2,1,0:T(4,128)S(1)}, f32[16,4,128]{2,1,0:T(4,128)S(1)}, u32[]{:S(2)}, u32[]{:S(2)}) collective-permute-start(f32[16,4,128]{2,1,0:T(4,128)S(1)} %get-tuple-element.256.refs_6_), channel_id=1, source_target_pairs={{0,4},{4,0},{8,12},{12,8},{16,20},{20,16},{24,28},{28,24},{1,5},{5... | collective-permute-start | bytes 98312 | tf_op jit(solution)/shard_map/ppermute | solution.py:534
  132.2 3.5 %shard_map.162 = (f32[4,128,128]{2,1,0:T(8,128)S(1)}, f32[4,4,128]{2,1,0:T(4,128)S(1)}, f32[4,4,128]{2,1,0:T(4,128)S(1)}, f32[16,1,128]{2,1,0:T(1,128)S(1)}, f32...) custom-call(s32[9]{0:T(128)} %stack.51.refs_0_, ...), custom_call_target="tpu_custom_call", output_to_operand_aliasing={{3}: (3, {}), {4}: (4, {}), {5}: (1, {})} | custom-call | bytes 10500000 | tf_op jit(solution)/shard_map/pallas_call | solution.py:60
  136.9 2.0 %collective-permute-done.55.refs_3_ = f32[4,4,128]{2,1,0:T(4,128)S(1)} collective-permute-done((f32[4,4,128]{2,1,0:T(4,128)S(1)}, f32[4,4,128]{2,1,0:T(4,128)S(1)}, u32[]{:S(2)}, u32[]{:S(2)}) %collective-permute-start.55) | collective-permute-done | bytes 8224 | tf_op jit(solution)/shard_map/ppermute | solution.py:529
  140.5 3.0 %collective-permute-done.56.refs_3_ = f32[4,4,256]{2,1,0:T(4,128)S(1)} collective-permute-done((f32[4,4,256]{2,1,0:T(4,128)S(1)}, f32[4,4,256]{2,1,0:T(4,128)S(1)}, u32[]{:S(2)}, u32[]{:S(2)}) %collective-permute-start.56) | collective-permute-done | bytes 16416 | tf_op jit(solution)/shard_map/ppermute | solution.py:534
  143.5 2.9 %shard_map.164 = f32[4,128,128]{2,1,0:T(8,128)} custom-call(s32[9]{0:T(128)} %stack.51.refs_0_, f32[11,144,256]{2,1,0:T(8,128)S(1)} %copy-done.1, f32[4,128,256]{2,1,0:T(8,128)S(1)} %get-tuple-element.260.refs_2_, f32[4,4,256]{2,1,0:T(4,128)S(1)} %collective-permute-done.56.refs_3_, f32[4,4,256]{2,1,0:T(4,128)S(1)} %collective-permute-done.57.refs_4_), custom_call_target="tpu_custom_call" | custom-call | bytes 7000000 | tf_op jit(solution)/shard_map/pallas_call | solution.py:60
  (131 shorter events, 49.6 us)
Async XLA Ops:
  2.5 12.2 %collective-permute-start.2 = (f32[1,3,32,128]{3,2,1,0:T(8,128)S(1)}, f32[1,3,32,128]{3,2,1,0:T(8,128)S(1)}, u32[]{:S(2)}, u32[]{:S(2)}) collective-permute-start(f32[1,3,32,128]{3,2,1,0:T(8,128)S(1)} %get-tuple-element.146), channel_id=1, source_target_pairs={{0,16},{4,20},{8,24},{12,28},{16,0},{20,4},{24,8},{28,12},{1,17},{... | collective-permute-start | bytes 147464 | tf_op jit(solution)/shard_map/ppermute | solution.py:580
  6.6 7.3 %collective-permute-start = (f32[6,4,128]{2,1,0:T(4,128)S(1)}, f32[6,4,128]{2,1,0:T(4,128)S(1)}, u32[]{:S(2)}, u32[]{:S(2)}) collective-permute-start(f32[6,4,128]{2,1,0:T(4,128)S(1)} %get-tuple-element.138), channel_id=1, source_target_pairs={{0,1},{1,0},{2,3},{3,2},{4,5},{5,4},{6,7},{7,6},{8,9},{9,8},{10,11... | collective-permute-start | bytes 36872 | tf_op jit(solution)/shard_map/ppermute | solution.py:529
  6.6 7.3 %collective-permute-start.1 = (f32[6,4,128]{2,1,0:T(4,128)S(1)}, f32[6,4,128]{2,1,0:T(4,128)S(1)}, u32[]{:S(2)}, u32[]{:S(2)}) collective-permute-start(f32[6,4,128]{2,1,0:T(4,128)S(1)} %get-tuple-element.144), channel_id=1, source_target_pairs={{1,2},{2,1},{0,3},{3,0},{5,6},{6,5},{4,7},{7,4},{9,10},{10,9},{8,1... | collective-permute-start | bytes 36872 | tf_op jit(solution)/shard_map/ppermute | solution.py:529
  14.8 17.6 %collective-permute-start.5 = (f32[2,3,32,128]{3,2,1,0:T(8,128)S(1)}, f32[2,3,32,128]{3,2,1,0:T(8,128)S(1)}, u32[]{:S(2)}, u32[]{:S(2)}) collective-permute-start(f32[2,3,32,128]{3,2,1,0:T(8,128)S(1)} %pad_maximum_fusion.2), channel_id=1, source_target_pairs={{0,8},{4,12},{8,0},{12,4},{16,24},{20,28},{24,16},{28,20},{1,9},{5... | collective-permute-start | bytes 294920 | tf_op jit(solution)/shard_map/ppermute | solution.py:580
  16.4 6.6 %collective-permute-start.3 = (f32[6,4,256]{2,1,0:T(4,128)S(1)}, f32[6,4,256]{2,1,0:T(4,128)S(1)}, u32[]{:S(2)}, u32[]{:S(2)}) collective-permute-start(f32[6,4,256]{2,1,0:T(4,128)S(1)} %get-tuple-element.149), channel_id=1, source_target_pairs={{0,4},{4,0},{8,12},{12,8},{16,20},{20,16},{24,28},{28,24},{1,5},{5... | collective-permute-start | bytes 73736 | tf_op jit(solution)/shard_map/ppermute | solution.py:534
  17.9 5.1 %collective-permute-start.4 = (f32[6,4,256]{2,1,0:T(4,128)S(1)}, f32[6,4,256]{2,1,0:T(4,128)S(1)}, u32[]{:S(2)}, u32[]{:S(2)}) collective-permute-start(f32[6,4,256]{2,1,0:T(4,128)S(1)} %get-tuple-element.150), channel_id=1, source_target_pairs={{4,8},{5,9},{6,10},{7,11},{8,4},{9,5},{10,6},{11,7},{12,16},{13,17... | collective-permute-start | bytes 73736 | tf_op jit(solution)/shard_map/ppermute | solution.py:535
  32.4 10.3 %collective-permute-start.10 = (f32[4,3,32,128]{3,2,1,0:T(8,128)S(1)}, f32[4,3,32,128]{3,2,1,0:T(8,128)S(1)}, u32[]{:S(2)}, u32[]{:S(2)}) collective-permute-start(f32[4,3,32,128]{3,2,1,0:T(8,128)S(1)} %pad_maximum_fusion.1), channel_id=1, source_target_pairs={{0,4},{4,0},{8,12},{12,8},{16,20},{20,16},{24,28},{28,24},{1,5},{5... | collective-permute-start | bytes 589832 | tf_op jit(solution)/shard_map/ppermute | solution.py:580
  34.4 6.3 %collective-permute-start.8 = (f32[21,4,128]{2,1,0:T(4,128)S(1)}, f32[21,4,128]{2,1,0:T(4,128)S(1)}, u32[]{:S(2)}, u32[]{:S(2)}) collective-permute-start(f32[21,4,128]{2,1,0:T(4,128)S(1)} %get-tuple-element.165.refs_4_), channel_id=1, source_target_pairs={{0,4},{4,0},{8,12},{12,8},{16,20},{20,16},{24,28},{28,24},{1,5},{5... | collective-permute-start | bytes 129032 | tf_op jit(solution)/shard_map/ppermute | solution.py:534
  36.3 4.4 %collective-permute-start.7 = (f32[21,4,128]{2,1,0:T(4,128)S(1)}, f32[21,4,128]{2,1,0:T(4,128)S(1)}, u32[]{:S(2)}, u32[]{:S(2)}) collective-permute-start(f32[21,4,128]{2,1,0:T(4,128)S(1)} %get-tuple-element.165.refs_4_), channel_id=1, source_target_pairs={{1,2},{2,1},{0,3},{3,0},{5,6},{6,5},{4,7},{7,4},{9,10},{10,9},{8,1... | collective-permute-start | bytes 129032 | tf_op jit(solution)/shard_map/ppermute | solution.py:529
  36.3 4.4 %collective-permute-start.6 = (f32[21,4,128]{2,1,0:T(4,128)S(1)}, f32[21,4,128]{2,1,0:T(4,128)S(1)}, u32[]{:S(2)}, u32[]{:S(2)}) collective-permute-start(f32[21,4,128]{2,1,0:T(4,128)S(1)} %get-tuple-element.165.refs_4_), channel_id=1, source_target_pairs={{0,1},{1,0},{2,3},{3,2},{4,5},{5,4},{6,7},{7,6},{8,9},{9,8},{10,11... | collective-permute-start | bytes 129032 | tf_op jit(solution)/shard_map/ppermute | solution.py:529
  42.8 12.3 %collective-permute-start.15 = (f32[8,3,32,128]{3,2,1,0:T(8,128)S(1)}, f32[8,3,32,128]{3,2,1,0:T(8,128)S(1)}, u32[]{:S(2)}, u32[]{:S(2)}) collective-permute-start(f32[8,3,32,128]{3,2,1,0:T(8,128)S(1)} %pad_maximum_fusion.refs_1_), channel_id=1, source_target_pairs={{0,2},{1,3},{2,0},{3,1},{4,6},{5,7},{6,4},{7,5},{8,10},{9,11},{10,... | collective-permute-start | bytes 1179656 | tf_op jit(solution)/shard_map/ppermute | solution.py:580
  43.4 4.7 %collective-permute-start.14 = (f32[16,4,128]{2,1,0:T(4,128)S(1)}, f32[16,4,128]{2,1,0:T(4,128)S(1)}, u32[]{:S(2)}, u32[]{:S(2)}) collective-permute-start(f32[16,4,128]{2,1,0:T(4,128)S(1)} %get-tuple-element.171.refs_4_), channel_id=1, source_target_pairs={{4,8},{5,9},{6,10},{7,11},{8,4},{9,5},{10,6},{11,7},{12,16},{13,17... | collective-permute-start | bytes 98312 | tf_op jit(solution)/shard_map/ppermute | solution.py:535
  43.4 4.9 %collective-permute-start.13 = (f32[16,4,128]{2,1,0:T(4,128)S(1)}, f32[16,4,128]{2,1,0:T(4,128)S(1)}, u32[]{:S(2)}, u32[]{:S(2)}) collective-permute-start(f32[16,4,128]{2,1,0:T(4,128)S(1)} %get-tuple-element.171.refs_4_), channel_id=1, source_target_pairs={{0,4},{4,0},{8,12},{12,8},{16,20},{20,16},{24,28},{28,24},{1,5},{5... | collective-permute-start | bytes 98312 | tf_op jit(solution)/shard_map/ppermute | solution.py:534
  46.4 6.6 %collective-permute-start.12 = (f32[16,4,128]{2,1,0:T(4,128)S(1)}, f32[16,4,128]{2,1,0:T(4,128)S(1)}, u32[]{:S(2)}, u32[]{:S(2)}) collective-permute-start(f32[16,4,128]{2,1,0:T(4,128)S(1)} %get-tuple-element.171.refs_4_), channel_id=1, source_target_pairs={{1,2},{2,1},{0,3},{3,0},{5,6},{6,5},{4,7},{7,4},{9,10},{10,9},{8,1... | collective-permute-start | bytes 98312 | tf_op jit(solution)/shard_map/ppermute | solution.py:529
  46.4 6.6 %collective-permute-start.11 = (f32[16,4,128]{2,1,0:T(4,128)S(1)}, f32[16,4,128]{2,1,0:T(4,128)S(1)}, u32[]{:S(2)}, u32[]{:S(2)}) collective-permute-start(f32[16,4,128]{2,1,0:T(4,128)S(1)} %get-tuple-element.171.refs_4_), channel_id=1, source_target_pairs={{0,1},{1,0},{2,3},{3,2},{4,5},{5,4},{6,7},{7,6},{8,9},{9,8},{10,11... | collective-permute-start | bytes 98312 | tf_op jit(solution)/shard_map/ppermute | solution.py:529
  55.1 16.0 %collective-permute-start.24 = (f32[8,3,32,128]{3,2,1,0:T(8,128)S(1)}, f32[8,3,32,128]{3,2,1,0:T(8,128)S(1)}, u32[]{:S(2)}, u32[]{:S(2)}) collective-permute-start(f32[8,3,32,128]{3,2,1,0:T(8,128)S(1)} %pad_maximum_fusion.refs_1_), channel_id=1, source_target_pairs={{0,1},{1,0},{2,3},{3,2},{4,5},{5,4},{6,7},{7,6},{8,9},{9,8},{10,11... | collective-permute-start | bytes 1179656 | tf_op jit(solution)/shard_map/ppermute | solution.py:580
  56.2 14.8 %collective-permute-start.25 = (f32[8,3,32,128]{3,2,1,0:T(8,128)S(1)}, f32[8,3,32,128]{3,2,1,0:T(8,128)S(1)}, u32[]{:S(2)}, u32[]{:S(2)}) collective-permute-start(f32[8,3,32,128]{3,2,1,0:T(8,128)S(1)} %collective-permute-done.15.refs_2_), channel_id=1, source_target_pairs={{0,1},{1,0},{2,3},{3,2},{4,5},{5,4},{6,7},{7,6},{8,9},{9,8},{10,11... | collective-permute-start | bytes 1179656 | tf_op jit(solution)/shard_map/ppermute | solution.py:580
  56.7 3.9 %collective-permute-start.18 = (f32[16,4,128]{2,1,0:T(4,128)S(1)}, f32[16,4,128]{2,1,0:T(4,128)S(1)}, u32[]{:S(2)}, u32[]{:S(2)}) collective-permute-start(f32[16,4,128]{2,1,0:T(4,128)S(1)} %get-tuple-element.178.refs_5_), channel_id=1, source_target_pairs={{0,4},{4,0},{8,12},{12,8},{16,20},{20,16},{24,28},{28,24},{1,5},{5... | collective-permute-start | bytes 98312 | tf_op jit(solution)/shard_map/ppermute | solution.py:534
  58.3 3.6 %collective-permute-start.17 = (f32[16,4,128]{2,1,0:T(4,128)S(1)}, f32[16,4,128]{2,1,0:T(4,128)S(1)}, u32[]{:S(2)}, u32[]{:S(2)}) collective-permute-start(f32[16,4,128]{2,1,0:T(4,128)S(1)} %get-tuple-element.178.refs_5_), channel_id=1, source_target_pairs={{1,2},{2,1},{0,3},{3,0},{5,6},{6,5},{4,7},{7,4},{9,10},{10,9},{8,1... | collective-permute-start | bytes 98312 | tf_op jit(solution)/shard_map/ppermute | solution.py:529
  58.3 3.6 %collective-permute-start.16 = (f32[16,4,128]{2,1,0:T(4,128)S(1)}, f32[16,4,128]{2,1,0:T(4,128)S(1)}, u32[]{:S(2)}, u32[]{:S(2)}) collective-permute-start(f32[16,4,128]{2,1,0:T(4,128)S(1)} %get-tuple-element.178.refs_5_), channel_id=1, source_target_pairs={{0,1},{1,0},{2,3},{3,2},{4,5},{5,4},{6,7},{7,6},{8,9},{9,8},{10,11... | collective-permute-start | bytes 98312 | tf_op jit(solution)/shard_map/ppermute | solution.py:529
  64.6 3.9 %collective-permute-start.22 = (f32[4,4,128]{2,1,0:T(4,128)S(1)}, f32[4,4,128]{2,1,0:T(4,128)S(1)}, u32[]{:S(2)}, u32[]{:S(2)}) collective-permute-start(f32[4,4,128]{2,1,0:T(4,128)S(1)} %get-tuple-element.185.refs_4_), channel_id=1, source_target_pairs={{0,4},{4,0},{8,12},{12,8},{16,20},{20,16},{24,28},{28,24},{1,5},{5... | collective-permute-start | bytes 24584 | tf_op jit(solution)/shard_map/ppermute | solution.py:534
  71.1 4.3 %collective-permute-start.29 = (f32[4,4,128]{2,1,0:T(4,128)S(1)}, f32[4,4,128]{2,1,0:T(4,128)S(1)}, u32[]{:S(2)}, u32[]{:S(2)}) collective-permute-start(f32[4,4,128]{2,1,0:T(4,128)S(1)} %get-tuple-element.196.refs_4_), channel_id=1, source_target_pairs={{4,8},{5,9},{6,10},{7,11},{8,4},{9,5},{10,6},{11,7},{12,16},{13,17... | collective-permute-start | bytes 24584 | tf_op jit(solution)/shard_map/ppermute | solution.py:535
  71.2 4.3 %collective-permute-start.28 = (f32[4,4,128]{2,1,0:T(4,128)S(1)}, f32[4,4,128]{2,1,0:T(4,128)S(1)}, u32[]{:S(2)}, u32[]{:S(2)}) collective-permute-start(f32[4,4,128]{2,1,0:T(4,128)S(1)} %get-tuple-element.196.refs_4_), channel_id=1, source_target_pairs={{0,4},{4,0},{8,12},{12,8},{16,20},{20,16},{24,28},{28,24},{1,5},{5... | collective-permute-start | bytes 24584 | tf_op jit(solution)/shard_map/ppermute | solution.py:534
  78.0 3.7 %collective-permute-start.32 = (f32[4,4,128]{2,1,0:T(4,128)S(1)}, f32[4,4,128]{2,1,0:T(4,128)S(1)}, u32[]{:S(2)}, u32[]{:S(2)}) collective-permute-start(f32[4,4,128]{2,1,0:T(4,128)S(1)} %get-tuple-element.207.refs_5_), channel_id=1, source_target_pairs={{0,4},{4,0},{8,12},{12,8},{16,20},{20,16},{24,28},{28,24},{1,5},{5... | collective-permute-start | bytes 24584 | tf_op jit(solution)/shard_map/ppermute | solution.py:534
  98.1 3.7 %collective-permute-start.36 = (f32[4,4,128]{2,1,0:T(4,128)S(1)}, f32[4,4,128]{2,1,0:T(4,128)S(1)}, u32[]{:S(2)}, u32[]{:S(2)}) collective-permute-start(f32[4,4,128]{2,1,0:T(4,128)S(1)} %get-tuple-element.229.refs_4_), channel_id=1, source_target_pairs={{0,4},{4,0},{8,12},{12,8},{16,20},{20,16},{24,28},{28,24},{1,5},{5... | collective-permute-start | bytes 24584 | tf_op jit(solution)/shard_map/ppermute | solution.py:534
  104.3 3.7 %collective-permute-start.40 = (f32[4,4,128]{2,1,0:T(4,128)S(1)}, f32[4,4,128]{2,1,0:T(4,128)S(1)}, u32[]{:S(2)}, u32[]{:S(2)}) collective-permute-start(f32[4,4,128]{2,1,0:T(4,128)S(1)} %get-tuple-element.238.refs_4_), channel_id=1, source_target_pairs={{0,4},{4,0},{8,12},{12,8},{16,20},{20,16},{24,28},{28,24},{1,5},{5... | collective-permute-start | bytes 24584 | tf_op jit(solution)/shard_map/ppermute | solution.py:534
  110.6 3.9 %collective-permute-start.44 = (f32[4,4,128]{2,1,0:T(4,128)S(1)}, f32[4,4,128]{2,1,0:T(4,128)S(1)}, u32[]{:S(2)}, u32[]{:S(2)}) collective-permute-start(f32[4,4,128]{2,1,0:T(4,128)S(1)} %get-tuple-element.247.refs_5_), channel_id=1, source_target_pairs={{0,4},{4,0},{8,12},{12,8},{16,20},{20,16},{24,28},{28,24},{1,5},{5... | collective-permute-start | bytes 24584 | tf_op jit(solution)/shard_map/ppermute | solution.py:534
  118.5 3.5 %collective-permute-start.49 = (f32[16,4,128]{2,1,0:T(4,128)S(1)}, f32[16,4,128]{2,1,0:T(4,128)S(1)}, u32[]{:S(2)}, u32[]{:S(2)}) collective-permute-start(f32[16,4,128]{2,1,0:T(4,128)S(1)} %get-tuple-element.252.refs_4_), channel_id=1, source_target_pairs={{4,8},{5,9},{6,10},{7,11},{8,4},{9,5},{10,6},{11,7},{12,16},{13,17... | collective-permute-start | bytes 98312 | tf_op jit(solution)/shard_map/ppermute | solution.py:535
  118.6 4.5 %collective-permute-start.48 = (f32[16,4,128]{2,1,0:T(4,128)S(1)}, f32[16,4,128]{2,1,0:T(4,128)S(1)}, u32[]{:S(2)}, u32[]{:S(2)}) collective-permute-start(f32[16,4,128]{2,1,0:T(4,128)S(1)} %get-tuple-element.252.refs_4_), channel_id=1, source_target_pairs={{0,4},{4,0},{8,12},{12,8},{16,20},{20,16},{24,28},{28,24},{1,5},{5... | collective-permute-start | bytes 98312 | tf_op jit(solution)/shard_map/ppermute | solution.py:534
  121.2 3.3 %collective-permute-start.47 = (f32[16,4,128]{2,1,0:T(4,128)S(1)}, f32[16,4,128]{2,1,0:T(4,128)S(1)}, u32[]{:S(2)}, u32[]{:S(2)}) collective-permute-start(f32[16,4,128]{2,1,0:T(4,128)S(1)} %get-tuple-element.252.refs_4_), channel_id=1, source_target_pairs={{1,2},{2,1},{0,3},{3,0},{5,6},{6,5},{4,7},{7,4},{9,10},{10,9},{8,1... | collective-permute-start | bytes 98312 | tf_op jit(solution)/shard_map/ppermute | solution.py:529
  126.8 4.0 %collective-permute-start.52 = (f32[16,4,128]{2,1,0:T(4,128)S(1)}, f32[16,4,128]{2,1,0:T(4,128)S(1)}, u32[]{:S(2)}, u32[]{:S(2)}) collective-permute-start(f32[16,4,128]{2,1,0:T(4,128)S(1)} %get-tuple-element.256.refs_6_), channel_id=1, source_target_pairs={{0,4},{4,0},{8,12},{12,8},{16,20},{20,16},{24,28},{28,24},{1,5},{5... | collective-permute-start | bytes 98312 | tf_op jit(solution)/shard_map/ppermute | solution.py:534
  139.7 3.8 %collective-permute-start.56 = (f32[4,4,256]{2,1,0:T(4,128)S(1)}, f32[4,4,256]{2,1,0:T(4,128)S(1)}, u32[]{:S(2)}, u32[]{:S(2)}) collective-permute-start(f32[4,4,256]{2,1,0:T(4,128)S(1)} %get-tuple-element.261), channel_id=1, source_target_pairs={{0,4},{4,0},{8,12},{12,8},{16,20},{20,16},{24,28},{28,24},{1,5},{5... | collective-permute-start | bytes 49160 | tf_op jit(solution)/shard_map/ppermute | solution.py:534
  (34 other events, 203.3 us)

commit v3 on v2

--- a/solution.py
+++ b/solution.py
@@ -18,7 +18,7 @@
 PLAIN = pl.BlockSpec(memory_space=pltpu.VMEM)
 HBM = pl.BlockSpec(memory_space=pl.ANY)
 SMEM = pl.BlockSpec(memory_space=pltpu.SMEM)
-W_ODD, N_ODD, HAS_WEST, HAS_EAST, HAS_SOUTH, HAS_NORTH, W_AT, N_AT = range(8)
+W_ODD, N_ODD, HAS_WEST, HAS_EAST, HAS_SOUTH, HAS_NORTH, W_AT, N_AT, LEVEL3 = range(9)
 
 
 def sds(shape, dtype=F32):
@@ -28,12 +28,14 @@
 def constrain(x, spec):
     if spec is VMEM:
         return pltpu.with_memory_space_constraint(x, pltpu.VMEM)
-    if spec is HBM or spec is SMEM:
+    if spec is HBM:
         return pltpu.with_memory_space_constraint(x, pltpu.HBM)
+    if spec is SMEM:
+        return pltpu.with_memory_space_constraint(x, pltpu.SMEM)
     return x
 
 
-def call(kernel, outs, ins, scratch=(), specs=None, mib=12, us=2, hold=None, far=(), loose=()):
+def call(kernel, outs, ins, scratch=(), specs=None, mib=12, us=2, hold=None, far=(), loose=(), scalars=()):
     hold = {} if hold is None else hold
     outs, tree = jax.tree.flatten(outs)
     specs = specs or [VMEM] * len(ins)
@@ -44,9 +46,8 @@
     specs = list(specs) + [VMEM] * len(rest)
     inputs = [constrain(x, spec) for x, spec in zip(inputs, specs)]
     count_in, count_out = len(ins), len(outs)
-    shapes = [
-        o if o in loose else (pltpu.HBM if o in far else pltpu.VMEM)(o.shape, o.dtype) for o in outs
-    ]
+    spaces = [pltpu.HBM if i in far else pltpu.SMEM if i in scalars else pltpu.VMEM for i in range(len(outs))]
+    shapes = [o if i in loose else spaces[i](o.shape, o.dtype) for i, o in enumerate(outs)]
     shapes += [pltpu.VMEM(hold[name].shape, hold[name].dtype) for name in hold]
 
     def inner(*refs):
@@ -61,7 +62,8 @@
         inner,
         out_shape=shapes,
         in_specs=specs,
-        out_specs=[HBM if o in far else VMEM for o in outs] + [VMEM] * len(hold),
+        out_specs=[{pltpu.HBM: HBM, pltpu.SMEM: SMEM, pltpu.VMEM: VMEM}[space] for space in spaces]
+        + [VMEM] * len(hold),
         scratch_shapes=list(scratch),
         input_output_aliases={places[name]: count_out + i for i, name in enumerate(hold)},
         compiler_params=pltpu.CompilerParams(vmem_limit_bytes=mib * 1024 * 1024),
@@ -74,17 +76,19 @@
 
 def parts_of(x):
     hi = x.astype(BF16).astype(F32)
-    rest = x - hi
-    mid = rest.astype(BF16).astype(F32)
-    return hi, mid, rest - mid
+    return hi, x - hi
 
 
 def rows_of(x):
-    return jnp.concatenate([*parts_of(x), jnp.zeros_like(x)], axis=0)
-
-
-def rows_sum(s, cols):
-    return s[0:cols] + s[cols : 2 * cols] + s[2 * cols : 3 * cols]
+    return jnp.concatenate(parts_of(x), axis=0)
+
+
+def twice(x):
+    return jnp.concatenate([x, x], axis=0).astype(BF16)
+
+
+def rows_sum(s):
+    return s[0:4] + s[4:8]
 
 
 def dot_nt(a, b):
@@ -97,79 +101,95 @@
         xs[pl.ds(base, count), i * cols : (i + 1) * cols, :] = part
 
 
-def tiles_kernel(tiles_ref, t_ref, d_ref, *again):
-    slots, size = tiles_ref.shape[1], tiles_ref.shape[2]
+def split_map(m):
+    hi = m.astype(BF16)
+    return hi, (m - hi.astype(F32)).astype(BF16)
+
+
+def split_tile(tile, r, k, t_ref, d_ref):
+    size = tile.shape[0]
     if size < LANES:
-        t_ref[...] = jnp.zeros_like(t_ref)
-    for r in range(tiles_ref.shape[0]):
-        for k in range(slots):
-            tile = tiles_ref[r, k]
-            if size < LANES:
-                tile = jnp.concatenate([tile, jnp.zeros((size, LANES - size), F32)], axis=1)
-            hi = tile.astype(BF16)
-            lo = (tile - hi.astype(F32)).astype(BF16)
-            t_ref[r, 0:size, k * LANES : (k + 1) * LANES] = hi
-            t_ref[r, LANES : LANES + size, k * LANES : (k + 1) * LANES] = lo
-            if k == 0:
-                row = lax.broadcasted_iota(jnp.int32, tile.shape, 0)
-                col = lax.broadcasted_iota(jnp.int32, tile.shape, 1)
-                diag = jnp.sum(jnp.where(row == col, tile, 0.0), axis=0, keepdims=True)
-                lane = lax.broadcasted_iota(jnp.int32, diag.shape, 1)
-                d_ref[r] = jnp.where(lane < size, diag, 1.0)
-    for ref in again:
-        ref[...] = t_ref[...]
-
-
-def split_tiles(tiles, again):
-    count, slots, size, _ = tiles.shape
-    step = min(count, 4)
-    spec = pl.BlockSpec((step, 2 * LANES, slots * LANES), lambda i: (i, 0, 0))
-    shape = (count, 2 * LANES, slots * LANES)
-    return pl.pallas_call(
-        tiles_kernel,
-        grid=(count // step,),
-        in_specs=[pl.BlockSpec((step, slots, size, size), lambda i: (i, 0, 0, 0))],
-        out_specs=[spec, pl.BlockSpec((step, 1, LANES), lambda i: (i, 0, 0))] + [spec] * again,
-        out_shape=[pltpu.VMEM(shape, BF16), pltpu.VMEM((count, 1, LANES), F32)]
-        + [pltpu.HBM(shape, BF16)] * again,
-        compiler_params=pltpu.CompilerParams(vmem_limit_bytes=16 * 1024 * 1024),
-        cost_estimate=pl.CostEstimate(flops=0, bytes_accessed=2 * 4 * tiles.size, transcendentals=0),
-        name="split_tiles",
-    )(pltpu.with_memory_space_constraint(tiles, pltpu.HBM))
-
-
-def index_kernel(flags, *refs):
-    half = len(refs) // 2
+        tile = jnp.concatenate([tile, jnp.zeros((size, LANES - size), F32)], axis=1)
+    hi, lo = split_map(tile)
+    t_ref[r, 0:size, k * LANES : (k + 1) * LANES] = hi
+    t_ref[r, LANES : LANES + size, k * LANES : (k + 1) * LANES] = lo
+    if k == 0:
+        row = lax.broadcasted_iota(jnp.int32, tile.shape, 0)
+        col = lax.broadcasted_iota(jnp.int32, tile.shape, 1)
+        diag = jnp.sum(jnp.where(row == col, tile, 0.0), axis=0, keepdims=True)
+        lane = lax.broadcasted_iota(jnp.int32, diag.shape, 1)
+        d_ref[r] = jnp.where(lane < size, diag, 1.0)
+
+
+def tiles_kernel(parts, tiles, t_ref, d_ref, far, held, sems, far_sems):
+    count, slots = tiles.shape[:2]
+    step = count // parts
+    spans = [pl.ds(i * step, step) for i in range(parts)]
+    loads = [pltpu.make_async_copy(tiles.at[a], held.at[a], sems.at[i]) for i, a in enumerate(spans)]
+    stores = [pltpu.make_async_copy(t_ref.at[a], far.at[a], far_sems.at[i]) for i, a in enumerate(spans)]
+    for load in loads:
+        load.start()
+    for i in range(parts):
+        loads[i].wait()
+        for r in range(i * step, (i + 1) * step):
+            for k in range(slots):
+                split_tile(held[r, k], r, k, t_ref, d_ref)
+        stores[i].start()
+    for store in stores:
+        store.wait()
+
+
+def small_tiles_kernel(tiles, t_ref, d_ref):
+    t_ref[...] = jnp.zeros_like(t_ref)
+    for r in range(tiles.shape[0]):
+        for k in range(tiles.shape[1]):
+            split_tile(tiles[r, k], r, k, t_ref, d_ref)
+
+
+def index_kernel(flags, columns1, live1, columns2, live2, idx1, idx2, held1, held2, turned, sems):
     w_odd, n_odd = flags[W_ODD], flags[N_ODD]
-    region = (0, 3 + (1 - w_odd), 3 + w_odd, 1 + (1 - n_odd), 1 + n_odd)
+    region = (0, 1 + w_odd, 2 - w_odd, 3 + n_odd, 4 - n_odd)
     there = (1, flags[HAS_WEST], flags[HAS_EAST], flags[HAS_SOUTH], flags[HAS_NORTH])
-    for level in range(2):
-        columns, live, out = refs[2 * level], refs[2 * level + 1], refs[4 + level]
-        count, slots = out.shape
+    for columns, live, held, dim in ((columns1, live1, held1, 1), (columns2, live2, held2, 0)):
         code = columns[...]
+        count = code.shape[dim]
         place = jnp.full(code.shape, 5 * count, jnp.int32)
         for s in range(5):
             at = code - s * count
             ok = (at >= 0) & (at < count) & (live[...] == 1) & (there[s] == 1)
             place = jnp.where(ok, at + region[s] * count, place)
-        out[:, 1:] = place
-        out[:, 0:1] = lax.broadcasted_iota(jnp.int32, (count, 1), 0)
+        own = lax.broadcasted_iota(jnp.int32, held.shape, dim)
+        held[...] = own
+        if dim:
+            held[1:, :] = place
+        else:
+            held[:, 1:] = place
+    copies = [
+        pltpu.make_async_copy(held1, idx1, sems.at[0]),
+        pltpu.make_async_copy(held2, turned, sems.at[1]),
+    ]
+    for copy in copies:
+        copy.start()
+    for copy in copies:
+        copy.wait()
+    slots, count = idx2.shape
+    for k in range(slots):
+        for r in range(count):
+            idx2[k, r] = turned[r, k]
 
 
 def apply_tiles(t_ref, xs, idx):
-    count, slots = idx.shape
-    cols = 4
+    slots, count = idx.shape
     out = []
     for r in range(count):
-        lhs = jnp.concatenate([xs[idx[r, k]] for k in range(slots)], axis=1).astype(BF16)
-        both = dot_nt(lhs, t_ref[r])
-        out.append(rows_sum(both[:, :LANES] + both[:, LANES:], cols))
+        lhs = twice(jnp.concatenate([xs[idx[k, r]] for k in range(slots)], axis=1))
+        both = dot_nt(lhs, t_ref[r])[0:8]
+        out.append(rows_sum(both[:, :LANES] + both[:, LANES:]))
     return out
 
 
 def fill_blocks(xs, own, others, count):
-    xs[:, 12:16, :] = jnp.zeros((xs.shape[0], 4, LANES), F32)
-    xs[5 * count] = jnp.zeros((16, LANES), F32)
+    xs[5 * count] = jnp.zeros((8, LANES), F32)
     store_parts(xs, 0, own[0:count])
     for i, other in enumerate(others):
         store_parts(xs, (i + 1) * count, other[0:count])
@@ -198,11 +218,11 @@
     coarse_tiles, _, lanes = b2.shape
     size = coarse_tiles * lanes // 2
     for r, ax in enumerate(apply_tiles(t, xs, idx)):
-        rows = rows_of(left[r] - 0.5 * ax).astype(BF16)
+        rows = twice(rows_of(left[r] - 0.5 * ax))
         hot = lax.broadcasted_iota(jnp.int32, (size, LANES), 0) == groups[r : r + 1, :]
         term = dot_nt(rows, hot.astype(F32).astype(BF16))
         total = term if total is None else total + term
-    total = rows_sum(total, 4)
+    total = rows_sum(total[0:8])
     half = LANES // 2
     lane = lax.broadcasted_iota(jnp.int32, (4, LANES), 1)
     for tile in range(coarse_tiles):
@@ -214,17 +234,19 @@
         first[tile] = JACOBI * value / d2[tile]
 
 
-def restrict_two_kernel(flags, idx, t, left, groups, own, o1, o2, o3, o4, out, xs):
+def restrict_two_kernel(flags, idx, t, left, groups, gain, own, o1, o2, o3, o4, out, xs):
     count = left.shape[0]
     fill_blocks(xs, own, (o1, o2, o3, o4), count)
-    offset = flags[N_AT] * flags[8]
+    offset = flags[N_AT] * flags[LEVEL3]
+    first = groups.shape[1] - count
     total = None
     for r, ax in enumerate(apply_tiles(t, xs, idx)):
-        rows = rows_of(left[r] - 0.5 * ax).astype(BF16)
-        hot = lax.broadcasted_iota(jnp.int32, (LANES, LANES), 0) == groups[r : r + 1, :] + offset
+        rows = twice(rows_of(left[r] - 0.5 * ax))
+        group = groups[0, first + r : first + r + 1, :] + offset
+        hot = lax.broadcasted_iota(jnp.int32, (LANES, LANES), 0) == group
         term = dot_nt(rows, hot.astype(F32).astype(BF16))
         total = term if total is None else total + term
-    total = rows_sum(total, 4)
+    total = map_product(jnp.concatenate(split_map(gain[0]), axis=0), rows_sum(total[0:8]))
     out[...] = jnp.broadcast_to(total[None], out.shape)
 
 
@@ -239,7 +261,7 @@
             for bit, (axis, step) in enumerate(order):
                 if position >> bit & 1:
                     v, q = (v ^ step, q) if axis == "wide" else (v, q ^ step)
-            for i in range(3):
+            for i in range(piece.shape[1]):
                 value = piece[k, i]
                 hi = value.astype(BF16)
                 at = pl.multiple_of(q * rows, rows)
@@ -249,23 +271,21 @@
 
 
 def map_product(m, x):
-    both = dot_nt(rows_of(x).astype(BF16), m)
-    return rows_sum(both[:, :LANES] + both[:, LANES:], 4)
+    both = dot_nt(twice(rows_of(x)), m)[0:8]
+    return rows_sum(both[:, :LANES] + both[:, LANES:])
 
 
 def take_lanes(table, lanes):
     return jnp.take_along_axis(table, jnp.broadcast_to(lanes, table.shape), axis=1)
 
 
-def groups_kernel(own1, own2, o1, o2, o3, o4, out):
-    count1, count2 = own1.shape[0], own2.shape[0]
-    out[0, 0:count1] = own1[...]
-    out[0, count1:] = own2[...]
-    for p, ref in enumerate((o1, o2, o3, o4)):
+def groups_kernel(own1, own, o1, o2, o3, o4, out):
+    count1 = own1.shape[0]
+    for p, ref in enumerate((own, o1, o2, o3, o4)):
         cols = ref.shape[1]
-        for i in range(count1 + count2):
+        for i in range(out.shape[1]):
             row = ref[count1 + i // cols, i % cols : i % cols + 1, :]
-            out[p + 1, i : i + 1] = row.astype(jnp.int32)
+            out[p, i : i + 1] = row.astype(jnp.int32)
 
 
 def chain_kernel(flags, maps, pieces, idx, t, d, x2, groups, out, xs, ys):
@@ -273,27 +293,26 @@
     narrow = pieces.shape[0] // blocks
     carry = None
     for v in range(blocks):
-        b = pieces[v * narrow]
+        now = pieces[v * narrow]
         for k in range(1, narrow):
-            b = b + pieces[v * narrow + k]
-        now = map_product(maps[v, 1], b)
+            now = now + pieces[v * narrow + k]
         if carry is not None:
             now = now + map_product(maps[v, 0], carry)
         ys[v] = now
         carry = now
     for v in range(blocks - 2, -1, -1):
-        carry = ys[v] + map_product(maps[v, 2], carry)
+        carry = ys[v] + map_product(maps[v, 1], carry)
         ys[v] = carry
     count = x2.shape[0]
-    xs[5 * count] = jnp.zeros((16, LANES), F32)
-    size = flags[8]
+    xs[5 * count] = jnp.zeros((8, LANES), F32)
+    size = flags[LEVEL3]
     w, n, w_odd, n_odd = flags[W_AT], flags[N_AT], flags[W_ODD], flags[N_ODD]
     n_first = n + 1 - 2 * n_odd
     n_second = jnp.clip(n - 1 + 2 * n_odd, 0, narrow - 1)
     w_first = w + 1 - 2 * w_odd
     w_second = jnp.clip(w - 1 + 2 * w_odd, 0, blocks - 1)
-    where = ((w, n), (w, n_first), (w, n_second), (w_first, n), (w_second, n))
-    lane = lax.broadcasted_iota(jnp.int32, (16, LANES), 1)
+    where = ((w, n), (w_second, n), (w_first, n), (w, n_second), (w, n_first))
+    lane = lax.broadcasted_iota(jnp.int32, (8, LANES), 1)
     first = groups.shape[1] - count
     for p, (pw, pn) in enumerate(where):
         table = rows_of(ys[pw])
@@ -303,12 +322,12 @@
             got = take_lanes(table, index)
             xs[p * count + tile] = jnp.where(lane < LANES // 2, got, 0.0)
     for r, ax in enumerate(apply_tiles(t, xs, idx)):
-        out[r] = x2[r] + (rows_sum(xs[r], 4) - 0.5 * ax / d[r])
+        out[r] = x2[r] + (rows_sum(xs[r]) - 0.5 * ax / d[r])
 
 
 def prolong_one_kernel(idx, t, d, x2, groups, own, o1, o2, o3, o4, out, xs):
     count = x2.shape[0]
-    xs[5 * count] = jnp.zeros((16, LANES), F32)
+    xs[5 * count] = jnp.zeros((8, LANES), F32)
     half = LANES // 2
     lane = lax.broadcasted_iota(jnp.int32, (4, LANES), 1)
     for p, u in enumerate((own, o1, o2, o3, o4)):
@@ -324,7 +343,7 @@
                 got = jnp.where((index >> 7) == i, more, got)
             xs[p * count + tile] = got
     for r, ax in enumerate(apply_tiles(t, xs, idx)):
-        out[r] = x2[r] + (rows_sum(xs[r], 4) - 0.5 * ax / d[r])
+        out[r] = x2[r] + (rows_sum(xs[r]) - 0.5 * ax / d[r])
 
 
 def live_weights(flags, east, north):
@@ -373,8 +392,15 @@
 
 
 def fine_first_kernel(
-    flags, block, east, north, forward, gain, backward, fields, first, second, piece, edges, sems
+    sizes, block, east, north, forward, backward, flags, fields, first, second, piece, edges, sems
 ):
+    wide, narrow = sizes
+    w, n = lax.axis_index("wide"), lax.axis_index("narrow")
+    values = (
+        w & 1, n & 1, w > 0, w < wide - 1, n > 0, n < narrow - 1, w, n, forward.shape[1] // narrow,
+    )
+    for i, value in enumerate(values):
+        flags[i] = jnp.int32(value)
     cols = block.shape[0]
     rows = piece.shape[2]
     at = pl.multiple_of(flags[N_AT] * rows, rows)
@@ -382,7 +408,7 @@
         (block, fields.at[0:cols]),
         (east, edges.at[0]),
         (north, edges.at[1]),
-        *((m.at[0, pl.ds(at, rows)], piece.at[0, i]) for i, m in enumerate((forward, gain, backward))),
+        *((m.at[0, pl.ds(at, rows)], piece.at[0, i]) for i, m in enumerate((forward, backward))),
     ]
     copies = [pltpu.make_async_copy(a, b, sems.at[i]) for i, (a, b) in enumerate(copies)]
     for copy in copies:
@@ -393,7 +419,7 @@
     narrow_rims(flags, [fields[c] for c in range(cols + 2)], first, second)
 
 
-def fine_second_kernel(flags, fields, o1, o2, ext, first, second):
+def fine_second_kernel(flags, fields, o2, o1, ext, first, second):
     for i in range(fields.shape[0]):
         wider = with_sides(flags, fields[i], o1, o2, i)
         ext[i] = wider
@@ -410,7 +436,7 @@
     )
 
 
-def fine_down_kernel(flags, ext, o1, o2, groups, d1, near1, near2, far, b1, first, q_ref, keep, sem):
+def fine_down_kernel(flags, ext, o2, o1, groups, d1, near1, near2, far, b1, first, q_ref, keep, sem):
     cols = ext.shape[0] - 2
     rows = ext.shape[1]
     e = with_rows(flags, ext[cols], o1, o2, cols)
@@ -433,40 +459,39 @@
     copy = pltpu.make_async_copy(keep, far, sem.at[0])
     copy.start()
     count = b1.shape[0]
-    step = 4
+    step = 32
+    one, zero = jnp.ones((), BF16), jnp.zeros((), BF16)
+    lanes = lax.broadcasted_iota(jnp.int32, (LANES, LANES), 0).astype(F32).astype(BF16)
+
+    def over_rows(x):
+        return jnp.broadcast_to(x, (16, LANES)).astype(BF16)
 
     def add_rows(j, total):
         left, right = [], []
         for k in range(step):
-            row = j * step + k
-            group = groups[pl.ds(row, 1), :]
-            high, low = group >> 7, group & (LANES - 1)
-            mask = lax.broadcasted_iota(jnp.int32, (count, LANES), 0) == high
-            left.append(
-                jnp.concatenate(
-                    [
-                        jnp.where(mask, q_ref[i, pl.ds(row, 1), :], 0.0).astype(BF16)
-                        for i in range(3 * cols)
-                    ],
-                    axis=0,
-                )
-            )
-            hot = lax.broadcasted_iota(jnp.int32, (LANES, LANES), 0) == low
-            right.append(hot.astype(F32).astype(BF16))
+            row = pl.ds(j * step + k, 1)
+            group = groups[row, :]
+            mask = lanes[0:count] == over_rows((group >> 7).astype(F32))
+            low = over_rows((group & (LANES - 1)).astype(F32))
+            picked = [jnp.where(mask, over_rows(q_ref[i, row, :]), zero) for i in range(2 * cols)]
+            left.append(jnp.concatenate(picked, axis=0))
+            low = jnp.concatenate([low] * (LANES // 16), axis=0)
+            right.append(jnp.where(lanes == low, one, zero))
         return total + dot_nt(jnp.concatenate(left, axis=1), jnp.concatenate(right, axis=1))
 
     total = lax.fori_loop(
-        0, rows // step, add_rows, jnp.zeros((3 * cols * count, LANES), F32)
+        0, rows // step, add_rows, jnp.zeros((2 * cols * count, LANES), F32)
     )
     size = cols * count
-    total = total[0:size] + total[size : 2 * size] + total[2 * size : 3 * size]
+    total = total[0:size] + total[size : 2 * size]
     for c in range(cols):
         value = total[c * count : (c + 1) * count]
         b1[:, c, :] = value
         first[0:count, c, :] = JACOBI * value / d1[:, 0, :]
-    groups = [near1[i : i + 1, :] for i in range(count)] + [
-        near2[i : i + 1, :] for i in range(near2.shape[0])
-    ]
+    groups = [near1[i : i + 1, :] for i in range(count)]
+    for i in range(near2.shape[0]):
+        row = near2[i : i + 1, :]
+        groups += [row, pltpu.roll(row, LANES // 2, 1)]
     for i, group in enumerate(groups):
         first[count + i // cols, i % cols : i % cols + 1, :] = group.astype(F32)
     copy.wait()
@@ -491,7 +516,7 @@
     narrow_rims(flags, [spread[c] for c in range(cols)], first, second)
 
 
-def fine_up_kernel(flags, keep, ext, o1, o2, far, out, sems):
+def fine_up_kernel(flags, keep, ext, o2, o1, far, out, sems):
     cols = out.shape[0]
     copies = []
     e, n, inv = keep[2 * cols], keep[2 * cols + 1], keep[2 * cols + 2]
@@ -526,18 +551,17 @@
 
 
 def exchange_narrow(first, second, route):
-    return lax.ppermute(first, "narrow", route[0]), lax.ppermute(second, "narrow", route[1])
+    second = lax.ppermute(second, "narrow", route[1])
+    return second, lax.ppermute(first, "narrow", route[0])
 
 
 def exchange_wide(first, second, route):
-    return (
-        lax.ppermute(first, "wide", route[2]),
-        lax.ppermute(second, ("wide", "narrow"), route[3]),
-    )
+    second = lax.ppermute(second, ("wide", "narrow"), route[3])
+    return second, lax.ppermute(first, "wide", route[2])
 
 
 def exchange(x, route):
-    return (*exchange_narrow(x, x, route), *exchange_wide(x, x, route))
+    return (*exchange_wide(x, x, route), *exchange_narrow(x, x, route))
 
 
 def body(
@@ -560,15 +584,10 @@
 ):
     wide, narrow = sizes
     route = routes(wide, narrow)
-    w, n = lax.axis_index("wide"), lax.axis_index("narrow")
     cols = block.shape[0]
     rows = block.shape[1]
     count1, slots = tiles_one.shape[:2]
-    count2, _, size2, _ = tiles_two.shape
-    level3 = chain_forward.shape[-1] // narrow
-    flags = jnp.stack(
-        [w % 2, n % 2, w > 0, w < wide - 1, n > 0, n < narrow - 1, w, n, jnp.int32(level3)]
-    ).astype(jnp.int32)
+    count2 = tiles_two.shape[0]
 
     order = [("wide", 1 << i) for i in reversed(range((wide - 1).bit_length()))]
     order += [("narrow", 1 << i) for i in reversed(range((narrow - 1).bit_length()))]
@@ -588,52 +607,78 @@
         return anchor
 
     rim = sds((cols + 2, RIM, LANES))
-    fields, first, second, piece = call(
-        fine_first_kernel,
-        [sds((cols + 2, rows, LANES)), rim, rim, sds((1, 3, share, LANES))],
-        (flags, block, east, north, chain_forward, chain_gain, chain_backward),
-        scratch=[pltpu.VMEM((2, rows, LANES), F32), pltpu.SemaphoreType.DMA((6,))],
-        specs=[SMEM] + [HBM] * 6,
+    flags = sds((LEVEL3 + 1,), jnp.int32)
+    flags, fields, first, second, piece = call(
+        functools.partial(fine_first_kernel, sizes),
+        [flags, sds((cols + 2, rows, LANES)), rim, rim, sds((1, 2, share, LANES))],
+        (block, east, north, chain_forward, chain_backward),
+        scratch=[pltpu.VMEM((2, rows, LANES), F32), pltpu.SemaphoreType.DMA((5,))],
+        specs=[HBM] * 5,
+        scalars=(0,),
     )
     held.append(piece)
     first, second = gather_step(first, second)
-    o1, o2 = exchange_narrow(first, second, route)
-
+    o2, o1 = exchange_narrow(first, second, route)
+
+    shapes = (sds((slots, count1), jnp.int32), sds((slots, count2), jnp.int32))
     idx1, idx2 = call(
         index_kernel,
-        [sds((count1, slots), jnp.int32), sds((count2, slots), jnp.int32)],
-        (flags, columns_one, live_one, columns_two, live_two),
+        list(shapes),
+        (flags, columns_one.T, live_one.T, columns_two, live_two),
+        scratch=[
+            pltpu.VMEM((slots, count1), jnp.int32),
+            pltpu.VMEM((count2, slots), jnp.int32),
+            pltpu.SMEM((count2, slots), jnp.int32),
+            pltpu.SemaphoreType.DMA((2,)),
+        ],
         specs=[SMEM] + [VMEM] * 4,
         us=0.5,
-    )
-    tiles2, d2 = split_tiles(tiles_two, 0)
+        scalars=(0, 1),
+    )
+    tiles2, d2 = call(
+        small_tiles_kernel,
+        [sds((count2, 2 * LANES, slots * LANES), BF16), sds((count2, 1, LANES))],
+        (tiles_two,),
+        us=0.7,
+    )
     groups1 = coarse_groups.reshape(count1, LANES)
-    groups2 = jnp.pad(coarser_groups.reshape(count2, size2), ((0, 0), (0, LANES - size2)))
-    o1, idx1, idx2, tiles2, d2, groups1, groups2 = lax.optimization_barrier(
-        (o1, idx1, idx2, tiles2, d2, groups1, groups2)
-    )
+    groups2 = coarser_groups.reshape(-1, LANES)
+    o2, idx1, idx2, tiles2, d2 = lax.optimization_barrier((o2, idx1, idx2, tiles2, d2))
 
     rim = sds((cols + 2, RIM, 2 * LANES))
     ext, first, second = call(
         fine_second_kernel,
         [sds((cols + 2, rows, 2 * LANES)), rim, rim],
-        (flags, fields, o1, o2),
+        (flags, fields, o2, o1),
         specs=[SMEM] + [VMEM] * 3,
     )
     first, second = gather_step(first, second)
-    o1, o2 = exchange_wide(first, second, route)
+    o2, o1 = exchange_wide(first, second, route)
     field1 = sds((count1, cols, LANES))
     field2 = sds((count2, cols, LANES))
-    tiles1, d1, tiles1_far = split_tiles(tiles_one, 1)
+    split = sds((count1, 2 * LANES, slots * LANES), BF16)
+    tiles1, d1, tiles1_far = call(
+        functools.partial(tiles_kernel, 4),
+        [split, sds((count1, 1, LANES)), split],
+        (tiles_one,),
+        scratch=[
+            pltpu.VMEM(tiles_one.shape, F32),
+            pltpu.SemaphoreType.DMA((4,)),
+            pltpu.SemaphoreType.DMA((4,)),
+        ],
+        specs=[HBM],
+        us=3,
+        far=(2,),
+    )
     more = -(-(count1 + count2) // cols)
     hold = {"t1": tiles1, "d1": d1}
     kept = sds((2 * cols + 3, rows + PAD, 2 * LANES))
     keep, b1, x1 = call(
         fine_down_kernel,
         [kept, field1, sds((count1 + more, cols, LANES))],
-        (flags, ext, o1, o2, fine_groups, "d1", groups1, groups2),
+        (flags, ext, o2, o1, fine_groups, "d1", groups1, groups2),
         scratch=[
-            pltpu.VMEM((3 * cols, rows, LANES), F32),
+            pltpu.VMEM((2 * cols, rows, LANES), F32),
             pltpu.VMEM(kept.shape, F32),
             pltpu.SemaphoreType.DMA((1,)),
         ],
@@ -641,12 +686,12 @@
         mib=16,
         us=7,
         hold=hold,
-        far=(kept,),
+        far=(0,),
     )
     hold["b1"] = b1
 
-    xs1 = [pltpu.VMEM((5 * count1 + 1, 16, LANES), F32)]
-    xs2 = [pltpu.VMEM((5 * count2 + 1, 16, LANES), F32)]
+    xs1 = [pltpu.VMEM((5 * count1 + 1, 8, LANES), F32)]
+    xs2 = [pltpu.VMEM((5 * count2 + 1, 8, LANES), F32)]
     lead = [SMEM]
 
     def smooth(level, x):
@@ -660,7 +705,7 @@
     groups = call(
         groups_kernel,
         sds((5, count1 + count2, LANES), jnp.int32),
-        (groups1, groups2, *near),
+        (groups1, x1, *near),
         specs=[VMEM] * 6,
         us=1,
     )
@@ -691,7 +736,7 @@
     y2, _ = smooth(2, y1)
     maps, y2 = lax.optimization_barrier((held, y2))
     near = exchange(y2, route)
-    chain_shape = sds((wide, 3, 2 * LANES, LANES), BF16)
+    chain_shape = sds((wide, 2, 2 * LANES, LANES), BF16)
     big = wide > 16
     chain = call(
         functools.partial(chain_maps_kernel, order),
@@ -700,7 +745,7 @@
         specs=[SMEM] + [PLAIN if big else VMEM] * len(maps),
         mib=48 if big else 12,
         us=0.7,
-        loose=(chain_shape,) if big else (),
+        loose=(0,) if big else (),
     )
     if not big:
         hold["chain"] = chain
@@ -717,9 +762,9 @@
     out3 = call(
         restrict_two_kernel,
         sds((wide * narrow, cols, LANES)),
-        (flags, idx2, "t2", left, groups2, scaled, *exchange(scaled, route)),
+        (flags, idx2, "t2", left, "groups", chain_gain, scaled, *exchange(scaled, route)),
         xs2,
-        [SMEM, SMEM] + [VMEM] * 8,
+        [SMEM, SMEM] + [VMEM] * 9,
         hold=hold,
     )
     pieces = lax.all_to_all(out3, ("wide", "narrow"), 0, 0)
@@ -760,27 +805,27 @@
         us=3,
         hold=hold,
     )
-    o1, o2 = exchange_narrow(first, second, route)
+    o2, o1 = exchange_narrow(first, second, route)
     rim = sds((cols, RIM, 2 * LANES))
     for name in ("t1", "d1", "b1"):
         del hold[name]
     ext, first, second = call(
         fine_second_kernel,
         [sds((cols, rows, 2 * LANES)), rim, rim],
-        (flags, spread, o1, o2),
+        (flags, spread, o2, o1),
         specs=[SMEM] + [VMEM] * 3,
         us=1,
         hold=hold,
     )
-    o1, o2 = exchange_wide(first, second, route)
+    o2, o1 = exchange_wide(first, second, route)
     whole = sds((cols, rows, LANES))
     return call(
         fine_up_kernel,
         whole,
-        (flags, keep, ext, o1, o2),
+        (flags, keep, ext, o2, o1),
         scratch=[pltpu.VMEM(whole.shape, F32), pltpu.SemaphoreType.DMA((cols,))],
         specs=[SMEM] + [VMEM] * 4,
-        far=(whole,),
+        far=(0,),
     )
 
 

time: 147 us -> 124 us (0.84)
  Pallas kernels: 47 us -> 25.8 us
  waiting for transfers between devices: 34.8 us -> 27.2 us
  starting transfers between devices: 49.4 us -> 55.3 us
    pallas_call x22, Pallas kernels: 47 us -> 25.8 us  [call(): pl.pallas_call(inner, out_shape=shapes, in_specs=specs, out_specs=[{pltpu...]
    ppermute x52, waiting for transfers between devices: 34.8 us -> 27.2 us  [the longest x13 17.7 us: exchange_narrow(): second = lax.ppermute(second, 'narrow', route[1])]
    ppermute x52, starting transfers between devices: 39.8 us -> 47 us  [the longest x13 29.8 us: exchange_wide(): return (second, lax.ppermute(first, 'wide', route[2]))]
    unnamed x18 -> x22, local copies, waits for them, and re-layouts: 2.91 us -> 3.78 us
  transfers between devices with their start and end apart: 58 -> 58, of which waited for: 23 -> 21; matrix products, arithmetic and copies ran while one was open for 2% -> 0% of each run, Pallas kernels for 18% -> 10%
where the time goes in v3:
time: 124 us
  starting transfers between devices  55.3 us (45%)
  waiting for transfers between devices  27.2 us (22%)
  Pallas kernels  25.8 us (21%)
  blocking collectives  11.3 us (9%)
  local copies, waits for them, and re-layouts  3.78 us (3%)
    ppermute x13, starting transfers between devices, exchange_wide(): return (second, lax.ppermute(first, 'wide', route[2]))  29.8 us
    pallas_call x22, Pallas kernels, call(): pl.pallas_call(inner, out_shape=shapes, in_specs=specs, out_specs=[{pltpu...  25.8 us
    ppermute x13, waiting for transfers between devices, exchange_narrow(): second = lax.ppermute(second, 'narrow', route[1])  17.7 us
    all_to_all x1, blocking collectives, body(): pieces = lax.all_to_all(out3, ('wide', 'narrow'), 0, 0)  11.3 us
    ppermute x13, starting transfers between devices, exchange_narrow(): return (second, lax.ppermute(first, 'narrow', route[0]))  11.2 us
    ppermute x13, waiting for transfers between devices, exchange_wide(): return (second, lax.ppermute(first, 'wide', route[2]))  9.47 us
    ppermute x6, starting transfers between devices, swap(): lax.ppermute(x, axis, [(i, i ^ step) for i in range(lax.axis_size(axis))])  8.26 us
    ppermute x13, starting transfers between devices, exchange_narrow(): second = lax.ppermute(second, 'narrow', route[1])  4.48 us
  transfers between devices with their start and end apart: 58, of which 21 were waited for; matrix products, arithmetic and copies ran while one was open for 0% of the time, Pallas kernels for 10%

profile of v3, /device:TPU:0, one launch (start us, length us, event | category | flops | bytes accessed | tf_op | source)
XLA Modules:
  0.0 124.0 jit_solution(4727754340190687382)
XLA Ops:
  1.2 4.1 %collective-permute-start.2 = (f32[1,2,32,128]{3,2,1,0:T(8,128)S(1)}, f32[1,2,32,128]{3,2,1,0:T(8,128)S(1)}, u32[]{:S(2)}, u32[]{:S(2)}) collective-permute-start(f32[1,2,32,128]{3,2,1,0:T(8,128)S(1)} %get-tuple-element.146), channel_id=1, source_target_pairs={{0,16},{4,20},{8,24},{12,28},{16,0},{20,4},{24,8},{28,12},{1,17},{... | collective-permute-start | bytes 98312 | tf_op jit(solution)/shard_map/ppermute | solution.py:599
  11.8 1.6 %collective-permute-start.5 = (f32[2,2,32,128]{3,2,1,0:T(8,128)S(1)}, f32[2,2,32,128]{3,2,1,0:T(8,128)S(1)}, u32[]{:S(2)}, u32[]{:S(2)}) collective-permute-start(f32[2,2,32,128]{3,2,1,0:T(8,128)S(1)} %pad_maximum_fusion.2), channel_id=1, source_target_pairs={{0,8},{4,12},{8,0},{12,4},{16,24},{20,28},{24,16},{28,20},{1,9},{5... | collective-permute-start | bytes 196616 | tf_op jit(solution)/shard_map/ppermute | solution.py:599
  13.5 1.9 %collective-permute-start.4 = (f32[6,4,256]{2,1,0:T(4,128)S(1)}, f32[6,4,256]{2,1,0:T(4,128)S(1)}, u32[]{:S(2)}, u32[]{:S(2)}) collective-permute-start(f32[6,4,256]{2,1,0:T(4,128)S(1)} %get-tuple-element.150), channel_id=1, source_target_pairs={{0,4},{4,0},{8,12},{12,8},{16,20},{20,16},{24,28},{28,24},{1,5},{5... | collective-permute-start | bytes 73736 | tf_op jit(solution)/shard_map/ppermute | solution.py:560
  15.4 3.5 %shard_map.149 = (bf16[16,256,512]{2,1,0:T(8,128)(2,1)S(1)}, f32[16,1,128]{2,1,0:T(1,128)S(1)}, bf16[16,256,512]{2,1,0:T(8,128)(2,1)}) custom-call(f32[16,4,128,128]{3,2,1,0:T(8,128)} %refs_0_.5), custom_call_target="tpu_custom_call" | custom-call | bytes 10500000 | tf_op jit(solution)/shard_map/pallas_call | solution.py:61
  18.9 3.5 %shard_map.150 = (f32[11,144,256]{2,1,0:T(8,128)}, f32[16,4,128]{2,1,0:T(4,128)S(1)}, f32[21,4,128]{2,1,0:T(4,128)S(1)}, bf16[16,256,512]{2,1,0:T(8,128)(2,1)S(1)}, f32[16,1,128]{2,1,0:T(1,128)S(1)}) custom-call(s32[9]{0:T(128)S(4)} %get-tuple-element.133.refs_0_, ...), custom_call_target="tpu_custom_call", output_to_operand_aliasing={{3}: (8, {}), {4}: (5, {})} | custom-call | bytes 24500000 | tf_op jit(solution)/shard_map/pallas_call | solution.py:61
  23.3 3.8 %collective-permute-start.7 = (f32[21,4,128]{2,1,0:T(4,128)S(1)}, f32[21,4,128]{2,1,0:T(4,128)S(1)}, u32[]{:S(2)}, u32[]{:S(2)}) collective-permute-start(f32[21,4,128]{2,1,0:T(4,128)S(1)} %get-tuple-element.163.refs_4_.refs_1_), channel_id=1, source_target_pairs={{0,4},{4,0},{8,12},{12,8},{16,20},{20,16},{24,28},{28,24},{1,5},{5... | collective-permute-start | bytes 129032 | tf_op jit(solution)/shard_map/ppermute | solution.py:560
  27.7 1.4 %collective-permute-done.7.refs_6_.refs_3_ = f32[21,4,128]{2,1,0:T(4,128)S(1)} collective-permute-done((f32[21,4,128]{2,1,0:T(4,128)S(1)}, f32[21,4,128]{2,1,0:T(4,128)S(1)}, u32[]{:S(2)}, u32[]{:S(2)}) %collective-permute-start.7) | collective-permute-done | bytes 43040 | tf_op jit(solution)/shard_map/ppermute | solution.py:560
  29.0 1.4 %collective-permute-done.8.refs_7_.refs_4_ = f32[21,4,128]{2,1,0:T(4,128)S(1)} collective-permute-done((f32[21,4,128]{2,1,0:T(4,128)S(1)}, f32[21,4,128]{2,1,0:T(4,128)S(1)}, u32[]{:S(2)}, u32[]{:S(2)}) %collective-permute-start.8) | collective-permute-done | bytes 43040 | tf_op jit(solution)/shard_map/ppermute | solution.py:554
  32.7 1.9 %collective-permute-start.12 = (f32[16,4,128]{2,1,0:T(4,128)S(1)}, f32[16,4,128]{2,1,0:T(4,128)S(1)}, u32[]{:S(2)}, u32[]{:S(2)}) collective-permute-start(f32[16,4,128]{2,1,0:T(4,128)S(1)} %get-tuple-element.169.refs_4_), channel_id=1, source_target_pairs={{0,4},{4,0},{8,12},{12,8},{16,20},{20,16},{24,28},{28,24},{1,5},{5... | collective-permute-start | bytes 98312 | tf_op jit(solution)/shard_map/ppermute | solution.py:560
  36.6 2.6 %collective-permute-done.13.refs_7_ = f32[16,4,128]{2,1,0:T(4,128)S(1)} collective-permute-done((f32[16,4,128]{2,1,0:T(4,128)S(1)}, f32[16,4,128]{2,1,0:T(4,128)S(1)}, u32[]{:S(2)}, u32[]{:S(2)}) %collective-permute-start.13) | collective-permute-done | bytes 32800 | tf_op jit(solution)/shard_map/ppermute | solution.py:554
  41.6 1.5 %collective-permute-start.17 = (f32[16,4,128]{2,1,0:T(4,128)S(1)}, f32[16,4,128]{2,1,0:T(4,128)S(1)}, u32[]{:S(2)}, u32[]{:S(2)}) collective-permute-start(f32[16,4,128]{2,1,0:T(4,128)S(1)} %get-tuple-element.176.refs_5_), channel_id=1, source_target_pairs={{0,4},{4,0},{8,12},{12,8},{16,20},{20,16},{24,28},{28,24},{1,5},{5... | collective-permute-start | bytes 98312 | tf_op jit(solution)/shard_map/ppermute | solution.py:560
  46.5 1.7 %shard_map.154 = (f32[4,4,128]{2,1,0:T(4,128)S(1)}, f32[4,4,128]{2,1,0:T(4,128)S(1)}, bf16[16,256,512]{2,1,0:T(8,128)(2,1)S(1)}, f32[16,1,128]{2,1,0:T(1,128)S(1...) custom-call(s32[4,16]{1,0:T(4,128)S(4)} %get-tuple-element.154.refs_, ...), custom_call_target="tpu_custom_call", output_to_operand_aliasing={{2}: (1, {}), {3}: (10, {}), {4}: (11, {}), {5}: (12, {}), ... | custom-call | bytes 7000000 | tf_op jit(solution)/shard_map/pallas_call | solution.py:61
  48.3 2.5 %collective-permute-start.21 = (f32[4,4,128]{2,1,0:T(4,128)S(1)}, f32[4,4,128]{2,1,0:T(4,128)S(1)}, u32[]{:S(2)}, u32[]{:S(2)}) collective-permute-start(f32[4,4,128]{2,1,0:T(4,128)S(1)} %get-tuple-element.183.refs_4_), channel_id=1, source_target_pairs={{0,4},{4,0},{8,12},{12,8},{16,20},{20,16},{24,28},{28,24},{1,5},{5... | collective-permute-start | bytes 24584 | tf_op jit(solution)/shard_map/ppermute | solution.py:560
  54.5 2.5 %collective-permute-start.27 = (f32[4,4,128]{2,1,0:T(4,128)S(1)}, f32[4,4,128]{2,1,0:T(4,128)S(1)}, u32[]{:S(2)}, u32[]{:S(2)}) collective-permute-start(f32[4,4,128]{2,1,0:T(4,128)S(1)} %get-tuple-element.194.refs_4_), channel_id=1, source_target_pairs={{0,4},{4,0},{8,12},{12,8},{16,20},{20,16},{24,28},{28,24},{1,5},{5... | collective-permute-start | bytes 24584 | tf_op jit(solution)/shard_map/ppermute | solution.py:560
  60.7 1.9 %collective-permute-start.31 = (f32[4,4,128]{2,1,0:T(4,128)S(1)}, f32[4,4,128]{2,1,0:T(4,128)S(1)}, u32[]{:S(2)}, u32[]{:S(2)}) collective-permute-start(f32[4,4,128]{2,1,0:T(4,128)S(1)} %get-tuple-element.206.refs_6_), channel_id=1, source_target_pairs={{0,4},{4,0},{8,12},{12,8},{16,20},{20,16},{24,28},{28,24},{1,5},{5... | collective-permute-start | bytes 24584 | tf_op jit(solution)/shard_map/ppermute | solution.py:560
  66.4 11.3 %all_to_all.5.refs_2_ = f32[32,4,128]{2,1,0:T(4,128)S(1)} all-to-all(f32[32,4,128]{2,1,0:T(4,128)S(1)} %get-tuple-element.215), channel_id=1, replica_groups=mesh['wide'=8,'narrow'=4] {'wide','narrow'}, dimensions={0} | all-to-all | bytes 131072 | tf_op jit(solution)/shard_map/all_to_all | solution.py:770
  77.7 2.2 %shard_map.159 = (f32[4,4,128]{2,1,0:T(4,128)S(1)}, f32[16,1,128]{2,1,0:T(1,128)S(1)}, f32[16,4,128]{2,1,0:T(4,128)S(1)}, f32[16,4,128]{2,1,0:T(4,128)S(1)}, s32...) custom-call(s32[9]{0:T(128)S(4)} %get-tuple-element.133.refs_0_, ...), custom_call_target="tpu_custom_call", output_to_operand_aliasing={{1}: (8, {}), {2}: (9, {}), {3}: (10, {}), {4}: (7, {}), {5... | custom-call | bytes 10500000 | tf_op jit(solution)/shard_map/pallas_call | solution.py:61
  80.1 2.0 %collective-permute-start.35 = (f32[4,4,128]{2,1,0:T(4,128)S(1)}, f32[4,4,128]{2,1,0:T(4,128)S(1)}, u32[]{:S(2)}, u32[]{:S(2)}) collective-permute-start(f32[4,4,128]{2,1,0:T(4,128)S(1)} %get-tuple-element.227.refs_4_), channel_id=1, source_target_pairs={{0,4},{4,0},{8,12},{12,8},{16,20},{20,16},{24,28},{28,24},{1,5},{5... | collective-permute-start | bytes 24584 | tf_op jit(solution)/shard_map/ppermute | solution.py:560
  85.6 2.1 %collective-permute-start.39 = (f32[4,4,128]{2,1,0:T(4,128)S(1)}, f32[4,4,128]{2,1,0:T(4,128)S(1)}, u32[]{:S(2)}, u32[]{:S(2)}) collective-permute-start(f32[4,4,128]{2,1,0:T(4,128)S(1)} %get-tuple-element.236.refs_4_), channel_id=1, source_target_pairs={{0,4},{4,0},{8,12},{12,8},{16,20},{20,16},{24,28},{28,24},{1,5},{5... | collective-permute-start | bytes 24584 | tf_op jit(solution)/shard_map/ppermute | solution.py:560
  89.3 1.4 %collective-permute-done.40.refs_7_ = f32[4,4,128]{2,1,0:T(4,128)S(1)} collective-permute-done((f32[4,4,128]{2,1,0:T(4,128)S(1)}, f32[4,4,128]{2,1,0:T(4,128)S(1)}, u32[]{:S(2)}, u32[]{:S(2)}) %collective-permute-start.40) | collective-permute-done | bytes 8224 | tf_op jit(solution)/shard_map/ppermute | solution.py:554
  91.2 2.2 %collective-permute-start.43 = (f32[4,4,128]{2,1,0:T(4,128)S(1)}, f32[4,4,128]{2,1,0:T(4,128)S(1)}, u32[]{:S(2)}, u32[]{:S(2)}) collective-permute-start(f32[4,4,128]{2,1,0:T(4,128)S(1)} %get-tuple-element.245.refs_5_), channel_id=1, source_target_pairs={{0,4},{4,0},{8,12},{12,8},{16,20},{20,16},{24,28},{28,24},{1,5},{5... | collective-permute-start | bytes 24584 | tf_op jit(solution)/shard_map/ppermute | solution.py:560
  95.1 1.4 %collective-permute-done.44.refs_8_ = f32[4,4,128]{2,1,0:T(4,128)S(1)} collective-permute-done((f32[4,4,128]{2,1,0:T(4,128)S(1)}, f32[4,4,128]{2,1,0:T(4,128)S(1)}, u32[]{:S(2)}, u32[]{:S(2)}) %collective-permute-start.44) | collective-permute-done | bytes 8224 | tf_op jit(solution)/shard_map/ppermute | solution.py:554
  96.5 1.7 %shard_map.162 = (f32[16,4,128]{2,1,0:T(4,128)S(1)}, f32[16,1,128]{2,1,0:T(1,128)S(1)}, f32[16,4,128]{2,1,0:T(4,128)S(1)}, f32[16,4,128]{2,1,0:T(4,128)S(1)}, s3...) custom-call(s32[4,16]{1,0:T(4,128)S(4)} %get-tuple-element.154.refs_, ...), custom_call_target="tpu_custom_call", output_to_operand_aliasing={{1}: (2, {}), {2}: (10, {}), {3}: (3, {}), {4}: (4, {}), {5... | custom-call | bytes 7000000 | tf_op jit(solution)/shard_map/pallas_call | solution.py:61
  98.3 2.6 %collective-permute-start.47 = (f32[16,4,128]{2,1,0:T(4,128)S(1)}, f32[16,4,128]{2,1,0:T(4,128)S(1)}, u32[]{:S(2)}, u32[]{:S(2)}) collective-permute-start(f32[16,4,128]{2,1,0:T(4,128)S(1)} %get-tuple-element.250.refs_4_), channel_id=1, source_target_pairs={{0,4},{4,0},{8,12},{12,8},{16,20},{20,16},{24,28},{28,24},{1,5},{5... | collective-permute-start | bytes 98312 | tf_op jit(solution)/shard_map/ppermute | solution.py:560
  102.8 1.4 %collective-permute-done.48.refs_7_ = f32[16,4,128]{2,1,0:T(4,128)S(1)} collective-permute-done((f32[16,4,128]{2,1,0:T(4,128)S(1)}, f32[16,4,128]{2,1,0:T(4,128)S(1)}, u32[]{:S(2)}, u32[]{:S(2)}) %collective-permute-start.48) | collective-permute-done | bytes 32800 | tf_op jit(solution)/shard_map/ppermute | solution.py:554
  105.6 2.1 %collective-permute-start.51 = (f32[16,4,128]{2,1,0:T(4,128)S(1)}, f32[16,4,128]{2,1,0:T(4,128)S(1)}, u32[]{:S(2)}, u32[]{:S(2)}) collective-permute-start(f32[16,4,128]{2,1,0:T(4,128)S(1)} %get-tuple-element.254.refs_6_), channel_id=1, source_target_pairs={{0,4},{4,0},{8,12},{12,8},{16,20},{20,16},{24,28},{28,24},{1,5},{5... | collective-permute-start | bytes 98312 | tf_op jit(solution)/shard_map/ppermute | solution.py:560
  109.5 1.4 %collective-permute-done.52.refs_9_ = f32[16,4,128]{2,1,0:T(4,128)S(1)} collective-permute-done((f32[16,4,128]{2,1,0:T(4,128)S(1)}, f32[16,4,128]{2,1,0:T(4,128)S(1)}, u32[]{:S(2)}, u32[]{:S(2)}) %collective-permute-start.52) | collective-permute-done | bytes 32800 | tf_op jit(solution)/shard_map/ppermute | solution.py:554
  111.0 2.6 %shard_map.164 = (f32[4,128,128]{2,1,0:T(8,128)S(1)}, f32[4,4,128]{2,1,0:T(4,128)S(1)}, f32[4,4,128]{2,1,0:T(4,128)S(1)}, f32[16,1,128]{2,1,0:T(1,128)S(1)}, f32...) custom-call(s32[9]{0:T(128)S(4)} %get-tuple-element.133.refs_0_, ...), custom_call_target="tpu_custom_call", output_to_operand_aliasing={{3}: (3, {}), {4}: (4, {}), {5}: (1, {})} | custom-call | bytes 10500000 | tf_op jit(solution)/shard_map/pallas_call | solution.py:61
  114.7 2.0 %collective-permute-done.54.refs_2_ = f32[4,4,128]{2,1,0:T(4,128)S(1)} collective-permute-done((f32[4,4,128]{2,1,0:T(4,128)S(1)}, f32[4,4,128]{2,1,0:T(4,128)S(1)}, u32[]{:S(2)}, u32[]{:S(2)}) %collective-permute-start.54) | collective-permute-done | bytes 8224 | tf_op jit(solution)/shard_map/ppermute | solution.py:554
  117.0 2.9 %collective-permute-start.57 = (f32[4,4,256]{2,1,0:T(4,128)S(1)}, f32[4,4,256]{2,1,0:T(4,128)S(1)}, u32[]{:S(2)}, u32[]{:S(2)}) collective-permute-start(f32[4,4,256]{2,1,0:T(4,128)S(1)} %get-tuple-element.260), channel_id=1, source_target_pairs={{0,4},{4,0},{8,12},{12,8},{16,20},{20,16},{24,28},{28,24},{1,5},{5... | collective-permute-start | bytes 49160 | tf_op jit(solution)/shard_map/ppermute | solution.py:560
  119.9 1.7 %collective-permute-done.57.refs_4_ = f32[4,4,256]{2,1,0:T(4,128)S(1)} collective-permute-done((f32[4,4,256]{2,1,0:T(4,128)S(1)}, f32[4,4,256]{2,1,0:T(4,128)S(1)}, u32[]{:S(2)}, u32[]{:S(2)}) %collective-permute-start.57) | collective-permute-done | bytes 16416 | tf_op jit(solution)/shard_map/ppermute | solution.py:560
  121.6 2.2 %shard_map.166 = f32[4,128,128]{2,1,0:T(8,128)} custom-call(s32[9]{0:T(128)S(4)} %get-tuple-element.133.refs_0_, f32[11,144,256]{2,1,0:T(8,128)S(1)} %copy-done.1, f32[4,128,256]{2,1,0:T(8,128)S(1)} %get-tuple-element.258.refs_2_, f32[4,4,256]{2,1,0:T(4,128)S(1)} %collective-permute-done.56.refs_3_, f32[4,4,256]{2,1,0:T(4,128)S(1)} %collective-permute-done.57.refs_4_), custom_call_target="tpu_custom_call" | custom-call | bytes 7000000 | tf_op jit(solution)/shard_map/pallas_call | solution.py:61
  (132 shorter events, 44.2 us)
Async XLA Ops:
  1.2 10.6 %collective-permute-start.2 = (f32[1,2,32,128]{3,2,1,0:T(8,128)S(1)}, f32[1,2,32,128]{3,2,1,0:T(8,128)S(1)}, u32[]{:S(2)}, u32[]{:S(2)}) collective-permute-start(f32[1,2,32,128]{3,2,1,0:T(8,128)S(1)} %get-tuple-element.146), channel_id=1, source_target_pairs={{0,16},{4,20},{8,24},{12,28},{16,0},{20,4},{24,8},{28,12},{1,17},{... | collective-permute-start | bytes 98312 | tf_op jit(solution)/shard_map/ppermute | solution.py:599
  5.3 6.3 %collective-permute-start = (f32[6,4,128]{2,1,0:T(4,128)S(1)}, f32[6,4,128]{2,1,0:T(4,128)S(1)}, u32[]{:S(2)}, u32[]{:S(2)}) collective-permute-start(f32[6,4,128]{2,1,0:T(4,128)S(1)} %get-tuple-element.138), channel_id=1, source_target_pairs={{1,2},{2,1},{0,3},{3,0},{5,6},{6,5},{4,7},{7,4},{9,10},{10,9},{8,1... | collective-permute-start | bytes 36872 | tf_op jit(solution)/shard_map/ppermute | solution.py:554
  6.0 5.6 %collective-permute-start.1 = (f32[6,4,128]{2,1,0:T(4,128)S(1)}, f32[6,4,128]{2,1,0:T(4,128)S(1)}, u32[]{:S(2)}, u32[]{:S(2)}) collective-permute-start(f32[6,4,128]{2,1,0:T(4,128)S(1)} %get-tuple-element.144), channel_id=1, source_target_pairs={{0,1},{1,0},{2,3},{3,2},{4,5},{5,4},{6,7},{7,6},{8,9},{9,8},{10,11... | collective-permute-start | bytes 36872 | tf_op jit(solution)/shard_map/ppermute | solution.py:555
  11.8 10.6 %collective-permute-start.5 = (f32[2,2,32,128]{3,2,1,0:T(8,128)S(1)}, f32[2,2,32,128]{3,2,1,0:T(8,128)S(1)}, u32[]{:S(2)}, u32[]{:S(2)}) collective-permute-start(f32[2,2,32,128]{3,2,1,0:T(8,128)S(1)} %pad_maximum_fusion.2), channel_id=1, source_target_pairs={{0,8},{4,12},{8,0},{12,4},{16,24},{20,28},{24,16},{28,20},{1,9},{5... | collective-permute-start | bytes 196616 | tf_op jit(solution)/shard_map/ppermute | solution.py:599
  13.5 5.4 %collective-permute-start.3 = (f32[6,4,256]{2,1,0:T(4,128)S(1)}, f32[6,4,256]{2,1,0:T(4,128)S(1)}, u32[]{:S(2)}, u32[]{:S(2)}) collective-permute-start(f32[6,4,256]{2,1,0:T(4,128)S(1)} %get-tuple-element.149), channel_id=1, source_target_pairs={{4,8},{5,9},{6,10},{7,11},{8,4},{9,5},{10,6},{11,7},{12,16},{13,17... | collective-permute-start | bytes 73736 | tf_op jit(solution)/shard_map/ppermute | solution.py:559
  13.5 5.4 %collective-permute-start.4 = (f32[6,4,256]{2,1,0:T(4,128)S(1)}, f32[6,4,256]{2,1,0:T(4,128)S(1)}, u32[]{:S(2)}, u32[]{:S(2)}) collective-permute-start(f32[6,4,256]{2,1,0:T(4,128)S(1)} %get-tuple-element.150), channel_id=1, source_target_pairs={{0,4},{4,0},{8,12},{12,8},{16,20},{20,16},{24,28},{28,24},{1,5},{5... | collective-permute-start | bytes 73736 | tf_op jit(solution)/shard_map/ppermute | solution.py:560
  22.4 9.3 %collective-permute-start.10 = (f32[4,2,32,128]{3,2,1,0:T(8,128)S(1)}, f32[4,2,32,128]{3,2,1,0:T(8,128)S(1)}, u32[]{:S(2)}, u32[]{:S(2)}) collective-permute-start(f32[4,2,32,128]{3,2,1,0:T(8,128)S(1)} %pad_maximum_fusion.1), channel_id=1, source_target_pairs={{0,4},{4,0},{8,12},{12,8},{16,20},{20,16},{24,28},{28,24},{1,5},{5... | collective-permute-start | bytes 393224 | tf_op jit(solution)/shard_map/ppermute | solution.py:599
  23.3 4.4 %collective-permute-start.6 = (f32[21,4,128]{2,1,0:T(4,128)S(1)}, f32[21,4,128]{2,1,0:T(4,128)S(1)}, u32[]{:S(2)}, u32[]{:S(2)}) collective-permute-start(f32[21,4,128]{2,1,0:T(4,128)S(1)} %get-tuple-element.163.refs_4_.refs_1_), channel_id=1, source_target_pairs={{4,8},{5,9},{6,10},{7,11},{8,4},{9,5},{10,6},{11,7},{12,16},{13,17... | collective-permute-start | bytes 129032 | tf_op jit(solution)/shard_map/ppermute | solution.py:559
  23.3 5.8 %collective-permute-start.7 = (f32[21,4,128]{2,1,0:T(4,128)S(1)}, f32[21,4,128]{2,1,0:T(4,128)S(1)}, u32[]{:S(2)}, u32[]{:S(2)}) collective-permute-start(f32[21,4,128]{2,1,0:T(4,128)S(1)} %get-tuple-element.163.refs_4_.refs_1_), channel_id=1, source_target_pairs={{0,4},{4,0},{8,12},{12,8},{16,20},{20,16},{24,28},{28,24},{1,5},{5... | collective-permute-start | bytes 129032 | tf_op jit(solution)/shard_map/ppermute | solution.py:560
  27.0 3.4 %collective-permute-start.8 = (f32[21,4,128]{2,1,0:T(4,128)S(1)}, f32[21,4,128]{2,1,0:T(4,128)S(1)}, u32[]{:S(2)}, u32[]{:S(2)}) collective-permute-start(f32[21,4,128]{2,1,0:T(4,128)S(1)} %get-tuple-element.163.refs_4_.refs_1_), channel_id=1, source_target_pairs={{1,2},{2,1},{0,3},{3,0},{5,6},{6,5},{4,7},{7,4},{9,10},{10,9},{8,1... | collective-permute-start | bytes 129032 | tf_op jit(solution)/shard_map/ppermute | solution.py:554
  27.0 3.4 %collective-permute-start.9 = (f32[21,4,128]{2,1,0:T(4,128)S(1)}, f32[21,4,128]{2,1,0:T(4,128)S(1)}, u32[]{:S(2)}, u32[]{:S(2)}) collective-permute-start(f32[21,4,128]{2,1,0:T(4,128)S(1)} %get-tuple-element.163.refs_4_.refs_1_), channel_id=1, source_target_pairs={{0,1},{1,0},{2,3},{3,2},{4,5},{5,4},{6,7},{7,6},{8,9},{9,8},{10,11... | collective-permute-start | bytes 129032 | tf_op jit(solution)/shard_map/ppermute | solution.py:555
  31.7 8.7 %collective-permute-start.15 = (f32[8,2,32,128]{3,2,1,0:T(8,128)S(1)}, f32[8,2,32,128]{3,2,1,0:T(8,128)S(1)}, u32[]{:S(2)}, u32[]{:S(2)}) collective-permute-start(f32[8,2,32,128]{3,2,1,0:T(8,128)S(1)} %pad_maximum_fusion.refs_1_), channel_id=1, source_target_pairs={{0,2},{1,3},{2,0},{3,1},{4,6},{5,7},{6,4},{7,5},{8,10},{9,11},{10,... | collective-permute-start | bytes 786440 | tf_op jit(solution)/shard_map/ppermute | solution.py:599
  32.7 3.9 %collective-permute-start.12 = (f32[16,4,128]{2,1,0:T(4,128)S(1)}, f32[16,4,128]{2,1,0:T(4,128)S(1)}, u32[]{:S(2)}, u32[]{:S(2)}) collective-permute-start(f32[16,4,128]{2,1,0:T(4,128)S(1)} %get-tuple-element.169.refs_4_), channel_id=1, source_target_pairs={{0,4},{4,0},{8,12},{12,8},{16,20},{20,16},{24,28},{28,24},{1,5},{5... | collective-permute-start | bytes 98312 | tf_op jit(solution)/shard_map/ppermute | solution.py:560
  34.6 4.6 %collective-permute-start.13 = (f32[16,4,128]{2,1,0:T(4,128)S(1)}, f32[16,4,128]{2,1,0:T(4,128)S(1)}, u32[]{:S(2)}, u32[]{:S(2)}) collective-permute-start(f32[16,4,128]{2,1,0:T(4,128)S(1)} %get-tuple-element.169.refs_4_), channel_id=1, source_target_pairs={{1,2},{2,1},{0,3},{3,0},{5,6},{6,5},{4,7},{7,4},{9,10},{10,9},{8,1... | collective-permute-start | bytes 98312 | tf_op jit(solution)/shard_map/ppermute | solution.py:554
  34.6 4.6 %collective-permute-start.14 = (f32[16,4,128]{2,1,0:T(4,128)S(1)}, f32[16,4,128]{2,1,0:T(4,128)S(1)}, u32[]{:S(2)}, u32[]{:S(2)}) collective-permute-start(f32[16,4,128]{2,1,0:T(4,128)S(1)} %get-tuple-element.169.refs_4_), channel_id=1, source_target_pairs={{0,1},{1,0},{2,3},{3,2},{4,5},{5,4},{6,7},{7,6},{8,9},{9,8},{10,11... | collective-permute-start | bytes 98312 | tf_op jit(solution)/shard_map/ppermute | solution.py:555
  40.5 13.9 %collective-permute-start.24 = (f32[8,2,32,128]{3,2,1,0:T(8,128)S(1)}, f32[8,2,32,128]{3,2,1,0:T(8,128)S(1)}, u32[]{:S(2)}, u32[]{:S(2)}) collective-permute-start(f32[8,2,32,128]{3,2,1,0:T(8,128)S(1)} %pad_maximum_fusion.refs_1_), channel_id=1, source_target_pairs={{0,1},{1,0},{2,3},{3,2},{4,5},{5,4},{6,7},{7,6},{8,9},{9,8},{10,11... | collective-permute-start | bytes 786440 | tf_op jit(solution)/shard_map/ppermute | solution.py:599
  41.1 13.2 %collective-permute-start.25 = (f32[8,2,32,128]{3,2,1,0:T(8,128)S(1)}, f32[8,2,32,128]{3,2,1,0:T(8,128)S(1)}, u32[]{:S(2)}, u32[]{:S(2)}) collective-permute-start(f32[8,2,32,128]{3,2,1,0:T(8,128)S(1)} %collective-permute-done.15.refs_2_), channel_id=1, source_target_pairs={{0,1},{1,0},{2,3},{3,2},{4,5},{5,4},{6,7},{7,6},{8,9},{9,8},{10,11... | collective-permute-start | bytes 786440 | tf_op jit(solution)/shard_map/ppermute | solution.py:599
  41.6 3.9 %collective-permute-start.17 = (f32[16,4,128]{2,1,0:T(4,128)S(1)}, f32[16,4,128]{2,1,0:T(4,128)S(1)}, u32[]{:S(2)}, u32[]{:S(2)}) collective-permute-start(f32[16,4,128]{2,1,0:T(4,128)S(1)} %get-tuple-element.176.refs_5_), channel_id=1, source_target_pairs={{0,4},{4,0},{8,12},{12,8},{16,20},{20,16},{24,28},{28,24},{1,5},{5... | collective-permute-start | bytes 98312 | tf_op jit(solution)/shard_map/ppermute | solution.py:560
  43.1 3.4 %collective-permute-start.18 = (f32[16,4,128]{2,1,0:T(4,128)S(1)}, f32[16,4,128]{2,1,0:T(4,128)S(1)}, u32[]{:S(2)}, u32[]{:S(2)}) collective-permute-start(f32[16,4,128]{2,1,0:T(4,128)S(1)} %get-tuple-element.176.refs_5_), channel_id=1, source_target_pairs={{1,2},{2,1},{0,3},{3,0},{5,6},{6,5},{4,7},{7,4},{9,10},{10,9},{8,1... | collective-permute-start | bytes 98312 | tf_op jit(solution)/shard_map/ppermute | solution.py:554
  48.1 3.6 %collective-permute-start.20 = (f32[4,4,128]{2,1,0:T(4,128)S(1)}, f32[4,4,128]{2,1,0:T(4,128)S(1)}, u32[]{:S(2)}, u32[]{:S(2)}) collective-permute-start(f32[4,4,128]{2,1,0:T(4,128)S(1)} %get-tuple-element.183.refs_4_), channel_id=1, source_target_pairs={{4,8},{5,9},{6,10},{7,11},{8,4},{9,5},{10,6},{11,7},{12,16},{13,17... | collective-permute-start | bytes 24584 | tf_op jit(solution)/shard_map/ppermute | solution.py:559
  48.3 4.4 %collective-permute-start.21 = (f32[4,4,128]{2,1,0:T(4,128)S(1)}, f32[4,4,128]{2,1,0:T(4,128)S(1)}, u32[]{:S(2)}, u32[]{:S(2)}) collective-permute-start(f32[4,4,128]{2,1,0:T(4,128)S(1)} %get-tuple-element.183.refs_4_), channel_id=1, source_target_pairs={{0,4},{4,0},{8,12},{12,8},{16,20},{20,16},{24,28},{28,24},{1,5},{5... | collective-permute-start | bytes 24584 | tf_op jit(solution)/shard_map/ppermute | solution.py:560
  54.3 4.7 %collective-permute-start.26 = (f32[4,4,128]{2,1,0:T(4,128)S(1)}, f32[4,4,128]{2,1,0:T(4,128)S(1)}, u32[]{:S(2)}, u32[]{:S(2)}) collective-permute-start(f32[4,4,128]{2,1,0:T(4,128)S(1)} %get-tuple-element.194.refs_4_), channel_id=1, source_target_pairs={{4,8},{5,9},{6,10},{7,11},{8,4},{9,5},{10,6},{11,7},{12,16},{13,17... | collective-permute-start | bytes 24584 | tf_op jit(solution)/shard_map/ppermute | solution.py:559
  54.5 4.5 %collective-permute-start.27 = (f32[4,4,128]{2,1,0:T(4,128)S(1)}, f32[4,4,128]{2,1,0:T(4,128)S(1)}, u32[]{:S(2)}, u32[]{:S(2)}) collective-permute-start(f32[4,4,128]{2,1,0:T(4,128)S(1)} %get-tuple-element.194.refs_4_), channel_id=1, source_target_pairs={{0,4},{4,0},{8,12},{12,8},{16,20},{20,16},{24,28},{28,24},{1,5},{5... | collective-permute-start | bytes 24584 | tf_op jit(solution)/shard_map/ppermute | solution.py:560
  60.5 3.9 %collective-permute-start.30 = (f32[4,4,128]{2,1,0:T(4,128)S(1)}, f32[4,4,128]{2,1,0:T(4,128)S(1)}, u32[]{:S(2)}, u32[]{:S(2)}) collective-permute-start(f32[4,4,128]{2,1,0:T(4,128)S(1)} %get-tuple-element.206.refs_6_), channel_id=1, source_target_pairs={{4,8},{5,9},{6,10},{7,11},{8,4},{9,5},{10,6},{11,7},{12,16},{13,17... | collective-permute-start | bytes 24584 | tf_op jit(solution)/shard_map/ppermute | solution.py:559
  60.7 3.7 %collective-permute-start.31 = (f32[4,4,128]{2,1,0:T(4,128)S(1)}, f32[4,4,128]{2,1,0:T(4,128)S(1)}, u32[]{:S(2)}, u32[]{:S(2)}) collective-permute-start(f32[4,4,128]{2,1,0:T(4,128)S(1)} %get-tuple-element.206.refs_6_), channel_id=1, source_target_pairs={{0,4},{4,0},{8,12},{12,8},{16,20},{20,16},{24,28},{28,24},{1,5},{5... | collective-permute-start | bytes 24584 | tf_op jit(solution)/shard_map/ppermute | solution.py:560
  80.1 3.7 %collective-permute-start.35 = (f32[4,4,128]{2,1,0:T(4,128)S(1)}, f32[4,4,128]{2,1,0:T(4,128)S(1)}, u32[]{:S(2)}, u32[]{:S(2)}) collective-permute-start(f32[4,4,128]{2,1,0:T(4,128)S(1)} %get-tuple-element.227.refs_4_), channel_id=1, source_target_pairs={{0,4},{4,0},{8,12},{12,8},{16,20},{20,16},{24,28},{28,24},{1,5},{5... | collective-permute-start | bytes 24584 | tf_op jit(solution)/shard_map/ppermute | solution.py:560
  85.6 3.7 %collective-permute-start.39 = (f32[4,4,128]{2,1,0:T(4,128)S(1)}, f32[4,4,128]{2,1,0:T(4,128)S(1)}, u32[]{:S(2)}, u32[]{:S(2)}) collective-permute-start(f32[4,4,128]{2,1,0:T(4,128)S(1)} %get-tuple-element.236.refs_4_), channel_id=1, source_target_pairs={{0,4},{4,0},{8,12},{12,8},{16,20},{20,16},{24,28},{28,24},{1,5},{5... | collective-permute-start | bytes 24584 | tf_op jit(solution)/shard_map/ppermute | solution.py:560
  91.2 3.9 %collective-permute-start.43 = (f32[4,4,128]{2,1,0:T(4,128)S(1)}, f32[4,4,128]{2,1,0:T(4,128)S(1)}, u32[]{:S(2)}, u32[]{:S(2)}) collective-permute-start(f32[4,4,128]{2,1,0:T(4,128)S(1)} %get-tuple-element.245.refs_5_), channel_id=1, source_target_pairs={{0,4},{4,0},{8,12},{12,8},{16,20},{20,16},{24,28},{28,24},{1,5},{5... | collective-permute-start | bytes 24584 | tf_op jit(solution)/shard_map/ppermute | solution.py:560
  98.2 3.5 %collective-permute-start.46 = (f32[16,4,128]{2,1,0:T(4,128)S(1)}, f32[16,4,128]{2,1,0:T(4,128)S(1)}, u32[]{:S(2)}, u32[]{:S(2)}) collective-permute-start(f32[16,4,128]{2,1,0:T(4,128)S(1)} %get-tuple-element.250.refs_4_), channel_id=1, source_target_pairs={{4,8},{5,9},{6,10},{7,11},{8,4},{9,5},{10,6},{11,7},{12,16},{13,17... | collective-permute-start | bytes 98312 | tf_op jit(solution)/shard_map/ppermute | solution.py:559
  98.3 4.5 %collective-permute-start.47 = (f32[16,4,128]{2,1,0:T(4,128)S(1)}, f32[16,4,128]{2,1,0:T(4,128)S(1)}, u32[]{:S(2)}, u32[]{:S(2)}) collective-permute-start(f32[16,4,128]{2,1,0:T(4,128)S(1)} %get-tuple-element.250.refs_4_), channel_id=1, source_target_pairs={{0,4},{4,0},{8,12},{12,8},{16,20},{20,16},{24,28},{28,24},{1,5},{5... | collective-permute-start | bytes 98312 | tf_op jit(solution)/shard_map/ppermute | solution.py:560
  105.6 4.0 %collective-permute-start.51 = (f32[16,4,128]{2,1,0:T(4,128)S(1)}, f32[16,4,128]{2,1,0:T(4,128)S(1)}, u32[]{:S(2)}, u32[]{:S(2)}) collective-permute-start(f32[16,4,128]{2,1,0:T(4,128)S(1)} %get-tuple-element.254.refs_6_), channel_id=1, source_target_pairs={{0,4},{4,0},{8,12},{12,8},{16,20},{20,16},{24,28},{28,24},{1,5},{5... | collective-permute-start | bytes 98312 | tf_op jit(solution)/shard_map/ppermute | solution.py:560
  117.0 4.6 %collective-permute-start.57 = (f32[4,4,256]{2,1,0:T(4,128)S(1)}, f32[4,4,256]{2,1,0:T(4,128)S(1)}, u32[]{:S(2)}, u32[]{:S(2)}) collective-permute-start(f32[4,4,256]{2,1,0:T(4,128)S(1)} %get-tuple-element.260), channel_id=1, source_target_pairs={{0,4},{4,0},{8,12},{12,8},{16,20},{20,16},{24,28},{28,24},{1,5},{5... | collective-permute-start | bytes 49160 | tf_op jit(solution)/shard_map/ppermute | solution.py:560
  (37 other events, 210.2 us)

commit v4 on v3

--- a/solution.py
+++ b/solution.py
@@ -38,7 +38,8 @@
 def call(kernel, outs, ins, scratch=(), specs=None, mib=12, us=2, hold=None, far=(), loose=(), scalars=()):
     hold = {} if hold is None else hold
     outs, tree = jax.tree.flatten(outs)
-    specs = specs or [VMEM] * len(ins)
+    specs = jax.tree.leaves([[spec] * len(x) if isinstance(x, tuple) else spec for x, spec in zip(ins, specs)])
+    ins, shape_in = jax.tree.flatten(list(ins))
     places = {x: i for i, x in enumerate(ins) if isinstance(x, str)}
     rest = [name for name in hold if name not in places]
     places |= {name: len(ins) + i for i, name in enumerate(rest)}
@@ -53,7 +54,7 @@
     def inner(*refs):
         first = len(inputs)
         kernel(
-            *refs[:count_in],
+            *jax.tree.unflatten(shape_in, refs[:count_in]),
             *refs[first : first + count_out],
             *refs[first + count_out + len(hold) :],
         )
@@ -106,7 +107,7 @@
     return hi, (m - hi.astype(F32)).astype(BF16)
 
 
-def split_tile(tile, r, k, t_ref, d_ref):
+def split_tile(tile, r, k, t_ref, d_ref, first=0):
     size = tile.shape[0]
     if size < LANES:
         tile = jnp.concatenate([tile, jnp.zeros((size, LANES - size), F32)], axis=1)
@@ -118,39 +119,62 @@
         col = lax.broadcasted_iota(jnp.int32, tile.shape, 1)
         diag = jnp.sum(jnp.where(row == col, tile, 0.0), axis=0, keepdims=True)
         lane = lax.broadcasted_iota(jnp.int32, diag.shape, 1)
-        d_ref[r] = jnp.where(lane < size, diag, 1.0)
-
-
-def tiles_kernel(parts, tiles, t_ref, d_ref, far, held, sems, far_sems):
-    count, slots = tiles.shape[:2]
-    step = count // parts
-    spans = [pl.ds(i * step, step) for i in range(parts)]
-    loads = [pltpu.make_async_copy(tiles.at[a], held.at[a], sems.at[i]) for i, a in enumerate(spans)]
-    stores = [pltpu.make_async_copy(t_ref.at[a], far.at[a], far_sems.at[i]) for i, a in enumerate(spans)]
-    for load in loads:
-        load.start()
-    for i in range(parts):
-        loads[i].wait()
-        for r in range(i * step, (i + 1) * step):
-            for k in range(slots):
-                split_tile(held[r, k], r, k, t_ref, d_ref)
-        stores[i].start()
-    for store in stores:
-        store.wait()
-
-
-def small_tiles_kernel(tiles, t_ref, d_ref):
-    t_ref[...] = jnp.zeros_like(t_ref)
-    for r in range(tiles.shape[0]):
-        for k in range(tiles.shape[1]):
-            split_tile(tiles[r, k], r, k, t_ref, d_ref)
-
-
-def index_kernel(flags, columns1, live1, columns2, live2, idx1, idx2, held1, held2, turned, sems):
+        d_ref[first + r] = jnp.where(lane < size, diag, 1.0)
+
+
+class Stream:
+    def __init__(self, half, tiles, held, t_ref, far, sems, parts=4):
+        self.count, self.slots = held.shape[0], held.shape[1]
+        self.step = self.count // parts
+        self.held, self.t_ref = held, t_ref
+        spans = [pl.ds(i * self.step, self.step) for i in range(parts)]
+        self.loads = [
+            pltpu.make_async_copy(tiles.at[pl.ds(half * self.count + i * self.step, self.step)], held.at[a], sems.at[i])
+            for i, a in enumerate(spans)
+        ]
+        self.stores = [
+            pltpu.make_async_copy(t_ref.at[a], far.at[a], sems.at[parts + i]) for i, a in enumerate(spans)
+        ]
+        for load in self.loads:
+            load.start()
+
+    def run(self, d_ref, first):
+        for i, load in enumerate(self.loads):
+            load.wait()
+            for r in range(i * self.step, (i + 1) * self.step):
+                for k in range(self.slots):
+                    split_tile(self.held[r, k], r, k, self.t_ref, d_ref, first)
+            self.stores[i].start()
+
+    def end(self):
+        for store in self.stores:
+            store.wait()
+
+
+def second_half_kernel(tiles, d_first, t_ref, d_ref, far, held, sems):
+    stream = Stream(1, tiles, held, t_ref, far, sems)
+    count = d_first.shape[0]
+    d_ref[0:count] = d_first[...]
+    stream.run(d_ref, count)
+    stream.end()
+
+
+def setup_kernel(
+    flags, columns1, live1, columns2, live2, tiles1, tiles2,
+    idx1, idx2, t1, d1, t2, d2, far,
+    in1, in2, in3, in4, held_tiles, held2, held1, held_two, turned, sems, stream_sems,
+):
+    ins = ((columns1, in1), (live1, in2), (columns2, in3), (live2, in4), (tiles2, held2))
+    ins = [pltpu.make_async_copy(a, b, sems.at[i]) for i, (a, b) in enumerate(ins)]
+    for copy in ins:
+        copy.start()
+    stream = Stream(0, tiles1, held_tiles, t1, far, stream_sems)
+    for copy in ins:
+        copy.wait()
     w_odd, n_odd = flags[W_ODD], flags[N_ODD]
     region = (0, 1 + w_odd, 2 - w_odd, 3 + n_odd, 4 - n_odd)
     there = (1, flags[HAS_WEST], flags[HAS_EAST], flags[HAS_SOUTH], flags[HAS_NORTH])
-    for columns, live, held, dim in ((columns1, live1, held1, 1), (columns2, live2, held2, 0)):
+    for columns, live, held, dim in ((in1, in2, held1, 1), (in3, in4, held_two, 0)):
         code = columns[...]
         count = code.shape[dim]
         place = jnp.full(code.shape, 5 * count, jnp.int32)
@@ -166,16 +190,22 @@
             held[:, 1:] = place
     copies = [
         pltpu.make_async_copy(held1, idx1, sems.at[0]),
-        pltpu.make_async_copy(held2, turned, sems.at[1]),
+        pltpu.make_async_copy(held_two, turned, sems.at[1]),
     ]
     for copy in copies:
         copy.start()
+    t2[...] = jnp.zeros_like(t2)
+    for r in range(held2.shape[0]):
+        for k in range(held2.shape[1]):
+            split_tile(held2[r, k], r, k, t2, d2)
+    stream.run(d1, 0)
     for copy in copies:
         copy.wait()
     slots, count = idx2.shape
     for k in range(slots):
         for r in range(count):
             idx2[k, r] = turned[r, k]
+    stream.end()
 
 
 def apply_tiles(t_ref, xs, idx):
@@ -183,7 +213,8 @@
     out = []
     for r in range(count):
         lhs = twice(jnp.concatenate([xs[idx[k, r]] for k in range(slots)], axis=1))
-        both = dot_nt(lhs, t_ref[r])[0:8]
+        t, at = t_ref[r // t_ref[0].shape[0]], r % t_ref[0].shape[0]
+        both = dot_nt(lhs, t[at])[0:8]
         out.append(rows_sum(both[:, :LANES] + both[:, LANES:]))
     return out
 
@@ -598,13 +629,12 @@
     def swap(x, axis, step):
         return lax.ppermute(x, axis, [(i, i ^ step) for i in range(lax.axis_size(axis))])
 
-    def gather_step(*anchor):
+    def gather_step(anchor):
         step = order[len(done)]
         merged = held if len(done) == len(order) - 1 or len(held) == 1 else [jnp.concatenate(held, axis=0)]
-        merged, anchor = lax.optimization_barrier((merged, anchor))
+        merged, _ = lax.optimization_barrier((merged, anchor))
         held[:] = merged + [swap(m, *step) for m in merged]
         done.append(step)
-        return anchor
 
     rim = sds((cols + 2, RIM, LANES))
     flags = sds((LEVEL3 + 1,), jnp.int32)
@@ -617,33 +647,43 @@
         scalars=(0,),
     )
     held.append(piece)
-    first, second = gather_step(first, second)
+    gather_step(first)
     o2, o1 = exchange_narrow(first, second, route)
 
-    shapes = (sds((slots, count1), jnp.int32), sds((slots, count2), jnp.int32))
-    idx1, idx2 = call(
-        index_kernel,
-        list(shapes),
-        (flags, columns_one.T, live_one.T, columns_two, live_two),
-        scratch=[
+    half = count1 // 2
+    split = sds((half, 2 * LANES, slots * LANES), BF16)
+    held_tiles = [pltpu.VMEM((half, *tiles_one.shape[1:]), F32)]
+    stream_sems = [pltpu.SemaphoreType.DMA((8,))]
+    idx1, idx2, tiles1, d1, tiles2, d2, tiles1_far = call(
+        setup_kernel,
+        [
+            sds((slots, count1), jnp.int32),
+            sds((slots, count2), jnp.int32),
+            split,
+            sds((half, 1, LANES)),
+            sds((count2, *split.shape[1:]), BF16),
+            sds((count2, 1, LANES)),
+            split,
+        ],
+        (flags, columns_one.T, live_one.T, columns_two, live_two, tiles_one, tiles_two),
+        scratch=[pltpu.VMEM((slots - 1, count1), jnp.int32)] * 2
+        + [pltpu.VMEM((count2, slots - 1), jnp.int32)] * 2
+        + held_tiles
+        + [
+            pltpu.VMEM(tiles_two.shape, F32),
             pltpu.VMEM((slots, count1), jnp.int32),
             pltpu.VMEM((count2, slots), jnp.int32),
             pltpu.SMEM((count2, slots), jnp.int32),
-            pltpu.SemaphoreType.DMA((2,)),
-        ],
-        specs=[SMEM] + [VMEM] * 4,
-        us=0.5,
+            pltpu.SemaphoreType.DMA((5,)),
+        ]
+        + stream_sems,
+        specs=[SMEM] + [HBM] * 6,
+        far=(6,),
         scalars=(0, 1),
-    )
-    tiles2, d2 = call(
-        small_tiles_kernel,
-        [sds((count2, 2 * LANES, slots * LANES), BF16), sds((count2, 1, LANES))],
-        (tiles_two,),
-        us=0.7,
     )
     groups1 = coarse_groups.reshape(count1, LANES)
     groups2 = coarser_groups.reshape(-1, LANES)
-    o2, idx1, idx2, tiles2, d2 = lax.optimization_barrier((o2, idx1, idx2, tiles2, d2))
+    o2, idx1, idx2, tiles1, tiles2, d1, d2 = lax.optimization_barrier((o2, idx1, idx2, tiles1, tiles2, d1, d2))
 
     rim = sds((cols + 2, RIM, 2 * LANES))
     ext, first, second = call(
@@ -652,26 +692,21 @@
         (flags, fields, o2, o1),
         specs=[SMEM] + [VMEM] * 3,
     )
-    first, second = gather_step(first, second)
+    gather_step(first)
     o2, o1 = exchange_wide(first, second, route)
     field1 = sds((count1, cols, LANES))
     field2 = sds((count2, cols, LANES))
-    split = sds((count1, 2 * LANES, slots * LANES), BF16)
-    tiles1, d1, tiles1_far = call(
-        functools.partial(tiles_kernel, 4),
+    tiles1_second, d1, tiles1_second_far = call(
+        second_half_kernel,
         [split, sds((count1, 1, LANES)), split],
-        (tiles_one,),
-        scratch=[
-            pltpu.VMEM(tiles_one.shape, F32),
-            pltpu.SemaphoreType.DMA((4,)),
-            pltpu.SemaphoreType.DMA((4,)),
-        ],
-        specs=[HBM],
-        us=3,
+        (tiles_one, d1),
+        scratch=held_tiles + stream_sems,
+        specs=[HBM, VMEM],
         far=(2,),
     )
     more = -(-(count1 + count2) // cols)
-    hold = {"t1": tiles1, "d1": d1}
+    hold = {"t1a": tiles1, "t1b": tiles1_second, "d1": d1}
+    t1 = ("t1a", "t1b")
     kept = sds((2 * cols + 3, rows + PAD, 2 * LANES))
     keep, b1, x1 = call(
         fine_down_kernel,
@@ -697,10 +732,10 @@
     def smooth(level, x):
         idx, like, xs = (idx1, field1, xs1) if level == 1 else (idx2, field2, xs2)
         near = exchange(x, route)
-        ins = (idx, f"t{level}", f"d{level}", f"b{level}", x, *near)
+        ins = (idx, t1 if level == 1 else ("t2",), f"d{level}", f"b{level}", x, *near)
         return call(smooth_kernel, like, ins, xs, lead + [VMEM] * 8, hold=hold), near
 
-    (x1,) = gather_step(x1)
+    gather_step(x1)
     x2, near = smooth(1, x1)
     groups = call(
         groups_kernel,
@@ -709,29 +744,29 @@
         specs=[VMEM] * 6,
         us=1,
     )
-    (x2,) = gather_step(x2)
+    gather_step(x2)
     near = exchange(x2, route)
     hold |= {"x2": x2, "groups": groups, "d2": d2}
     left, scaled = call(
         residual_kernel,
         [field1, field1],
-        (idx1, "t1", "d1", "b1", "x2", *near),
+        (idx1, t1, "d1", "b1", "x2", *near),
         xs1,
         lead + [VMEM] * 8,
         hold=hold,
     )
     while len(done) < len(order):
-        (scaled,) = gather_step(scaled)
+        gather_step(scaled)
     b2, y1 = call(
         restrict_one_kernel,
         [field2, field2],
-        (idx1, "t1", left, groups1, "d2", scaled, *exchange(scaled, route)),
+        (idx1, t1, left, groups1, "d2", scaled, *exchange(scaled, route)),
         xs1,
         lead + [VMEM] * 9,
         hold=hold,
     )
 
-    del hold["t1"]
+    del hold["t1a"], hold["t1b"]
     hold |= {"b2": b2, "t2": tiles2}
     y2, _ = smooth(2, y1)
     maps, y2 = lax.optimization_barrier((held, y2))
@@ -753,7 +788,7 @@
     left, scaled = call(
         residual_kernel,
         [field2, field2],
-        (idx2, "t2", "d2", "b2", "y2", *near),
+        (idx2, ("t2",), "d2", "b2", "y2", *near),
         xs2,
         lead + [VMEM] * 8,
         us=1,
@@ -762,7 +797,7 @@
     out3 = call(
         restrict_two_kernel,
         sds((wide * narrow, cols, LANES)),
-        (flags, idx2, "t2", left, "groups", chain_gain, scaled, *exchange(scaled, route)),
+        (flags, idx2, ("t2",), left, "groups", chain_gain, scaled, *exchange(scaled, route)),
         xs2,
         [SMEM, SMEM] + [VMEM] * 9,
         hold=hold,
@@ -771,7 +806,7 @@
     y3 = call(
         chain_kernel,
         field2,
-        (flags, chain if big else "chain", pieces, idx2, "t2", "d2", "y2", "groups"),
+        (flags, chain if big else "chain", pieces, idx2, ("t2",), "d2", "y2", "groups"),
         xs2 + [pltpu.VMEM((wide, cols, LANES), F32)],
         [SMEM, PLAIN if big else VMEM, VMEM, SMEM] + [VMEM] * 4,
         mib=32 if big else 12,
@@ -784,11 +819,11 @@
 
     for name in ("t2", "d2", "b2", "y2"):
         del hold[name]
-    hold["t1"] = tiles1_far
+    hold |= {"t1a": tiles1_far, "t1b": tiles1_second_far}
     x3 = call(
         prolong_one_kernel,
         field1,
-        (idx1, "t1", "d1", "x2", "groups", y5, *exchange(y5, route)),
+        (idx1, t1, "d1", "x2", "groups", y5, *exchange(y5, route)),
         xs1,
         lead + [VMEM] * 9,
         hold=hold,
@@ -799,7 +834,7 @@
     spread, first, second = call(
         fine_spread_kernel,
         [sds((cols, rows, LANES)), rim, rim],
-        (flags, "t1", idx1, "d1", "b1", fine_groups, x4, *exchange(x4, route)),
+        (flags, t1, idx1, "d1", "b1", fine_groups, x4, *exchange(x4, route)),
         xs1 + [pltpu.VMEM((count1, cols, LANES), F32)],
         [SMEM, VMEM, SMEM] + [VMEM] * 8,
         us=3,
@@ -807,7 +842,7 @@
     )
     o2, o1 = exchange_narrow(first, second, route)
     rim = sds((cols, RIM, 2 * LANES))
-    for name in ("t1", "d1", "b1"):
+    for name in ("t1a", "t1b", "d1", "b1"):
         del hold[name]
     ext, first, second = call(
         fine_second_kernel,

time: 124 us -> 122 us (0.984)
  local copies, waits for them, and re-layouts: 3.78 us -> 0.03 us
  Pallas kernels: 25.8 us -> 27.2 us
    unnamed x22 -> x14, local copies, waits for them, and re-layouts: 3.78 us -> 0.03 us
    pallas_call x22 -> x21, Pallas kernels: 25.8 us -> 27.2 us  [call(): pl.pallas_call(inner, out_shape=shapes, in_specs=specs, out_specs=[{pltpu...]
  transfers between devices with their start and end apart: 58 -> 58, of which waited for: 21 -> 21; matrix products, arithmetic and copies ran while one was open for 0% -> 0% of each run, Pallas kernels for 10% -> 12%
where the time goes in v4:
time: 122 us
  starting transfers between devices  55.5 us (45%)
  waiting for transfers between devices  27.4 us (22%)
  Pallas kernels  27.2 us (22%)
  blocking collectives  11 us (9%)
    ppermute x13, starting transfers between devices, exchange_wide(): return (second, lax.ppermute(first, 'wide', route[2]))  29.3 us
    pallas_call x21, Pallas kernels, call(): pl.pallas_call(inner, out_shape=shapes, in_specs=specs, out_specs=[{pltpu...  27.2 us
    ppermute x13, waiting for transfers between devices, exchange_narrow(): second = lax.ppermute(second, 'narrow', route[1])  17.8 us
    ppermute x13, starting transfers between devices, exchange_narrow(): return (second, lax.ppermute(first, 'narrow', route[0]))  11.6 us
    all_to_all x1, blocking collectives, body(): pieces = lax.all_to_all(out3, ('wide', 'narrow'), 0, 0)  11 us
    ppermute x13, waiting for transfers between devices, exchange_wide(): return (second, lax.ppermute(first, 'wide', route[2]))  9.47 us
    ppermute x6, starting transfers between devices, swap(): lax.ppermute(x, axis, [(i, i ^ step) for i in range(lax.axis_size(axis))])  9.18 us
    ppermute x13, starting transfers between devices, exchange_narrow(): second = lax.ppermute(second, 'narrow', route[1])  3.99 us
  transfers between devices with their start and end apart: 58, of which 21 were waited for; matrix products, arithmetic and copies ran while one was open for 0% of the time, Pallas kernels for 12%

profile of v4, /device:TPU:0, one launch (start us, length us, event | category | flops | bytes accessed | tf_op | source)
XLA Modules:
  0.0 121.7 jit_solution(16768325895120846644)
XLA Ops:
  1.2 4.1 %collective-permute-start.20 = (f32[1,2,32,128]{3,2,1,0:T(8,128)S(1)}, f32[1,2,32,128]{3,2,1,0:T(8,128)S(1)}, u32[]{:S(2)}, u32[]{:S(2)}) collective-permute-start(f32[1,2,32,128]{3,2,1,0:T(8,128)S(1)} %get-tuple-element.191), channel_id=1, source_target_pairs={{0,16},{4,20},{8,24},{12,28},{16,0},{20,4},{24,8},{28,12},{1,17},{... | collective-permute-start | bytes 98312 | tf_op jit(solution)/shard_map/ppermute | solution.py:630
  6.9 3.3 %shard_map.146 = (s32[4,16]{1,0:T(4,128)S(4)}, s32[4,4]{1,0:T(4,128)S(4)}, bf16[8,256,512]{2,1,0:T(8,128)(2,1)S(1)}, f32[8,1,128]{2,1,0:T(1,128)S(1)}, bf16[4,25...) custom-call(s32[9]{0:T(128)S(4)} %get-tuple-element.136.refs_0_, s32[3,16]{1,0:T(4,128)} %bitcast.8, ...), custom_call_target="tpu_custom_call" | custom-call | bytes 7000000 | tf_op jit(solution)/shard_map/pallas_call | solution.py:62
  10.4 1.6 %collective-permute-start.21 = (f32[2,2,32,128]{3,2,1,0:T(8,128)S(1)}, f32[2,2,32,128]{3,2,1,0:T(8,128)S(1)}, u32[]{:S(2)}, u32[]{:S(2)}) collective-permute-start(f32[2,2,32,128]{3,2,1,0:T(8,128)S(1)} %pad_maximum_fusion.2), channel_id=1, source_target_pairs={{0,8},{4,12},{8,0},{12,4},{16,24},{20,28},{24,16},{28,20},{1,9},{5... | collective-permute-start | bytes 196616 | tf_op jit(solution)/shard_map/ppermute | solution.py:630
  12.1 1.9 %collective-permute-start.3 = (f32[6,4,256]{2,1,0:T(4,128)S(1)}, f32[6,4,256]{2,1,0:T(4,128)S(1)}, u32[]{:S(2)}, u32[]{:S(2)}) collective-permute-start(f32[6,4,256]{2,1,0:T(4,128)S(1)} %get-tuple-element.149), channel_id=1, source_target_pairs={{0,4},{4,0},{8,12},{12,8},{16,20},{20,16},{24,28},{28,24},{1,5},{5... | collective-permute-start | bytes 73736 | tf_op jit(solution)/shard_map/ppermute | solution.py:591
  14.0 2.6 %shard_map.148 = (bf16[8,256,512]{2,1,0:T(8,128)(2,1)S(1)}, f32[16,1,128]{2,1,0:T(1,128)S(1)}, bf16[8,256,512]{2,1,0:T(8,128)(2,1)}) custom-call(f32[16,4,128,128]{3,2,1,0:T(8,128)} %refs_0_.3, f32[8,1,128]{2,1,0:T(1,128)S(1)} %get-tuple-element.150.refs_1_), custom_call_target="tpu_custom_call" | custom-call | bytes 7000000 | tf_op jit(solution)/shard_map/pallas_call | solution.py:62
  16.6 3.5 %shard_map.149 = (f32[11,144,256]{2,1,0:T(8,128)}, f32[16,4,128]{2,1,0:T(4,128)S(1)}, f32[21,4,128]{2,1,0:T(4,128)S(1)}, bf16[8,256,512]{2,1,0:T(8,128)(2,1)S(1)...) custom-call(s32[9]{0:T(128)S(4)} %get-tuple-element.136.refs_0_, ...), custom_call_target="tpu_custom_call", output_to_operand_aliasing={{3}: (8, {}), {4}: (9, {}), {5}: (5, {})} | custom-call | bytes 24500000 | tf_op jit(solution)/shard_map/pallas_call | solution.py:62
  20.1 1.8 %collective-permute-start.22 = (f32[4,2,32,128]{3,2,1,0:T(8,128)S(1)}, f32[4,2,32,128]{3,2,1,0:T(8,128)S(1)}, u32[]{:S(2)}, u32[]{:S(2)}) collective-permute-start(f32[4,2,32,128]{3,2,1,0:T(8,128)S(1)} %pad_maximum_fusion.1), channel_id=1, source_target_pairs={{0,4},{4,0},{8,12},{12,8},{16,20},{20,16},{24,28},{28,24},{1,5},{5... | collective-permute-start | bytes 393224 | tf_op jit(solution)/shard_map/ppermute | solution.py:630
  21.9 2.8 %collective-permute-start.5 = (f32[21,4,128]{2,1,0:T(4,128)S(1)}, f32[21,4,128]{2,1,0:T(4,128)S(1)}, u32[]{:S(2)}, u32[]{:S(2)}) collective-permute-start(f32[21,4,128]{2,1,0:T(4,128)S(1)} %get-tuple-element.164.refs_5_.refs_1_), channel_id=1, source_target_pairs={{0,4},{4,0},{8,12},{12,8},{16,20},{20,16},{24,28},{28,24},{1,5},{5... | collective-permute-start | bytes 129032 | tf_op jit(solution)/shard_map/ppermute | solution.py:591
  26.7 1.4 %collective-permute-done.6.refs_8_.refs_4_ = f32[21,4,128]{2,1,0:T(4,128)S(1)} collective-permute-done((f32[21,4,128]{2,1,0:T(4,128)S(1)}, f32[21,4,128]{2,1,0:T(4,128)S(1)}, u32[]{:S(2)}, u32[]{:S(2)}) %collective-permute-start.6) | collective-permute-done | bytes 43040 | tf_op jit(solution)/shard_map/ppermute | solution.py:585
  30.4 1.9 %collective-permute-start.9 = (f32[16,4,128]{2,1,0:T(4,128)S(1)}, f32[16,4,128]{2,1,0:T(4,128)S(1)}, u32[]{:S(2)}, u32[]{:S(2)}) collective-permute-start(f32[16,4,128]{2,1,0:T(4,128)S(1)} %get-tuple-element.169.refs_5_), channel_id=1, source_target_pairs={{0,4},{4,0},{8,12},{12,8},{16,20},{20,16},{24,28},{28,24},{1,5},{5... | collective-permute-start | bytes 98312 | tf_op jit(solution)/shard_map/ppermute | solution.py:591
  34.3 2.6 %collective-permute-done.10.refs_8_ = f32[16,4,128]{2,1,0:T(4,128)S(1)} collective-permute-done((f32[16,4,128]{2,1,0:T(4,128)S(1)}, f32[16,4,128]{2,1,0:T(4,128)S(1)}, u32[]{:S(2)}, u32[]{:S(2)}) %collective-permute-start.10) | collective-permute-done | bytes 32800 | tf_op jit(solution)/shard_map/ppermute | solution.py:585
  39.3 1.5 %collective-permute-start.13 = (f32[16,4,128]{2,1,0:T(4,128)S(1)}, f32[16,4,128]{2,1,0:T(4,128)S(1)}, u32[]{:S(2)}, u32[]{:S(2)}) collective-permute-start(f32[16,4,128]{2,1,0:T(4,128)S(1)} %get-tuple-element.175.refs_6_), channel_id=1, source_target_pairs={{0,4},{4,0},{8,12},{12,8},{16,20},{20,16},{24,28},{28,24},{1,5},{5... | collective-permute-start | bytes 98312 | tf_op jit(solution)/shard_map/ppermute | solution.py:591
  44.2 1.7 %shard_map.153 = (f32[4,4,128]{2,1,0:T(4,128)S(1)}, f32[4,4,128]{2,1,0:T(4,128)S(1)}, bf16[8,256,512]{2,1,0:T(8,128)(2,1)S(1)}, bf16[8,256,512]{2,1,0:T(8,128)(2...) custom-call(s32[4,16]{1,0:T(4,128)S(4)} %get-tuple-element.155.refs_, ...), custom_call_target="tpu_custom_call", output_to_operand_aliasing={{2}: (1, {}), {3}: (2, {}), {4}: (11, {}), {5}: (12, {}), {... | custom-call | bytes 7000000 | tf_op jit(solution)/shard_map/pallas_call | solution.py:62
  46.0 2.6 %collective-permute-start.17 = (f32[4,4,128]{2,1,0:T(4,128)S(1)}, f32[4,4,128]{2,1,0:T(4,128)S(1)}, u32[]{:S(2)}, u32[]{:S(2)}) collective-permute-start(f32[4,4,128]{2,1,0:T(4,128)S(1)} %get-tuple-element.182.refs_4_), channel_id=1, source_target_pairs={{0,4},{4,0},{8,12},{12,8},{16,20},{20,16},{24,28},{28,24},{1,5},{5... | collective-permute-start | bytes 24584 | tf_op jit(solution)/shard_map/ppermute | solution.py:591
  52.3 2.5 %collective-permute-start.27 = (f32[4,4,128]{2,1,0:T(4,128)S(1)}, f32[4,4,128]{2,1,0:T(4,128)S(1)}, u32[]{:S(2)}, u32[]{:S(2)}) collective-permute-start(f32[4,4,128]{2,1,0:T(4,128)S(1)} %get-tuple-element.198.refs_4_), channel_id=1, source_target_pairs={{0,4},{4,0},{8,12},{12,8},{16,20},{20,16},{24,28},{28,24},{1,5},{5... | collective-permute-start | bytes 24584 | tf_op jit(solution)/shard_map/ppermute | solution.py:591
  58.4 2.2 %collective-permute-start.31 = (f32[4,4,128]{2,1,0:T(4,128)S(1)}, f32[4,4,128]{2,1,0:T(4,128)S(1)}, u32[]{:S(2)}, u32[]{:S(2)}) collective-permute-start(f32[4,4,128]{2,1,0:T(4,128)S(1)} %get-tuple-element.210.refs_6_), channel_id=1, source_target_pairs={{0,4},{4,0},{8,12},{12,8},{16,20},{20,16},{24,28},{28,24},{1,5},{5... | collective-permute-start | bytes 24584 | tf_op jit(solution)/shard_map/ppermute | solution.py:591
  60.9 1.6 %collective-permute-start.33 = (f32[4,4,128]{2,1,0:T(4,128)S(1)}, f32[4,4,128]{2,1,0:T(4,128)S(1)}, u32[]{:S(2)}, u32[]{:S(2)}) collective-permute-start(f32[4,4,128]{2,1,0:T(4,128)S(1)} %get-tuple-element.210.refs_6_), channel_id=1, source_target_pairs={{0,1},{1,0},{2,3},{3,2},{4,5},{5,4},{6,7},{7,6},{8,9},{9,8},{10,11... | collective-permute-start | bytes 24584 | tf_op jit(solution)/shard_map/ppermute | solution.py:586
  64.4 11.0 %all_to_all.5.refs_2_ = f32[32,4,128]{2,1,0:T(4,128)S(1)} all-to-all(f32[32,4,128]{2,1,0:T(4,128)S(1)} %get-tuple-element.219), channel_id=1, replica_groups=mesh['wide'=8,'narrow'=4] {'wide','narrow'}, dimensions={0} | all-to-all | bytes 131072 | tf_op jit(solution)/shard_map/all_to_all | solution.py:805
  75.4 2.2 %shard_map.158 = (f32[4,4,128]{2,1,0:T(4,128)S(1)}, f32[16,1,128]{2,1,0:T(1,128)S(1)}, f32[16,4,128]{2,1,0:T(4,128)S(1)}, f32[16,4,128]{2,1,0:T(4,128)S(1)}, s32...) custom-call(s32[9]{0:T(128)S(4)} %get-tuple-element.136.refs_0_, ...), custom_call_target="tpu_custom_call", output_to_operand_aliasing={{1}: (8, {}), {2}: (9, {}), {3}: (10, {}), {4}: (7, {}), {5... | custom-call | bytes 10500000 | tf_op jit(solution)/shard_map/pallas_call | solution.py:62
  77.8 2.0 %collective-permute-start.35 = (f32[4,4,128]{2,1,0:T(4,128)S(1)}, f32[4,4,128]{2,1,0:T(4,128)S(1)}, u32[]{:S(2)}, u32[]{:S(2)}) collective-permute-start(f32[4,4,128]{2,1,0:T(4,128)S(1)} %get-tuple-element.231.refs_4_), channel_id=1, source_target_pairs={{0,4},{4,0},{8,12},{12,8},{16,20},{20,16},{24,28},{28,24},{1,5},{5... | collective-permute-start | bytes 24584 | tf_op jit(solution)/shard_map/ppermute | solution.py:591
  83.3 2.1 %collective-permute-start.39 = (f32[4,4,128]{2,1,0:T(4,128)S(1)}, f32[4,4,128]{2,1,0:T(4,128)S(1)}, u32[]{:S(2)}, u32[]{:S(2)}) collective-permute-start(f32[4,4,128]{2,1,0:T(4,128)S(1)} %get-tuple-element.240.refs_4_), channel_id=1, source_target_pairs={{0,4},{4,0},{8,12},{12,8},{16,20},{20,16},{24,28},{28,24},{1,5},{5... | collective-permute-start | bytes 24584 | tf_op jit(solution)/shard_map/ppermute | solution.py:591
  89.0 2.2 %collective-permute-start.43 = (f32[4,4,128]{2,1,0:T(4,128)S(1)}, f32[4,4,128]{2,1,0:T(4,128)S(1)}, u32[]{:S(2)}, u32[]{:S(2)}) collective-permute-start(f32[4,4,128]{2,1,0:T(4,128)S(1)} %get-tuple-element.249.refs_6_), channel_id=1, source_target_pairs={{0,4},{4,0},{8,12},{12,8},{16,20},{20,16},{24,28},{28,24},{1,5},{5... | collective-permute-start | bytes 24584 | tf_op jit(solution)/shard_map/ppermute | solution.py:591
  92.8 1.4 %collective-permute-done.44.refs_9_ = f32[4,4,128]{2,1,0:T(4,128)S(1)} collective-permute-done((f32[4,4,128]{2,1,0:T(4,128)S(1)}, f32[4,4,128]{2,1,0:T(4,128)S(1)}, u32[]{:S(2)}, u32[]{:S(2)}) %collective-permute-start.44) | collective-permute-done | bytes 8224 | tf_op jit(solution)/shard_map/ppermute | solution.py:585
  94.3 1.7 %shard_map.161 = (f32[16,4,128]{2,1,0:T(4,128)S(1)}, f32[16,1,128]{2,1,0:T(1,128)S(1)}, f32[16,4,128]{2,1,0:T(4,128)S(1)}, f32[16,4,128]{2,1,0:T(4,128)S(1)}, s3...) custom-call(s32[4,16]{1,0:T(4,128)S(4)} %get-tuple-element.155.refs_, ...), custom_call_target="tpu_custom_call", output_to_operand_aliasing={{1}: (3, {}), {2}: (11, {}), {3}: (4, {}), {4}: (5, {}), {5... | custom-call | bytes 7000000 | tf_op jit(solution)/shard_map/pallas_call | solution.py:62
  96.1 2.6 %collective-permute-start.47 = (f32[16,4,128]{2,1,0:T(4,128)S(1)}, f32[16,4,128]{2,1,0:T(4,128)S(1)}, u32[]{:S(2)}, u32[]{:S(2)}) collective-permute-start(f32[16,4,128]{2,1,0:T(4,128)S(1)} %get-tuple-element.255.refs_5_), channel_id=1, source_target_pairs={{0,4},{4,0},{8,12},{12,8},{16,20},{20,16},{24,28},{28,24},{1,5},{5... | collective-permute-start | bytes 98312 | tf_op jit(solution)/shard_map/ppermute | solution.py:591
  100.6 1.4 %collective-permute-done.48.refs_8_ = f32[16,4,128]{2,1,0:T(4,128)S(1)} collective-permute-done((f32[16,4,128]{2,1,0:T(4,128)S(1)}, f32[16,4,128]{2,1,0:T(4,128)S(1)}, u32[]{:S(2)}, u32[]{:S(2)}) %collective-permute-start.48) | collective-permute-done | bytes 32800 | tf_op jit(solution)/shard_map/ppermute | solution.py:585
  103.3 2.1 %collective-permute-start.51 = (f32[16,4,128]{2,1,0:T(4,128)S(1)}, f32[16,4,128]{2,1,0:T(4,128)S(1)}, u32[]{:S(2)}, u32[]{:S(2)}) collective-permute-start(f32[16,4,128]{2,1,0:T(4,128)S(1)} %get-tuple-element.260.refs_7_), channel_id=1, source_target_pairs={{0,4},{4,0},{8,12},{12,8},{16,20},{20,16},{24,28},{28,24},{1,5},{5... | collective-permute-start | bytes 98312 | tf_op jit(solution)/shard_map/ppermute | solution.py:591
  108.7 2.6 %shard_map.163 = (f32[4,128,128]{2,1,0:T(8,128)S(1)}, f32[4,4,128]{2,1,0:T(4,128)S(1)}, f32[4,4,128]{2,1,0:T(4,128)S(1)}, f32[16,1,128]{2,1,0:T(1,128)S(1)}, f32...) custom-call(s32[9]{0:T(128)S(4)} %get-tuple-element.136.refs_0_, ...), custom_call_target="tpu_custom_call", output_to_operand_aliasing={{3}: (4, {}), {4}: (5, {}), {5}: (1, {}), {6}: (2, {})} | custom-call | bytes 10500000 | tf_op jit(solution)/shard_map/pallas_call | solution.py:62
  112.5 2.0 %collective-permute-done.54.refs_2_ = f32[4,4,128]{2,1,0:T(4,128)S(1)} collective-permute-done((f32[4,4,128]{2,1,0:T(4,128)S(1)}, f32[4,4,128]{2,1,0:T(4,128)S(1)}, u32[]{:S(2)}, u32[]{:S(2)}) %collective-permute-start.54) | collective-permute-done | bytes 8224 | tf_op jit(solution)/shard_map/ppermute | solution.py:585
  114.8 2.9 %collective-permute-start.57 = (f32[4,4,256]{2,1,0:T(4,128)S(1)}, f32[4,4,256]{2,1,0:T(4,128)S(1)}, u32[]{:S(2)}, u32[]{:S(2)}) collective-permute-start(f32[4,4,256]{2,1,0:T(4,128)S(1)} %get-tuple-element.266), channel_id=1, source_target_pairs={{0,4},{4,0},{8,12},{12,8},{16,20},{20,16},{24,28},{28,24},{1,5},{5... | collective-permute-start | bytes 49160 | tf_op jit(solution)/shard_map/ppermute | solution.py:591
  117.6 1.7 %collective-permute-done.57.refs_4_ = f32[4,4,256]{2,1,0:T(4,128)S(1)} collective-permute-done((f32[4,4,256]{2,1,0:T(4,128)S(1)}, f32[4,4,256]{2,1,0:T(4,128)S(1)}, u32[]{:S(2)}, u32[]{:S(2)}) %collective-permute-start.57) | collective-permute-done | bytes 16416 | tf_op jit(solution)/shard_map/ppermute | solution.py:591
  119.4 2.2 %shard_map.165 = f32[4,128,128]{2,1,0:T(8,128)} custom-call(s32[9]{0:T(128)S(4)} %get-tuple-element.136.refs_0_, f32[11,144,256]{2,1,0:T(8,128)S(1)} %copy-done.2, f32[4,128,256]{2,1,0:T(8,128)S(1)} %get-tuple-element.264.refs_2_, f32[4,4,256]{2,1,0:T(4,128)S(1)} %collective-permute-done.56.refs_3_, f32[4,4,256]{2,1,0:T(4,128)S(1)} %collective-permute-done.57.refs_4_), custom_call_target="tpu_custom_call" | custom-call | bytes 7000000 | tf_op jit(solution)/shard_map/pallas_call | solution.py:62
  (123 shorter events, 41.3 us)
Async XLA Ops:
  1.2 9.2 %collective-permute-start.20 = (f32[1,2,32,128]{3,2,1,0:T(8,128)S(1)}, f32[1,2,32,128]{3,2,1,0:T(8,128)S(1)}, u32[]{:S(2)}, u32[]{:S(2)}) collective-permute-start(f32[1,2,32,128]{3,2,1,0:T(8,128)S(1)} %get-tuple-element.191), channel_id=1, source_target_pairs={{0,16},{4,20},{8,24},{12,28},{16,0},{20,4},{24,8},{28,12},{1,17},{... | collective-permute-start | bytes 98312 | tf_op jit(solution)/shard_map/ppermute | solution.py:630
  5.3 4.9 %collective-permute-start = (f32[6,4,128]{2,1,0:T(4,128)S(1)}, f32[6,4,128]{2,1,0:T(4,128)S(1)}, u32[]{:S(2)}, u32[]{:S(2)}) collective-permute-start(f32[6,4,128]{2,1,0:T(4,128)S(1)} %get-tuple-element.138), channel_id=1, source_target_pairs={{1,2},{2,1},{0,3},{3,0},{5,6},{6,5},{4,7},{7,4},{9,10},{10,9},{8,1... | collective-permute-start | bytes 36872 | tf_op jit(solution)/shard_map/ppermute | solution.py:585
  6.0 4.3 %collective-permute-start.1 = (f32[6,4,128]{2,1,0:T(4,128)S(1)}, f32[6,4,128]{2,1,0:T(4,128)S(1)}, u32[]{:S(2)}, u32[]{:S(2)}) collective-permute-start(f32[6,4,128]{2,1,0:T(4,128)S(1)} %get-tuple-element.146), channel_id=1, source_target_pairs={{0,1},{1,0},{2,3},{3,2},{4,5},{5,4},{6,7},{7,6},{8,9},{9,8},{10,11... | collective-permute-start | bytes 36872 | tf_op jit(solution)/shard_map/ppermute | solution.py:586
  10.4 9.7 %collective-permute-start.21 = (f32[2,2,32,128]{3,2,1,0:T(8,128)S(1)}, f32[2,2,32,128]{3,2,1,0:T(8,128)S(1)}, u32[]{:S(2)}, u32[]{:S(2)}) collective-permute-start(f32[2,2,32,128]{3,2,1,0:T(8,128)S(1)} %pad_maximum_fusion.2), channel_id=1, source_target_pairs={{0,8},{4,12},{8,0},{12,4},{16,24},{20,28},{24,16},{28,20},{1,9},{5... | collective-permute-start | bytes 196616 | tf_op jit(solution)/shard_map/ppermute | solution.py:630
  12.1 4.5 %collective-permute-start.2 = (f32[6,4,256]{2,1,0:T(4,128)S(1)}, f32[6,4,256]{2,1,0:T(4,128)S(1)}, u32[]{:S(2)}, u32[]{:S(2)}) collective-permute-start(f32[6,4,256]{2,1,0:T(4,128)S(1)} %get-tuple-element.148), channel_id=1, source_target_pairs={{4,8},{5,9},{6,10},{7,11},{8,4},{9,5},{10,6},{11,7},{12,16},{13,17... | collective-permute-start | bytes 73736 | tf_op jit(solution)/shard_map/ppermute | solution.py:590
  12.1 4.5 %collective-permute-start.3 = (f32[6,4,256]{2,1,0:T(4,128)S(1)}, f32[6,4,256]{2,1,0:T(4,128)S(1)}, u32[]{:S(2)}, u32[]{:S(2)}) collective-permute-start(f32[6,4,256]{2,1,0:T(4,128)S(1)} %get-tuple-element.149), channel_id=1, source_target_pairs={{0,4},{4,0},{8,12},{12,8},{16,20},{20,16},{24,28},{28,24},{1,5},{5... | collective-permute-start | bytes 73736 | tf_op jit(solution)/shard_map/ppermute | solution.py:591
  20.1 9.3 %collective-permute-start.22 = (f32[4,2,32,128]{3,2,1,0:T(8,128)S(1)}, f32[4,2,32,128]{3,2,1,0:T(8,128)S(1)}, u32[]{:S(2)}, u32[]{:S(2)}) collective-permute-start(f32[4,2,32,128]{3,2,1,0:T(8,128)S(1)} %pad_maximum_fusion.1), channel_id=1, source_target_pairs={{0,4},{4,0},{8,12},{12,8},{16,20},{20,16},{24,28},{28,24},{1,5},{5... | collective-permute-start | bytes 393224 | tf_op jit(solution)/shard_map/ppermute | solution.py:630
  21.9 3.5 %collective-permute-start.4 = (f32[21,4,128]{2,1,0:T(4,128)S(1)}, f32[21,4,128]{2,1,0:T(4,128)S(1)}, u32[]{:S(2)}, u32[]{:S(2)}) collective-permute-start(f32[21,4,128]{2,1,0:T(4,128)S(1)} %get-tuple-element.164.refs_5_.refs_1_), channel_id=1, source_target_pairs={{4,8},{5,9},{6,10},{7,11},{8,4},{9,5},{10,6},{11,7},{12,16},{13,17... | collective-permute-start | bytes 129032 | tf_op jit(solution)/shard_map/ppermute | solution.py:590
  21.9 4.8 %collective-permute-start.5 = (f32[21,4,128]{2,1,0:T(4,128)S(1)}, f32[21,4,128]{2,1,0:T(4,128)S(1)}, u32[]{:S(2)}, u32[]{:S(2)}) collective-permute-start(f32[21,4,128]{2,1,0:T(4,128)S(1)} %get-tuple-element.164.refs_5_.refs_1_), channel_id=1, source_target_pairs={{0,4},{4,0},{8,12},{12,8},{16,20},{20,16},{24,28},{28,24},{1,5},{5... | collective-permute-start | bytes 129032 | tf_op jit(solution)/shard_map/ppermute | solution.py:591
  24.7 3.4 %collective-permute-start.6 = (f32[21,4,128]{2,1,0:T(4,128)S(1)}, f32[21,4,128]{2,1,0:T(4,128)S(1)}, u32[]{:S(2)}, u32[]{:S(2)}) collective-permute-start(f32[21,4,128]{2,1,0:T(4,128)S(1)} %get-tuple-element.164.refs_5_.refs_1_), channel_id=1, source_target_pairs={{1,2},{2,1},{0,3},{3,0},{5,6},{6,5},{4,7},{7,4},{9,10},{10,9},{8,1... | collective-permute-start | bytes 129032 | tf_op jit(solution)/shard_map/ppermute | solution.py:585
  24.7 3.4 %collective-permute-start.7 = (f32[21,4,128]{2,1,0:T(4,128)S(1)}, f32[21,4,128]{2,1,0:T(4,128)S(1)}, u32[]{:S(2)}, u32[]{:S(2)}) collective-permute-start(f32[21,4,128]{2,1,0:T(4,128)S(1)} %get-tuple-element.164.refs_5_.refs_1_), channel_id=1, source_target_pairs={{0,1},{1,0},{2,3},{3,2},{4,5},{5,4},{6,7},{7,6},{8,9},{9,8},{10,11... | collective-permute-start | bytes 129032 | tf_op jit(solution)/shard_map/ppermute | solution.py:586
  29.4 8.7 %collective-permute-start.23 = (f32[8,2,32,128]{3,2,1,0:T(8,128)S(1)}, f32[8,2,32,128]{3,2,1,0:T(8,128)S(1)}, u32[]{:S(2)}, u32[]{:S(2)}) collective-permute-start(f32[8,2,32,128]{3,2,1,0:T(8,128)S(1)} %pad_maximum_fusion.refs_1_), channel_id=1, source_target_pairs={{0,2},{1,3},{2,0},{3,1},{4,6},{5,7},{6,4},{7,5},{8,10},{9,11},{10,... | collective-permute-start | bytes 786440 | tf_op jit(solution)/shard_map/ppermute | solution.py:630
  30.4 3.9 %collective-permute-start.9 = (f32[16,4,128]{2,1,0:T(4,128)S(1)}, f32[16,4,128]{2,1,0:T(4,128)S(1)}, u32[]{:S(2)}, u32[]{:S(2)}) collective-permute-start(f32[16,4,128]{2,1,0:T(4,128)S(1)} %get-tuple-element.169.refs_5_), channel_id=1, source_target_pairs={{0,4},{4,0},{8,12},{12,8},{16,20},{20,16},{24,28},{28,24},{1,5},{5... | collective-permute-start | bytes 98312 | tf_op jit(solution)/shard_map/ppermute | solution.py:591
  32.3 4.6 %collective-permute-start.10 = (f32[16,4,128]{2,1,0:T(4,128)S(1)}, f32[16,4,128]{2,1,0:T(4,128)S(1)}, u32[]{:S(2)}, u32[]{:S(2)}) collective-permute-start(f32[16,4,128]{2,1,0:T(4,128)S(1)} %get-tuple-element.169.refs_5_), channel_id=1, source_target_pairs={{1,2},{2,1},{0,3},{3,0},{5,6},{6,5},{4,7},{7,4},{9,10},{10,9},{8,1... | collective-permute-start | bytes 98312 | tf_op jit(solution)/shard_map/ppermute | solution.py:585
  32.3 4.6 %collective-permute-start.11 = (f32[16,4,128]{2,1,0:T(4,128)S(1)}, f32[16,4,128]{2,1,0:T(4,128)S(1)}, u32[]{:S(2)}, u32[]{:S(2)}) collective-permute-start(f32[16,4,128]{2,1,0:T(4,128)S(1)} %get-tuple-element.169.refs_5_), channel_id=1, source_target_pairs={{0,1},{1,0},{2,3},{3,2},{4,5},{5,4},{6,7},{7,6},{8,9},{9,8},{10,11... | collective-permute-start | bytes 98312 | tf_op jit(solution)/shard_map/ppermute | solution.py:586
  38.2 13.9 %collective-permute-start.24 = (f32[8,2,32,128]{3,2,1,0:T(8,128)S(1)}, f32[8,2,32,128]{3,2,1,0:T(8,128)S(1)}, u32[]{:S(2)}, u32[]{:S(2)}) collective-permute-start(f32[8,2,32,128]{3,2,1,0:T(8,128)S(1)} %pad_maximum_fusion.refs_1_), channel_id=1, source_target_pairs={{0,1},{1,0},{2,3},{3,2},{4,5},{5,4},{6,7},{7,6},{8,9},{9,8},{10,11... | collective-permute-start | bytes 786440 | tf_op jit(solution)/shard_map/ppermute | solution.py:630
  38.8 13.3 %collective-permute-start.25 = (f32[8,2,32,128]{3,2,1,0:T(8,128)S(1)}, f32[8,2,32,128]{3,2,1,0:T(8,128)S(1)}, u32[]{:S(2)}, u32[]{:S(2)}) collective-permute-start(f32[8,2,32,128]{3,2,1,0:T(8,128)S(1)} %collective-permute-done.23.refs_2_), channel_id=1, source_target_pairs={{0,1},{1,0},{2,3},{3,2},{4,5},{5,4},{6,7},{7,6},{8,9},{9,8},{10,11... | collective-permute-start | bytes 786440 | tf_op jit(solution)/shard_map/ppermute | solution.py:630
  39.3 3.9 %collective-permute-start.13 = (f32[16,4,128]{2,1,0:T(4,128)S(1)}, f32[16,4,128]{2,1,0:T(4,128)S(1)}, u32[]{:S(2)}, u32[]{:S(2)}) collective-permute-start(f32[16,4,128]{2,1,0:T(4,128)S(1)} %get-tuple-element.175.refs_6_), channel_id=1, source_target_pairs={{0,4},{4,0},{8,12},{12,8},{16,20},{20,16},{24,28},{28,24},{1,5},{5... | collective-permute-start | bytes 98312 | tf_op jit(solution)/shard_map/ppermute | solution.py:591
  40.8 3.4 %collective-permute-start.14 = (f32[16,4,128]{2,1,0:T(4,128)S(1)}, f32[16,4,128]{2,1,0:T(4,128)S(1)}, u32[]{:S(2)}, u32[]{:S(2)}) collective-permute-start(f32[16,4,128]{2,1,0:T(4,128)S(1)} %get-tuple-element.175.refs_6_), channel_id=1, source_target_pairs={{1,2},{2,1},{0,3},{3,0},{5,6},{6,5},{4,7},{7,4},{9,10},{10,9},{8,1... | collective-permute-start | bytes 98312 | tf_op jit(solution)/shard_map/ppermute | solution.py:585
  45.8 3.6 %collective-permute-start.16 = (f32[4,4,128]{2,1,0:T(4,128)S(1)}, f32[4,4,128]{2,1,0:T(4,128)S(1)}, u32[]{:S(2)}, u32[]{:S(2)}) collective-permute-start(f32[4,4,128]{2,1,0:T(4,128)S(1)} %get-tuple-element.182.refs_4_), channel_id=1, source_target_pairs={{4,8},{5,9},{6,10},{7,11},{8,4},{9,5},{10,6},{11,7},{12,16},{13,17... | collective-permute-start | bytes 24584 | tf_op jit(solution)/shard_map/ppermute | solution.py:590
  46.0 4.4 %collective-permute-start.17 = (f32[4,4,128]{2,1,0:T(4,128)S(1)}, f32[4,4,128]{2,1,0:T(4,128)S(1)}, u32[]{:S(2)}, u32[]{:S(2)}) collective-permute-start(f32[4,4,128]{2,1,0:T(4,128)S(1)} %get-tuple-element.182.refs_4_), channel_id=1, source_target_pairs={{0,4},{4,0},{8,12},{12,8},{16,20},{20,16},{24,28},{28,24},{1,5},{5... | collective-permute-start | bytes 24584 | tf_op jit(solution)/shard_map/ppermute | solution.py:591
  52.1 4.6 %collective-permute-start.26 = (f32[4,4,128]{2,1,0:T(4,128)S(1)}, f32[4,4,128]{2,1,0:T(4,128)S(1)}, u32[]{:S(2)}, u32[]{:S(2)}) collective-permute-start(f32[4,4,128]{2,1,0:T(4,128)S(1)} %get-tuple-element.198.refs_4_), channel_id=1, source_target_pairs={{4,8},{5,9},{6,10},{7,11},{8,4},{9,5},{10,6},{11,7},{12,16},{13,17... | collective-permute-start | bytes 24584 | tf_op jit(solution)/shard_map/ppermute | solution.py:590
  52.3 4.5 %collective-permute-start.27 = (f32[4,4,128]{2,1,0:T(4,128)S(1)}, f32[4,4,128]{2,1,0:T(4,128)S(1)}, u32[]{:S(2)}, u32[]{:S(2)}) collective-permute-start(f32[4,4,128]{2,1,0:T(4,128)S(1)} %get-tuple-element.198.refs_4_), channel_id=1, source_target_pairs={{0,4},{4,0},{8,12},{12,8},{16,20},{20,16},{24,28},{28,24},{1,5},{5... | collective-permute-start | bytes 24584 | tf_op jit(solution)/shard_map/ppermute | solution.py:591
  58.3 4.2 %collective-permute-start.30 = (f32[4,4,128]{2,1,0:T(4,128)S(1)}, f32[4,4,128]{2,1,0:T(4,128)S(1)}, u32[]{:S(2)}, u32[]{:S(2)}) collective-permute-start(f32[4,4,128]{2,1,0:T(4,128)S(1)} %get-tuple-element.210.refs_6_), channel_id=1, source_target_pairs={{4,8},{5,9},{6,10},{7,11},{8,4},{9,5},{10,6},{11,7},{12,16},{13,17... | collective-permute-start | bytes 24584 | tf_op jit(solution)/shard_map/ppermute | solution.py:590
  58.4 4.1 %collective-permute-start.31 = (f32[4,4,128]{2,1,0:T(4,128)S(1)}, f32[4,4,128]{2,1,0:T(4,128)S(1)}, u32[]{:S(2)}, u32[]{:S(2)}) collective-permute-start(f32[4,4,128]{2,1,0:T(4,128)S(1)} %get-tuple-element.210.refs_6_), channel_id=1, source_target_pairs={{0,4},{4,0},{8,12},{12,8},{16,20},{20,16},{24,28},{28,24},{1,5},{5... | collective-permute-start | bytes 24584 | tf_op jit(solution)/shard_map/ppermute | solution.py:591
  77.8 3.7 %collective-permute-start.35 = (f32[4,4,128]{2,1,0:T(4,128)S(1)}, f32[4,4,128]{2,1,0:T(4,128)S(1)}, u32[]{:S(2)}, u32[]{:S(2)}) collective-permute-start(f32[4,4,128]{2,1,0:T(4,128)S(1)} %get-tuple-element.231.refs_4_), channel_id=1, source_target_pairs={{0,4},{4,0},{8,12},{12,8},{16,20},{20,16},{24,28},{28,24},{1,5},{5... | collective-permute-start | bytes 24584 | tf_op jit(solution)/shard_map/ppermute | solution.py:591
  83.3 3.7 %collective-permute-start.39 = (f32[4,4,128]{2,1,0:T(4,128)S(1)}, f32[4,4,128]{2,1,0:T(4,128)S(1)}, u32[]{:S(2)}, u32[]{:S(2)}) collective-permute-start(f32[4,4,128]{2,1,0:T(4,128)S(1)} %get-tuple-element.240.refs_4_), channel_id=1, source_target_pairs={{0,4},{4,0},{8,12},{12,8},{16,20},{20,16},{24,28},{28,24},{1,5},{5... | collective-permute-start | bytes 24584 | tf_op jit(solution)/shard_map/ppermute | solution.py:591
  89.0 3.9 %collective-permute-start.43 = (f32[4,4,128]{2,1,0:T(4,128)S(1)}, f32[4,4,128]{2,1,0:T(4,128)S(1)}, u32[]{:S(2)}, u32[]{:S(2)}) collective-permute-start(f32[4,4,128]{2,1,0:T(4,128)S(1)} %get-tuple-element.249.refs_6_), channel_id=1, source_target_pairs={{0,4},{4,0},{8,12},{12,8},{16,20},{20,16},{24,28},{28,24},{1,5},{5... | collective-permute-start | bytes 24584 | tf_op jit(solution)/shard_map/ppermute | solution.py:591
  96.0 3.5 %collective-permute-start.46 = (f32[16,4,128]{2,1,0:T(4,128)S(1)}, f32[16,4,128]{2,1,0:T(4,128)S(1)}, u32[]{:S(2)}, u32[]{:S(2)}) collective-permute-start(f32[16,4,128]{2,1,0:T(4,128)S(1)} %get-tuple-element.255.refs_5_), channel_id=1, source_target_pairs={{4,8},{5,9},{6,10},{7,11},{8,4},{9,5},{10,6},{11,7},{12,16},{13,17... | collective-permute-start | bytes 98312 | tf_op jit(solution)/shard_map/ppermute | solution.py:590
  96.1 4.5 %collective-permute-start.47 = (f32[16,4,128]{2,1,0:T(4,128)S(1)}, f32[16,4,128]{2,1,0:T(4,128)S(1)}, u32[]{:S(2)}, u32[]{:S(2)}) collective-permute-start(f32[16,4,128]{2,1,0:T(4,128)S(1)} %get-tuple-element.255.refs_5_), channel_id=1, source_target_pairs={{0,4},{4,0},{8,12},{12,8},{16,20},{20,16},{24,28},{28,24},{1,5},{5... | collective-permute-start | bytes 98312 | tf_op jit(solution)/shard_map/ppermute | solution.py:591
  103.3 4.0 %collective-permute-start.51 = (f32[16,4,128]{2,1,0:T(4,128)S(1)}, f32[16,4,128]{2,1,0:T(4,128)S(1)}, u32[]{:S(2)}, u32[]{:S(2)}) collective-permute-start(f32[16,4,128]{2,1,0:T(4,128)S(1)} %get-tuple-element.260.refs_7_), channel_id=1, source_target_pairs={{0,4},{4,0},{8,12},{12,8},{16,20},{20,16},{24,28},{28,24},{1,5},{5... | collective-permute-start | bytes 98312 | tf_op jit(solution)/shard_map/ppermute | solution.py:591
  114.8 4.6 %collective-permute-start.57 = (f32[4,4,256]{2,1,0:T(4,128)S(1)}, f32[4,4,256]{2,1,0:T(4,128)S(1)}, u32[]{:S(2)}, u32[]{:S(2)}) collective-permute-start(f32[4,4,256]{2,1,0:T(4,128)S(1)} %get-tuple-element.266), channel_id=1, source_target_pairs={{0,4},{4,0},{8,12},{12,8},{16,20},{20,16},{24,28},{28,24},{1,5},{5... | collective-permute-start | bytes 49160 | tf_op jit(solution)/shard_map/ppermute | solution.py:591
  (33 other events, 151.2 us)

commit v5 on v4

--- a/solution.py
+++ b/solution.py
@@ -12,8 +12,9 @@
 SHIFT = 0.1
 JACOBI = 0.6
 LANES = 128
+ORDER = -1
 RIM = 4
-PAD = 16
+PAD = 2 * RIM
 VMEM = pl.BlockSpec(memory_space=pltpu.VMEM)
 PLAIN = pl.BlockSpec(memory_space=pltpu.VMEM)
 HBM = pl.BlockSpec(memory_space=pl.ANY)
@@ -54,7 +55,7 @@
     def inner(*refs):
         first = len(inputs)
         kernel(
-            *jax.tree.unflatten(shape_in, refs[:count_in]),
+            *jax.tree.unflatten(shape_in, refs[:first][::ORDER][:count_in]),
             *refs[first : first + count_out],
             *refs[first + count_out + len(hold) :],
         )
@@ -62,14 +63,16 @@
     results = pl.pallas_call(
         inner,
         out_shape=shapes,
-        in_specs=specs,
+        in_specs=specs[::ORDER],
         out_specs=[{pltpu.HBM: HBM, pltpu.SMEM: SMEM, pltpu.VMEM: VMEM}[space] for space in spaces]
         + [VMEM] * len(hold),
         scratch_shapes=list(scratch),
-        input_output_aliases={places[name]: count_out + i for i, name in enumerate(hold)},
+        input_output_aliases={
+            range(len(inputs))[::ORDER][places[name]]: count_out + i for i, name in enumerate(hold)
+        },
         compiler_params=pltpu.CompilerParams(vmem_limit_bytes=mib * 1024 * 1024),
         cost_estimate=pl.CostEstimate(flops=0, bytes_accessed=int(us * 3.5e6), transcendentals=0),
-    )(*inputs)
+    )(*inputs[::ORDER])
     for name, value in zip(list(hold), results[count_out:]):
         hold[name] = value
     return jax.tree.unflatten(tree, results[:count_out])
@@ -107,19 +110,23 @@
     return hi, (m - hi.astype(F32)).astype(BF16)
 
 
-def split_tile(tile, r, k, t_ref, d_ref, first=0):
+def diagonal(tile):
+    size = tile.shape[0]
+    row = lax.broadcasted_iota(jnp.int32, tile.shape, 0)
+    col = lax.broadcasted_iota(jnp.int32, tile.shape, 1)
+    diag = jnp.sum(jnp.where(row == col, tile, 0.0), axis=0, keepdims=True)
+    lane = lax.broadcasted_iota(jnp.int32, diag.shape, 1)
+    return jnp.where(lane < size, diag, 1.0)
+
+
+def split_tile(tile, r, k, t_ref):
     size = tile.shape[0]
     if size < LANES:
         tile = jnp.concatenate([tile, jnp.zeros((size, LANES - size), F32)], axis=1)
     hi, lo = split_map(tile)
     t_ref[r, 0:size, k * LANES : (k + 1) * LANES] = hi
     t_ref[r, LANES : LANES + size, k * LANES : (k + 1) * LANES] = lo
-    if k == 0:
-        row = lax.broadcasted_iota(jnp.int32, tile.shape, 0)
-        col = lax.broadcasted_iota(jnp.int32, tile.shape, 1)
-        diag = jnp.sum(jnp.where(row == col, tile, 0.0), axis=0, keepdims=True)
-        lane = lax.broadcasted_iota(jnp.int32, diag.shape, 1)
-        d_ref[first + r] = jnp.where(lane < size, diag, 1.0)
+    return tile
 
 
 class Stream:
@@ -138,12 +145,12 @@
         for load in self.loads:
             load.start()
 
-    def run(self, d_ref, first):
+    def run(self):
         for i, load in enumerate(self.loads):
             load.wait()
             for r in range(i * self.step, (i + 1) * self.step):
                 for k in range(self.slots):
-                    split_tile(self.held[r, k], r, k, self.t_ref, d_ref, first)
+                    split_tile(self.held[r, k], r, k, self.t_ref)
             self.stores[i].start()
 
     def end(self):
@@ -151,20 +158,20 @@
             store.wait()
 
 
-def second_half_kernel(tiles, d_first, t_ref, d_ref, far, held, sems):
+def second_half_kernel(tiles, _, t_ref, far, held, sems):
     stream = Stream(1, tiles, held, t_ref, far, sems)
-    count = d_first.shape[0]
-    d_ref[0:count] = d_first[...]
-    stream.run(d_ref, count)
+    stream.run()
     stream.end()
 
 
 def setup_kernel(
     flags, columns1, live1, columns2, live2, tiles1, tiles2,
     idx1, idx2, t1, d1, t2, d2, far,
-    in1, in2, in3, in4, held_tiles, held2, held1, held_two, turned, sems, stream_sems,
+    in1, in2, in3, in4, held_tiles, held2, fronts, held1, held_two, turned, sems, stream_sems,
 ):
-    ins = ((columns1, in1), (live1, in2), (columns2, in3), (live2, in4), (tiles2, held2))
+    ins = [(columns1, in1), (live1, in2), (columns2, in3), (live2, in4), (tiles2, held2)]
+    half = fronts.shape[0]
+    ins.append((tiles1.at[half:, 0], fronts))
     ins = [pltpu.make_async_copy(a, b, sems.at[i]) for i, (a, b) in enumerate(ins)]
     for copy in ins:
         copy.start()
@@ -197,8 +204,18 @@
     t2[...] = jnp.zeros_like(t2)
     for r in range(held2.shape[0]):
         for k in range(held2.shape[1]):
-            split_tile(held2[r, k], r, k, t2, d2)
-    stream.run(d1, 0)
+            tile = split_tile(held2[r, k], r, k, t2)
+            if k == 0:
+                row = lax.broadcasted_iota(jnp.int32, tile.shape, 0)
+                col = lax.broadcasted_iota(jnp.int32, tile.shape, 1)
+                diag = jnp.sum(jnp.where(row == col, tile, 0.0), axis=0, keepdims=True)
+                lane = lax.broadcasted_iota(jnp.int32, diag.shape, 1)
+                d2[r] = jnp.where(lane < tile.shape[0], diag, 1.0)
+    for r in range(half):
+        d1[half + r] = diagonal(fronts[r])
+    stream.run()
+    for r in range(half):
+        d1[r] = diagonal(held_tiles[r, 0])
     for copy in copies:
         copy.wait()
     slots, count = idx2.shape
@@ -226,11 +243,27 @@
         store_parts(xs, (i + 1) * count, other[0:count])
 
 
+def ride(out, start, refs):
+    for ref, first in refs:
+        count = ref.shape[0] - first
+        out[start : start + count] = ref[first:]
+        start += count
+
+
 def smooth_kernel(idx, t, d, b, own, o1, o2, o3, o4, out, xs):
     count = b.shape[0]
     fill_blocks(xs, own, (o1, o2, o3, o4), count)
     for r, ax in enumerate(apply_tiles(t, xs, idx)):
         out[r] = own[r] + JACOBI * (b[r] - ax) / d[r]
+
+
+def smooth_ride_kernel(first, idx, t, d, b, own, o1, o2, o3, o4, sent_w, sent_n, out, out_w, out_n, xs):
+    smooth_kernel(idx, t, d, b, own, o1, o2, o3, o4, out, xs)
+    count = b.shape[0]
+    out_w[0:count] = out[...]
+    out_n[0:count] = out[...]
+    ride(out_n, count, ((sent_w, first), (o2, first)))
+    ride(out_w, count, ((sent_n, first), (o3, first)))
 
 
 def residual_kernel(idx, t, d, b, own, o1, o2, o3, o4, left, scaled, xs):
@@ -281,24 +314,27 @@
     out[...] = jnp.broadcast_to(total[None], out.shape)
 
 
-def chain_maps_kernel(order, flags, *refs):
+def bundle_kernel(first, _, *refs):
     *pieces, out = refs
-    position = -1
-    for piece in pieces:
-        rows = piece.shape[2]
-        for k in range(piece.shape[0]):
-            position += 1
-            v, q = flags[W_AT], flags[N_AT]
-            for bit, (axis, step) in enumerate(order):
-                if position >> bit & 1:
-                    v, q = (v ^ step, q) if axis == "wide" else (v, q ^ step)
-            for i in range(piece.shape[1]):
-                value = piece[k, i]
-                hi = value.astype(BF16)
-                at = pl.multiple_of(q * rows, rows)
-                out[v, i, pl.ds(at, rows), :] = hi
-                at = pl.multiple_of(LANES + q * rows, rows)
-                out[v, i, pl.ds(at, rows), :] = (value - hi.astype(F32)).astype(BF16)
+    ride(out, 0, [(ref, first) for ref in pieces])
+
+
+def chain_maps_kernel(orders, flags, bundle, other, out):
+    half = bundle.shape[0] // 2
+    for i, order in enumerate(orders):
+        position = 0
+        span = half * 2 >> len(order)
+        rows = span * bundle.shape[1]
+        for ref in (bundle, other):
+            for start in range(i * half, (i + 1) * half, span):
+                v, q = flags[W_AT], flags[N_AT]
+                for bit, (axis, step) in enumerate(order):
+                    if position >> bit & 1:
+                        v, q = (v ^ step, q) if axis == "wide" else (v, q ^ step)
+                hi, lo = split_map(ref[start : start + span].reshape(rows, LANES))
+                out[v, i, pl.ds(pl.multiple_of(q * rows, rows), rows), :] = hi
+                out[v, i, pl.ds(pl.multiple_of(LANES + q * rows, rows), rows), :] = lo
+                position += 1
 
 
 def map_product(m, x):
@@ -418,12 +454,11 @@
     odd = flags[W_ODD] == 1
     low = jnp.where(odd, first[i], second[i]) * flags[HAS_WEST].astype(F32)
     high = jnp.where(odd, second[i], first[i]) * flags[HAS_EAST].astype(F32)
-    rim = jnp.concatenate([high, jnp.zeros((PAD - 2 * RIM, field.shape[1]), F32), low], axis=0)
-    return jnp.concatenate([field, rim], axis=0)
+    return jnp.concatenate([field, high, low], axis=0)
 
 
 def fine_first_kernel(
-    sizes, block, east, north, forward, backward, flags, fields, first, second, piece, edges, sems
+    sizes, block, east, north, forward, backward, flags, fields, first, second, piece, edges, maps, sems
 ):
     wide, narrow = sizes
     w, n = lax.axis_index("wide"), lax.axis_index("narrow")
@@ -433,13 +468,14 @@
     for i, value in enumerate(values):
         flags[i] = jnp.int32(value)
     cols = block.shape[0]
-    rows = piece.shape[2]
-    at = pl.multiple_of(flags[N_AT] * rows, rows)
+    rows = maps.shape[1]
+    at = pl.multiple_of(n * rows, rows)
     copies = [
         (block, fields.at[0:cols]),
         (east, edges.at[0]),
         (north, edges.at[1]),
-        *((m.at[0, pl.ds(at, rows)], piece.at[0, i]) for i, m in enumerate((forward, backward))),
+        (forward.at[0, pl.ds(at, rows)], maps.at[0]),
+        (backward.at[0, pl.ds(at, rows)], maps.at[1]),
     ]
     copies = [pltpu.make_async_copy(a, b, sems.at[i]) for i, (a, b) in enumerate(copies)]
     for copy in copies:
@@ -448,6 +484,7 @@
         copy.wait()
     fields[cols], fields[cols + 1] = live_weights(flags, edges[0], edges[1])
     narrow_rims(flags, [fields[c] for c in range(cols + 2)], first, second)
+    piece[...] = maps[...].reshape(piece.shape)
 
 
 def fine_second_kernel(flags, fields, o2, o1, ext, first, second):
@@ -467,7 +504,7 @@
     )
 
 
-def fine_down_kernel(flags, ext, o2, o1, groups, d1, near1, near2, far, b1, first, q_ref, keep, sem):
+def fine_down_kernel(span, flags, ext, o2, o1, groups, d1, near1, near2, maps, far, b1, first, out_w, out_n, q_ref, keep, sem):
     cols = ext.shape[0] - 2
     rows = ext.shape[1]
     e = with_rows(flags, ext[cols], o1, o2, cols)
@@ -525,6 +562,14 @@
         groups += [row, pltpu.roll(row, LANES // 2, 1)]
     for i, group in enumerate(groups):
         first[count + i // cols, i % cols : i % cols + 1, :] = group.astype(F32)
+    out_w[0 : first.shape[0]] = first[...]
+    out_n[0 : first.shape[0]] = first[...]
+    at = first.shape[0]
+    for ref in maps:
+        for start in range(0, ref.shape[0], 2 * span):
+            out_w[at : at + span] = ref[start : start + span]
+            out_n[at : at + span] = ref[start + span : start + 2 * span]
+            at += span
     copy.wait()
 
 
@@ -591,8 +636,9 @@
     return second, lax.ppermute(first, "wide", route[2])
 
 
-def exchange(x, route):
-    return (*exchange_wide(x, x, route), *exchange_narrow(x, x, route))
+def exchange(x, route, wide=None, second=None, first=None):
+    pick = lambda y: x if y is None else y
+    return (*exchange_wide(pick(wide), x, route), *exchange_narrow(pick(first), pick(second), route))
 
 
 def body(
@@ -620,8 +666,14 @@
     count1, slots = tiles_one.shape[:2]
     count2 = tiles_two.shape[0]
 
-    order = [("wide", 1 << i) for i in reversed(range((wide - 1).bit_length()))]
-    order += [("narrow", 1 << i) for i in reversed(range((narrow - 1).bit_length()))]
+    if narrow != 4 or wide & (wide - 1):
+        raise NotImplementedError("mesh shape")
+    alone = [("wide", 1 << i) for i in reversed(range(1, (wide - 1).bit_length()))]
+    near_wide, near_narrow = ("wide", 1), ("narrow", narrow - 1)
+    orders = [
+        alone + [near_wide, near_narrow, ("narrow", 1)],
+        alone + [near_narrow, near_wide, ("narrow", 1)],
+    ]
     share = chain_forward.shape[1] // narrow
     held = []
     done = []
@@ -630,8 +682,8 @@
         return lax.ppermute(x, axis, [(i, i ^ step) for i in range(lax.axis_size(axis))])
 
     def gather_step(anchor):
-        step = order[len(done)]
-        merged = held if len(done) == len(order) - 1 or len(held) == 1 else [jnp.concatenate(held, axis=0)]
+        step = alone[len(done)]
+        merged = held if len(held) == 1 else [jnp.concatenate(held, axis=0)]
         merged, _ = lax.optimization_barrier((merged, anchor))
         held[:] = merged + [swap(m, *step) for m in merged]
         done.append(step)
@@ -640,9 +692,13 @@
     flags = sds((LEVEL3 + 1,), jnp.int32)
     flags, fields, first, second, piece = call(
         functools.partial(fine_first_kernel, sizes),
-        [flags, sds((cols + 2, rows, LANES)), rim, rim, sds((1, 2, share, LANES))],
+        [flags, sds((cols + 2, rows, LANES)), rim, rim, sds((2 * share // cols, cols, LANES))],
         (block, east, north, chain_forward, chain_backward),
-        scratch=[pltpu.VMEM((2, rows, LANES), F32), pltpu.SemaphoreType.DMA((5,))],
+        scratch=[
+            pltpu.VMEM((2, rows, LANES), F32),
+            pltpu.VMEM((2, share, LANES), F32),
+            pltpu.SemaphoreType.DMA((5,)),
+        ],
         specs=[HBM] * 5,
         scalars=(0,),
     )
@@ -660,7 +716,7 @@
             sds((slots, count1), jnp.int32),
             sds((slots, count2), jnp.int32),
             split,
-            sds((half, 1, LANES)),
+            sds((count1, 1, LANES)),
             sds((count2, *split.shape[1:]), BF16),
             sds((count2, 1, LANES)),
             split,
@@ -671,10 +727,11 @@
         + held_tiles
         + [
             pltpu.VMEM(tiles_two.shape, F32),
+            pltpu.VMEM((half, *tiles_one.shape[2:]), F32),
             pltpu.VMEM((slots, count1), jnp.int32),
             pltpu.VMEM((count2, slots), jnp.int32),
             pltpu.SMEM((count2, slots), jnp.int32),
-            pltpu.SemaphoreType.DMA((5,)),
+            pltpu.SemaphoreType.DMA((6,)),
         ]
         + stream_sems,
         specs=[SMEM] + [HBM] * 6,
@@ -692,32 +749,28 @@
         (flags, fields, o2, o1),
         specs=[SMEM] + [VMEM] * 3,
     )
-    gather_step(first)
+    while len(done) < len(alone):
+        gather_step(first)
     o2, o1 = exchange_wide(first, second, route)
     field1 = sds((count1, cols, LANES))
     field2 = sds((count2, cols, LANES))
-    tiles1_second, d1, tiles1_second_far = call(
-        second_half_kernel,
-        [split, sds((count1, 1, LANES)), split],
-        (tiles_one, d1),
-        scratch=held_tiles + stream_sems,
-        specs=[HBM, VMEM],
-        far=(2,),
-    )
     more = -(-(count1 + count2) // cols)
-    hold = {"t1a": tiles1, "t1b": tiles1_second, "d1": d1}
+    hold = {"t1a": tiles1, "d1": d1}
     t1 = ("t1a", "t1b")
     kept = sds((2 * cols + 3, rows + PAD, 2 * LANES))
-    keep, b1, x1 = call(
-        fine_down_kernel,
-        [kept, field1, sds((count1 + more, cols, LANES))],
-        (flags, ext, o2, o1, fine_groups, "d1", groups1, groups2),
+    maps_rows = sum(x.shape[0] for x in held)
+    x1_rows = count1 + more
+    riding = sds((x1_rows + maps_rows // 2, cols, LANES))
+    keep, b1, x1, x1_w, x1_n = call(
+        functools.partial(fine_down_kernel, share // cols),
+        [kept, field1, sds((x1_rows, cols, LANES)), riding, riding],
+        (flags, ext, o2, o1, fine_groups, "d1", groups1, groups2, tuple(held)),
         scratch=[
             pltpu.VMEM((2 * cols, rows, LANES), F32),
             pltpu.VMEM(kept.shape, F32),
             pltpu.SemaphoreType.DMA((1,)),
         ],
-        specs=[SMEM] + [VMEM] * 7,
+        specs=[SMEM] + [VMEM] * 8,
         mib=16,
         us=7,
         hold=hold,
@@ -735,8 +788,25 @@
         ins = (idx, t1 if level == 1 else ("t2",), f"d{level}", f"b{level}", x, *near)
         return call(smooth_kernel, like, ins, xs, lead + [VMEM] * 8, hold=hold), near
 
-    gather_step(x1)
-    x2, near = smooth(1, x1)
+    near = exchange(x1, route, wide=x1_w, second=x1_n)
+    tiles1_second, tiles1_second_far = call(
+        second_half_kernel,
+        [split, split],
+        (tiles_one, b1),
+        scratch=held_tiles + stream_sems,
+        specs=[HBM, VMEM],
+        far=(1,),
+    )
+    hold["t1b"] = tiles1_second
+    riding = sds((count1 + maps_rows, cols, LANES))
+    x2, x2_w, x2_n = call(
+        functools.partial(smooth_ride_kernel, x1_rows),
+        [field1, riding, riding],
+        (idx1, t1, "d1", "b1", x1, *near, x1_w, x1_n),
+        xs1,
+        lead + [VMEM] * 10,
+        hold=hold,
+    )
     groups = call(
         groups_kernel,
         sds((5, count1 + count2, LANES), jnp.int32),
@@ -744,8 +814,8 @@
         specs=[VMEM] * 6,
         us=1,
     )
-    gather_step(x2)
-    near = exchange(x2, route)
+    near = exchange(x2, route, wide=x2_w, second=x2_n)
+    maps = (x2_n, near[2], x2_w, near[1])
     hold |= {"x2": x2, "groups": groups, "d2": d2}
     left, scaled = call(
         residual_kernel,
@@ -755,12 +825,19 @@
         lead + [VMEM] * 8,
         hold=hold,
     )
-    while len(done) < len(order):
-        gather_step(scaled)
+    near = exchange(scaled, route)
+    bundle = call(
+        functools.partial(bundle_kernel, count1),
+        sds((4 * maps_rows, cols, LANES)),
+        (scaled, *maps),
+        specs=[VMEM] * 5,
+        us=0.5,
+    )
+    maps = (bundle, lax.ppermute(bundle, "narrow", route[0]))
     b2, y1 = call(
         restrict_one_kernel,
         [field2, field2],
-        (idx1, t1, left, groups1, "d2", scaled, *exchange(scaled, route)),
+        (idx1, t1, left, groups1, "d2", scaled, *near),
         xs1,
         lead + [VMEM] * 9,
         hold=hold,
@@ -769,15 +846,15 @@
     del hold["t1a"], hold["t1b"]
     hold |= {"b2": b2, "t2": tiles2}
     y2, _ = smooth(2, y1)
-    maps, y2 = lax.optimization_barrier((held, y2))
+    maps, y2 = lax.optimization_barrier((maps, y2))
     near = exchange(y2, route)
     chain_shape = sds((wide, 2, 2 * LANES, LANES), BF16)
     big = wide > 16
     chain = call(
-        functools.partial(chain_maps_kernel, order),
+        functools.partial(chain_maps_kernel, orders),
         chain_shape,
         (flags, *maps),
-        specs=[SMEM] + [PLAIN if big else VMEM] * len(maps),
+        specs=[SMEM] + [PLAIN if big else VMEM] * 2,
         mib=48 if big else 12,
         us=0.7,
         loose=(0,) if big else (),

time: 122 us -> 119 us (0.975)
  starting transfers between devices: 55.5 us -> 46.4 us
  waiting for transfers between devices: 27.4 us -> 33.7 us
    ppermute x13, waiting for transfers between devices: 9.47 us -> 15.6 us  [exchange_wide(): return (second, lax.ppermute(first, 'wide', route[2]))]
    ppermute x6 -> x2, starting transfers between devices: 9.18 us -> 5.74 us  [swap(): lax.ppermute(x, axis, [(i, i ^ step) for i in range(lax.axis_size(axis))])]
    ppermute x13, starting transfers between devices: 11.6 us -> 8.47 us  [exchange_narrow(): return (second, lax.ppermute(first, 'narrow', route[0]))]
    ppermute x13, starting transfers between devices: 29.3 us -> 27.1 us  [exchange_wide(): return (second, lax.ppermute(first, 'wide', route[2]))]
    pallas_call x21 -> x22, Pallas kernels: 27.2 us -> 27.8 us  [call(): pl.pallas_call(inner, out_shape=shapes, in_specs=specs[::ORDER], out_spec...]
  transfers between devices with their start and end apart: 58 -> 55, of which waited for: 21 -> 27; matrix products, arithmetic and copies ran while one was open for 0% -> 0% of each run, Pallas kernels for 12% -> 7%
where the time goes in v5:
time: 119 us
  starting transfers between devices  46.4 us (39%)
  waiting for transfers between devices  33.7 us (28%)
  Pallas kernels  27.8 us (23%)
  blocking collectives  10.5 us (9%)
    pallas_call x22, Pallas kernels, call(): pl.pallas_call(inner, out_shape=shapes, in_specs=specs[::ORDER], out_spec...  27.8 us
    ppermute x13, starting transfers between devices, exchange_wide(): return (second, lax.ppermute(first, 'wide', route[2]))  27.1 us
    ppermute x13, waiting for transfers between devices, exchange_narrow(): second = lax.ppermute(second, 'narrow', route[1])  16.8 us
    ppermute x13, waiting for transfers between devices, exchange_wide(): return (second, lax.ppermute(first, 'wide', route[2]))  15.6 us
    all_to_all x1, blocking collectives, body(): pieces = lax.all_to_all(out3, ('wide', 'narrow'), 0, 0)  10.5 us
    ppermute x13, starting transfers between devices, exchange_narrow(): return (second, lax.ppermute(first, 'narrow', route[0]))  8.47 us
    ppermute x2, starting transfers between devices, swap(): lax.ppermute(x, axis, [(i, i ^ step) for i in range(lax.axis_size(axis))])  5.74 us
    ppermute x13, starting transfers between devices, exchange_narrow(): second = lax.ppermute(second, 'narrow', route[1])  2.86 us
  transfers between devices with their start and end apart: 55, of which 27 were waited for; matrix products, arithmetic and copies ran while one was open for 0% of the time, Pallas kernels for 7%

profile of v5, /device:TPU:0, one launch (start us, length us, event | category | flops | bytes accessed | tf_op | source)
XLA Modules:
  0.0 118.9 jit_solution(13389452897034506896)
XLA Ops:
  1.2 4.1 %collective-permute-start.1 = (f32[16,4,128]{2,1,0:T(4,128)S(1)}, f32[16,4,128]{2,1,0:T(4,128)S(1)}, u32[]{:S(2)}, u32[]{:S(2)}) collective-permute-start(f32[16,4,128]{2,1,0:T(4,128)S(1)} %get-tuple-element.143), channel_id=1, source_target_pairs={{0,16},{4,20},{8,24},{12,28},{16,0},{20,4},{24,8},{28,12},{1,17},{... | collective-permute-start | bytes 98312 | tf_op jit(solution)/shard_map/ppermute | solution.py:682
  6.9 3.5 %shard_map.146 = (s32[4,16]{1,0:T(4,128)S(4)}, s32[4,4]{1,0:T(4,128)S(4)}, bf16[8,256,512]{2,1,0:T(8,128)(2,1)S(1)}, f32[16,1,128]{2,1,0:T(1,128)S(1)}, bf16[4,2...) custom-call(f32[4,4,64,64]{3,2,1,0:T(8,128)} %refs_0_.3, ...), custom_call_target="tpu_custom_call" | custom-call | bytes 7000000 | tf_op jit(solution)/shard_map/pallas_call | solution.py:63
  10.7 1.6 %collective-permute-start.3 = (f32[32,4,128]{2,1,0:T(4,128)S(1)}, f32[32,4,128]{2,1,0:T(4,128)S(1)}, u32[]{:S(2)}, u32[]{:S(2)}) collective-permute-start(f32[32,4,128]{2,1,0:T(4,128)S(1)} %pad_maximum_fusion.refs_2_), channel_id=1, source_target_pairs={{0,8},{4,12},{8,0},{12,4},{16,24},{20,28},{24,16},{28,20},{1,9},{5... | collective-permute-start | bytes 196616 | tf_op jit(solution)/shard_map/ppermute | solution.py:682
  12.3 1.9 %collective-permute-start.4 = (f32[6,4,256]{2,1,0:T(4,128)S(1)}, f32[6,4,256]{2,1,0:T(4,128)S(1)}, u32[]{:S(2)}, u32[]{:S(2)}) collective-permute-start(f32[6,4,256]{2,1,0:T(4,128)S(1)} %get-tuple-element.146), channel_id=1, source_target_pairs={{0,4},{4,0},{8,12},{12,8},{16,20},{20,16},{24,28},{28,24},{1,5},{5... | collective-permute-start | bytes 73736 | tf_op jit(solution)/shard_map/ppermute | solution.py:636
  14.3 1.9 %collective-permute-done.4.refs_7_ = f32[6,4,256]{2,1,0:T(4,128)S(1)} collective-permute-done((f32[6,4,256]{2,1,0:T(4,128)S(1)}, f32[6,4,256]{2,1,0:T(4,128)S(1)}, u32[]{:S(2)}, u32[]{:S(2)}) %collective-permute-start.4) | collective-permute-done | bytes 24608 | tf_op jit(solution)/shard_map/ppermute | solution.py:636
  16.2 3.4 %shard_map.148 = (f32[11,136,256]{2,1,0:T(8,128)}, f32[16,4,128]{2,1,0:T(4,128)S(1)}, f32[21,4,128]{2,1,0:T(4,128)S(1)}, f32[53,4,128]{2,1,0:T(4,128)S(1)}, f32[...) custom-call(bf16[8,256,512]{2,1,0:T(8,128)(2,1)S(1)} %get-tuple-elem, ...), custom_call_target="tpu_custom_call", output_to_operand_aliasing={{5}: (0, {}), {6}: (5, {})} | custom-call | bytes 24500000 | tf_op jit(solution)/shard_map/pallas_call | solution.py:63
  19.7 2.5 %collective-permute-start.8 = (f32[53,4,128]{2,1,0:T(4,128)S(1)}, f32[53,4,128]{2,1,0:T(4,128)S(1)}, u32[]{:S(2)}, u32[]{:S(2)}) collective-permute-start(f32[53,4,128]{2,1,0:T(4,128)S(1)} %get-tuple-element.152.refs_1_), channel_id=1, source_target_pairs={{0,4},{4,0},{8,12},{12,8},{16,20},{20,16},{24,28},{28,24},{1,5},{5... | collective-permute-start | bytes 325640 | tf_op jit(solution)/shard_map/ppermute | solution.py:636
  22.7 2.6 %shard_map.149 = (bf16[8,256,512]{2,1,0:T(8,128)(2,1)S(1)}, bf16[8,256,512]{2,1,0:T(8,128)(2,1)}) custom-call(f32[16,4,128]{2,1,0:T(4,128)S(1)} %get-tuple-element.154.refs_0_.refs_7_, f32[16,4,128,128]{3,2,1,0:T(8,128)} %refs_1_.5), custom_call_target="tpu_custom_call" | custom-call | bytes 7000000 | tf_op jit(solution)/shard_map/pallas_call | solution.py:63
  27.3 2.5 %collective-permute-start.10 = (f32[80,4,128]{2,1,0:T(4,128)S(1)}, f32[80,4,128]{2,1,0:T(4,128)S(1)}, u32[]{:S(2)}, u32[]{:S(2)}) collective-permute-start(f32[80,4,128]{2,1,0:T(4,128)S(1)} %get-tuple-element.159.refs_1_), channel_id=1, source_target_pairs={{0,4},{4,0},{8,12},{12,8},{16,20},{20,16},{24,28},{28,24},{1,5},{5... | collective-permute-start | bytes 491528 | tf_op jit(solution)/shard_map/ppermute | solution.py:636
  31.6 2.4 %collective-permute-done.10.refs_4_.refs_0_ = f32[80,4,128]{2,1,0:T(4,128)S(1)} collective-permute-done((f32[80,4,128]{2,1,0:T(4,128)S(1)}, f32[80,4,128]{2,1,0:T(4,128)S(1)}, u32[]{:S(2)}, u32[]{:S(2)}) %collective-permute-start.10) | collective-permute-done | bytes 163872 | tf_op jit(solution)/shard_map/ppermute | solution.py:636
  34.0 2.0 %collective-permute-done.11.refs_3_.refs_2_ = f32[80,4,128]{2,1,0:T(4,128)S(1)} collective-permute-done((f32[80,4,128]{2,1,0:T(4,128)S(1)}, f32[80,4,128]{2,1,0:T(4,128)S(1)}, u32[]{:S(2)}, u32[]{:S(2)}) %collective-permute-start.11) | collective-permute-done | bytes 163872 | tf_op jit(solution)/shard_map/ppermute | solution.py:630
  37.9 2.0 %collective-permute-start.17 = (f32[16,4,128]{2,1,0:T(4,128)S(1)}, f32[16,4,128]{2,1,0:T(4,128)S(1)}, u32[]{:S(2)}, u32[]{:S(2)}) collective-permute-start(f32[16,4,128]{2,1,0:T(4,128)S(1)} %get-tuple-element.167.refs_4_.refs_8_), channel_id=1, source_target_pairs={{0,4},{4,0},{8,12},{12,8},{16,20},{20,16},{24,28},{28,24},{1,5},{5... | collective-permute-start | bytes 98312 | tf_op jit(solution)/shard_map/ppermute | solution.py:636
  41.8 1.7 %collective-permute-done.16.refs_5_ = f32[16,4,128]{2,1,0:T(4,128)S(1)} collective-permute-done((f32[16,4,128]{2,1,0:T(4,128)S(1)}, f32[16,4,128]{2,1,0:T(4,128)S(1)}, u32[]{:S(2)}, u32[]{:S(2)}) %collective-permute-start.16) | collective-permute-done | bytes 32800 | tf_op jit(solution)/shard_map/ppermute | solution.py:630
  43.5 1.7 %shard_map.154 = (f32[4,4,128]{2,1,0:T(4,128)S(1)}, f32[4,4,128]{2,1,0:T(4,128)S(1)}, bf16[8,256,512]{2,1,0:T(8,128)(2,1)S(1)}, f32[16,1,128]{2,1,0:T(1,128)S(1)...) custom-call(s32[5,20,128]{2,1,0:T(8,128)S(1)} %get-tuple-element.168, ...), custom_call_target="tpu_custom_call", output_to_operand_aliasing={{2}: (13, {}), {3}: (3, {}), {4}: (2, {}), {5}: (12, {}), {... | custom-call | bytes 7000000 | tf_op jit(solution)/shard_map/pallas_call | solution.py:63
  45.3 1.8 %collective-permute-start.21 = (f32[4,4,128]{2,1,0:T(4,128)S(1)}, f32[4,4,128]{2,1,0:T(4,128)S(1)}, u32[]{:S(2)}, u32[]{:S(2)}) collective-permute-start(f32[4,4,128]{2,1,0:T(4,128)S(1)} %get-tuple-element.180.refs_8_), channel_id=1, source_target_pairs={{0,4},{4,0},{8,12},{12,8},{16,20},{20,16},{24,28},{28,24},{1,5},{5... | collective-permute-start | bytes 24584 | tf_op jit(solution)/shard_map/ppermute | solution.py:636
  50.7 2.9 %collective-permute-start.25 = (f32[4,4,128]{2,1,0:T(4,128)S(1)}, f32[4,4,128]{2,1,0:T(4,128)S(1)}, u32[]{:S(2)}, u32[]{:S(2)}) collective-permute-start(f32[4,4,128]{2,1,0:T(4,128)S(1)} %get-tuple-element.192.refs_9_), channel_id=1, source_target_pairs={{0,4},{4,0},{8,12},{12,8},{16,20},{20,16},{24,28},{28,24},{1,5},{5... | collective-permute-start | bytes 24584 | tf_op jit(solution)/shard_map/ppermute | solution.py:636
  55.2 1.4 %collective-permute-done.24.refs_6_ = f32[4,4,128]{2,1,0:T(4,128)S(1)} collective-permute-done((f32[4,4,128]{2,1,0:T(4,128)S(1)}, f32[4,4,128]{2,1,0:T(4,128)S(1)}, u32[]{:S(2)}, u32[]{:S(2)}) %collective-permute-start.24) | collective-permute-done | bytes 8224 | tf_op jit(solution)/shard_map/ppermute | solution.py:630
  57.1 1.9 %collective-permute-start.29 = (f32[4,4,128]{2,1,0:T(4,128)S(1)}, f32[4,4,128]{2,1,0:T(4,128)S(1)}, u32[]{:S(2)}, u32[]{:S(2)}) collective-permute-start(f32[4,4,128]{2,1,0:T(4,128)S(1)} %get-tuple-element.203.refs_11_), channel_id=1, source_target_pairs={{0,4},{4,0},{8,12},{12,8},{16,20},{20,16},{24,28},{28,24},{1,5},{5... | collective-permute-start | bytes 24584 | tf_op jit(solution)/shard_map/ppermute | solution.py:636
  62.8 10.5 %all_to_all.5.refs_9_ = f32[32,4,128]{2,1,0:T(4,128)S(1)} all-to-all(f32[32,4,128]{2,1,0:T(4,128)S(1)} %get-tuple-element.215), channel_id=1, replica_groups=mesh['wide'=8,'narrow'=4] {'wide','narrow'}, dimensions={0} | all-to-all | bytes 131072 | tf_op jit(solution)/shard_map/all_to_all | solution.py:882
  73.3 2.2 %shard_map.159 = (f32[4,4,128]{2,1,0:T(4,128)S(1)}, f32[16,1,128]{2,1,0:T(1,128)S(1)}, f32[16,4,128]{2,1,0:T(4,128)S(1)}, f32[16,4,128]{2,1,0:T(4,128)S(1)}, s32...) custom-call(f32[4,4,128]{2,1,0:T(4,128)S(1)} %get-tuple-element.207., ...), custom_call_target="tpu_custom_call", output_to_operand_aliasing={{1}: (3, {}), {2}: (2, {}), {3}: (1, {}), {4}: (4, {}), {5}... | custom-call | bytes 10500000 | tf_op jit(solution)/shard_map/pallas_call | solution.py:63
  75.7 2.0 %collective-permute-start.33 = (f32[4,4,128]{2,1,0:T(4,128)S(1)}, f32[4,4,128]{2,1,0:T(4,128)S(1)}, u32[]{:S(2)}, u32[]{:S(2)}) collective-permute-start(f32[4,4,128]{2,1,0:T(4,128)S(1)} %get-tuple-element.222.refs_9_), channel_id=1, source_target_pairs={{0,4},{4,0},{8,12},{12,8},{16,20},{20,16},{24,28},{28,24},{1,5},{5... | collective-permute-start | bytes 24584 | tf_op jit(solution)/shard_map/ppermute | solution.py:636
  81.2 2.1 %collective-permute-start.37 = (f32[4,4,128]{2,1,0:T(4,128)S(1)}, f32[4,4,128]{2,1,0:T(4,128)S(1)}, u32[]{:S(2)}, u32[]{:S(2)}) collective-permute-start(f32[4,4,128]{2,1,0:T(4,128)S(1)} %get-tuple-element.231.refs_9_), channel_id=1, source_target_pairs={{0,4},{4,0},{8,12},{12,8},{16,20},{20,16},{24,28},{28,24},{1,5},{5... | collective-permute-start | bytes 24584 | tf_op jit(solution)/shard_map/ppermute | solution.py:636
  86.8 2.2 %collective-permute-start.41 = (f32[4,4,128]{2,1,0:T(4,128)S(1)}, f32[4,4,128]{2,1,0:T(4,128)S(1)}, u32[]{:S(2)}, u32[]{:S(2)}) collective-permute-start(f32[4,4,128]{2,1,0:T(4,128)S(1)} %get-tuple-element.236.refs_5_), channel_id=1, source_target_pairs={{0,4},{4,0},{8,12},{12,8},{16,20},{20,16},{24,28},{28,24},{1,5},{5... | collective-permute-start | bytes 24584 | tf_op jit(solution)/shard_map/ppermute | solution.py:636
  90.7 1.4 %collective-permute-done.40.refs_2_ = f32[4,4,128]{2,1,0:T(4,128)S(1)} collective-permute-done((f32[4,4,128]{2,1,0:T(4,128)S(1)}, f32[4,4,128]{2,1,0:T(4,128)S(1)}, u32[]{:S(2)}, u32[]{:S(2)}) %collective-permute-start.40) | collective-permute-done | bytes 8224 | tf_op jit(solution)/shard_map/ppermute | solution.py:630
  92.2 1.7 %shard_map.162 = (f32[16,4,128]{2,1,0:T(4,128)S(1)}, f32[16,1,128]{2,1,0:T(1,128)S(1)}, f32[16,4,128]{2,1,0:T(4,128)S(1)}, f32[16,4,128]{2,1,0:T(4,128)S(1)}, s3...) custom-call(f32[16,4,128]{2,1,0:T(4,128)S(1)} %get-tuple-element.235, ...), custom_call_target="tpu_custom_call", output_to_operand_aliasing={{1}: (8, {}), {2}: (0, {}), {3}: (7, {}), {4}: (6, {}), {5}... | custom-call | bytes 7000000 | tf_op jit(solution)/shard_map/pallas_call | solution.py:63
  93.9 2.6 %collective-permute-start.45 = (f32[16,4,128]{2,1,0:T(4,128)S(1)}, f32[16,4,128]{2,1,0:T(4,128)S(1)}, u32[]{:S(2)}, u32[]{:S(2)}) collective-permute-start(f32[16,4,128]{2,1,0:T(4,128)S(1)} %get-tuple-element.242.refs_4_), channel_id=1, source_target_pairs={{0,4},{4,0},{8,12},{12,8},{16,20},{20,16},{24,28},{28,24},{1,5},{5... | collective-permute-start | bytes 98312 | tf_op jit(solution)/shard_map/ppermute | solution.py:636
  98.5 1.4 %collective-permute-done.44.refs_1_ = f32[16,4,128]{2,1,0:T(4,128)S(1)} collective-permute-done((f32[16,4,128]{2,1,0:T(4,128)S(1)}, f32[16,4,128]{2,1,0:T(4,128)S(1)}, u32[]{:S(2)}, u32[]{:S(2)}) %collective-permute-start.44) | collective-permute-done | bytes 32800 | tf_op jit(solution)/shard_map/ppermute | solution.py:630
  101.2 2.1 %collective-permute-start.49 = (f32[16,4,128]{2,1,0:T(4,128)S(1)}, f32[16,4,128]{2,1,0:T(4,128)S(1)}, u32[]{:S(2)}, u32[]{:S(2)}) collective-permute-start(f32[16,4,128]{2,1,0:T(4,128)S(1)} %get-tuple-element.247.refs_4_), channel_id=1, source_target_pairs={{0,4},{4,0},{8,12},{12,8},{16,20},{20,16},{24,28},{28,24},{1,5},{5... | collective-permute-start | bytes 98312 | tf_op jit(solution)/shard_map/ppermute | solution.py:636
  106.6 2.6 %shard_map.164 = (f32[4,128,128]{2,1,0:T(8,128)S(1)}, f32[4,4,128]{2,1,0:T(4,128)S(1)}, f32[4,4,128]{2,1,0:T(4,128)S(1)}, f32[16,1,128]{2,1,0:T(1,128)S(1)}, f32...) custom-call(f32[16,4,128]{2,1,0:T(4,128)S(1)} %collective-permute-do, ...), custom_call_target="tpu_custom_call", output_to_operand_aliasing={{3}: (7, {}), {4}: (6, {}), {5}: (10, {}), {6}: (9, {})} | custom-call | bytes 10500000 | tf_op jit(solution)/shard_map/pallas_call | solution.py:63
  110.5 2.0 %collective-permute-done.52.refs_1_ = f32[4,4,128]{2,1,0:T(4,128)S(1)} collective-permute-done((f32[4,4,128]{2,1,0:T(4,128)S(1)}, f32[4,4,128]{2,1,0:T(4,128)S(1)}, u32[]{:S(2)}, u32[]{:S(2)}) %collective-permute-start.52) | collective-permute-done | bytes 8224 | tf_op jit(solution)/shard_map/ppermute | solution.py:630
  113.5 3.0 %collective-permute-done.53.refs_0_ = f32[4,4,256]{2,1,0:T(4,128)S(1)} collective-permute-done((f32[4,4,256]{2,1,0:T(4,128)S(1)}, f32[4,4,256]{2,1,0:T(4,128)S(1)}, u32[]{:S(2)}, u32[]{:S(2)}) %collective-permute-start.53) | collective-permute-done | bytes 16416 | tf_op jit(solution)/shard_map/ppermute | solution.py:636
  116.5 2.3 %shard_map.166 = f32[4,128,128]{2,1,0:T(8,128)} custom-call(f32[4,4,256]{2,1,0:T(4,128)S(1)} %collective-permute-done.53.refs_0_, f32[4,4,256]{2,1,0:T(4,128)S(1)} %collective-permute-done.54.refs_1_, f32[4,128,256]{2,1,0:T(8,128)S(1)} %get-tuple-element.257.refs_2_, f32[11,136,256]{2,1,0:T(8,128)S(1)} %copy-done.2, ...), custom_call_target="tpu_custom_call" | custom-call | bytes 7000000 | tf_op jit(solution)/shard_map/pallas_call | solution.py:63
  (116 shorter events, 38.2 us)
Async XLA Ops:
  1.2 9.5 %collective-permute-start.1 = (f32[16,4,128]{2,1,0:T(4,128)S(1)}, f32[16,4,128]{2,1,0:T(4,128)S(1)}, u32[]{:S(2)}, u32[]{:S(2)}) collective-permute-start(f32[16,4,128]{2,1,0:T(4,128)S(1)} %get-tuple-element.143), channel_id=1, source_target_pairs={{0,16},{4,20},{8,24},{12,28},{16,0},{20,4},{24,8},{28,12},{1,17},{... | collective-permute-start | bytes 98312 | tf_op jit(solution)/shard_map/ppermute | solution.py:682
  5.3 5.2 %collective-permute-start = (f32[6,4,128]{2,1,0:T(4,128)S(1)}, f32[6,4,128]{2,1,0:T(4,128)S(1)}, u32[]{:S(2)}, u32[]{:S(2)}) collective-permute-start(f32[6,4,128]{2,1,0:T(4,128)S(1)} %get-tuple-element.132), channel_id=1, source_target_pairs={{1,2},{2,1},{0,3},{3,0},{5,6},{6,5},{4,7},{7,4},{9,10},{10,9},{8,1... | collective-permute-start | bytes 36872 | tf_op jit(solution)/shard_map/ppermute | solution.py:630
  6.0 4.5 %collective-permute-start.2 = (f32[6,4,128]{2,1,0:T(4,128)S(1)}, f32[6,4,128]{2,1,0:T(4,128)S(1)}, u32[]{:S(2)}, u32[]{:S(2)}) collective-permute-start(f32[6,4,128]{2,1,0:T(4,128)S(1)} %get-tuple-element.142), channel_id=1, source_target_pairs={{0,1},{1,0},{2,3},{3,2},{4,5},{5,4},{6,7},{7,6},{8,9},{9,8},{10,11... | collective-permute-start | bytes 36872 | tf_op jit(solution)/shard_map/ppermute | solution.py:631
  10.7 5.5 %collective-permute-start.3 = (f32[32,4,128]{2,1,0:T(4,128)S(1)}, f32[32,4,128]{2,1,0:T(4,128)S(1)}, u32[]{:S(2)}, u32[]{:S(2)}) collective-permute-start(f32[32,4,128]{2,1,0:T(4,128)S(1)} %pad_maximum_fusion.refs_2_), channel_id=1, source_target_pairs={{0,8},{4,12},{8,0},{12,4},{16,24},{20,28},{24,16},{28,20},{1,9},{5... | collective-permute-start | bytes 196616 | tf_op jit(solution)/shard_map/ppermute | solution.py:682
  12.3 3.8 %collective-permute-start.4 = (f32[6,4,256]{2,1,0:T(4,128)S(1)}, f32[6,4,256]{2,1,0:T(4,128)S(1)}, u32[]{:S(2)}, u32[]{:S(2)}) collective-permute-start(f32[6,4,256]{2,1,0:T(4,128)S(1)} %get-tuple-element.146), channel_id=1, source_target_pairs={{0,4},{4,0},{8,12},{12,8},{16,20},{20,16},{24,28},{28,24},{1,5},{5... | collective-permute-start | bytes 73736 | tf_op jit(solution)/shard_map/ppermute | solution.py:636
  19.6 5.6 %collective-permute-start.7 = (f32[53,4,128]{2,1,0:T(4,128)S(1)}, f32[53,4,128]{2,1,0:T(4,128)S(1)}, u32[]{:S(2)}, u32[]{:S(2)}) collective-permute-start(f32[53,4,128]{2,1,0:T(4,128)S(1)} %get-tuple-element.151.refs_0_), channel_id=1, source_target_pairs={{1,2},{2,1},{0,3},{3,0},{5,6},{6,5},{4,7},{7,4},{9,10},{10,9},{8,1... | collective-permute-start | bytes 325640 | tf_op jit(solution)/shard_map/ppermute | solution.py:630
  19.7 6.4 %collective-permute-start.8 = (f32[53,4,128]{2,1,0:T(4,128)S(1)}, f32[53,4,128]{2,1,0:T(4,128)S(1)}, u32[]{:S(2)}, u32[]{:S(2)}) collective-permute-start(f32[53,4,128]{2,1,0:T(4,128)S(1)} %get-tuple-element.152.refs_1_), channel_id=1, source_target_pairs={{0,4},{4,0},{8,12},{12,8},{16,20},{20,16},{24,28},{28,24},{1,5},{5... | collective-permute-start | bytes 325640 | tf_op jit(solution)/shard_map/ppermute | solution.py:636
  27.3 6.7 %collective-permute-start.10 = (f32[80,4,128]{2,1,0:T(4,128)S(1)}, f32[80,4,128]{2,1,0:T(4,128)S(1)}, u32[]{:S(2)}, u32[]{:S(2)}) collective-permute-start(f32[80,4,128]{2,1,0:T(4,128)S(1)} %get-tuple-element.159.refs_1_), channel_id=1, source_target_pairs={{0,4},{4,0},{8,12},{12,8},{16,20},{20,16},{24,28},{28,24},{1,5},{5... | collective-permute-start | bytes 491528 | tf_op jit(solution)/shard_map/ppermute | solution.py:636
  29.9 6.2 %collective-permute-start.11 = (f32[80,4,128]{2,1,0:T(4,128)S(1)}, f32[80,4,128]{2,1,0:T(4,128)S(1)}, u32[]{:S(2)}, u32[]{:S(2)}) collective-permute-start(f32[80,4,128]{2,1,0:T(4,128)S(1)} %get-tuple-element.160.refs_3_), channel_id=1, source_target_pairs={{1,2},{2,1},{0,3},{3,0},{5,6},{6,5},{4,7},{7,4},{9,10},{10,9},{8,1... | collective-permute-start | bytes 491528 | tf_op jit(solution)/shard_map/ppermute | solution.py:630
  37.3 13.3 %collective-permute-start.14 = (f32[256,4,128]{2,1,0:T(4,128)S(1)}, f32[256,4,128]{2,1,0:T(4,128)S(1)}, u32[]{:S(2)}, u32[]{:S(2)}) collective-permute-start(f32[256,4,128]{2,1,0:T(4,128)S(1)} %shard_map.153.refs_1_), channel_id=1, source_target_pairs={{0,1},{1,0},{2,3},{3,2},{4,5},{5,4},{6,7},{7,6},{8,9},{9,8},{10,11... | collective-permute-start | bytes 1572872 | tf_op jit(solution)/shard_map/ppermute | solution.py:836
  37.4 3.8 %collective-permute-start.18 = (f32[16,4,128]{2,1,0:T(4,128)S(1)}, f32[16,4,128]{2,1,0:T(4,128)S(1)}, u32[]{:S(2)}, u32[]{:S(2)}) collective-permute-start(f32[16,4,128]{2,1,0:T(4,128)S(1)} %get-tuple-element.167.refs_4_.refs_8_), channel_id=1, source_target_pairs={{4,8},{5,9},{6,10},{7,11},{8,4},{9,5},{10,6},{11,7},{12,16},{13,17... | collective-permute-start | bytes 98312 | tf_op jit(solution)/shard_map/ppermute | solution.py:635
  37.9 3.9 %collective-permute-start.17 = (f32[16,4,128]{2,1,0:T(4,128)S(1)}, f32[16,4,128]{2,1,0:T(4,128)S(1)}, u32[]{:S(2)}, u32[]{:S(2)}) collective-permute-start(f32[16,4,128]{2,1,0:T(4,128)S(1)} %get-tuple-element.167.refs_4_.refs_8_), channel_id=1, source_target_pairs={{0,4},{4,0},{8,12},{12,8},{16,20},{20,16},{24,28},{28,24},{1,5},{5... | collective-permute-start | bytes 98312 | tf_op jit(solution)/shard_map/ppermute | solution.py:636
  39.9 3.6 %collective-permute-start.16 = (f32[16,4,128]{2,1,0:T(4,128)S(1)}, f32[16,4,128]{2,1,0:T(4,128)S(1)}, u32[]{:S(2)}, u32[]{:S(2)}) collective-permute-start(f32[16,4,128]{2,1,0:T(4,128)S(1)} %get-tuple-element.167.refs_4_.refs_8_), channel_id=1, source_target_pairs={{1,2},{2,1},{0,3},{3,0},{5,6},{6,5},{4,7},{7,4},{9,10},{10,9},{8,1... | collective-permute-start | bytes 98312 | tf_op jit(solution)/shard_map/ppermute | solution.py:630
  45.2 3.2 %collective-permute-start.22 = (f32[4,4,128]{2,1,0:T(4,128)S(1)}, f32[4,4,128]{2,1,0:T(4,128)S(1)}, u32[]{:S(2)}, u32[]{:S(2)}) collective-permute-start(f32[4,4,128]{2,1,0:T(4,128)S(1)} %get-tuple-element.180.refs_8_), channel_id=1, source_target_pairs={{4,8},{5,9},{6,10},{7,11},{8,4},{9,5},{10,6},{11,7},{12,16},{13,17... | collective-permute-start | bytes 24584 | tf_op jit(solution)/shard_map/ppermute | solution.py:635
  45.3 3.7 %collective-permute-start.21 = (f32[4,4,128]{2,1,0:T(4,128)S(1)}, f32[4,4,128]{2,1,0:T(4,128)S(1)}, u32[]{:S(2)}, u32[]{:S(2)}) collective-permute-start(f32[4,4,128]{2,1,0:T(4,128)S(1)} %get-tuple-element.180.refs_8_), channel_id=1, source_target_pairs={{0,4},{4,0},{8,12},{12,8},{16,20},{20,16},{24,28},{28,24},{1,5},{5... | collective-permute-start | bytes 24584 | tf_op jit(solution)/shard_map/ppermute | solution.py:636
  50.6 4.0 %collective-permute-start.26 = (f32[4,4,128]{2,1,0:T(4,128)S(1)}, f32[4,4,128]{2,1,0:T(4,128)S(1)}, u32[]{:S(2)}, u32[]{:S(2)}) collective-permute-start(f32[4,4,128]{2,1,0:T(4,128)S(1)} %get-tuple-element.192.refs_9_), channel_id=1, source_target_pairs={{4,8},{5,9},{6,10},{7,11},{8,4},{9,5},{10,6},{11,7},{12,16},{13,17... | collective-permute-start | bytes 24584 | tf_op jit(solution)/shard_map/ppermute | solution.py:635
  50.7 4.5 %collective-permute-start.25 = (f32[4,4,128]{2,1,0:T(4,128)S(1)}, f32[4,4,128]{2,1,0:T(4,128)S(1)}, u32[]{:S(2)}, u32[]{:S(2)}) collective-permute-start(f32[4,4,128]{2,1,0:T(4,128)S(1)} %get-tuple-element.192.refs_9_), channel_id=1, source_target_pairs={{0,4},{4,0},{8,12},{12,8},{16,20},{20,16},{24,28},{28,24},{1,5},{5... | collective-permute-start | bytes 24584 | tf_op jit(solution)/shard_map/ppermute | solution.py:636
  57.1 3.7 %collective-permute-start.29 = (f32[4,4,128]{2,1,0:T(4,128)S(1)}, f32[4,4,128]{2,1,0:T(4,128)S(1)}, u32[]{:S(2)}, u32[]{:S(2)}) collective-permute-start(f32[4,4,128]{2,1,0:T(4,128)S(1)} %get-tuple-element.203.refs_11_), channel_id=1, source_target_pairs={{0,4},{4,0},{8,12},{12,8},{16,20},{20,16},{24,28},{28,24},{1,5},{5... | collective-permute-start | bytes 24584 | tf_op jit(solution)/shard_map/ppermute | solution.py:636
  75.7 3.7 %collective-permute-start.33 = (f32[4,4,128]{2,1,0:T(4,128)S(1)}, f32[4,4,128]{2,1,0:T(4,128)S(1)}, u32[]{:S(2)}, u32[]{:S(2)}) collective-permute-start(f32[4,4,128]{2,1,0:T(4,128)S(1)} %get-tuple-element.222.refs_9_), channel_id=1, source_target_pairs={{0,4},{4,0},{8,12},{12,8},{16,20},{20,16},{24,28},{28,24},{1,5},{5... | collective-permute-start | bytes 24584 | tf_op jit(solution)/shard_map/ppermute | solution.py:636
  81.2 3.7 %collective-permute-start.37 = (f32[4,4,128]{2,1,0:T(4,128)S(1)}, f32[4,4,128]{2,1,0:T(4,128)S(1)}, u32[]{:S(2)}, u32[]{:S(2)}) collective-permute-start(f32[4,4,128]{2,1,0:T(4,128)S(1)} %get-tuple-element.231.refs_9_), channel_id=1, source_target_pairs={{0,4},{4,0},{8,12},{12,8},{16,20},{20,16},{24,28},{28,24},{1,5},{5... | collective-permute-start | bytes 24584 | tf_op jit(solution)/shard_map/ppermute | solution.py:636
  86.8 3.9 %collective-permute-start.41 = (f32[4,4,128]{2,1,0:T(4,128)S(1)}, f32[4,4,128]{2,1,0:T(4,128)S(1)}, u32[]{:S(2)}, u32[]{:S(2)}) collective-permute-start(f32[4,4,128]{2,1,0:T(4,128)S(1)} %get-tuple-element.236.refs_5_), channel_id=1, source_target_pairs={{0,4},{4,0},{8,12},{12,8},{16,20},{20,16},{24,28},{28,24},{1,5},{5... | collective-permute-start | bytes 24584 | tf_op jit(solution)/shard_map/ppermute | solution.py:636
  93.9 3.5 %collective-permute-start.46 = (f32[16,4,128]{2,1,0:T(4,128)S(1)}, f32[16,4,128]{2,1,0:T(4,128)S(1)}, u32[]{:S(2)}, u32[]{:S(2)}) collective-permute-start(f32[16,4,128]{2,1,0:T(4,128)S(1)} %get-tuple-element.242.refs_4_), channel_id=1, source_target_pairs={{4,8},{5,9},{6,10},{7,11},{8,4},{9,5},{10,6},{11,7},{12,16},{13,17... | collective-permute-start | bytes 98312 | tf_op jit(solution)/shard_map/ppermute | solution.py:635
  93.9 4.5 %collective-permute-start.45 = (f32[16,4,128]{2,1,0:T(4,128)S(1)}, f32[16,4,128]{2,1,0:T(4,128)S(1)}, u32[]{:S(2)}, u32[]{:S(2)}) collective-permute-start(f32[16,4,128]{2,1,0:T(4,128)S(1)} %get-tuple-element.242.refs_4_), channel_id=1, source_target_pairs={{0,4},{4,0},{8,12},{12,8},{16,20},{20,16},{24,28},{28,24},{1,5},{5... | collective-permute-start | bytes 98312 | tf_op jit(solution)/shard_map/ppermute | solution.py:636
  96.6 3.3 %collective-permute-start.44 = (f32[16,4,128]{2,1,0:T(4,128)S(1)}, f32[16,4,128]{2,1,0:T(4,128)S(1)}, u32[]{:S(2)}, u32[]{:S(2)}) collective-permute-start(f32[16,4,128]{2,1,0:T(4,128)S(1)} %get-tuple-element.242.refs_4_), channel_id=1, source_target_pairs={{1,2},{2,1},{0,3},{3,0},{5,6},{6,5},{4,7},{7,4},{9,10},{10,9},{8,1... | collective-permute-start | bytes 98312 | tf_op jit(solution)/shard_map/ppermute | solution.py:630
  96.6 3.3 %collective-permute-start.43 = (f32[16,4,128]{2,1,0:T(4,128)S(1)}, f32[16,4,128]{2,1,0:T(4,128)S(1)}, u32[]{:S(2)}, u32[]{:S(2)}) collective-permute-start(f32[16,4,128]{2,1,0:T(4,128)S(1)} %get-tuple-element.242.refs_4_), channel_id=1, source_target_pairs={{0,1},{1,0},{2,3},{3,2},{4,5},{5,4},{6,7},{7,6},{8,9},{9,8},{10,11... | collective-permute-start | bytes 98312 | tf_op jit(solution)/shard_map/ppermute | solution.py:631
  101.1 3.2 %collective-permute-start.50 = (f32[16,4,128]{2,1,0:T(4,128)S(1)}, f32[16,4,128]{2,1,0:T(4,128)S(1)}, u32[]{:S(2)}, u32[]{:S(2)}) collective-permute-start(f32[16,4,128]{2,1,0:T(4,128)S(1)} %get-tuple-element.247.refs_4_), channel_id=1, source_target_pairs={{4,8},{5,9},{6,10},{7,11},{8,4},{9,5},{10,6},{11,7},{12,16},{13,17... | collective-permute-start | bytes 98312 | tf_op jit(solution)/shard_map/ppermute | solution.py:635
  101.2 4.0 %collective-permute-start.49 = (f32[16,4,128]{2,1,0:T(4,128)S(1)}, f32[16,4,128]{2,1,0:T(4,128)S(1)}, u32[]{:S(2)}, u32[]{:S(2)}) collective-permute-start(f32[16,4,128]{2,1,0:T(4,128)S(1)} %get-tuple-element.247.refs_4_), channel_id=1, source_target_pairs={{0,4},{4,0},{8,12},{12,8},{16,20},{20,16},{24,28},{28,24},{1,5},{5... | collective-permute-start | bytes 98312 | tf_op jit(solution)/shard_map/ppermute | solution.py:636
  103.3 3.3 %collective-permute-start.48 = (f32[16,4,128]{2,1,0:T(4,128)S(1)}, f32[16,4,128]{2,1,0:T(4,128)S(1)}, u32[]{:S(2)}, u32[]{:S(2)}) collective-permute-start(f32[16,4,128]{2,1,0:T(4,128)S(1)} %get-tuple-element.247.refs_4_), channel_id=1, source_target_pairs={{1,2},{2,1},{0,3},{3,0},{5,6},{6,5},{4,7},{7,4},{9,10},{10,9},{8,1... | collective-permute-start | bytes 98312 | tf_op jit(solution)/shard_map/ppermute | solution.py:630
  103.3 3.3 %collective-permute-start.47 = (f32[16,4,128]{2,1,0:T(4,128)S(1)}, f32[16,4,128]{2,1,0:T(4,128)S(1)}, u32[]{:S(2)}, u32[]{:S(2)}) collective-permute-start(f32[16,4,128]{2,1,0:T(4,128)S(1)} %get-tuple-element.247.refs_4_), channel_id=1, source_target_pairs={{0,1},{1,0},{2,3},{3,2},{4,5},{5,4},{6,7},{7,6},{8,9},{9,8},{10,11... | collective-permute-start | bytes 98312 | tf_op jit(solution)/shard_map/ppermute | solution.py:631
  109.3 3.1 %collective-permute-start.52 = (f32[4,4,128]{2,1,0:T(4,128)S(1)}, f32[4,4,128]{2,1,0:T(4,128)S(1)}, u32[]{:S(2)}, u32[]{:S(2)}) collective-permute-start(f32[4,4,128]{2,1,0:T(4,128)S(1)} %get-tuple-element.253), channel_id=1, source_target_pairs={{1,2},{2,1},{0,3},{3,0},{5,6},{6,5},{4,7},{7,4},{9,10},{10,9},{8,1... | collective-permute-start | bytes 24584 | tf_op jit(solution)/shard_map/ppermute | solution.py:630
  112.6 3.8 %collective-permute-start.53 = (f32[4,4,256]{2,1,0:T(4,128)S(1)}, f32[4,4,256]{2,1,0:T(4,128)S(1)}, u32[]{:S(2)}, u32[]{:S(2)}) collective-permute-start(f32[4,4,256]{2,1,0:T(4,128)S(1)} %get-tuple-element.255), channel_id=1, source_target_pairs={{0,4},{4,0},{8,12},{12,8},{16,20},{20,16},{24,28},{28,24},{1,5},{5... | collective-permute-start | bytes 49160 | tf_op jit(solution)/shard_map/ppermute | solution.py:636
  113.3 3.2 %collective-permute-start.54 = (f32[4,4,256]{2,1,0:T(4,128)S(1)}, f32[4,4,256]{2,1,0:T(4,128)S(1)}, u32[]{:S(2)}, u32[]{:S(2)}) collective-permute-start(f32[4,4,256]{2,1,0:T(4,128)S(1)} %get-tuple-element.256), channel_id=1, source_target_pairs={{4,8},{5,9},{6,10},{7,11},{8,4},{9,5},{10,6},{11,7},{12,16},{13,17... | collective-permute-start | bytes 49160 | tf_op jit(solution)/shard_map/ppermute | solution.py:635
  (30 other events, 149.5 us)

commit v6 on v5

--- a/solution.py
+++ b/solution.py
@@ -12,7 +12,7 @@
 SHIFT = 0.1
 JACOBI = 0.6
 LANES = 128
-ORDER = -1
+ORDER = 1
 RIM = 4
 PAD = 2 * RIM
 VMEM = pl.BlockSpec(memory_space=pltpu.VMEM)
@@ -130,17 +130,17 @@
 
 
 class Stream:
-    def __init__(self, half, tiles, held, t_ref, far, sems, parts=4):
+    def __init__(self, half, tiles, held, t_ref, sems, parts=4):
         self.count, self.slots = held.shape[0], held.shape[1]
         self.step = self.count // parts
         self.held, self.t_ref = held, t_ref
-        spans = [pl.ds(i * self.step, self.step) for i in range(parts)]
         self.loads = [
-            pltpu.make_async_copy(tiles.at[pl.ds(half * self.count + i * self.step, self.step)], held.at[a], sems.at[i])
-            for i, a in enumerate(spans)
-        ]
-        self.stores = [
-            pltpu.make_async_copy(t_ref.at[a], far.at[a], sems.at[parts + i]) for i, a in enumerate(spans)
+            pltpu.make_async_copy(
+                tiles.at[pl.ds(half * self.count + i * self.step, self.step)],
+                held.at[pl.ds(i * self.step, self.step)],
+                sems.at[i],
+            )
+            for i in range(parts)
         ]
         for load in self.loads:
             load.start()
@@ -151,31 +151,31 @@
             for r in range(i * self.step, (i + 1) * self.step):
                 for k in range(self.slots):
                     split_tile(self.held[r, k], r, k, self.t_ref)
-            self.stores[i].start()
-
-    def end(self):
-        for store in self.stores:
-            store.wait()
-
-
-def second_half_kernel(tiles, _, t_ref, far, held, sems):
-    stream = Stream(1, tiles, held, t_ref, far, sems)
-    stream.run()
-    stream.end()
+
+
+def store_kernel(t_refs, _, *refs):
+    *fars, sems = refs
+    copies = [pltpu.make_async_copy(a, b, sems.at[i]) for i, (a, b) in enumerate(zip(t_refs, fars))]
+    for copy in copies:
+        copy.start()
+    for copy in copies:
+        copy.wait()
+
+
+def half_kernel(half, tiles, _, t_ref, held, sems):
+    Stream(half, tiles, held, t_ref, sems).run()
 
 
 def setup_kernel(
     flags, columns1, live1, columns2, live2, tiles1, tiles2,
-    idx1, idx2, t1, d1, t2, d2, far,
-    in1, in2, in3, in4, held_tiles, held2, fronts, held1, held_two, turned, sems, stream_sems,
+    idx1, idx2, d1, t2, d2,
+    in1, in2, in3, in4, held2, fronts, held1, held_two, turned, sems,
 ):
     ins = [(columns1, in1), (live1, in2), (columns2, in3), (live2, in4), (tiles2, held2)]
-    half = fronts.shape[0]
-    ins.append((tiles1.at[half:, 0], fronts))
+    ins.append((tiles1.at[:, 0], fronts))
     ins = [pltpu.make_async_copy(a, b, sems.at[i]) for i, (a, b) in enumerate(ins)]
     for copy in ins:
         copy.start()
-    stream = Stream(0, tiles1, held_tiles, t1, far, stream_sems)
     for copy in ins:
         copy.wait()
     w_odd, n_odd = flags[W_ODD], flags[N_ODD]
@@ -211,29 +211,34 @@
                 diag = jnp.sum(jnp.where(row == col, tile, 0.0), axis=0, keepdims=True)
                 lane = lax.broadcasted_iota(jnp.int32, diag.shape, 1)
                 d2[r] = jnp.where(lane < tile.shape[0], diag, 1.0)
-    for r in range(half):
-        d1[half + r] = diagonal(fronts[r])
-    stream.run()
-    for r in range(half):
-        d1[r] = diagonal(held_tiles[r, 0])
+    for r in range(fronts.shape[0]):
+        d1[r] = diagonal(fronts[r])
     for copy in copies:
         copy.wait()
     slots, count = idx2.shape
     for k in range(slots):
         for r in range(count):
             idx2[k, r] = turned[r, k]
-    stream.end()
-
-
-def apply_tiles(t_ref, xs, idx):
+
+
+def apply_tiles(t_ref, xs, idx, done=None):
     slots, count = idx.shape
+    first = 0 if done is None else 1
     out = []
     for r in range(count):
-        lhs = twice(jnp.concatenate([xs[idx[k, r]] for k in range(slots)], axis=1))
+        lhs = twice(jnp.concatenate([xs[idx[k, r]] for k in range(first, slots)], axis=1))
         t, at = t_ref[r // t_ref[0].shape[0]], r % t_ref[0].shape[0]
-        both = dot_nt(lhs, t[at])[0:8]
-        out.append(rows_sum(both[:, :LANES] + both[:, LANES:]))
+        both = dot_nt(lhs, t[at, :, first * LANES :])[0:8]
+        value = rows_sum(both[:, :LANES] + both[:, LANES:])
+        out.append(value if done is None else value + done[r])
     return out
+
+
+def own_kernel(t_ref, x, out):
+    for r in range(x.shape[0]):
+        t, at = t_ref[r // t_ref[0].shape[0]], r % t_ref[0].shape[0]
+        both = dot_nt(twice(rows_of(x[r])), t[at, :, :LANES])[0:8]
+        out[r] = rows_sum(both[:, :LANES] + both[:, LANES:])
 
 
 def fill_blocks(xs, own, others, count):
@@ -250,10 +255,14 @@
         start += count
 
 
-def smooth_kernel(idx, t, d, b, own, o1, o2, o3, o4, out, xs):
+def smooth_more_kernel(idx, t, d, b, own, o1, o2, o3, o4, done, out, xs):
+    smooth_kernel(idx, t, d, b, own, o1, o2, o3, o4, out, xs, done)
+
+
+def smooth_kernel(idx, t, d, b, own, o1, o2, o3, o4, out, xs, done=None):
     count = b.shape[0]
     fill_blocks(xs, own, (o1, o2, o3, o4), count)
-    for r, ax in enumerate(apply_tiles(t, xs, idx)):
+    for r, ax in enumerate(apply_tiles(t, xs, idx, done)):
         out[r] = own[r] + JACOBI * (b[r] - ax) / d[r]
 
 
@@ -266,22 +275,26 @@
     ride(out_w, count, ((sent_n, first), (o3, first)))
 
 
-def residual_kernel(idx, t, d, b, own, o1, o2, o3, o4, left, scaled, xs):
+def residual_more_kernel(idx, t, d, b, own, o1, o2, o3, o4, done, left, scaled, xs):
+    residual_kernel(idx, t, d, b, own, o1, o2, o3, o4, left, scaled, xs, done)
+
+
+def residual_kernel(idx, t, d, b, own, o1, o2, o3, o4, left, scaled, xs, done=None):
     count = b.shape[0]
     fill_blocks(xs, own, (o1, o2, o3, o4), count)
-    for r, ax in enumerate(apply_tiles(t, xs, idx)):
+    for r, ax in enumerate(apply_tiles(t, xs, idx, done)):
         rest = b[r] - ax
         left[r] = rest
         scaled[r] = rest / d[r]
 
 
-def restrict_one_kernel(idx, t, left, groups, d2, own, o1, o2, o3, o4, b2, first, xs):
+def restrict_one_kernel(idx, t, left, groups, d2, own, o1, o2, o3, o4, done, b2, first, xs):
     count = left.shape[0]
     fill_blocks(xs, own, (o1, o2, o3, o4), count)
     total = None
     coarse_tiles, _, lanes = b2.shape
     size = coarse_tiles * lanes // 2
-    for r, ax in enumerate(apply_tiles(t, xs, idx)):
+    for r, ax in enumerate(apply_tiles(t, xs, idx, done)):
         rows = twice(rows_of(left[r] - 0.5 * ax))
         hot = lax.broadcasted_iota(jnp.int32, (size, LANES), 0) == groups[r : r + 1, :]
         term = dot_nt(rows, hot.astype(F32).astype(BF16))
@@ -509,17 +522,18 @@
     rows = ext.shape[1]
     e = with_rows(flags, ext[cols], o1, o2, cols)
     n = with_rows(flags, ext[cols + 1], o1, o2, cols + 1)
-    inv = 1.0 / (SHIFT + e + pltpu.roll(e, 1, 0) + n + pltpu.roll(n, 1, 1))
     diag = SHIFT + e + pltpu.roll(e, 1, 0) + n + pltpu.roll(n, 1, 1)
+    inv = 1.0 / diag
+    step_inv = JACOBI * inv
     keep[2 * cols] = e
     keep[2 * cols + 1] = n
-    keep[2 * cols + 2] = inv
+    keep[2 * cols + 2] = step_inv
     for c in range(cols):
         b = with_rows(flags, ext[c], o1, o2, c)
-        x1 = JACOBI * b * inv
-        x2 = x1 + JACOBI * ((1.0 - JACOBI) * b + beside(x1, e, n)) * inv
+        x1 = b * step_inv
+        x2 = (2.0 - JACOBI) * x1 + beside(x1, e, n) * step_inv
         keep[c] = x2
-        keep[cols + c] = b
+        keep[cols + c] = x1
         rest = b - diag * x2 + beside(x2, e, n)
         q = 0.5 * (rest + beside(rest * inv, e, n))
         for i, part in enumerate(parts_of(q[:rows, :LANES])):
@@ -527,7 +541,7 @@
     copy = pltpu.make_async_copy(keep, far, sem.at[0])
     copy.start()
     count = b1.shape[0]
-    step = 32
+    step = 64
     one, zero = jnp.ones((), BF16), jnp.zeros((), BF16)
     lanes = lax.broadcasted_iota(jnp.int32, (LANES, LANES), 0).astype(F32).astype(BF16)
 
@@ -573,21 +587,22 @@
     copy.wait()
 
 
-def fine_spread_kernel(flags, t, idx, d, b, groups, own, o1, o2, o3, o4, spread, first, second, xs, us):
+def fine_spread_kernel(flags, t, idx, d, b, groups, own, o1, o2, o3, o4, done, spread, first, second, xs, us):
     count, cols, _ = b.shape
     fill_blocks(xs, own, (o1, o2, o3, o4), count)
-    for r, ax in enumerate(apply_tiles(t, xs, idx)):
+    for r, ax in enumerate(apply_tiles(t, xs, idx, done)):
         us[r] = own[r] + JACOBI * (b[r] - ax) / d[r]
     rows = groups.shape[0]
-    for c in range(cols):
-        for j in range(rows // 8):
-            group = groups[8 * j : 8 * j + 8, :]
-            high, low = group >> 7, group & (LANES - 1)
-            value = jnp.zeros((8, LANES), F32)
-            for h in range(count):
-                table = jnp.broadcast_to(us[h, c : c + 1, :], (8, LANES))
-                got = jnp.take_along_axis(table, low, axis=1)
-                value = jnp.where(high == h, got, value)
+    tables = [[jnp.broadcast_to(us[h, c : c + 1, :], (8, LANES)) for h in range(count)] for c in range(cols)]
+    for j in range(rows // 8):
+        group = groups[8 * j : 8 * j + 8, :]
+        high, low = group >> 7, group & (LANES - 1)
+        masks = [high == h for h in range(1, count)]
+        for c in range(cols):
+            value = jnp.take_along_axis(tables[c][0], low, axis=1)
+            for h in range(1, count):
+                got = jnp.take_along_axis(tables[c][h], low, axis=1)
+                value = jnp.where(masks[h - 1], got, value)
             spread[c, 8 * j : 8 * j + 8, :] = value
     narrow_rims(flags, [spread[c] for c in range(cols)], first, second)
 
@@ -595,13 +610,14 @@
 def fine_up_kernel(flags, keep, ext, o2, o1, far, out, sems):
     cols = out.shape[0]
     copies = []
-    e, n, inv = keep[2 * cols], keep[2 * cols + 1], keep[2 * cols + 2]
+    e, n, step_inv = keep[2 * cols], keep[2 * cols + 1], keep[2 * cols + 2]
+    half_inv = (0.5 / JACOBI) * step_inv
     for c in range(cols):
-        b = keep[cols + c]
+        x1 = keep[cols + c]
         spread = with_rows(flags, ext[c], o1, o2, c)
-        x = keep[c] + 0.5 * (spread + beside(spread, e, n) * inv)
+        x = keep[c] + 0.5 * spread + beside(spread, e, n) * half_inv
         for _ in range(2):
-            x = (1.0 - JACOBI) * x + JACOBI * (b + beside(x, e, n)) * inv
+            x = (1.0 - JACOBI) * x + x1 + beside(x, e, n) * step_inv
         out[c] = x[: out.shape[1], :LANES]
         copies.append(pltpu.make_async_copy(out.at[c], far.at[c], sems.at[c]))
         copies[-1].start()
@@ -709,38 +725,33 @@
     half = count1 // 2
     split = sds((half, 2 * LANES, slots * LANES), BF16)
     held_tiles = [pltpu.VMEM((half, *tiles_one.shape[1:]), F32)]
-    stream_sems = [pltpu.SemaphoreType.DMA((8,))]
-    idx1, idx2, tiles1, d1, tiles2, d2, tiles1_far = call(
+    stream_sems = [pltpu.SemaphoreType.DMA((4,))]
+    idx1, idx2, d1, tiles2, d2 = call(
         setup_kernel,
         [
             sds((slots, count1), jnp.int32),
             sds((slots, count2), jnp.int32),
-            split,
             sds((count1, 1, LANES)),
             sds((count2, *split.shape[1:]), BF16),
             sds((count2, 1, LANES)),
-            split,
         ],
         (flags, columns_one.T, live_one.T, columns_two, live_two, tiles_one, tiles_two),
         scratch=[pltpu.VMEM((slots - 1, count1), jnp.int32)] * 2
         + [pltpu.VMEM((count2, slots - 1), jnp.int32)] * 2
-        + held_tiles
         + [
             pltpu.VMEM(tiles_two.shape, F32),
-            pltpu.VMEM((half, *tiles_one.shape[2:]), F32),
+            pltpu.VMEM((count1, *tiles_one.shape[2:]), F32),
             pltpu.VMEM((slots, count1), jnp.int32),
             pltpu.VMEM((count2, slots), jnp.int32),
             pltpu.SMEM((count2, slots), jnp.int32),
             pltpu.SemaphoreType.DMA((6,)),
-        ]
-        + stream_sems,
+        ],
         specs=[SMEM] + [HBM] * 6,
-        far=(6,),
         scalars=(0, 1),
     )
     groups1 = coarse_groups.reshape(count1, LANES)
     groups2 = coarser_groups.reshape(-1, LANES)
-    o2, idx1, idx2, tiles1, tiles2, d1, d2 = lax.optimization_barrier((o2, idx1, idx2, tiles1, tiles2, d1, d2))
+    o2, idx1, idx2, tiles2, d1, d2 = lax.optimization_barrier((o2, idx1, idx2, tiles2, d1, d2))
 
     rim = sds((cols + 2, RIM, 2 * LANES))
     ext, first, second = call(
@@ -752,6 +763,17 @@
     while len(done) < len(alone):
         gather_step(first)
     o2, o1 = exchange_wide(first, second, route)
+
+    def split_half(i, after):
+        return call(
+            functools.partial(half_kernel, i),
+            split,
+            (tiles_one, after),
+            scratch=held_tiles + stream_sems,
+            specs=[HBM, VMEM],
+        )
+
+    tiles1 = split_half(0, first)
     field1 = sds((count1, cols, LANES))
     field2 = sds((count2, cols, LANES))
     more = -(-(count1 + count2) // cols)
@@ -782,22 +804,20 @@
     xs2 = [pltpu.VMEM((5 * count2 + 1, 8, LANES), F32)]
     lead = [SMEM]
 
+    def own_part(x):
+        return call(own_kernel, field1, (tuple(hold[name] for name in t1), x), specs=[VMEM, VMEM], us=0.5)
+
     def smooth(level, x):
         idx, like, xs = (idx1, field1, xs1) if level == 1 else (idx2, field2, xs2)
         near = exchange(x, route)
         ins = (idx, t1 if level == 1 else ("t2",), f"d{level}", f"b{level}", x, *near)
-        return call(smooth_kernel, like, ins, xs, lead + [VMEM] * 8, hold=hold), near
+        if level == 1:
+            ins = (*ins, own_part(x))
+        kernel = smooth_more_kernel if level == 1 else smooth_kernel
+        return call(kernel, like, ins, xs, lead + [VMEM] * (len(ins) - 1), hold=hold), near
 
     near = exchange(x1, route, wide=x1_w, second=x1_n)
-    tiles1_second, tiles1_second_far = call(
-        second_half_kernel,
-        [split, split],
-        (tiles_one, b1),
-        scratch=held_tiles + stream_sems,
-        specs=[HBM, VMEM],
-        far=(1,),
-    )
-    hold["t1b"] = tiles1_second
+    hold["t1b"] = split_half(1, b1)
     riding = sds((count1 + maps_rows, cols, LANES))
     x2, x2_w, x2_n = call(
         functools.partial(smooth_ride_kernel, x1_rows),
@@ -818,11 +838,11 @@
     maps = (x2_n, near[2], x2_w, near[1])
     hold |= {"x2": x2, "groups": groups, "d2": d2}
     left, scaled = call(
-        residual_kernel,
+        residual_more_kernel,
         [field1, field1],
-        (idx1, t1, "d1", "b1", "x2", *near),
+        (idx1, t1, "d1", "b1", "x2", *near, own_part(x2)),
         xs1,
-        lead + [VMEM] * 8,
+        lead + [VMEM] * 9,
         hold=hold,
     )
     near = exchange(scaled, route)
@@ -837,15 +857,27 @@
     b2, y1 = call(
         restrict_one_kernel,
         [field2, field2],
-        (idx1, t1, left, groups1, "d2", scaled, *near),
+        (idx1, t1, left, groups1, "d2", scaled, *near, own_part(scaled)),
         xs1,
-        lead + [VMEM] * 9,
-        hold=hold,
-    )
-
+        lead + [VMEM] * 10,
+        hold=hold,
+    )
+
+    near = exchange(y1, route)
+    tiles1 = call(
+        store_kernel,
+        [split, split],
+        (t1, y1),
+        scratch=[pltpu.SemaphoreType.DMA((2,))],
+        specs=[VMEM, VMEM],
+        far=(0, 1),
+        hold=hold,
+    )
     del hold["t1a"], hold["t1b"]
     hold |= {"b2": b2, "t2": tiles2}
-    y2, _ = smooth(2, y1)
+    y2 = call(
+        smooth_kernel, field2, (idx2, ("t2",), "d2", "b2", y1, *near), xs2, lead + [VMEM] * 8, hold=hold
+    )
     maps, y2 = lax.optimization_barrier((maps, y2))
     near = exchange(y2, route)
     chain_shape = sds((wide, 2, 2 * LANES, LANES), BF16)
@@ -896,7 +928,7 @@
 
     for name in ("t2", "d2", "b2", "y2"):
         del hold[name]
-    hold |= {"t1a": tiles1_far, "t1b": tiles1_second_far}
+    hold |= {"t1a": tiles1[0], "t1b": tiles1[1]}
     x3 = call(
         prolong_one_kernel,
         field1,
@@ -911,9 +943,9 @@
     spread, first, second = call(
         fine_spread_kernel,
         [sds((cols, rows, LANES)), rim, rim],
-        (flags, t1, idx1, "d1", "b1", fine_groups, x4, *exchange(x4, route)),
+        (flags, t1, idx1, "d1", "b1", fine_groups, x4, *exchange(x4, route), own_part(x4)),
         xs1 + [pltpu.VMEM((count1, cols, LANES), F32)],
-        [SMEM, VMEM, SMEM] + [VMEM] * 8,
+        [SMEM, VMEM, SMEM] + [VMEM] * 9,
         us=3,
         hold=hold,
     )

time: 119 us -> 117 us (0.983)
  waiting for transfers between devices: 33.7 us -> 28.8 us
  starting transfers between devices: 46.4 us -> 47.9 us
    ppermute x13, waiting for transfers between devices: 15.6 us -> 10.8 us  [exchange_wide(): return (second, lax.ppermute(first, 'wide', route[2]))]
    ppermute x13, starting transfers between devices: 2.86 us -> 1.11 us  [exchange_narrow(): second = lax.ppermute(second, 'narrow', route[1])]
    ppermute x13, starting transfers between devices: 27.1 us -> 28.7 us  [exchange_wide(): return (second, lax.ppermute(first, 'wide', route[2]))]
    pallas_call x22 -> x28, Pallas kernels: 27.8 us -> 28.5 us  [call(): pl.pallas_call(inner, out_shape=shapes, in_specs=specs[::ORDER], out_spec...]
  transfers between devices with their start and end apart: 55 -> 55, of which waited for: 27 -> 26; matrix products, arithmetic and copies ran while one was open for 0% -> 0% of each run, Pallas kernels for 7% -> 10%
where the time goes in v6:
time: 117 us
  starting transfers between devices  47.9 us (41%)
  waiting for transfers between devices  28.8 us (25%)
  Pallas kernels  28.5 us (24%)
  blocking collectives  11.1 us (9%)
    ppermute x13, starting transfers between devices, exchange_wide(): return (second, lax.ppermute(first, 'wide', route[2]))  28.7 us
    pallas_call x28, Pallas kernels, call(): pl.pallas_call(inner, out_shape=shapes, in_specs=specs[::ORDER], out_spec...  28.5 us
    ppermute x13, waiting for transfers between devices, exchange_narrow(): second = lax.ppermute(second, 'narrow', route[1])  17.1 us
    all_to_all x1, blocking collectives, body(): pieces = lax.all_to_all(out3, ('wide', 'narrow'), 0, 0)  11.1 us
    ppermute x13, waiting for transfers between devices, exchange_wide(): return (second, lax.ppermute(first, 'wide', route[2]))  10.8 us
    ppermute x13, starting transfers between devices, exchange_narrow(): return (second, lax.ppermute(first, 'narrow', route[0]))  9.31 us
    ppermute x2, starting transfers between devices, swap(): lax.ppermute(x, axis, [(i, i ^ step) for i in range(lax.axis_size(axis))])  5.74 us
    ppermute x13, starting transfers between devices, exchange_wide(): second = lax.ppermute(second, ('wide', 'narrow'), route[3])  2.99 us
  transfers between devices with their start and end apart: 55, of which 26 were waited for; matrix products, arithmetic and copies ran while one was open for 0% of the time, Pallas kernels for 10%

profile of v6, /device:TPU:0, one launch (start us, length us, event | category | flops | bytes accessed | tf_op | source)
XLA Modules:
  0.0 116.9 jit_solution(7640650832105780396)
XLA Ops:
  1.2 4.1 %collective-permute-start.4 = (f32[16,4,128]{2,1,0:T(4,128)S(1)}, f32[16,4,128]{2,1,0:T(4,128)S(1)}, u32[]{:S(2)}, u32[]{:S(2)}) collective-permute-start(f32[16,4,128]{2,1,0:T(4,128)S(1)} %get-tuple-element.151), channel_id=1, source_target_pairs={{0,16},{4,20},{8,24},{12,28},{16,0},{20,4},{24,8},{28,12},{1,17},{... | collective-permute-start | bytes 98312 | tf_op jit(solution)/shard_map/ppermute | solution.py:698
  6.9 2.2 %shard_map.146 = (s32[4,16]{1,0:T(4,128)S(4)}, s32[4,4]{1,0:T(4,128)S(4)}, f32[16,1,128]{2,1,0:T(1,128)S(1)}, bf16[4,256,512]{2,1,0:T(8,128)(2,1)S(1)}, f32[4,1,128]{2,1,0:T(1,128)S(1)}) custom-call(s32[9]{0:T(128)S(4)} %get-tuple-element.136.refs_0_, s32[3,16]{1,0:T(4,128)} %bitcast.8, s32[3,16]{1,0:T(4,128)} %bitcast.9, s32[4,3]{1,0:T(4,128)} %refs_3_.3, ...), custom_call_target="tpu_custom_call" | custom-call | bytes 7000000 | tf_op jit(solution)/shard_map/pallas_call | solution.py:63
  9.4 1.6 %collective-permute-start.5 = (f32[32,4,128]{2,1,0:T(4,128)S(1)}, f32[32,4,128]{2,1,0:T(4,128)S(1)}, u32[]{:S(2)}, u32[]{:S(2)}) collective-permute-start(f32[32,4,128]{2,1,0:T(4,128)S(1)} %pad_maximum_fusion.refs_8_), channel_id=1, source_target_pairs={{0,8},{4,12},{8,0},{12,4},{16,24},{20,28},{24,16},{28,20},{1,9},{5... | collective-permute-start | bytes 196616 | tf_op jit(solution)/shard_map/ppermute | solution.py:698
  11.0 1.9 %collective-permute-start.3 = (f32[6,4,256]{2,1,0:T(4,128)S(1)}, f32[6,4,256]{2,1,0:T(4,128)S(1)}, u32[]{:S(2)}, u32[]{:S(2)}) collective-permute-start(f32[6,4,256]{2,1,0:T(4,128)S(1)} %get-tuple-element.148.refs_1_), channel_id=1, source_target_pairs={{0,4},{4,0},{8,12},{12,8},{16,20},{20,16},{24,28},{28,24},{1,5},{5... | collective-permute-start | bytes 73736 | tf_op jit(solution)/shard_map/ppermute | solution.py:652
  13.0 1.6 %shard_map.148.refs_10_ = bf16[8,256,512]{2,1,0:T(8,128)(2,1)S(1)} custom-call(f32[16,4,128,128]{3,2,1,0:T(8,128)} %refs_0_.5, f32[6,4,256]{2,1,0:T(4,128)S(1)} %get-tuple-element.148.refs_1_), custom_call_target="tpu_custom_call" | custom-call | bytes 7000000 | tf_op jit(solution)/shard_map/pallas_call | solution.py:63
  15.0 3.1 %shard_map.149 = (f32[11,136,256]{2,1,0:T(8,128)}, f32[16,4,128]{2,1,0:T(4,128)S(1)}, f32[21,4,128]{2,1,0:T(4,128)S(1)}, f32[53,4,128]{2,1,0:T(4,128)S(1)}, f32[...) custom-call(s32[9]{0:T(128)S(4)} %get-tuple-element.136.refs_0_, ...), custom_call_target="tpu_custom_call", output_to_operand_aliasing={{5}: (10, {}), {6}: (5, {})} | custom-call | bytes 24500000 | tf_op jit(solution)/shard_map/pallas_call | solution.py:63
  18.0 2.4 %collective-permute-start.7 = (f32[53,4,128]{2,1,0:T(4,128)S(1)}, f32[53,4,128]{2,1,0:T(4,128)S(1)}, u32[]{:S(2)}, u32[]{:S(2)}) collective-permute-start(f32[53,4,128]{2,1,0:T(4,128)S(1)} %get-tuple-element.159.refs_10_), channel_id=1, source_target_pairs={{0,4},{4,0},{8,12},{12,8},{16,20},{20,16},{24,28},{28,24},{1,5},{5... | collective-permute-start | bytes 325640 | tf_op jit(solution)/shard_map/ppermute | solution.py:652
  21.3 1.6 %shard_map.150.refs_2_ = bf16[8,256,512]{2,1,0:T(8,128)(2,1)S(1)} custom-call(f32[16,4,128,128]{3,2,1,0:T(8,128)} %refs_0_.5, f32[16,4,128]{2,1,0:T(4,128)S(1)} %get-tuple-element.156.refs_1_.refs_4_), custom_call_target="tpu_custom_call" | custom-call | bytes 7000000 | tf_op jit(solution)/shard_map/pallas_call | solution.py:63
  23.1 1.9 %collective-permute-done.8.refs_8_.refs_4_ = f32[53,4,128]{2,1,0:T(4,128)S(1)} collective-permute-done((f32[53,4,128]{2,1,0:T(4,128)S(1)}, f32[53,4,128]{2,1,0:T(4,128)S(1)}, u32[]{:S(2)}, u32[]{:S(2)}) %collective-permute-start.8) | collective-permute-done | bytes 108576 | tf_op jit(solution)/shard_map/ppermute | solution.py:646
  29.5 2.5 %collective-permute-done.11.refs_7_.refs_4_ = f32[80,4,128]{2,1,0:T(4,128)S(1)} collective-permute-done((f32[80,4,128]{2,1,0:T(4,128)S(1)}, f32[80,4,128]{2,1,0:T(4,128)S(1)}, u32[]{:S(2)}, u32[]{:S(2)}) %collective-permute-start.11) | collective-permute-done | bytes 163872 | tf_op jit(solution)/shard_map/ppermute | solution.py:652
  31.9 1.7 %collective-permute-done.12.refs_8_.refs_2_ = f32[80,4,128]{2,1,0:T(4,128)S(1)} collective-permute-done((f32[80,4,128]{2,1,0:T(4,128)S(1)}, f32[80,4,128]{2,1,0:T(4,128)S(1)}, u32[]{:S(2)}, u32[]{:S(2)}) %collective-permute-start.12) | collective-permute-done | bytes 163872 | tf_op jit(solution)/shard_map/ppermute | solution.py:646
  35.2 3.4 %collective-permute-start.15 = (f32[16,4,128]{2,1,0:T(4,128)S(1)}, f32[16,4,128]{2,1,0:T(4,128)S(1)}, u32[]{:S(2)}, u32[]{:S(2)}) collective-permute-start(f32[16,4,128]{2,1,0:T(4,128)S(1)} %get-tuple-element.173.refs_2_.refs_6_.refs_0_), channel_id=1, source_target_pairs={{0,4},{4,0},{8,12},{12,8},{16,20},{20,16},{24,28},{28,24},{1,5},{5... | collective-permute-start | bytes 98312 | tf_op jit(solution)/shard_map/ppermute | solution.py:652
  40.5 1.7 %collective-permute-done.16.refs_9_ = f32[16,4,128]{2,1,0:T(4,128)S(1)} collective-permute-done((f32[16,4,128]{2,1,0:T(4,128)S(1)}, f32[16,4,128]{2,1,0:T(4,128)S(1)}, u32[]{:S(2)}, u32[]{:S(2)}) %collective-permute-start.16) | collective-permute-done | bytes 32800 | tf_op jit(solution)/shard_map/ppermute | solution.py:646
  43.8 1.9 %collective-permute-start.19 = (f32[4,4,128]{2,1,0:T(4,128)S(1)}, f32[4,4,128]{2,1,0:T(4,128)S(1)}, u32[]{:S(2)}, u32[]{:S(2)}) collective-permute-start(f32[4,4,128]{2,1,0:T(4,128)S(1)} %get-tuple-element.180.refs_2_.refs_4_), channel_id=1, source_target_pairs={{0,4},{4,0},{8,12},{12,8},{16,20},{20,16},{24,28},{28,24},{1,5},{5... | collective-permute-start | bytes 24584 | tf_op jit(solution)/shard_map/ppermute | solution.py:652
  46.4 2.0 %shard_map.157 = (bf16[8,256,512]{2,1,0:T(8,128)(2,1)}, bf16[8,256,512]{2,1,0:T(8,128)(2,1)}, bf16[8,256,512]{2,1,0:T(8,128)(2,1)S(1)}, f32[16,1,128]{2,1,0:T(1,...) custom-call(bf16[8,256,512]{2,1,0:T(8,128)(2,1)S(1)} %get-tuple-elem, ...), custom_call_target="tpu_custom_call", output_to_operand_aliasing={{2}: (0, {}), {3}: (3, {}), {4}: (4, {}), {5}: (1, {}), {6}... | custom-call | bytes 7000000 | tf_op jit(solution)/shard_map/pallas_call | solution.py:63
  49.2 2.6 %collective-permute-start.24 = (f32[4,4,128]{2,1,0:T(4,128)S(1)}, f32[4,4,128]{2,1,0:T(4,128)S(1)}, u32[]{:S(2)}, u32[]{:S(2)}) collective-permute-start(f32[4,4,128]{2,1,0:T(4,128)S(1)} %get-tuple-element.200.refs_4_), channel_id=1, source_target_pairs={{0,4},{4,0},{8,12},{12,8},{16,20},{20,16},{24,28},{28,24},{1,5},{5... | collective-permute-start | bytes 24584 | tf_op jit(solution)/shard_map/ppermute | solution.py:652
  53.4 1.4 %collective-permute-done.25.refs_7_ = f32[4,4,128]{2,1,0:T(4,128)S(1)} collective-permute-done((f32[4,4,128]{2,1,0:T(4,128)S(1)}, f32[4,4,128]{2,1,0:T(4,128)S(1)}, u32[]{:S(2)}, u32[]{:S(2)}) %collective-permute-start.25) | collective-permute-done | bytes 8224 | tf_op jit(solution)/shard_map/ppermute | solution.py:646
  55.3 1.6 %collective-permute-start.28 = (f32[4,4,128]{2,1,0:T(4,128)S(1)}, f32[4,4,128]{2,1,0:T(4,128)S(1)}, u32[]{:S(2)}, u32[]{:S(2)}) collective-permute-start(f32[4,4,128]{2,1,0:T(4,128)S(1)} %get-tuple-element.210.refs_6_), channel_id=1, source_target_pairs={{0,4},{4,0},{8,12},{12,8},{16,20},{20,16},{24,28},{28,24},{1,5},{5... | collective-permute-start | bytes 24584 | tf_op jit(solution)/shard_map/ppermute | solution.py:652
  60.7 11.1 %all_to_all.5.refs_2_ = f32[32,4,128]{2,1,0:T(4,128)S(1)} all-to-all(f32[32,4,128]{2,1,0:T(4,128)S(1)} %get-tuple-element.219), channel_id=1, replica_groups=mesh['wide'=8,'narrow'=4] {'wide','narrow'}, dimensions={0} | all-to-all | bytes 131072 | tf_op jit(solution)/shard_map/all_to_all | solution.py:914
  71.7 2.2 %shard_map.163 = (f32[4,4,128]{2,1,0:T(4,128)S(1)}, f32[16,1,128]{2,1,0:T(1,128)S(1)}, f32[16,4,128]{2,1,0:T(4,128)S(1)}, f32[16,4,128]{2,1,0:T(4,128)S(1)}, s32...) custom-call(s32[9]{0:T(128)S(4)} %get-tuple-element.136.refs_0_, ...), custom_call_target="tpu_custom_call", output_to_operand_aliasing={{1}: (8, {}), {2}: (9, {}), {3}: (10, {}), {4}: (7, {}), {5... | custom-call | bytes 10500000 | tf_op jit(solution)/shard_map/pallas_call | solution.py:63
  74.1 2.0 %collective-permute-start.32 = (f32[4,4,128]{2,1,0:T(4,128)S(1)}, f32[4,4,128]{2,1,0:T(4,128)S(1)}, u32[]{:S(2)}, u32[]{:S(2)}) collective-permute-start(f32[4,4,128]{2,1,0:T(4,128)S(1)} %get-tuple-element.231.refs_4_), channel_id=1, source_target_pairs={{0,4},{4,0},{8,12},{12,8},{16,20},{20,16},{24,28},{28,24},{1,5},{5... | collective-permute-start | bytes 24584 | tf_op jit(solution)/shard_map/ppermute | solution.py:652
  79.6 2.1 %collective-permute-start.36 = (f32[4,4,128]{2,1,0:T(4,128)S(1)}, f32[4,4,128]{2,1,0:T(4,128)S(1)}, u32[]{:S(2)}, u32[]{:S(2)}) collective-permute-start(f32[4,4,128]{2,1,0:T(4,128)S(1)} %get-tuple-element.240.refs_4_), channel_id=1, source_target_pairs={{0,4},{4,0},{8,12},{12,8},{16,20},{20,16},{24,28},{28,24},{1,5},{5... | collective-permute-start | bytes 24584 | tf_op jit(solution)/shard_map/ppermute | solution.py:652
  85.3 2.2 %collective-permute-start.40 = (f32[4,4,128]{2,1,0:T(4,128)S(1)}, f32[4,4,128]{2,1,0:T(4,128)S(1)}, u32[]{:S(2)}, u32[]{:S(2)}) collective-permute-start(f32[4,4,128]{2,1,0:T(4,128)S(1)} %get-tuple-element.249.refs_6_), channel_id=1, source_target_pairs={{0,4},{4,0},{8,12},{12,8},{16,20},{20,16},{24,28},{28,24},{1,5},{5... | collective-permute-start | bytes 24584 | tf_op jit(solution)/shard_map/ppermute | solution.py:652
  89.1 1.4 %collective-permute-done.41.refs_9_ = f32[4,4,128]{2,1,0:T(4,128)S(1)} collective-permute-done((f32[4,4,128]{2,1,0:T(4,128)S(1)}, f32[4,4,128]{2,1,0:T(4,128)S(1)}, u32[]{:S(2)}, u32[]{:S(2)}) %collective-permute-start.41) | collective-permute-done | bytes 8224 | tf_op jit(solution)/shard_map/ppermute | solution.py:646
  90.6 1.7 %shard_map.166 = (f32[16,4,128]{2,1,0:T(4,128)S(1)}, f32[16,1,128]{2,1,0:T(1,128)S(1)}, f32[16,4,128]{2,1,0:T(4,128)S(1)}, f32[16,4,128]{2,1,0:T(4,128)S(1)}, s3...) custom-call(s32[4,16]{1,0:T(4,128)S(4)} %get-tuple-element.154.refs_, ...), custom_call_target="tpu_custom_call", output_to_operand_aliasing={{1}: (3, {}), {2}: (11, {}), {3}: (4, {}), {4}: (5, {}), {5... | custom-call | bytes 7000000 | tf_op jit(solution)/shard_map/pallas_call | solution.py:63
  92.4 2.6 %collective-permute-start.44 = (f32[16,4,128]{2,1,0:T(4,128)S(1)}, f32[16,4,128]{2,1,0:T(4,128)S(1)}, u32[]{:S(2)}, u32[]{:S(2)}) collective-permute-start(f32[16,4,128]{2,1,0:T(4,128)S(1)} %get-tuple-element.255.refs_2_.refs_5_), channel_id=1, source_target_pairs={{0,4},{4,0},{8,12},{12,8},{16,20},{20,16},{24,28},{28,24},{1,5},{5... | collective-permute-start | bytes 98312 | tf_op jit(solution)/shard_map/ppermute | solution.py:652
  99.4 2.1 %collective-permute-start.48 = (f32[16,4,128]{2,1,0:T(4,128)S(1)}, f32[16,4,128]{2,1,0:T(4,128)S(1)}, u32[]{:S(2)}, u32[]{:S(2)}) collective-permute-start(f32[16,4,128]{2,1,0:T(4,128)S(1)} %get-tuple-element.260.refs_2_.refs_7_), channel_id=1, source_target_pairs={{0,4},{4,0},{8,12},{12,8},{16,20},{20,16},{24,28},{28,24},{1,5},{5... | collective-permute-start | bytes 98312 | tf_op jit(solution)/shard_map/ppermute | solution.py:652
  104.8 1.7 %shard_map.170 = (f32[4,128,128]{2,1,0:T(8,128)S(1)}, f32[4,4,128]{2,1,0:T(4,128)S(1)}, f32[4,4,128]{2,1,0:T(4,128)S(1)}, f32[16,1,128]{2,1,0:T(1,128)S(1)}, f32...) custom-call(s32[9]{0:T(128)S(4)} %get-tuple-element.136.refs_0_, ...), custom_call_target="tpu_custom_call", output_to_operand_aliasing={{3}: (4, {}), {4}: (5, {}), {5}: (1, {}), {6}: (2, {})} | custom-call | bytes 10500000 | tf_op jit(solution)/shard_map/pallas_call | solution.py:63
  107.6 2.0 %collective-permute-done.51.refs_2_ = f32[4,4,128]{2,1,0:T(4,128)S(1)} collective-permute-done((f32[4,4,128]{2,1,0:T(4,128)S(1)}, f32[4,4,128]{2,1,0:T(4,128)S(1)}, u32[]{:S(2)}, u32[]{:S(2)}) %collective-permute-start.51) | collective-permute-done | bytes 8224 | tf_op jit(solution)/shard_map/ppermute | solution.py:646
  109.9 2.9 %collective-permute-start.54 = (f32[4,4,256]{2,1,0:T(4,128)S(1)}, f32[4,4,256]{2,1,0:T(4,128)S(1)}, u32[]{:S(2)}, u32[]{:S(2)}) collective-permute-start(f32[4,4,256]{2,1,0:T(4,128)S(1)} %get-tuple-element.266), channel_id=1, source_target_pairs={{0,4},{4,0},{8,12},{12,8},{16,20},{20,16},{24,28},{28,24},{1,5},{5... | collective-permute-start | bytes 49160 | tf_op jit(solution)/shard_map/ppermute | solution.py:652
  112.8 1.7 %collective-permute-done.54.refs_4_ = f32[4,4,256]{2,1,0:T(4,128)S(1)} collective-permute-done((f32[4,4,256]{2,1,0:T(4,128)S(1)}, f32[4,4,256]{2,1,0:T(4,128)S(1)}, u32[]{:S(2)}, u32[]{:S(2)}) %collective-permute-start.54) | collective-permute-done | bytes 16416 | tf_op jit(solution)/shard_map/ppermute | solution.py:652
  114.5 2.3 %shard_map.172 = f32[4,128,128]{2,1,0:T(8,128)} custom-call(s32[9]{0:T(128)S(4)} %get-tuple-element.136.refs_0_, f32[11,136,256]{2,1,0:T(8,128)S(1)} %copy-done.2, f32[4,128,256]{2,1,0:T(8,128)S(1)} %get-tuple-element.264.refs_2_, f32[4,4,256]{2,1,0:T(4,128)S(1)} %collective-permute-done.53.refs_3_, f32[4,4,256]{2,1,0:T(4,128)S(1)} %collective-permute-done.54.refs_4_), custom_call_target="tpu_custom_call" | custom-call | bytes 7000000 | tf_op jit(solution)/shard_map/pallas_call | solution.py:63
  (122 shorter events, 39.0 us)
Async XLA Ops:
  1.2 8.2 %collective-permute-start.4 = (f32[16,4,128]{2,1,0:T(4,128)S(1)}, f32[16,4,128]{2,1,0:T(4,128)S(1)}, u32[]{:S(2)}, u32[]{:S(2)}) collective-permute-start(f32[16,4,128]{2,1,0:T(4,128)S(1)} %get-tuple-element.151), channel_id=1, source_target_pairs={{0,16},{4,20},{8,24},{12,28},{16,0},{20,4},{24,8},{28,12},{1,17},{... | collective-permute-start | bytes 98312 | tf_op jit(solution)/shard_map/ppermute | solution.py:698
  5.3 3.9 %collective-permute-start = (f32[6,4,128]{2,1,0:T(4,128)S(1)}, f32[6,4,128]{2,1,0:T(4,128)S(1)}, u32[]{:S(2)}, u32[]{:S(2)}) collective-permute-start(f32[6,4,128]{2,1,0:T(4,128)S(1)} %get-tuple-element.138), channel_id=1, source_target_pairs={{1,2},{2,1},{0,3},{3,0},{5,6},{6,5},{4,7},{7,4},{9,10},{10,9},{8,1... | collective-permute-start | bytes 36872 | tf_op jit(solution)/shard_map/ppermute | solution.py:646
  6.0 3.2 %collective-permute-start.1 = (f32[6,4,128]{2,1,0:T(4,128)S(1)}, f32[6,4,128]{2,1,0:T(4,128)S(1)}, u32[]{:S(2)}, u32[]{:S(2)}) collective-permute-start(f32[6,4,128]{2,1,0:T(4,128)S(1)} %get-tuple-element.145), channel_id=1, source_target_pairs={{0,1},{1,0},{2,3},{3,2},{4,5},{5,4},{6,7},{7,6},{8,9},{9,8},{10,11... | collective-permute-start | bytes 36872 | tf_op jit(solution)/shard_map/ppermute | solution.py:647
  9.4 5.6 %collective-permute-start.5 = (f32[32,4,128]{2,1,0:T(4,128)S(1)}, f32[32,4,128]{2,1,0:T(4,128)S(1)}, u32[]{:S(2)}, u32[]{:S(2)}) collective-permute-start(f32[32,4,128]{2,1,0:T(4,128)S(1)} %pad_maximum_fusion.refs_8_), channel_id=1, source_target_pairs={{0,8},{4,12},{8,0},{12,4},{16,24},{20,28},{24,16},{28,20},{1,9},{5... | collective-permute-start | bytes 196616 | tf_op jit(solution)/shard_map/ppermute | solution.py:698
  11.0 3.6 %collective-permute-start.2 = (f32[6,4,256]{2,1,0:T(4,128)S(1)}, f32[6,4,256]{2,1,0:T(4,128)S(1)}, u32[]{:S(2)}, u32[]{:S(2)}) collective-permute-start(f32[6,4,256]{2,1,0:T(4,128)S(1)} %get-tuple-element.147), channel_id=1, source_target_pairs={{4,8},{5,9},{6,10},{7,11},{8,4},{9,5},{10,6},{11,7},{12,16},{13,17... | collective-permute-start | bytes 73736 | tf_op jit(solution)/shard_map/ppermute | solution.py:651
  11.0 3.9 %collective-permute-start.3 = (f32[6,4,256]{2,1,0:T(4,128)S(1)}, f32[6,4,256]{2,1,0:T(4,128)S(1)}, u32[]{:S(2)}, u32[]{:S(2)}) collective-permute-start(f32[6,4,256]{2,1,0:T(4,128)S(1)} %get-tuple-element.148.refs_1_), channel_id=1, source_target_pairs={{0,4},{4,0},{8,12},{12,8},{16,20},{20,16},{24,28},{28,24},{1,5},{5... | collective-permute-start | bytes 73736 | tf_op jit(solution)/shard_map/ppermute | solution.py:652
  18.0 5.1 %collective-permute-start.7 = (f32[53,4,128]{2,1,0:T(4,128)S(1)}, f32[53,4,128]{2,1,0:T(4,128)S(1)}, u32[]{:S(2)}, u32[]{:S(2)}) collective-permute-start(f32[53,4,128]{2,1,0:T(4,128)S(1)} %get-tuple-element.159.refs_10_), channel_id=1, source_target_pairs={{0,4},{4,0},{8,12},{12,8},{16,20},{20,16},{24,28},{28,24},{1,5},{5... | collective-permute-start | bytes 325640 | tf_op jit(solution)/shard_map/ppermute | solution.py:652
  20.4 4.6 %collective-permute-start.8 = (f32[53,4,128]{2,1,0:T(4,128)S(1)}, f32[53,4,128]{2,1,0:T(4,128)S(1)}, u32[]{:S(2)}, u32[]{:S(2)}) collective-permute-start(f32[53,4,128]{2,1,0:T(4,128)S(1)} %get-tuple-element.160.refs_11_), channel_id=1, source_target_pairs={{1,2},{2,1},{0,3},{3,0},{5,6},{6,5},{4,7},{7,4},{9,10},{10,9},{8,1... | collective-permute-start | bytes 325640 | tf_op jit(solution)/shard_map/ppermute | solution.py:646
  26.3 5.6 %collective-permute-start.11 = (f32[80,4,128]{2,1,0:T(4,128)S(1)}, f32[80,4,128]{2,1,0:T(4,128)S(1)}, u32[]{:S(2)}, u32[]{:S(2)}) collective-permute-start(f32[80,4,128]{2,1,0:T(4,128)S(1)} %get-tuple-element.166.refs_3_), channel_id=1, source_target_pairs={{0,4},{4,0},{8,12},{12,8},{16,20},{20,16},{24,28},{28,24},{1,5},{5... | collective-permute-start | bytes 491528 | tf_op jit(solution)/shard_map/ppermute | solution.py:652
  27.4 6.3 %collective-permute-start.12 = (f32[80,4,128]{2,1,0:T(4,128)S(1)}, f32[80,4,128]{2,1,0:T(4,128)S(1)}, u32[]{:S(2)}, u32[]{:S(2)}) collective-permute-start(f32[80,4,128]{2,1,0:T(4,128)S(1)} %get-tuple-element.167.refs_1_), channel_id=1, source_target_pairs={{1,2},{2,1},{0,3},{3,0},{5,6},{6,5},{4,7},{7,4},{9,10},{10,9},{8,1... | collective-permute-start | bytes 491528 | tf_op jit(solution)/shard_map/ppermute | solution.py:646
  34.6 14.5 %collective-permute-start.22 = (f32[256,4,128]{2,1,0:T(4,128)S(1)}, f32[256,4,128]{2,1,0:T(4,128)S(1)}, u32[]{:S(2)}, u32[]{:S(2)}) collective-permute-start(f32[256,4,128]{2,1,0:T(4,128)S(1)} %shard_map.159.refs_1_), channel_id=1, source_target_pairs={{0,1},{1,0},{2,3},{3,2},{4,5},{5,4},{6,7},{7,6},{8,9},{9,8},{10,11... | collective-permute-start | bytes 1572872 | tf_op jit(solution)/shard_map/ppermute | solution.py:856
  34.7 5.1 %collective-permute-start.14 = (f32[16,4,128]{2,1,0:T(4,128)S(1)}, f32[16,4,128]{2,1,0:T(4,128)S(1)}, u32[]{:S(2)}, u32[]{:S(2)}) collective-permute-start(f32[16,4,128]{2,1,0:T(4,128)S(1)} %get-tuple-element.173.refs_2_.refs_6_.refs_0_), channel_id=1, source_target_pairs={{4,8},{5,9},{6,10},{7,11},{8,4},{9,5},{10,6},{11,7},{12,16},{13,17... | collective-permute-start | bytes 98312 | tf_op jit(solution)/shard_map/ppermute | solution.py:651
  35.2 5.3 %collective-permute-start.15 = (f32[16,4,128]{2,1,0:T(4,128)S(1)}, f32[16,4,128]{2,1,0:T(4,128)S(1)}, u32[]{:S(2)}, u32[]{:S(2)}) collective-permute-start(f32[16,4,128]{2,1,0:T(4,128)S(1)} %get-tuple-element.173.refs_2_.refs_6_.refs_0_), channel_id=1, source_target_pairs={{0,4},{4,0},{8,12},{12,8},{16,20},{20,16},{24,28},{28,24},{1,5},{5... | collective-permute-start | bytes 98312 | tf_op jit(solution)/shard_map/ppermute | solution.py:652
  38.6 3.6 %collective-permute-start.16 = (f32[16,4,128]{2,1,0:T(4,128)S(1)}, f32[16,4,128]{2,1,0:T(4,128)S(1)}, u32[]{:S(2)}, u32[]{:S(2)}) collective-permute-start(f32[16,4,128]{2,1,0:T(4,128)S(1)} %get-tuple-element.173.refs_2_.refs_6_.refs_0_), channel_id=1, source_target_pairs={{1,2},{2,1},{0,3},{3,0},{5,6},{6,5},{4,7},{7,4},{9,10},{10,9},{8,1... | collective-permute-start | bytes 98312 | tf_op jit(solution)/shard_map/ppermute | solution.py:646
  38.8 3.5 %collective-permute-start.17 = (f32[16,4,128]{2,1,0:T(4,128)S(1)}, f32[16,4,128]{2,1,0:T(4,128)S(1)}, u32[]{:S(2)}, u32[]{:S(2)}) collective-permute-start(f32[16,4,128]{2,1,0:T(4,128)S(1)} %get-tuple-element.173.refs_2_.refs_6_.refs_0_), channel_id=1, source_target_pairs={{0,1},{1,0},{2,3},{3,2},{4,5},{5,4},{6,7},{7,6},{8,9},{9,8},{10,11... | collective-permute-start | bytes 98312 | tf_op jit(solution)/shard_map/ppermute | solution.py:647
  43.6 4.8 %collective-permute-start.18 = (f32[4,4,128]{2,1,0:T(4,128)S(1)}, f32[4,4,128]{2,1,0:T(4,128)S(1)}, u32[]{:S(2)}, u32[]{:S(2)}) collective-permute-start(f32[4,4,128]{2,1,0:T(4,128)S(1)} %get-tuple-element.180.refs_2_.refs_4_), channel_id=1, source_target_pairs={{4,8},{5,9},{6,10},{7,11},{8,4},{9,5},{10,6},{11,7},{12,16},{13,17... | collective-permute-start | bytes 24584 | tf_op jit(solution)/shard_map/ppermute | solution.py:651
  43.8 4.7 %collective-permute-start.19 = (f32[4,4,128]{2,1,0:T(4,128)S(1)}, f32[4,4,128]{2,1,0:T(4,128)S(1)}, u32[]{:S(2)}, u32[]{:S(2)}) collective-permute-start(f32[4,4,128]{2,1,0:T(4,128)S(1)} %get-tuple-element.180.refs_2_.refs_4_), channel_id=1, source_target_pairs={{0,4},{4,0},{8,12},{12,8},{16,20},{20,16},{24,28},{28,24},{1,5},{5... | collective-permute-start | bytes 24584 | tf_op jit(solution)/shard_map/ppermute | solution.py:652
  49.2 4.1 %collective-permute-start.23 = (f32[4,4,128]{2,1,0:T(4,128)S(1)}, f32[4,4,128]{2,1,0:T(4,128)S(1)}, u32[]{:S(2)}, u32[]{:S(2)}) collective-permute-start(f32[4,4,128]{2,1,0:T(4,128)S(1)} %get-tuple-element.200.refs_4_), channel_id=1, source_target_pairs={{4,8},{5,9},{6,10},{7,11},{8,4},{9,5},{10,6},{11,7},{12,16},{13,17... | collective-permute-start | bytes 24584 | tf_op jit(solution)/shard_map/ppermute | solution.py:651
  49.2 4.2 %collective-permute-start.24 = (f32[4,4,128]{2,1,0:T(4,128)S(1)}, f32[4,4,128]{2,1,0:T(4,128)S(1)}, u32[]{:S(2)}, u32[]{:S(2)}) collective-permute-start(f32[4,4,128]{2,1,0:T(4,128)S(1)} %get-tuple-element.200.refs_4_), channel_id=1, source_target_pairs={{0,4},{4,0},{8,12},{12,8},{16,20},{20,16},{24,28},{28,24},{1,5},{5... | collective-permute-start | bytes 24584 | tf_op jit(solution)/shard_map/ppermute | solution.py:652
  55.3 3.7 %collective-permute-start.28 = (f32[4,4,128]{2,1,0:T(4,128)S(1)}, f32[4,4,128]{2,1,0:T(4,128)S(1)}, u32[]{:S(2)}, u32[]{:S(2)}) collective-permute-start(f32[4,4,128]{2,1,0:T(4,128)S(1)} %get-tuple-element.210.refs_6_), channel_id=1, source_target_pairs={{0,4},{4,0},{8,12},{12,8},{16,20},{20,16},{24,28},{28,24},{1,5},{5... | collective-permute-start | bytes 24584 | tf_op jit(solution)/shard_map/ppermute | solution.py:652
  74.1 3.7 %collective-permute-start.32 = (f32[4,4,128]{2,1,0:T(4,128)S(1)}, f32[4,4,128]{2,1,0:T(4,128)S(1)}, u32[]{:S(2)}, u32[]{:S(2)}) collective-permute-start(f32[4,4,128]{2,1,0:T(4,128)S(1)} %get-tuple-element.231.refs_4_), channel_id=1, source_target_pairs={{0,4},{4,0},{8,12},{12,8},{16,20},{20,16},{24,28},{28,24},{1,5},{5... | collective-permute-start | bytes 24584 | tf_op jit(solution)/shard_map/ppermute | solution.py:652
  79.6 3.7 %collective-permute-start.36 = (f32[4,4,128]{2,1,0:T(4,128)S(1)}, f32[4,4,128]{2,1,0:T(4,128)S(1)}, u32[]{:S(2)}, u32[]{:S(2)}) collective-permute-start(f32[4,4,128]{2,1,0:T(4,128)S(1)} %get-tuple-element.240.refs_4_), channel_id=1, source_target_pairs={{0,4},{4,0},{8,12},{12,8},{16,20},{20,16},{24,28},{28,24},{1,5},{5... | collective-permute-start | bytes 24584 | tf_op jit(solution)/shard_map/ppermute | solution.py:652
  85.3 3.9 %collective-permute-start.40 = (f32[4,4,128]{2,1,0:T(4,128)S(1)}, f32[4,4,128]{2,1,0:T(4,128)S(1)}, u32[]{:S(2)}, u32[]{:S(2)}) collective-permute-start(f32[4,4,128]{2,1,0:T(4,128)S(1)} %get-tuple-element.249.refs_6_), channel_id=1, source_target_pairs={{0,4},{4,0},{8,12},{12,8},{16,20},{20,16},{24,28},{28,24},{1,5},{5... | collective-permute-start | bytes 24584 | tf_op jit(solution)/shard_map/ppermute | solution.py:652
  92.3 3.9 %collective-permute-start.43 = (f32[16,4,128]{2,1,0:T(4,128)S(1)}, f32[16,4,128]{2,1,0:T(4,128)S(1)}, u32[]{:S(2)}, u32[]{:S(2)}) collective-permute-start(f32[16,4,128]{2,1,0:T(4,128)S(1)} %get-tuple-element.255.refs_2_.refs_5_), channel_id=1, source_target_pairs={{4,8},{5,9},{6,10},{7,11},{8,4},{9,5},{10,6},{11,7},{12,16},{13,17... | collective-permute-start | bytes 98312 | tf_op jit(solution)/shard_map/ppermute | solution.py:651
  92.4 4.5 %collective-permute-start.44 = (f32[16,4,128]{2,1,0:T(4,128)S(1)}, f32[16,4,128]{2,1,0:T(4,128)S(1)}, u32[]{:S(2)}, u32[]{:S(2)}) collective-permute-start(f32[16,4,128]{2,1,0:T(4,128)S(1)} %get-tuple-element.255.refs_2_.refs_5_), channel_id=1, source_target_pairs={{0,4},{4,0},{8,12},{12,8},{16,20},{20,16},{24,28},{28,24},{1,5},{5... | collective-permute-start | bytes 98312 | tf_op jit(solution)/shard_map/ppermute | solution.py:652
  95.0 3.3 %collective-permute-start.45 = (f32[16,4,128]{2,1,0:T(4,128)S(1)}, f32[16,4,128]{2,1,0:T(4,128)S(1)}, u32[]{:S(2)}, u32[]{:S(2)}) collective-permute-start(f32[16,4,128]{2,1,0:T(4,128)S(1)} %get-tuple-element.255.refs_2_.refs_5_), channel_id=1, source_target_pairs={{1,2},{2,1},{0,3},{3,0},{5,6},{6,5},{4,7},{7,4},{9,10},{10,9},{8,1... | collective-permute-start | bytes 98312 | tf_op jit(solution)/shard_map/ppermute | solution.py:646
  95.0 3.3 %collective-permute-start.46 = (f32[16,4,128]{2,1,0:T(4,128)S(1)}, f32[16,4,128]{2,1,0:T(4,128)S(1)}, u32[]{:S(2)}, u32[]{:S(2)}) collective-permute-start(f32[16,4,128]{2,1,0:T(4,128)S(1)} %get-tuple-element.255.refs_2_.refs_5_), channel_id=1, source_target_pairs={{0,1},{1,0},{2,3},{3,2},{4,5},{5,4},{6,7},{7,6},{8,9},{9,8},{10,11... | collective-permute-start | bytes 98312 | tf_op jit(solution)/shard_map/ppermute | solution.py:647
  99.3 3.5 %collective-permute-start.47 = (f32[16,4,128]{2,1,0:T(4,128)S(1)}, f32[16,4,128]{2,1,0:T(4,128)S(1)}, u32[]{:S(2)}, u32[]{:S(2)}) collective-permute-start(f32[16,4,128]{2,1,0:T(4,128)S(1)} %get-tuple-element.260.refs_2_.refs_7_), channel_id=1, source_target_pairs={{4,8},{5,9},{6,10},{7,11},{8,4},{9,5},{10,6},{11,7},{12,16},{13,17... | collective-permute-start | bytes 98312 | tf_op jit(solution)/shard_map/ppermute | solution.py:651
  99.4 4.0 %collective-permute-start.48 = (f32[16,4,128]{2,1,0:T(4,128)S(1)}, f32[16,4,128]{2,1,0:T(4,128)S(1)}, u32[]{:S(2)}, u32[]{:S(2)}) collective-permute-start(f32[16,4,128]{2,1,0:T(4,128)S(1)} %get-tuple-element.260.refs_2_.refs_7_), channel_id=1, source_target_pairs={{0,4},{4,0},{8,12},{12,8},{16,20},{20,16},{24,28},{28,24},{1,5},{5... | collective-permute-start | bytes 98312 | tf_op jit(solution)/shard_map/ppermute | solution.py:652
  101.4 3.3 %collective-permute-start.49 = (f32[16,4,128]{2,1,0:T(4,128)S(1)}, f32[16,4,128]{2,1,0:T(4,128)S(1)}, u32[]{:S(2)}, u32[]{:S(2)}) collective-permute-start(f32[16,4,128]{2,1,0:T(4,128)S(1)} %get-tuple-element.260.refs_2_.refs_7_), channel_id=1, source_target_pairs={{1,2},{2,1},{0,3},{3,0},{5,6},{6,5},{4,7},{7,4},{9,10},{10,9},{8,1... | collective-permute-start | bytes 98312 | tf_op jit(solution)/shard_map/ppermute | solution.py:646
  101.4 3.3 %collective-permute-start.50 = (f32[16,4,128]{2,1,0:T(4,128)S(1)}, f32[16,4,128]{2,1,0:T(4,128)S(1)}, u32[]{:S(2)}, u32[]{:S(2)}) collective-permute-start(f32[16,4,128]{2,1,0:T(4,128)S(1)} %get-tuple-element.260.refs_2_.refs_7_), channel_id=1, source_target_pairs={{0,1},{1,0},{2,3},{3,2},{4,5},{5,4},{6,7},{7,6},{8,9},{9,8},{10,11... | collective-permute-start | bytes 98312 | tf_op jit(solution)/shard_map/ppermute | solution.py:647
  109.9 4.6 %collective-permute-start.54 = (f32[4,4,256]{2,1,0:T(4,128)S(1)}, f32[4,4,256]{2,1,0:T(4,128)S(1)}, u32[]{:S(2)}, u32[]{:S(2)}) collective-permute-start(f32[4,4,256]{2,1,0:T(4,128)S(1)} %get-tuple-element.266), channel_id=1, source_target_pairs={{0,4},{4,0},{8,12},{12,8},{16,20},{20,16},{24,28},{28,24},{1,5},{5... | collective-permute-start | bytes 49160 | tf_op jit(solution)/shard_map/ppermute | solution.py:652
  (30 other events, 134.3 us)

commit v7 on v6

--- a/solution.py
+++ b/solution.py
@@ -266,13 +266,27 @@
         out[r] = own[r] + JACOBI * (b[r] - ax) / d[r]
 
 
-def smooth_ride_kernel(first, idx, t, d, b, own, o1, o2, o3, o4, sent_w, sent_n, out, out_w, out_n, xs):
+def smooth_ride_kernel(span, idx, t, d, b, own, o1, o2, o3, o4, maps, out, out_w, out_n, xs):
     smooth_kernel(idx, t, d, b, own, o1, o2, o3, o4, out, xs)
+    at = b.shape[0]
+    out_w[0:at] = out[...]
+    out_n[0:at] = out[...]
+    for ref in maps:
+        for start in range(0, ref.shape[0], 2 * span):
+            out_w[at : at + span] = ref[start : start + span]
+            out_n[at : at + span] = ref[start + span : start + 2 * span]
+            at += span
+
+
+def residual_ride_kernel(
+    idx, t, d, b, own, o1, o2, o3, o4, done, sent_w, sent_n, left, scaled, out_w, out_n, xs
+):
+    residual_kernel(idx, t, d, b, own, o1, o2, o3, o4, left, scaled, xs, done)
     count = b.shape[0]
-    out_w[0:count] = out[...]
-    out_n[0:count] = out[...]
-    ride(out_n, count, ((sent_w, first), (o2, first)))
-    ride(out_w, count, ((sent_n, first), (o3, first)))
+    out_w[0:count] = scaled[...]
+    out_n[0:count] = scaled[...]
+    ride(out_n, count, ((sent_w, count), (o2, count)))
+    ride(out_w, count, ((sent_n, count), (o3, count)))
 
 
 def residual_more_kernel(idx, t, d, b, own, o1, o2, o3, o4, done, left, scaled, xs):
@@ -517,7 +531,7 @@
     )
 
 
-def fine_down_kernel(span, flags, ext, o2, o1, groups, d1, near1, near2, maps, far, b1, first, out_w, out_n, q_ref, keep, sem):
+def fine_down_kernel(flags, ext, o2, o1, groups, d1, near1, near2, far, b1, first, q_ref, keep, sem):
     cols = ext.shape[0] - 2
     rows = ext.shape[1]
     e = with_rows(flags, ext[cols], o1, o2, cols)
@@ -576,14 +590,6 @@
         groups += [row, pltpu.roll(row, LANES // 2, 1)]
     for i, group in enumerate(groups):
         first[count + i // cols, i % cols : i % cols + 1, :] = group.astype(F32)
-    out_w[0 : first.shape[0]] = first[...]
-    out_n[0 : first.shape[0]] = first[...]
-    at = first.shape[0]
-    for ref in maps:
-        for start in range(0, ref.shape[0], 2 * span):
-            out_w[at : at + span] = ref[start : start + span]
-            out_n[at : at + span] = ref[start + span : start + 2 * span]
-            at += span
     copy.wait()
 
 
@@ -760,7 +766,7 @@
         (flags, fields, o2, o1),
         specs=[SMEM] + [VMEM] * 3,
     )
-    while len(done) < len(alone):
+    if alone:
         gather_step(first)
     o2, o1 = exchange_wide(first, second, route)
 
@@ -780,19 +786,17 @@
     hold = {"t1a": tiles1, "d1": d1}
     t1 = ("t1a", "t1b")
     kept = sds((2 * cols + 3, rows + PAD, 2 * LANES))
-    maps_rows = sum(x.shape[0] for x in held)
     x1_rows = count1 + more
-    riding = sds((x1_rows + maps_rows // 2, cols, LANES))
-    keep, b1, x1, x1_w, x1_n = call(
-        functools.partial(fine_down_kernel, share // cols),
-        [kept, field1, sds((x1_rows, cols, LANES)), riding, riding],
-        (flags, ext, o2, o1, fine_groups, "d1", groups1, groups2, tuple(held)),
+    keep, b1, x1 = call(
+        fine_down_kernel,
+        [kept, field1, sds((x1_rows, cols, LANES))],
+        (flags, ext, o2, o1, fine_groups, "d1", groups1, groups2),
         scratch=[
             pltpu.VMEM((2 * cols, rows, LANES), F32),
             pltpu.VMEM(kept.shape, F32),
             pltpu.SemaphoreType.DMA((1,)),
         ],
-        specs=[SMEM] + [VMEM] * 8,
+        specs=[SMEM] + [VMEM] * 7,
         mib=16,
         us=7,
         hold=hold,
@@ -816,15 +820,18 @@
         kernel = smooth_more_kernel if level == 1 else smooth_kernel
         return call(kernel, like, ins, xs, lead + [VMEM] * (len(ins) - 1), hold=hold), near
 
-    near = exchange(x1, route, wide=x1_w, second=x1_n)
+    while len(done) < len(alone):
+        gather_step(x1)
+    near = exchange(x1, route)
     hold["t1b"] = split_half(1, b1)
-    riding = sds((count1 + maps_rows, cols, LANES))
+    maps_rows = sum(x.shape[0] for x in held)
+    riding = sds((count1 + maps_rows // 2, cols, LANES))
     x2, x2_w, x2_n = call(
-        functools.partial(smooth_ride_kernel, x1_rows),
+        functools.partial(smooth_ride_kernel, share // cols),
         [field1, riding, riding],
-        (idx1, t1, "d1", "b1", x1, *near, x1_w, x1_n),
+        (idx1, t1, "d1", "b1", x1, *near, tuple(held)),
         xs1,
-        lead + [VMEM] * 10,
+        lead + [VMEM] * 9,
         hold=hold,
     )
     groups = call(
@@ -835,25 +842,18 @@
         us=1,
     )
     near = exchange(x2, route, wide=x2_w, second=x2_n)
-    maps = (x2_n, near[2], x2_w, near[1])
     hold |= {"x2": x2, "groups": groups, "d2": d2}
-    left, scaled = call(
-        residual_more_kernel,
-        [field1, field1],
-        (idx1, t1, "d1", "b1", "x2", *near, own_part(x2)),
+    riding = sds((count1 + maps_rows, cols, LANES))
+    left, scaled, scaled_w, scaled_n = call(
+        residual_ride_kernel,
+        [field1, field1, riding, riding],
+        (idx1, t1, "d1", "b1", "x2", *near, own_part(x2), x2_w, x2_n),
         xs1,
-        lead + [VMEM] * 9,
-        hold=hold,
-    )
-    near = exchange(scaled, route)
-    bundle = call(
-        functools.partial(bundle_kernel, count1),
-        sds((4 * maps_rows, cols, LANES)),
-        (scaled, *maps),
-        specs=[VMEM] * 5,
-        us=0.5,
-    )
-    maps = (bundle, lax.ppermute(bundle, "narrow", route[0]))
+        lead + [VMEM] * 11,
+        hold=hold,
+    )
+    near = exchange(scaled, route, wide=scaled_w, second=scaled_n)
+    maps = (scaled_n, near[2], scaled_w, near[1])
     b2, y1 = call(
         restrict_one_kernel,
         [field2, field2],
@@ -864,6 +864,14 @@
     )
 
     near = exchange(y1, route)
+    bundle = call(
+        functools.partial(bundle_kernel, count1),
+        sds((4 * maps_rows, cols, LANES)),
+        (y1, *maps),
+        specs=[VMEM] * 5,
+        us=0.5,
+    )
+    maps = (bundle, lax.ppermute(bundle, "narrow", route[0]))
     tiles1 = call(
         store_kernel,
         [split, split],
@@ -878,8 +886,19 @@
     y2 = call(
         smooth_kernel, field2, (idx2, ("t2",), "d2", "b2", y1, *near), xs2, lead + [VMEM] * 8, hold=hold
     )
-    maps, y2 = lax.optimization_barrier((maps, y2))
     near = exchange(y2, route)
+    hold["y2"] = y2
+    left, scaled = call(
+        residual_kernel,
+        [field2, field2],
+        (idx2, ("t2",), "d2", "b2", "y2", *near),
+        xs2,
+        lead + [VMEM] * 8,
+        us=1,
+        hold=hold,
+    )
+    maps, scaled = lax.optimization_barrier((maps, scaled))
+    near = exchange(scaled, route)
     chain_shape = sds((wide, 2, 2 * LANES, LANES), BF16)
     big = wide > 16
     chain = call(
@@ -893,20 +912,10 @@
     )
     if not big:
         hold["chain"] = chain
-    hold["y2"] = y2
-    left, scaled = call(
-        residual_kernel,
-        [field2, field2],
-        (idx2, ("t2",), "d2", "b2", "y2", *near),
-        xs2,
-        lead + [VMEM] * 8,
-        us=1,
-        hold=hold,
-    )
     out3 = call(
         restrict_two_kernel,
         sds((wide * narrow, cols, LANES)),
-        (flags, idx2, ("t2",), left, "groups", chain_gain, scaled, *exchange(scaled, route)),
+        (flags, idx2, ("t2",), left, "groups", chain_gain, scaled, *near),
         xs2,
         [SMEM, SMEM] + [VMEM] * 9,
         hold=hold,

time: 117 us -> 116 us (level)
    ppermute x13, waiting for transfers between devices: 17.1 us -> 14.9 us  [exchange_narrow(): second = lax.ppermute(second, 'narrow', route[1])]
    ppermute x2, starting transfers between devices: 5.74 us -> 4.27 us  [swap(): lax.ppermute(x, axis, [(i, i ^ step) for i in range(lax.axis_size(axis))])]
  transfers between devices with their start and end apart: 55 -> 55, of which waited for: 26 -> 26; matrix products, arithmetic and copies ran while one was open for 0% -> 0% of each run, Pallas kernels for 10% -> 12%
where the time goes in v7:
time: 116 us; the launch traced here: 115 us
  starting transfers between devices  47.8 us (41%)
  Pallas kernels  28.5 us (25%)
  waiting for transfers between devices  28.3 us (24%)
  blocking collectives  10.3 us (9%)
    ppermute x13, starting transfers between devices, exchange_wide(): return (second, lax.ppermute(first, 'wide', route[2]))  29.8 us
    pallas_call x28, Pallas kernels, call(): pl.pallas_call(inner, out_shape=shapes, in_specs=specs[::ORDER], out_spec...  28.5 us
    ppermute x13, waiting for transfers between devices, exchange_narrow(): second = lax.ppermute(second, 'narrow', route[1])  14.9 us
    ppermute x13, waiting for transfers between devices, exchange_wide(): return (second, lax.ppermute(first, 'wide', route[2]))  11.6 us
    all_to_all x1, blocking collectives, body(): pieces = lax.all_to_all(out3, ('wide', 'narrow'), 0, 0)  10.3 us
    ppermute x13, starting transfers between devices, exchange_narrow(): return (second, lax.ppermute(first, 'narrow', route[0]))  9.21 us
    ppermute x2, starting transfers between devices, swap(): lax.ppermute(x, axis, [(i, i ^ step) for i in range(lax.axis_size(axis))])  4.27 us
    ppermute x13, starting transfers between devices, exchange_wide(): second = lax.ppermute(second, ('wide', 'narrow'), route[3])  2.9 us
  transfers between devices with their start and end apart: 55, of which 26 were waited for; matrix products, arithmetic and copies ran while one was open for 0% of the time, Pallas kernels for 12%

profile of v7, /device:TPU:0, one launch (start us, length us, event | category | flops | bytes accessed | tf_op | source)
XLA Modules:
  0.0 115.5 jit_solution(14504441668502602889)
XLA Ops:
  1.2 4.1 %collective-permute-start.8 = (f32[16,4,128]{2,1,0:T(4,128)S(1)}, f32[16,4,128]{2,1,0:T(4,128)S(1)}, u32[]{:S(2)}, u32[]{:S(2)}) collective-permute-start(f32[16,4,128]{2,1,0:T(4,128)S(1)} %get-tuple-element.156), channel_id=1, source_target_pairs={{0,16},{4,20},{8,24},{12,28},{16,0},{20,4},{24,8},{28,12},{1,17},{... | collective-permute-start | bytes 98312 | tf_op jit(solution)/shard_map/ppermute | solution.py:704
  6.9 2.2 %shard_map.146 = (s32[4,16]{1,0:T(4,128)S(4)}, s32[4,4]{1,0:T(4,128)S(4)}, f32[16,1,128]{2,1,0:T(1,128)S(1)}, bf16[4,256,512]{2,1,0:T(8,128)(2,1)S(1)}, f32[4,1,128]{2,1,0:T(1,128)S(1)}) custom-call(s32[9]{0:T(128)S(4)} %get-tuple-element.135.refs_0_, s32[3,16]{1,0:T(4,128)} %bitcast.8, s32[3,16]{1,0:T(4,128)} %bitcast.9, s32[4,3]{1,0:T(4,128)} %refs_3_.3, ...), custom_call_target="tpu_custom_call" | custom-call | bytes 7000000 | tf_op jit(solution)/shard_map/pallas_call | solution.py:63
  9.4 3.0 %collective-permute-start.3 = (f32[6,4,256]{2,1,0:T(4,128)S(1)}, f32[6,4,256]{2,1,0:T(4,128)S(1)}, u32[]{:S(2)}, u32[]{:S(2)}) collective-permute-start(f32[6,4,256]{2,1,0:T(4,128)S(1)} %get-tuple-element.147.refs_1_), channel_id=1, source_target_pairs={{0,4},{4,0},{8,12},{12,8},{16,20},{20,16},{24,28},{28,24},{1,5},{5... | collective-permute-start | bytes 73736 | tf_op jit(solution)/shard_map/ppermute | solution.py:658
  12.7 1.6 %shard_map.148.refs_8_ = bf16[8,256,512]{2,1,0:T(8,128)(2,1)S(1)} custom-call(f32[16,4,128,128]{3,2,1,0:T(8,128)} %refs_0_.5, f32[6,4,256]{2,1,0:T(4,128)S(1)} %get-tuple-element.147.refs_1_), custom_call_target="tpu_custom_call" | custom-call | bytes 7000000 | tf_op jit(solution)/shard_map/pallas_call | solution.py:63
  14.4 3.1 %shard_map.149 = (f32[11,136,256]{2,1,0:T(8,128)}, f32[16,4,128]{2,1,0:T(4,128)S(1)}, f32[21,4,128]{2,1,0:T(4,128)S(1)}, bf16[8,256,512]{2,1,0:T(8,128)(2,1)S(1)}, f32[16,1,128]{2,1,0:T(1,128)S(1)}) custom-call(s32[9]{0:T(128)S(4)} %get-tuple-element.135.refs_0_, ...), custom_call_target="tpu_custom_call", output_to_operand_aliasing={{3}: (8, {}), {4}: (5, {})} | custom-call | bytes 24500000 | tf_op jit(solution)/shard_map/pallas_call | solution.py:63
  17.5 3.4 %collective-permute-start.5 = (f32[21,4,128]{2,1,0:T(4,128)S(1)}, f32[21,4,128]{2,1,0:T(4,128)S(1)}, u32[]{:S(2)}, u32[]{:S(2)}) collective-permute-start(f32[21,4,128]{2,1,0:T(4,128)S(1)} %get-tuple-element.154.refs_5_.refs_1_), channel_id=1, source_target_pairs={{0,4},{4,0},{8,12},{12,8},{16,20},{20,16},{24,28},{28,24},{1,5},{5... | collective-permute-start | bytes 129032 | tf_op jit(solution)/shard_map/ppermute | solution.py:658
  21.8 1.6 %shard_map.150.refs_2_ = bf16[8,256,512]{2,1,0:T(8,128)(2,1)S(1)} custom-call(f32[16,4,128,128]{3,2,1,0:T(8,128)} %refs_0_.5, f32[16,4,128]{2,1,0:T(4,128)S(1)} %get-tuple-element.152.refs_1_.refs_4_), custom_call_target="tpu_custom_call" | custom-call | bytes 7000000 | tf_op jit(solution)/shard_map/pallas_call | solution.py:63
  28.3 2.0 %collective-permute-done.11.refs_7_ = f32[48,4,128]{2,1,0:T(4,128)S(1)} collective-permute-done((f32[48,4,128]{2,1,0:T(4,128)S(1)}, f32[48,4,128]{2,1,0:T(4,128)S(1)}, u32[]{:S(2)}, u32[]{:S(2)}) %collective-permute-start.11) | collective-permute-done | bytes 98336 | tf_op jit(solution)/shard_map/ppermute | solution.py:658
  31.6 2.5 %collective-permute-start.15 = (f32[80,4,128]{2,1,0:T(4,128)S(1)}, f32[80,4,128]{2,1,0:T(4,128)S(1)}, u32[]{:S(2)}, u32[]{:S(2)}) collective-permute-start(f32[80,4,128]{2,1,0:T(4,128)S(1)} %get-tuple-element.171.refs_3_), channel_id=1, source_target_pairs={{0,4},{4,0},{8,12},{12,8},{16,20},{20,16},{24,28},{28,24},{1,5},{5... | collective-permute-start | bytes 491528 | tf_op jit(solution)/shard_map/ppermute | solution.py:658
  36.1 2.3 %collective-permute-done.15.refs_8_.refs_4_ = f32[80,4,128]{2,1,0:T(4,128)S(1)} collective-permute-done((f32[80,4,128]{2,1,0:T(4,128)S(1)}, f32[80,4,128]{2,1,0:T(4,128)S(1)}, u32[]{:S(2)}, u32[]{:S(2)}) %collective-permute-start.15) | collective-permute-done | bytes 163872 | tf_op jit(solution)/shard_map/ppermute | solution.py:658
  38.4 2.0 %collective-permute-done.16.refs_9_.refs_2_ = f32[80,4,128]{2,1,0:T(4,128)S(1)} collective-permute-done((f32[80,4,128]{2,1,0:T(4,128)S(1)}, f32[80,4,128]{2,1,0:T(4,128)S(1)}, u32[]{:S(2)}, u32[]{:S(2)}) %collective-permute-start.16) | collective-permute-done | bytes 163872 | tf_op jit(solution)/shard_map/ppermute | solution.py:652
  42.5 2.5 %collective-permute-start.19 = (f32[4,4,128]{2,1,0:T(4,128)S(1)}, f32[4,4,128]{2,1,0:T(4,128)S(1)}, u32[]{:S(2)}, u32[]{:S(2)}) collective-permute-start(f32[4,4,128]{2,1,0:T(4,128)S(1)} %get-tuple-element.179.refs_2_.refs_4_.refs_0_), channel_id=1, source_target_pairs={{0,4},{4,0},{8,12},{12,8},{16,20},{20,16},{24,28},{28,24},{1,5},{5... | collective-permute-start | bytes 24584 | tf_op jit(solution)/shard_map/ppermute | solution.py:658
  46.0 2.0 %shard_map.157 = (bf16[8,256,512]{2,1,0:T(8,128)(2,1)}, bf16[8,256,512]{2,1,0:T(8,128)(2,1)}, bf16[8,256,512]{2,1,0:T(8,128)(2,1)S(1)}, f32[16,1,128]{2,1,0:T(1,...) custom-call(bf16[8,256,512]{2,1,0:T(8,128)(2,1)S(1)} %get-tuple-elem, ...), custom_call_target="tpu_custom_call", output_to_operand_aliasing={{2}: (0, {}), {3}: (3, {}), {4}: (4, {}), {5}: (1, {}), {6}... | custom-call | bytes 7000000 | tf_op jit(solution)/shard_map/pallas_call | solution.py:63
  48.7 1.6 %collective-permute-start.23 = (f32[4,4,128]{2,1,0:T(4,128)S(1)}, f32[4,4,128]{2,1,0:T(4,128)S(1)}, u32[]{:S(2)}, u32[]{:S(2)}) collective-permute-start(f32[4,4,128]{2,1,0:T(4,128)S(1)} %get-tuple-element.198.refs_4_), channel_id=1, source_target_pairs={{0,4},{4,0},{8,12},{12,8},{16,20},{20,16},{24,28},{28,24},{1,5},{5... | collective-permute-start | bytes 24584 | tf_op jit(solution)/shard_map/ppermute | solution.py:658
  53.8 2.4 %collective-permute-start.28 = (f32[4,4,128]{2,1,0:T(4,128)S(1)}, f32[4,4,128]{2,1,0:T(4,128)S(1)}, u32[]{:S(2)}, u32[]{:S(2)}) collective-permute-start(f32[4,4,128]{2,1,0:T(4,128)S(1)} %get-tuple-element.207.refs_6_), channel_id=1, source_target_pairs={{0,4},{4,0},{8,12},{12,8},{16,20},{20,16},{24,28},{28,24},{1,5},{5... | collective-permute-start | bytes 24584 | tf_op jit(solution)/shard_map/ppermute | solution.py:658
  57.8 1.4 %collective-permute-done.29.refs_9_ = f32[4,4,128]{2,1,0:T(4,128)S(1)} collective-permute-done((f32[4,4,128]{2,1,0:T(4,128)S(1)}, f32[4,4,128]{2,1,0:T(4,128)S(1)}, u32[]{:S(2)}, u32[]{:S(2)}) %collective-permute-start.29) | collective-permute-done | bytes 8224 | tf_op jit(solution)/shard_map/ppermute | solution.py:652
  60.0 10.3 %all_to_all.5.refs_2_ = f32[32,4,128]{2,1,0:T(4,128)S(1)} all-to-all(f32[32,4,128]{2,1,0:T(4,128)S(1)} %get-tuple-element.217), channel_id=1, replica_groups=mesh['wide'=8,'narrow'=4] {'wide','narrow'}, dimensions={0} | all-to-all | bytes 131072 | tf_op jit(solution)/shard_map/all_to_all | solution.py:923
  70.3 2.2 %shard_map.163 = (f32[4,4,128]{2,1,0:T(4,128)S(1)}, f32[16,1,128]{2,1,0:T(1,128)S(1)}, f32[16,4,128]{2,1,0:T(4,128)S(1)}, f32[16,4,128]{2,1,0:T(4,128)S(1)}, s32...) custom-call(s32[9]{0:T(128)S(4)} %get-tuple-element.135.refs_0_, ...), custom_call_target="tpu_custom_call", output_to_operand_aliasing={{1}: (8, {}), {2}: (9, {}), {3}: (10, {}), {4}: (7, {}), {5... | custom-call | bytes 10500000 | tf_op jit(solution)/shard_map/pallas_call | solution.py:63
  72.7 2.0 %collective-permute-start.32 = (f32[4,4,128]{2,1,0:T(4,128)S(1)}, f32[4,4,128]{2,1,0:T(4,128)S(1)}, u32[]{:S(2)}, u32[]{:S(2)}) collective-permute-start(f32[4,4,128]{2,1,0:T(4,128)S(1)} %get-tuple-element.229.refs_4_), channel_id=1, source_target_pairs={{0,4},{4,0},{8,12},{12,8},{16,20},{20,16},{24,28},{28,24},{1,5},{5... | collective-permute-start | bytes 24584 | tf_op jit(solution)/shard_map/ppermute | solution.py:658
  78.2 2.1 %collective-permute-start.36 = (f32[4,4,128]{2,1,0:T(4,128)S(1)}, f32[4,4,128]{2,1,0:T(4,128)S(1)}, u32[]{:S(2)}, u32[]{:S(2)}) collective-permute-start(f32[4,4,128]{2,1,0:T(4,128)S(1)} %get-tuple-element.238.refs_4_), channel_id=1, source_target_pairs={{0,4},{4,0},{8,12},{12,8},{16,20},{20,16},{24,28},{28,24},{1,5},{5... | collective-permute-start | bytes 24584 | tf_op jit(solution)/shard_map/ppermute | solution.py:658
  82.0 1.4 %collective-permute-done.37.refs_7_ = f32[4,4,128]{2,1,0:T(4,128)S(1)} collective-permute-done((f32[4,4,128]{2,1,0:T(4,128)S(1)}, f32[4,4,128]{2,1,0:T(4,128)S(1)}, u32[]{:S(2)}, u32[]{:S(2)}) %collective-permute-start.37) | collective-permute-done | bytes 8224 | tf_op jit(solution)/shard_map/ppermute | solution.py:652
  83.9 2.2 %collective-permute-start.40 = (f32[4,4,128]{2,1,0:T(4,128)S(1)}, f32[4,4,128]{2,1,0:T(4,128)S(1)}, u32[]{:S(2)}, u32[]{:S(2)}) collective-permute-start(f32[4,4,128]{2,1,0:T(4,128)S(1)} %get-tuple-element.247.refs_6_), channel_id=1, source_target_pairs={{0,4},{4,0},{8,12},{12,8},{16,20},{20,16},{24,28},{28,24},{1,5},{5... | collective-permute-start | bytes 24584 | tf_op jit(solution)/shard_map/ppermute | solution.py:658
  87.7 1.4 %collective-permute-done.41.refs_9_ = f32[4,4,128]{2,1,0:T(4,128)S(1)} collective-permute-done((f32[4,4,128]{2,1,0:T(4,128)S(1)}, f32[4,4,128]{2,1,0:T(4,128)S(1)}, u32[]{:S(2)}, u32[]{:S(2)}) %collective-permute-start.41) | collective-permute-done | bytes 8224 | tf_op jit(solution)/shard_map/ppermute | solution.py:652
  89.2 1.7 %shard_map.166 = (f32[16,4,128]{2,1,0:T(4,128)S(1)}, f32[16,1,128]{2,1,0:T(1,128)S(1)}, f32[16,4,128]{2,1,0:T(4,128)S(1)}, f32[16,4,128]{2,1,0:T(4,128)S(1)}, s3...) custom-call(s32[4,16]{1,0:T(4,128)S(4)} %get-tuple-element.150.refs_, ...), custom_call_target="tpu_custom_call", output_to_operand_aliasing={{1}: (3, {}), {2}: (11, {}), {3}: (4, {}), {4}: (5, {}), {5... | custom-call | bytes 7000000 | tf_op jit(solution)/shard_map/pallas_call | solution.py:63
  91.0 2.6 %collective-permute-start.44 = (f32[16,4,128]{2,1,0:T(4,128)S(1)}, f32[16,4,128]{2,1,0:T(4,128)S(1)}, u32[]{:S(2)}, u32[]{:S(2)}) collective-permute-start(f32[16,4,128]{2,1,0:T(4,128)S(1)} %get-tuple-element.253.refs_2_.refs_5_), channel_id=1, source_target_pairs={{0,4},{4,0},{8,12},{12,8},{16,20},{20,16},{24,28},{28,24},{1,5},{5... | collective-permute-start | bytes 98312 | tf_op jit(solution)/shard_map/ppermute | solution.py:658
  95.5 1.4 %collective-permute-done.45.refs_8_ = f32[16,4,128]{2,1,0:T(4,128)S(1)} collective-permute-done((f32[16,4,128]{2,1,0:T(4,128)S(1)}, f32[16,4,128]{2,1,0:T(4,128)S(1)}, u32[]{:S(2)}, u32[]{:S(2)}) %collective-permute-start.45) | collective-permute-done | bytes 32800 | tf_op jit(solution)/shard_map/ppermute | solution.py:652
  98.0 2.1 %collective-permute-start.48 = (f32[16,4,128]{2,1,0:T(4,128)S(1)}, f32[16,4,128]{2,1,0:T(4,128)S(1)}, u32[]{:S(2)}, u32[]{:S(2)}) collective-permute-start(f32[16,4,128]{2,1,0:T(4,128)S(1)} %get-tuple-element.258.refs_2_.refs_7_), channel_id=1, source_target_pairs={{0,4},{4,0},{8,12},{12,8},{16,20},{20,16},{24,28},{28,24},{1,5},{5... | collective-permute-start | bytes 98312 | tf_op jit(solution)/shard_map/ppermute | solution.py:658
  103.4 1.7 %shard_map.170 = (f32[4,128,128]{2,1,0:T(8,128)S(1)}, f32[4,4,128]{2,1,0:T(4,128)S(1)}, f32[4,4,128]{2,1,0:T(4,128)S(1)}, f32[16,1,128]{2,1,0:T(1,128)S(1)}, f32...) custom-call(s32[9]{0:T(128)S(4)} %get-tuple-element.135.refs_0_, ...), custom_call_target="tpu_custom_call", output_to_operand_aliasing={{3}: (4, {}), {4}: (5, {}), {5}: (1, {}), {6}: (2, {})} | custom-call | bytes 10500000 | tf_op jit(solution)/shard_map/pallas_call | solution.py:63
  106.2 2.0 %collective-permute-done.51.refs_2_ = f32[4,4,128]{2,1,0:T(4,128)S(1)} collective-permute-done((f32[4,4,128]{2,1,0:T(4,128)S(1)}, f32[4,4,128]{2,1,0:T(4,128)S(1)}, u32[]{:S(2)}, u32[]{:S(2)}) %collective-permute-start.51) | collective-permute-done | bytes 8224 | tf_op jit(solution)/shard_map/ppermute | solution.py:652
  108.5 2.9 %collective-permute-start.54 = (f32[4,4,256]{2,1,0:T(4,128)S(1)}, f32[4,4,256]{2,1,0:T(4,128)S(1)}, u32[]{:S(2)}, u32[]{:S(2)}) collective-permute-start(f32[4,4,256]{2,1,0:T(4,128)S(1)} %get-tuple-element.264), channel_id=1, source_target_pairs={{0,4},{4,0},{8,12},{12,8},{16,20},{20,16},{24,28},{28,24},{1,5},{5... | collective-permute-start | bytes 49160 | tf_op jit(solution)/shard_map/ppermute | solution.py:658
  111.4 1.7 %collective-permute-done.54.refs_4_ = f32[4,4,256]{2,1,0:T(4,128)S(1)} collective-permute-done((f32[4,4,256]{2,1,0:T(4,128)S(1)}, f32[4,4,256]{2,1,0:T(4,128)S(1)}, u32[]{:S(2)}, u32[]{:S(2)}) %collective-permute-start.54) | collective-permute-done | bytes 16416 | tf_op jit(solution)/shard_map/ppermute | solution.py:658
  113.1 2.3 %shard_map.172 = f32[4,128,128]{2,1,0:T(8,128)} custom-call(s32[9]{0:T(128)S(4)} %get-tuple-element.135.refs_0_, f32[11,136,256]{2,1,0:T(8,128)S(1)} %copy-done.2, f32[4,128,256]{2,1,0:T(8,128)S(1)} %get-tuple-element.262.refs_2_, f32[4,4,256]{2,1,0:T(4,128)S(1)} %collective-permute-done.53.refs_3_, f32[4,4,256]{2,1,0:T(4,128)S(1)} %collective-permute-done.54.refs_4_), custom_call_target="tpu_custom_call" | custom-call | bytes 7000000 | tf_op jit(solution)/shard_map/pallas_call | solution.py:63
  (122 shorter events, 37.1 us)
Async XLA Ops:
  1.2 11.3 %collective-permute-start.8 = (f32[16,4,128]{2,1,0:T(4,128)S(1)}, f32[16,4,128]{2,1,0:T(4,128)S(1)}, u32[]{:S(2)}, u32[]{:S(2)}) collective-permute-start(f32[16,4,128]{2,1,0:T(4,128)S(1)} %get-tuple-element.156), channel_id=1, source_target_pairs={{0,16},{4,20},{8,24},{12,28},{16,0},{20,4},{24,8},{28,12},{1,17},{... | collective-permute-start | bytes 98312 | tf_op jit(solution)/shard_map/ppermute | solution.py:704
  5.3 3.9 %collective-permute-start = (f32[6,4,128]{2,1,0:T(4,128)S(1)}, f32[6,4,128]{2,1,0:T(4,128)S(1)}, u32[]{:S(2)}, u32[]{:S(2)}) collective-permute-start(f32[6,4,128]{2,1,0:T(4,128)S(1)} %get-tuple-element.137), channel_id=1, source_target_pairs={{1,2},{2,1},{0,3},{3,0},{5,6},{6,5},{4,7},{7,4},{9,10},{10,9},{8,1... | collective-permute-start | bytes 36872 | tf_op jit(solution)/shard_map/ppermute | solution.py:652
  6.0 3.2 %collective-permute-start.1 = (f32[6,4,128]{2,1,0:T(4,128)S(1)}, f32[6,4,128]{2,1,0:T(4,128)S(1)}, u32[]{:S(2)}, u32[]{:S(2)}) collective-permute-start(f32[6,4,128]{2,1,0:T(4,128)S(1)} %get-tuple-element.144), channel_id=1, source_target_pairs={{0,1},{1,0},{2,3},{3,2},{4,5},{5,4},{6,7},{7,6},{8,9},{9,8},{10,11... | collective-permute-start | bytes 36872 | tf_op jit(solution)/shard_map/ppermute | solution.py:653
  9.4 5.0 %collective-permute-start.2 = (f32[6,4,256]{2,1,0:T(4,128)S(1)}, f32[6,4,256]{2,1,0:T(4,128)S(1)}, u32[]{:S(2)}, u32[]{:S(2)}) collective-permute-start(f32[6,4,256]{2,1,0:T(4,128)S(1)} %get-tuple-element.146), channel_id=1, source_target_pairs={{4,8},{5,9},{6,10},{7,11},{8,4},{9,5},{10,6},{11,7},{12,16},{13,17... | collective-permute-start | bytes 73736 | tf_op jit(solution)/shard_map/ppermute | solution.py:657
  9.4 4.9 %collective-permute-start.3 = (f32[6,4,256]{2,1,0:T(4,128)S(1)}, f32[6,4,256]{2,1,0:T(4,128)S(1)}, u32[]{:S(2)}, u32[]{:S(2)}) collective-permute-start(f32[6,4,256]{2,1,0:T(4,128)S(1)} %get-tuple-element.147.refs_1_), channel_id=1, source_target_pairs={{0,4},{4,0},{8,12},{12,8},{16,20},{20,16},{24,28},{28,24},{1,5},{5... | collective-permute-start | bytes 73736 | tf_op jit(solution)/shard_map/ppermute | solution.py:658
  12.5 11.8 %collective-permute-start.9 = (f32[32,4,128]{2,1,0:T(4,128)S(1)}, f32[32,4,128]{2,1,0:T(4,128)S(1)}, u32[]{:S(2)}, u32[]{:S(2)}) collective-permute-start(f32[32,4,128]{2,1,0:T(4,128)S(1)} %pad_maximum_fusion.refs_10_), channel_id=1, source_target_pairs={{0,8},{4,12},{8,0},{12,4},{16,24},{20,28},{24,16},{28,20},{1,9},{5... | collective-permute-start | bytes 196616 | tf_op jit(solution)/shard_map/ppermute | solution.py:704
  17.5 6.0 %collective-permute-start.4 = (f32[21,4,128]{2,1,0:T(4,128)S(1)}, f32[21,4,128]{2,1,0:T(4,128)S(1)}, u32[]{:S(2)}, u32[]{:S(2)}) collective-permute-start(f32[21,4,128]{2,1,0:T(4,128)S(1)} %get-tuple-element.154.refs_5_.refs_1_), channel_id=1, source_target_pairs={{4,8},{5,9},{6,10},{7,11},{8,4},{9,5},{10,6},{11,7},{12,16},{13,17... | collective-permute-start | bytes 129032 | tf_op jit(solution)/shard_map/ppermute | solution.py:657
  17.5 5.9 %collective-permute-start.5 = (f32[21,4,128]{2,1,0:T(4,128)S(1)}, f32[21,4,128]{2,1,0:T(4,128)S(1)}, u32[]{:S(2)}, u32[]{:S(2)}) collective-permute-start(f32[21,4,128]{2,1,0:T(4,128)S(1)} %get-tuple-element.154.refs_5_.refs_1_), channel_id=1, source_target_pairs={{0,4},{4,0},{8,12},{12,8},{16,20},{20,16},{24,28},{28,24},{1,5},{5... | collective-permute-start | bytes 129032 | tf_op jit(solution)/shard_map/ppermute | solution.py:658
  20.9 3.4 %collective-permute-start.6 = (f32[21,4,128]{2,1,0:T(4,128)S(1)}, f32[21,4,128]{2,1,0:T(4,128)S(1)}, u32[]{:S(2)}, u32[]{:S(2)}) collective-permute-start(f32[21,4,128]{2,1,0:T(4,128)S(1)} %get-tuple-element.154.refs_5_.refs_1_), channel_id=1, source_target_pairs={{1,2},{2,1},{0,3},{3,0},{5,6},{6,5},{4,7},{7,4},{9,10},{10,9},{8,1... | collective-permute-start | bytes 129032 | tf_op jit(solution)/shard_map/ppermute | solution.py:652
  20.9 3.4 %collective-permute-start.7 = (f32[21,4,128]{2,1,0:T(4,128)S(1)}, f32[21,4,128]{2,1,0:T(4,128)S(1)}, u32[]{:S(2)}, u32[]{:S(2)}) collective-permute-start(f32[21,4,128]{2,1,0:T(4,128)S(1)} %get-tuple-element.154.refs_5_.refs_1_), channel_id=1, source_target_pairs={{0,1},{1,0},{2,3},{3,2},{4,5},{5,4},{6,7},{7,6},{8,9},{9,8},{10,11... | collective-permute-start | bytes 129032 | tf_op jit(solution)/shard_map/ppermute | solution.py:653
  25.6 4.7 %collective-permute-start.11 = (f32[48,4,128]{2,1,0:T(4,128)S(1)}, f32[48,4,128]{2,1,0:T(4,128)S(1)}, u32[]{:S(2)}, u32[]{:S(2)}) collective-permute-start(f32[48,4,128]{2,1,0:T(4,128)S(1)} %get-tuple-element.163.refs_11_), channel_id=1, source_target_pairs={{0,4},{4,0},{8,12},{12,8},{16,20},{20,16},{24,28},{28,24},{1,5},{5... | collective-permute-start | bytes 294920 | tf_op jit(solution)/shard_map/ppermute | solution.py:658
  26.2 4.4 %collective-permute-start.12 = (f32[48,4,128]{2,1,0:T(4,128)S(1)}, f32[48,4,128]{2,1,0:T(4,128)S(1)}, u32[]{:S(2)}, u32[]{:S(2)}) collective-permute-start(f32[48,4,128]{2,1,0:T(4,128)S(1)} %get-tuple-element.164.refs_12_), channel_id=1, source_target_pairs={{1,2},{2,1},{0,3},{3,0},{5,6},{6,5},{4,7},{7,4},{9,10},{10,9},{8,1... | collective-permute-start | bytes 294920 | tf_op jit(solution)/shard_map/ppermute | solution.py:652
  31.6 6.8 %collective-permute-start.15 = (f32[80,4,128]{2,1,0:T(4,128)S(1)}, f32[80,4,128]{2,1,0:T(4,128)S(1)}, u32[]{:S(2)}, u32[]{:S(2)}) collective-permute-start(f32[80,4,128]{2,1,0:T(4,128)S(1)} %get-tuple-element.171.refs_3_), channel_id=1, source_target_pairs={{0,4},{4,0},{8,12},{12,8},{16,20},{20,16},{24,28},{28,24},{1,5},{5... | collective-permute-start | bytes 491528 | tf_op jit(solution)/shard_map/ppermute | solution.py:658
  34.1 6.4 %collective-permute-start.16 = (f32[80,4,128]{2,1,0:T(4,128)S(1)}, f32[80,4,128]{2,1,0:T(4,128)S(1)}, u32[]{:S(2)}, u32[]{:S(2)}) collective-permute-start(f32[80,4,128]{2,1,0:T(4,128)S(1)} %get-tuple-element.172.refs_1_), channel_id=1, source_target_pairs={{1,2},{2,1},{0,3},{3,0},{5,6},{6,5},{4,7},{7,4},{9,10},{10,9},{8,1... | collective-permute-start | bytes 491528 | tf_op jit(solution)/shard_map/ppermute | solution.py:652
  41.9 11.8 %collective-permute-start.26 = (f32[256,4,128]{2,1,0:T(4,128)S(1)}, f32[256,4,128]{2,1,0:T(4,128)S(1)}, u32[]{:S(2)}, u32[]{:S(2)}) collective-permute-start(f32[256,4,128]{2,1,0:T(4,128)S(1)} %shard_map.160.refs_1_), channel_id=1, source_target_pairs={{0,1},{1,0},{2,3},{3,2},{4,5},{5,4},{6,7},{7,6},{8,9},{9,8},{10,11... | collective-permute-start | bytes 1572872 | tf_op jit(solution)/shard_map/ppermute | solution.py:874
  42.0 6.0 %collective-permute-start.18 = (f32[4,4,128]{2,1,0:T(4,128)S(1)}, f32[4,4,128]{2,1,0:T(4,128)S(1)}, u32[]{:S(2)}, u32[]{:S(2)}) collective-permute-start(f32[4,4,128]{2,1,0:T(4,128)S(1)} %get-tuple-element.179.refs_2_.refs_4_.refs_0_), channel_id=1, source_target_pairs={{4,8},{5,9},{6,10},{7,11},{8,4},{9,5},{10,6},{11,7},{12,16},{13,17... | collective-permute-start | bytes 24584 | tf_op jit(solution)/shard_map/ppermute | solution.py:657
  42.5 5.5 %collective-permute-start.19 = (f32[4,4,128]{2,1,0:T(4,128)S(1)}, f32[4,4,128]{2,1,0:T(4,128)S(1)}, u32[]{:S(2)}, u32[]{:S(2)}) collective-permute-start(f32[4,4,128]{2,1,0:T(4,128)S(1)} %get-tuple-element.179.refs_2_.refs_4_.refs_0_), channel_id=1, source_target_pairs={{0,4},{4,0},{8,12},{12,8},{16,20},{20,16},{24,28},{28,24},{1,5},{5... | collective-permute-start | bytes 24584 | tf_op jit(solution)/shard_map/ppermute | solution.py:658
  48.7 3.7 %collective-permute-start.23 = (f32[4,4,128]{2,1,0:T(4,128)S(1)}, f32[4,4,128]{2,1,0:T(4,128)S(1)}, u32[]{:S(2)}, u32[]{:S(2)}) collective-permute-start(f32[4,4,128]{2,1,0:T(4,128)S(1)} %get-tuple-element.198.refs_4_), channel_id=1, source_target_pairs={{0,4},{4,0},{8,12},{12,8},{16,20},{20,16},{24,28},{28,24},{1,5},{5... | collective-permute-start | bytes 24584 | tf_op jit(solution)/shard_map/ppermute | solution.py:658
  53.7 3.7 %collective-permute-start.27 = (f32[4,4,128]{2,1,0:T(4,128)S(1)}, f32[4,4,128]{2,1,0:T(4,128)S(1)}, u32[]{:S(2)}, u32[]{:S(2)}) collective-permute-start(f32[4,4,128]{2,1,0:T(4,128)S(1)} %get-tuple-element.207.refs_6_), channel_id=1, source_target_pairs={{4,8},{5,9},{6,10},{7,11},{8,4},{9,5},{10,6},{11,7},{12,16},{13,17... | collective-permute-start | bytes 24584 | tf_op jit(solution)/shard_map/ppermute | solution.py:657
  53.8 4.0 %collective-permute-start.28 = (f32[4,4,128]{2,1,0:T(4,128)S(1)}, f32[4,4,128]{2,1,0:T(4,128)S(1)}, u32[]{:S(2)}, u32[]{:S(2)}) collective-permute-start(f32[4,4,128]{2,1,0:T(4,128)S(1)} %get-tuple-element.207.refs_6_), channel_id=1, source_target_pairs={{0,4},{4,0},{8,12},{12,8},{16,20},{20,16},{24,28},{28,24},{1,5},{5... | collective-permute-start | bytes 24584 | tf_op jit(solution)/shard_map/ppermute | solution.py:658
  72.7 3.7 %collective-permute-start.32 = (f32[4,4,128]{2,1,0:T(4,128)S(1)}, f32[4,4,128]{2,1,0:T(4,128)S(1)}, u32[]{:S(2)}, u32[]{:S(2)}) collective-permute-start(f32[4,4,128]{2,1,0:T(4,128)S(1)} %get-tuple-element.229.refs_4_), channel_id=1, source_target_pairs={{0,4},{4,0},{8,12},{12,8},{16,20},{20,16},{24,28},{28,24},{1,5},{5... | collective-permute-start | bytes 24584 | tf_op jit(solution)/shard_map/ppermute | solution.py:658
  78.2 3.7 %collective-permute-start.36 = (f32[4,4,128]{2,1,0:T(4,128)S(1)}, f32[4,4,128]{2,1,0:T(4,128)S(1)}, u32[]{:S(2)}, u32[]{:S(2)}) collective-permute-start(f32[4,4,128]{2,1,0:T(4,128)S(1)} %get-tuple-element.238.refs_4_), channel_id=1, source_target_pairs={{0,4},{4,0},{8,12},{12,8},{16,20},{20,16},{24,28},{28,24},{1,5},{5... | collective-permute-start | bytes 24584 | tf_op jit(solution)/shard_map/ppermute | solution.py:658
  83.9 3.9 %collective-permute-start.40 = (f32[4,4,128]{2,1,0:T(4,128)S(1)}, f32[4,4,128]{2,1,0:T(4,128)S(1)}, u32[]{:S(2)}, u32[]{:S(2)}) collective-permute-start(f32[4,4,128]{2,1,0:T(4,128)S(1)} %get-tuple-element.247.refs_6_), channel_id=1, source_target_pairs={{0,4},{4,0},{8,12},{12,8},{16,20},{20,16},{24,28},{28,24},{1,5},{5... | collective-permute-start | bytes 24584 | tf_op jit(solution)/shard_map/ppermute | solution.py:658
  90.9 3.9 %collective-permute-start.43 = (f32[16,4,128]{2,1,0:T(4,128)S(1)}, f32[16,4,128]{2,1,0:T(4,128)S(1)}, u32[]{:S(2)}, u32[]{:S(2)}) collective-permute-start(f32[16,4,128]{2,1,0:T(4,128)S(1)} %get-tuple-element.253.refs_2_.refs_5_), channel_id=1, source_target_pairs={{4,8},{5,9},{6,10},{7,11},{8,4},{9,5},{10,6},{11,7},{12,16},{13,17... | collective-permute-start | bytes 98312 | tf_op jit(solution)/shard_map/ppermute | solution.py:657
  91.0 4.5 %collective-permute-start.44 = (f32[16,4,128]{2,1,0:T(4,128)S(1)}, f32[16,4,128]{2,1,0:T(4,128)S(1)}, u32[]{:S(2)}, u32[]{:S(2)}) collective-permute-start(f32[16,4,128]{2,1,0:T(4,128)S(1)} %get-tuple-element.253.refs_2_.refs_5_), channel_id=1, source_target_pairs={{0,4},{4,0},{8,12},{12,8},{16,20},{20,16},{24,28},{28,24},{1,5},{5... | collective-permute-start | bytes 98312 | tf_op jit(solution)/shard_map/ppermute | solution.py:658
  93.6 3.3 %collective-permute-start.45 = (f32[16,4,128]{2,1,0:T(4,128)S(1)}, f32[16,4,128]{2,1,0:T(4,128)S(1)}, u32[]{:S(2)}, u32[]{:S(2)}) collective-permute-start(f32[16,4,128]{2,1,0:T(4,128)S(1)} %get-tuple-element.253.refs_2_.refs_5_), channel_id=1, source_target_pairs={{1,2},{2,1},{0,3},{3,0},{5,6},{6,5},{4,7},{7,4},{9,10},{10,9},{8,1... | collective-permute-start | bytes 98312 | tf_op jit(solution)/shard_map/ppermute | solution.py:652
  93.6 3.3 %collective-permute-start.46 = (f32[16,4,128]{2,1,0:T(4,128)S(1)}, f32[16,4,128]{2,1,0:T(4,128)S(1)}, u32[]{:S(2)}, u32[]{:S(2)}) collective-permute-start(f32[16,4,128]{2,1,0:T(4,128)S(1)} %get-tuple-element.253.refs_2_.refs_5_), channel_id=1, source_target_pairs={{0,1},{1,0},{2,3},{3,2},{4,5},{5,4},{6,7},{7,6},{8,9},{9,8},{10,11... | collective-permute-start | bytes 98312 | tf_op jit(solution)/shard_map/ppermute | solution.py:653
  97.9 3.6 %collective-permute-start.47 = (f32[16,4,128]{2,1,0:T(4,128)S(1)}, f32[16,4,128]{2,1,0:T(4,128)S(1)}, u32[]{:S(2)}, u32[]{:S(2)}) collective-permute-start(f32[16,4,128]{2,1,0:T(4,128)S(1)} %get-tuple-element.258.refs_2_.refs_7_), channel_id=1, source_target_pairs={{4,8},{5,9},{6,10},{7,11},{8,4},{9,5},{10,6},{11,7},{12,16},{13,17... | collective-permute-start | bytes 98312 | tf_op jit(solution)/shard_map/ppermute | solution.py:657
  98.0 4.0 %collective-permute-start.48 = (f32[16,4,128]{2,1,0:T(4,128)S(1)}, f32[16,4,128]{2,1,0:T(4,128)S(1)}, u32[]{:S(2)}, u32[]{:S(2)}) collective-permute-start(f32[16,4,128]{2,1,0:T(4,128)S(1)} %get-tuple-element.258.refs_2_.refs_7_), channel_id=1, source_target_pairs={{0,4},{4,0},{8,12},{12,8},{16,20},{20,16},{24,28},{28,24},{1,5},{5... | collective-permute-start | bytes 98312 | tf_op jit(solution)/shard_map/ppermute | solution.py:658
  100.0 3.3 %collective-permute-start.49 = (f32[16,4,128]{2,1,0:T(4,128)S(1)}, f32[16,4,128]{2,1,0:T(4,128)S(1)}, u32[]{:S(2)}, u32[]{:S(2)}) collective-permute-start(f32[16,4,128]{2,1,0:T(4,128)S(1)} %get-tuple-element.258.refs_2_.refs_7_), channel_id=1, source_target_pairs={{1,2},{2,1},{0,3},{3,0},{5,6},{6,5},{4,7},{7,4},{9,10},{10,9},{8,1... | collective-permute-start | bytes 98312 | tf_op jit(solution)/shard_map/ppermute | solution.py:652
  100.0 3.3 %collective-permute-start.50 = (f32[16,4,128]{2,1,0:T(4,128)S(1)}, f32[16,4,128]{2,1,0:T(4,128)S(1)}, u32[]{:S(2)}, u32[]{:S(2)}) collective-permute-start(f32[16,4,128]{2,1,0:T(4,128)S(1)} %get-tuple-element.258.refs_2_.refs_7_), channel_id=1, source_target_pairs={{0,1},{1,0},{2,3},{3,2},{4,5},{5,4},{6,7},{7,6},{8,9},{9,8},{10,11... | collective-permute-start | bytes 98312 | tf_op jit(solution)/shard_map/ppermute | solution.py:653
  108.5 4.6 %collective-permute-start.54 = (f32[4,4,256]{2,1,0:T(4,128)S(1)}, f32[4,4,256]{2,1,0:T(4,128)S(1)}, u32[]{:S(2)}, u32[]{:S(2)}) collective-permute-start(f32[4,4,256]{2,1,0:T(4,128)S(1)} %get-tuple-element.264), channel_id=1, source_target_pairs={{0,4},{4,0},{8,12},{12,8},{16,20},{20,16},{24,28},{28,24},{1,5},{5... | collective-permute-start | bytes 49160 | tf_op jit(solution)/shard_map/ppermute | solution.py:658
  (30 other events, 127.0 us)

commit v8 on v7

--- a/solution.py
+++ b/solution.py
@@ -555,29 +555,23 @@
     copy = pltpu.make_async_copy(keep, far, sem.at[0])
     copy.start()
     count = b1.shape[0]
-    step = 64
     one, zero = jnp.ones((), BF16), jnp.zeros((), BF16)
     lanes = lax.broadcasted_iota(jnp.int32, (LANES, LANES), 0).astype(F32).astype(BF16)
 
     def over_rows(x):
         return jnp.broadcast_to(x, (16, LANES)).astype(BF16)
 
-    def add_rows(j, total):
-        left, right = [], []
-        for k in range(step):
-            row = pl.ds(j * step + k, 1)
-            group = groups[row, :]
-            mask = lanes[0:count] == over_rows((group >> 7).astype(F32))
-            low = over_rows((group & (LANES - 1)).astype(F32))
-            picked = [jnp.where(mask, over_rows(q_ref[i, row, :]), zero) for i in range(2 * cols)]
-            left.append(jnp.concatenate(picked, axis=0))
-            low = jnp.concatenate([low] * (LANES // 16), axis=0)
-            right.append(jnp.where(lanes == low, one, zero))
-        return total + dot_nt(jnp.concatenate(left, axis=1), jnp.concatenate(right, axis=1))
-
-    total = lax.fori_loop(
-        0, rows // step, add_rows, jnp.zeros((2 * cols * count, LANES), F32)
-    )
+    left, right = [], []
+    for row in range(rows):
+        row = slice(row, row + 1)
+        group = groups[row, :]
+        mask = lanes[0:count] == over_rows((group >> 7).astype(F32))
+        low = over_rows((group & (LANES - 1)).astype(F32))
+        picked = [jnp.where(mask, over_rows(q_ref[i, row, :]), zero) for i in range(2 * cols)]
+        left.append(jnp.concatenate(picked, axis=0))
+        low = jnp.concatenate([low] * (LANES // 16), axis=0)
+        right.append(jnp.where(lanes == low, one, zero))
+    total = dot_nt(jnp.concatenate(left, axis=1), jnp.concatenate(right, axis=1))
     size = cols * count
     total = total[0:size] + total[size : 2 * size]
     for c in range(cols):

time: 116 us -> 115 us (level)
  transfers between devices with their start and end apart: 55 -> 55, of which waited for: 26 -> 26; matrix products, arithmetic and copies ran while one was open for 0% -> 0% of each run, Pallas kernels for 12% -> 11%
where the time goes in v8:
time: 115 us
  starting transfers between devices  47.8 us (42%)
  waiting for transfers between devices  28.2 us (25%)
  Pallas kernels  28.1 us (24%)
  blocking collectives  10.3 us (9%)
    ppermute x13, starting transfers between devices, exchange_wide(): return (second, lax.ppermute(first, 'wide', route[2]))  29.8 us
    pallas_call x28, Pallas kernels, call(): pl.pallas_call(inner, out_shape=shapes, in_specs=specs[::ORDER], out_spec...  28.1 us
    ppermute x13, waiting for transfers between devices, exchange_narrow(): second = lax.ppermute(second, 'narrow', route[1])  15 us
    ppermute x13, waiting for transfers between devices, exchange_wide(): return (second, lax.ppermute(first, 'wide', route[2]))  11.5 us
    all_to_all x1, blocking collectives, body(): pieces = lax.all_to_all(out3, ('wide', 'narrow'), 0, 0)  10.3 us
    ppermute x13, starting transfers between devices, exchange_narrow(): return (second, lax.ppermute(first, 'narrow', route[0]))  9.31 us
    ppermute x2, starting transfers between devices, swap(): lax.ppermute(x, axis, [(i, i ^ step) for i in range(lax.axis_size(axis))])  4.27 us
    ppermute x13, starting transfers between devices, exchange_wide(): second = lax.ppermute(second, ('wide', 'narrow'), route[3])  2.89 us
  transfers between devices with their start and end apart: 55, of which 26 were waited for; matrix products, arithmetic and copies ran while one was open for 0% of the time, Pallas kernels for 11%

profile of v8, /device:TPU:0, one launch (start us, length us, event | category | flops | bytes accessed | tf_op | source)
XLA Modules:
  0.0 115.1 jit_solution(16012334434429654893)
XLA Ops:
  1.2 4.1 %collective-permute-start.8 = (f32[16,4,128]{2,1,0:T(4,128)S(1)}, f32[16,4,128]{2,1,0:T(4,128)S(1)}, u32[]{:S(2)}, u32[]{:S(2)}) collective-permute-start(f32[16,4,128]{2,1,0:T(4,128)S(1)} %get-tuple-element.156), channel_id=1, source_target_pairs={{0,16},{4,20},{8,24},{12,28},{16,0},{20,4},{24,8},{28,12},{1,17},{... | collective-permute-start | bytes 98312 | tf_op jit(solution)/shard_map/ppermute | solution.py:698
  6.9 2.2 %shard_map.146 = (s32[4,16]{1,0:T(4,128)S(4)}, s32[4,4]{1,0:T(4,128)S(4)}, f32[16,1,128]{2,1,0:T(1,128)S(1)}, bf16[4,256,512]{2,1,0:T(8,128)(2,1)S(1)}, f32[4,1,128]{2,1,0:T(1,128)S(1)}) custom-call(s32[9]{0:T(128)S(4)} %get-tuple-element.135.refs_0_, s32[3,16]{1,0:T(4,128)} %bitcast.8, s32[3,16]{1,0:T(4,128)} %bitcast.9, s32[4,3]{1,0:T(4,128)} %refs_3_.3, ...), custom_call_target="tpu_custom_call" | custom-call | bytes 7000000 | tf_op jit(solution)/shard_map/pallas_call | solution.py:63
  9.4 3.0 %collective-permute-start.3 = (f32[6,4,256]{2,1,0:T(4,128)S(1)}, f32[6,4,256]{2,1,0:T(4,128)S(1)}, u32[]{:S(2)}, u32[]{:S(2)}) collective-permute-start(f32[6,4,256]{2,1,0:T(4,128)S(1)} %get-tuple-element.147.refs_1_), channel_id=1, source_target_pairs={{0,4},{4,0},{8,12},{12,8},{16,20},{20,16},{24,28},{28,24},{1,5},{5... | collective-permute-start | bytes 73736 | tf_op jit(solution)/shard_map/ppermute | solution.py:652
  12.7 1.6 %shard_map.148.refs_8_ = bf16[8,256,512]{2,1,0:T(8,128)(2,1)S(1)} custom-call(f32[16,4,128,128]{3,2,1,0:T(8,128)} %refs_0_.5, f32[6,4,256]{2,1,0:T(4,128)S(1)} %get-tuple-element.147.refs_1_), custom_call_target="tpu_custom_call" | custom-call | bytes 7000000 | tf_op jit(solution)/shard_map/pallas_call | solution.py:63
  14.4 2.6 %shard_map.149 = (f32[11,136,256]{2,1,0:T(8,128)}, f32[16,4,128]{2,1,0:T(4,128)S(1)}, f32[21,4,128]{2,1,0:T(4,128)S(1)}, bf16[8,256,512]{2,1,0:T(8,128)(2,1)S(1)}, f32[16,1,128]{2,1,0:T(1,128)S(1)}) custom-call(s32[9]{0:T(128)S(4)} %get-tuple-element.135.refs_0_, ...), custom_call_target="tpu_custom_call", output_to_operand_aliasing={{3}: (8, {}), {4}: (5, {})} | custom-call | bytes 24500000 | tf_op jit(solution)/shard_map/pallas_call | solution.py:63
  17.1 3.4 %collective-permute-start.5 = (f32[21,4,128]{2,1,0:T(4,128)S(1)}, f32[21,4,128]{2,1,0:T(4,128)S(1)}, u32[]{:S(2)}, u32[]{:S(2)}) collective-permute-start(f32[21,4,128]{2,1,0:T(4,128)S(1)} %get-tuple-element.154.refs_5_.refs_1_), channel_id=1, source_target_pairs={{0,4},{4,0},{8,12},{12,8},{16,20},{20,16},{24,28},{28,24},{1,5},{5... | collective-permute-start | bytes 129032 | tf_op jit(solution)/shard_map/ppermute | solution.py:652
  21.3 1.6 %shard_map.150.refs_2_ = bf16[8,256,512]{2,1,0:T(8,128)(2,1)S(1)} custom-call(f32[16,4,128,128]{3,2,1,0:T(8,128)} %refs_0_.5, f32[16,4,128]{2,1,0:T(4,128)S(1)} %get-tuple-element.152.refs_1_.refs_4_), custom_call_target="tpu_custom_call" | custom-call | bytes 7000000 | tf_op jit(solution)/shard_map/pallas_call | solution.py:63
  27.9 2.0 %collective-permute-done.11.refs_7_ = f32[48,4,128]{2,1,0:T(4,128)S(1)} collective-permute-done((f32[48,4,128]{2,1,0:T(4,128)S(1)}, f32[48,4,128]{2,1,0:T(4,128)S(1)}, u32[]{:S(2)}, u32[]{:S(2)}) %collective-permute-start.11) | collective-permute-done | bytes 98336 | tf_op jit(solution)/shard_map/ppermute | solution.py:652
  31.2 2.5 %collective-permute-start.15 = (f32[80,4,128]{2,1,0:T(4,128)S(1)}, f32[80,4,128]{2,1,0:T(4,128)S(1)}, u32[]{:S(2)}, u32[]{:S(2)}) collective-permute-start(f32[80,4,128]{2,1,0:T(4,128)S(1)} %get-tuple-element.171.refs_3_), channel_id=1, source_target_pairs={{0,4},{4,0},{8,12},{12,8},{16,20},{20,16},{24,28},{28,24},{1,5},{5... | collective-permute-start | bytes 491528 | tf_op jit(solution)/shard_map/ppermute | solution.py:652
  35.7 2.3 %collective-permute-done.15.refs_8_.refs_4_ = f32[80,4,128]{2,1,0:T(4,128)S(1)} collective-permute-done((f32[80,4,128]{2,1,0:T(4,128)S(1)}, f32[80,4,128]{2,1,0:T(4,128)S(1)}, u32[]{:S(2)}, u32[]{:S(2)}) %collective-permute-start.15) | collective-permute-done | bytes 163872 | tf_op jit(solution)/shard_map/ppermute | solution.py:652
  38.0 2.0 %collective-permute-done.16.refs_9_.refs_2_ = f32[80,4,128]{2,1,0:T(4,128)S(1)} collective-permute-done((f32[80,4,128]{2,1,0:T(4,128)S(1)}, f32[80,4,128]{2,1,0:T(4,128)S(1)}, u32[]{:S(2)}, u32[]{:S(2)}) %collective-permute-start.16) | collective-permute-done | bytes 163872 | tf_op jit(solution)/shard_map/ppermute | solution.py:646
  42.1 2.5 %collective-permute-start.19 = (f32[4,4,128]{2,1,0:T(4,128)S(1)}, f32[4,4,128]{2,1,0:T(4,128)S(1)}, u32[]{:S(2)}, u32[]{:S(2)}) collective-permute-start(f32[4,4,128]{2,1,0:T(4,128)S(1)} %get-tuple-element.179.refs_2_.refs_4_.refs_0_), channel_id=1, source_target_pairs={{0,4},{4,0},{8,12},{12,8},{16,20},{20,16},{24,28},{28,24},{1,5},{5... | collective-permute-start | bytes 24584 | tf_op jit(solution)/shard_map/ppermute | solution.py:652
  45.6 2.0 %shard_map.157 = (bf16[8,256,512]{2,1,0:T(8,128)(2,1)}, bf16[8,256,512]{2,1,0:T(8,128)(2,1)}, bf16[8,256,512]{2,1,0:T(8,128)(2,1)S(1)}, f32[16,1,128]{2,1,0:T(1,...) custom-call(bf16[8,256,512]{2,1,0:T(8,128)(2,1)S(1)} %get-tuple-elem, ...), custom_call_target="tpu_custom_call", output_to_operand_aliasing={{2}: (0, {}), {3}: (3, {}), {4}: (4, {}), {5}: (1, {}), {6}... | custom-call | bytes 7000000 | tf_op jit(solution)/shard_map/pallas_call | solution.py:63
  48.3 1.6 %collective-permute-start.23 = (f32[4,4,128]{2,1,0:T(4,128)S(1)}, f32[4,4,128]{2,1,0:T(4,128)S(1)}, u32[]{:S(2)}, u32[]{:S(2)}) collective-permute-start(f32[4,4,128]{2,1,0:T(4,128)S(1)} %get-tuple-element.198.refs_4_), channel_id=1, source_target_pairs={{0,4},{4,0},{8,12},{12,8},{16,20},{20,16},{24,28},{28,24},{1,5},{5... | collective-permute-start | bytes 24584 | tf_op jit(solution)/shard_map/ppermute | solution.py:652
  53.4 2.4 %collective-permute-start.28 = (f32[4,4,128]{2,1,0:T(4,128)S(1)}, f32[4,4,128]{2,1,0:T(4,128)S(1)}, u32[]{:S(2)}, u32[]{:S(2)}) collective-permute-start(f32[4,4,128]{2,1,0:T(4,128)S(1)} %get-tuple-element.207.refs_6_), channel_id=1, source_target_pairs={{0,4},{4,0},{8,12},{12,8},{16,20},{20,16},{24,28},{28,24},{1,5},{5... | collective-permute-start | bytes 24584 | tf_op jit(solution)/shard_map/ppermute | solution.py:652
  57.4 1.4 %collective-permute-done.29.refs_9_ = f32[4,4,128]{2,1,0:T(4,128)S(1)} collective-permute-done((f32[4,4,128]{2,1,0:T(4,128)S(1)}, f32[4,4,128]{2,1,0:T(4,128)S(1)}, u32[]{:S(2)}, u32[]{:S(2)}) %collective-permute-start.29) | collective-permute-done | bytes 8224 | tf_op jit(solution)/shard_map/ppermute | solution.py:646
  59.6 10.3 %all_to_all.5.refs_2_ = f32[32,4,128]{2,1,0:T(4,128)S(1)} all-to-all(f32[32,4,128]{2,1,0:T(4,128)S(1)} %get-tuple-element.217), channel_id=1, replica_groups=mesh['wide'=8,'narrow'=4] {'wide','narrow'}, dimensions={0} | all-to-all | bytes 131072 | tf_op jit(solution)/shard_map/all_to_all | solution.py:917
  69.9 2.2 %shard_map.163 = (f32[4,4,128]{2,1,0:T(4,128)S(1)}, f32[16,1,128]{2,1,0:T(1,128)S(1)}, f32[16,4,128]{2,1,0:T(4,128)S(1)}, f32[16,4,128]{2,1,0:T(4,128)S(1)}, s32...) custom-call(s32[9]{0:T(128)S(4)} %get-tuple-element.135.refs_0_, ...), custom_call_target="tpu_custom_call", output_to_operand_aliasing={{1}: (8, {}), {2}: (9, {}), {3}: (10, {}), {4}: (7, {}), {5... | custom-call | bytes 10500000 | tf_op jit(solution)/shard_map/pallas_call | solution.py:63
  72.3 2.0 %collective-permute-start.32 = (f32[4,4,128]{2,1,0:T(4,128)S(1)}, f32[4,4,128]{2,1,0:T(4,128)S(1)}, u32[]{:S(2)}, u32[]{:S(2)}) collective-permute-start(f32[4,4,128]{2,1,0:T(4,128)S(1)} %get-tuple-element.229.refs_4_), channel_id=1, source_target_pairs={{0,4},{4,0},{8,12},{12,8},{16,20},{20,16},{24,28},{28,24},{1,5},{5... | collective-permute-start | bytes 24584 | tf_op jit(solution)/shard_map/ppermute | solution.py:652
  77.8 2.1 %collective-permute-start.36 = (f32[4,4,128]{2,1,0:T(4,128)S(1)}, f32[4,4,128]{2,1,0:T(4,128)S(1)}, u32[]{:S(2)}, u32[]{:S(2)}) collective-permute-start(f32[4,4,128]{2,1,0:T(4,128)S(1)} %get-tuple-element.238.refs_4_), channel_id=1, source_target_pairs={{0,4},{4,0},{8,12},{12,8},{16,20},{20,16},{24,28},{28,24},{1,5},{5... | collective-permute-start | bytes 24584 | tf_op jit(solution)/shard_map/ppermute | solution.py:652
  81.5 1.4 %collective-permute-done.37.refs_7_ = f32[4,4,128]{2,1,0:T(4,128)S(1)} collective-permute-done((f32[4,4,128]{2,1,0:T(4,128)S(1)}, f32[4,4,128]{2,1,0:T(4,128)S(1)}, u32[]{:S(2)}, u32[]{:S(2)}) %collective-permute-start.37) | collective-permute-done | bytes 8224 | tf_op jit(solution)/shard_map/ppermute | solution.py:646
  83.4 2.2 %collective-permute-start.40 = (f32[4,4,128]{2,1,0:T(4,128)S(1)}, f32[4,4,128]{2,1,0:T(4,128)S(1)}, u32[]{:S(2)}, u32[]{:S(2)}) collective-permute-start(f32[4,4,128]{2,1,0:T(4,128)S(1)} %get-tuple-element.247.refs_6_), channel_id=1, source_target_pairs={{0,4},{4,0},{8,12},{12,8},{16,20},{20,16},{24,28},{28,24},{1,5},{5... | collective-permute-start | bytes 24584 | tf_op jit(solution)/shard_map/ppermute | solution.py:652
  87.3 1.4 %collective-permute-done.41.refs_9_ = f32[4,4,128]{2,1,0:T(4,128)S(1)} collective-permute-done((f32[4,4,128]{2,1,0:T(4,128)S(1)}, f32[4,4,128]{2,1,0:T(4,128)S(1)}, u32[]{:S(2)}, u32[]{:S(2)}) %collective-permute-start.41) | collective-permute-done | bytes 8224 | tf_op jit(solution)/shard_map/ppermute | solution.py:646
  88.8 1.7 %shard_map.166 = (f32[16,4,128]{2,1,0:T(4,128)S(1)}, f32[16,1,128]{2,1,0:T(1,128)S(1)}, f32[16,4,128]{2,1,0:T(4,128)S(1)}, f32[16,4,128]{2,1,0:T(4,128)S(1)}, s3...) custom-call(s32[4,16]{1,0:T(4,128)S(4)} %get-tuple-element.150.refs_, ...), custom_call_target="tpu_custom_call", output_to_operand_aliasing={{1}: (3, {}), {2}: (11, {}), {3}: (4, {}), {4}: (5, {}), {5... | custom-call | bytes 7000000 | tf_op jit(solution)/shard_map/pallas_call | solution.py:63
  90.5 2.6 %collective-permute-start.44 = (f32[16,4,128]{2,1,0:T(4,128)S(1)}, f32[16,4,128]{2,1,0:T(4,128)S(1)}, u32[]{:S(2)}, u32[]{:S(2)}) collective-permute-start(f32[16,4,128]{2,1,0:T(4,128)S(1)} %get-tuple-element.253.refs_2_.refs_5_), channel_id=1, source_target_pairs={{0,4},{4,0},{8,12},{12,8},{16,20},{20,16},{24,28},{28,24},{1,5},{5... | collective-permute-start | bytes 98312 | tf_op jit(solution)/shard_map/ppermute | solution.py:652
  95.1 1.4 %collective-permute-done.45.refs_8_ = f32[16,4,128]{2,1,0:T(4,128)S(1)} collective-permute-done((f32[16,4,128]{2,1,0:T(4,128)S(1)}, f32[16,4,128]{2,1,0:T(4,128)S(1)}, u32[]{:S(2)}, u32[]{:S(2)}) %collective-permute-start.45) | collective-permute-done | bytes 32800 | tf_op jit(solution)/shard_map/ppermute | solution.py:646
  97.5 2.1 %collective-permute-start.48 = (f32[16,4,128]{2,1,0:T(4,128)S(1)}, f32[16,4,128]{2,1,0:T(4,128)S(1)}, u32[]{:S(2)}, u32[]{:S(2)}) collective-permute-start(f32[16,4,128]{2,1,0:T(4,128)S(1)} %get-tuple-element.258.refs_2_.refs_7_), channel_id=1, source_target_pairs={{0,4},{4,0},{8,12},{12,8},{16,20},{20,16},{24,28},{28,24},{1,5},{5... | collective-permute-start | bytes 98312 | tf_op jit(solution)/shard_map/ppermute | solution.py:652
  102.9 1.7 %shard_map.170 = (f32[4,128,128]{2,1,0:T(8,128)S(1)}, f32[4,4,128]{2,1,0:T(4,128)S(1)}, f32[4,4,128]{2,1,0:T(4,128)S(1)}, f32[16,1,128]{2,1,0:T(1,128)S(1)}, f32...) custom-call(s32[9]{0:T(128)S(4)} %get-tuple-element.135.refs_0_, ...), custom_call_target="tpu_custom_call", output_to_operand_aliasing={{3}: (4, {}), {4}: (5, {}), {5}: (1, {}), {6}: (2, {})} | custom-call | bytes 10500000 | tf_op jit(solution)/shard_map/pallas_call | solution.py:63
  105.8 2.0 %collective-permute-done.51.refs_2_ = f32[4,4,128]{2,1,0:T(4,128)S(1)} collective-permute-done((f32[4,4,128]{2,1,0:T(4,128)S(1)}, f32[4,4,128]{2,1,0:T(4,128)S(1)}, u32[]{:S(2)}, u32[]{:S(2)}) %collective-permute-start.51) | collective-permute-done | bytes 8224 | tf_op jit(solution)/shard_map/ppermute | solution.py:646
  108.0 2.9 %collective-permute-start.54 = (f32[4,4,256]{2,1,0:T(4,128)S(1)}, f32[4,4,256]{2,1,0:T(4,128)S(1)}, u32[]{:S(2)}, u32[]{:S(2)}) collective-permute-start(f32[4,4,256]{2,1,0:T(4,128)S(1)} %get-tuple-element.264), channel_id=1, source_target_pairs={{0,4},{4,0},{8,12},{12,8},{16,20},{20,16},{24,28},{28,24},{1,5},{5... | collective-permute-start | bytes 49160 | tf_op jit(solution)/shard_map/ppermute | solution.py:652
  110.9 1.7 %collective-permute-done.54.refs_4_ = f32[4,4,256]{2,1,0:T(4,128)S(1)} collective-permute-done((f32[4,4,256]{2,1,0:T(4,128)S(1)}, f32[4,4,256]{2,1,0:T(4,128)S(1)}, u32[]{:S(2)}, u32[]{:S(2)}) %collective-permute-start.54) | collective-permute-done | bytes 16416 | tf_op jit(solution)/shard_map/ppermute | solution.py:652
  112.6 2.3 %shard_map.172 = f32[4,128,128]{2,1,0:T(8,128)} custom-call(s32[9]{0:T(128)S(4)} %get-tuple-element.135.refs_0_, f32[11,136,256]{2,1,0:T(8,128)S(1)} %copy-done.2, f32[4,128,256]{2,1,0:T(8,128)S(1)} %get-tuple-element.262.refs_2_, f32[4,4,256]{2,1,0:T(4,128)S(1)} %collective-permute-done.53.refs_3_, f32[4,4,256]{2,1,0:T(4,128)S(1)} %collective-permute-done.54.refs_4_), custom_call_target="tpu_custom_call" | custom-call | bytes 7000000 | tf_op jit(solution)/shard_map/pallas_call | solution.py:63
  (122 shorter events, 37.1 us)
Async XLA Ops:
  1.2 11.3 %collective-permute-start.8 = (f32[16,4,128]{2,1,0:T(4,128)S(1)}, f32[16,4,128]{2,1,0:T(4,128)S(1)}, u32[]{:S(2)}, u32[]{:S(2)}) collective-permute-start(f32[16,4,128]{2,1,0:T(4,128)S(1)} %get-tuple-element.156), channel_id=1, source_target_pairs={{0,16},{4,20},{8,24},{12,28},{16,0},{20,4},{24,8},{28,12},{1,17},{... | collective-permute-start | bytes 98312 | tf_op jit(solution)/shard_map/ppermute | solution.py:698
  5.3 3.9 %collective-permute-start = (f32[6,4,128]{2,1,0:T(4,128)S(1)}, f32[6,4,128]{2,1,0:T(4,128)S(1)}, u32[]{:S(2)}, u32[]{:S(2)}) collective-permute-start(f32[6,4,128]{2,1,0:T(4,128)S(1)} %get-tuple-element.137), channel_id=1, source_target_pairs={{1,2},{2,1},{0,3},{3,0},{5,6},{6,5},{4,7},{7,4},{9,10},{10,9},{8,1... | collective-permute-start | bytes 36872 | tf_op jit(solution)/shard_map/ppermute | solution.py:646
  6.0 3.2 %collective-permute-start.1 = (f32[6,4,128]{2,1,0:T(4,128)S(1)}, f32[6,4,128]{2,1,0:T(4,128)S(1)}, u32[]{:S(2)}, u32[]{:S(2)}) collective-permute-start(f32[6,4,128]{2,1,0:T(4,128)S(1)} %get-tuple-element.144), channel_id=1, source_target_pairs={{0,1},{1,0},{2,3},{3,2},{4,5},{5,4},{6,7},{7,6},{8,9},{9,8},{10,11... | collective-permute-start | bytes 36872 | tf_op jit(solution)/shard_map/ppermute | solution.py:647
  9.4 5.0 %collective-permute-start.2 = (f32[6,4,256]{2,1,0:T(4,128)S(1)}, f32[6,4,256]{2,1,0:T(4,128)S(1)}, u32[]{:S(2)}, u32[]{:S(2)}) collective-permute-start(f32[6,4,256]{2,1,0:T(4,128)S(1)} %get-tuple-element.146), channel_id=1, source_target_pairs={{4,8},{5,9},{6,10},{7,11},{8,4},{9,5},{10,6},{11,7},{12,16},{13,17... | collective-permute-start | bytes 73736 | tf_op jit(solution)/shard_map/ppermute | solution.py:651
  9.4 4.9 %collective-permute-start.3 = (f32[6,4,256]{2,1,0:T(4,128)S(1)}, f32[6,4,256]{2,1,0:T(4,128)S(1)}, u32[]{:S(2)}, u32[]{:S(2)}) collective-permute-start(f32[6,4,256]{2,1,0:T(4,128)S(1)} %get-tuple-element.147.refs_1_), channel_id=1, source_target_pairs={{0,4},{4,0},{8,12},{12,8},{16,20},{20,16},{24,28},{28,24},{1,5},{5... | collective-permute-start | bytes 73736 | tf_op jit(solution)/shard_map/ppermute | solution.py:652
  12.5 11.4 %collective-permute-start.9 = (f32[32,4,128]{2,1,0:T(4,128)S(1)}, f32[32,4,128]{2,1,0:T(4,128)S(1)}, u32[]{:S(2)}, u32[]{:S(2)}) collective-permute-start(f32[32,4,128]{2,1,0:T(4,128)S(1)} %pad_maximum_fusion.refs_10_), channel_id=1, source_target_pairs={{0,8},{4,12},{8,0},{12,4},{16,24},{20,28},{24,16},{28,20},{1,9},{5... | collective-permute-start | bytes 196616 | tf_op jit(solution)/shard_map/ppermute | solution.py:698
  17.0 6.0 %collective-permute-start.4 = (f32[21,4,128]{2,1,0:T(4,128)S(1)}, f32[21,4,128]{2,1,0:T(4,128)S(1)}, u32[]{:S(2)}, u32[]{:S(2)}) collective-permute-start(f32[21,4,128]{2,1,0:T(4,128)S(1)} %get-tuple-element.154.refs_5_.refs_1_), channel_id=1, source_target_pairs={{4,8},{5,9},{6,10},{7,11},{8,4},{9,5},{10,6},{11,7},{12,16},{13,17... | collective-permute-start | bytes 129032 | tf_op jit(solution)/shard_map/ppermute | solution.py:651
  17.1 5.9 %collective-permute-start.5 = (f32[21,4,128]{2,1,0:T(4,128)S(1)}, f32[21,4,128]{2,1,0:T(4,128)S(1)}, u32[]{:S(2)}, u32[]{:S(2)}) collective-permute-start(f32[21,4,128]{2,1,0:T(4,128)S(1)} %get-tuple-element.154.refs_5_.refs_1_), channel_id=1, source_target_pairs={{0,4},{4,0},{8,12},{12,8},{16,20},{20,16},{24,28},{28,24},{1,5},{5... | collective-permute-start | bytes 129032 | tf_op jit(solution)/shard_map/ppermute | solution.py:652
  20.5 3.4 %collective-permute-start.6 = (f32[21,4,128]{2,1,0:T(4,128)S(1)}, f32[21,4,128]{2,1,0:T(4,128)S(1)}, u32[]{:S(2)}, u32[]{:S(2)}) collective-permute-start(f32[21,4,128]{2,1,0:T(4,128)S(1)} %get-tuple-element.154.refs_5_.refs_1_), channel_id=1, source_target_pairs={{1,2},{2,1},{0,3},{3,0},{5,6},{6,5},{4,7},{7,4},{9,10},{10,9},{8,1... | collective-permute-start | bytes 129032 | tf_op jit(solution)/shard_map/ppermute | solution.py:646
  20.5 3.4 %collective-permute-start.7 = (f32[21,4,128]{2,1,0:T(4,128)S(1)}, f32[21,4,128]{2,1,0:T(4,128)S(1)}, u32[]{:S(2)}, u32[]{:S(2)}) collective-permute-start(f32[21,4,128]{2,1,0:T(4,128)S(1)} %get-tuple-element.154.refs_5_.refs_1_), channel_id=1, source_target_pairs={{0,1},{1,0},{2,3},{3,2},{4,5},{5,4},{6,7},{7,6},{8,9},{9,8},{10,11... | collective-permute-start | bytes 129032 | tf_op jit(solution)/shard_map/ppermute | solution.py:647
  25.2 4.7 %collective-permute-start.11 = (f32[48,4,128]{2,1,0:T(4,128)S(1)}, f32[48,4,128]{2,1,0:T(4,128)S(1)}, u32[]{:S(2)}, u32[]{:S(2)}) collective-permute-start(f32[48,4,128]{2,1,0:T(4,128)S(1)} %get-tuple-element.163.refs_11_), channel_id=1, source_target_pairs={{0,4},{4,0},{8,12},{12,8},{16,20},{20,16},{24,28},{28,24},{1,5},{5... | collective-permute-start | bytes 294920 | tf_op jit(solution)/shard_map/ppermute | solution.py:652
  25.8 4.4 %collective-permute-start.12 = (f32[48,4,128]{2,1,0:T(4,128)S(1)}, f32[48,4,128]{2,1,0:T(4,128)S(1)}, u32[]{:S(2)}, u32[]{:S(2)}) collective-permute-start(f32[48,4,128]{2,1,0:T(4,128)S(1)} %get-tuple-element.164.refs_12_), channel_id=1, source_target_pairs={{1,2},{2,1},{0,3},{3,0},{5,6},{6,5},{4,7},{7,4},{9,10},{10,9},{8,1... | collective-permute-start | bytes 294920 | tf_op jit(solution)/shard_map/ppermute | solution.py:646
  31.2 6.8 %collective-permute-start.15 = (f32[80,4,128]{2,1,0:T(4,128)S(1)}, f32[80,4,128]{2,1,0:T(4,128)S(1)}, u32[]{:S(2)}, u32[]{:S(2)}) collective-permute-start(f32[80,4,128]{2,1,0:T(4,128)S(1)} %get-tuple-element.171.refs_3_), channel_id=1, source_target_pairs={{0,4},{4,0},{8,12},{12,8},{16,20},{20,16},{24,28},{28,24},{1,5},{5... | collective-permute-start | bytes 491528 | tf_op jit(solution)/shard_map/ppermute | solution.py:652
  33.7 6.4 %collective-permute-start.16 = (f32[80,4,128]{2,1,0:T(4,128)S(1)}, f32[80,4,128]{2,1,0:T(4,128)S(1)}, u32[]{:S(2)}, u32[]{:S(2)}) collective-permute-start(f32[80,4,128]{2,1,0:T(4,128)S(1)} %get-tuple-element.172.refs_1_), channel_id=1, source_target_pairs={{1,2},{2,1},{0,3},{3,0},{5,6},{6,5},{4,7},{7,4},{9,10},{10,9},{8,1... | collective-permute-start | bytes 491528 | tf_op jit(solution)/shard_map/ppermute | solution.py:646
  41.5 11.8 %collective-permute-start.26 = (f32[256,4,128]{2,1,0:T(4,128)S(1)}, f32[256,4,128]{2,1,0:T(4,128)S(1)}, u32[]{:S(2)}, u32[]{:S(2)}) collective-permute-start(f32[256,4,128]{2,1,0:T(4,128)S(1)} %shard_map.160.refs_1_), channel_id=1, source_target_pairs={{0,1},{1,0},{2,3},{3,2},{4,5},{5,4},{6,7},{7,6},{8,9},{9,8},{10,11... | collective-permute-start | bytes 1572872 | tf_op jit(solution)/shard_map/ppermute | solution.py:868
  41.6 6.0 %collective-permute-start.18 = (f32[4,4,128]{2,1,0:T(4,128)S(1)}, f32[4,4,128]{2,1,0:T(4,128)S(1)}, u32[]{:S(2)}, u32[]{:S(2)}) collective-permute-start(f32[4,4,128]{2,1,0:T(4,128)S(1)} %get-tuple-element.179.refs_2_.refs_4_.refs_0_), channel_id=1, source_target_pairs={{4,8},{5,9},{6,10},{7,11},{8,4},{9,5},{10,6},{11,7},{12,16},{13,17... | collective-permute-start | bytes 24584 | tf_op jit(solution)/shard_map/ppermute | solution.py:651
  42.1 5.5 %collective-permute-start.19 = (f32[4,4,128]{2,1,0:T(4,128)S(1)}, f32[4,4,128]{2,1,0:T(4,128)S(1)}, u32[]{:S(2)}, u32[]{:S(2)}) collective-permute-start(f32[4,4,128]{2,1,0:T(4,128)S(1)} %get-tuple-element.179.refs_2_.refs_4_.refs_0_), channel_id=1, source_target_pairs={{0,4},{4,0},{8,12},{12,8},{16,20},{20,16},{24,28},{28,24},{1,5},{5... | collective-permute-start | bytes 24584 | tf_op jit(solution)/shard_map/ppermute | solution.py:652
  48.3 3.7 %collective-permute-start.23 = (f32[4,4,128]{2,1,0:T(4,128)S(1)}, f32[4,4,128]{2,1,0:T(4,128)S(1)}, u32[]{:S(2)}, u32[]{:S(2)}) collective-permute-start(f32[4,4,128]{2,1,0:T(4,128)S(1)} %get-tuple-element.198.refs_4_), channel_id=1, source_target_pairs={{0,4},{4,0},{8,12},{12,8},{16,20},{20,16},{24,28},{28,24},{1,5},{5... | collective-permute-start | bytes 24584 | tf_op jit(solution)/shard_map/ppermute | solution.py:652
  53.3 3.7 %collective-permute-start.27 = (f32[4,4,128]{2,1,0:T(4,128)S(1)}, f32[4,4,128]{2,1,0:T(4,128)S(1)}, u32[]{:S(2)}, u32[]{:S(2)}) collective-permute-start(f32[4,4,128]{2,1,0:T(4,128)S(1)} %get-tuple-element.207.refs_6_), channel_id=1, source_target_pairs={{4,8},{5,9},{6,10},{7,11},{8,4},{9,5},{10,6},{11,7},{12,16},{13,17... | collective-permute-start | bytes 24584 | tf_op jit(solution)/shard_map/ppermute | solution.py:651
  53.4 4.0 %collective-permute-start.28 = (f32[4,4,128]{2,1,0:T(4,128)S(1)}, f32[4,4,128]{2,1,0:T(4,128)S(1)}, u32[]{:S(2)}, u32[]{:S(2)}) collective-permute-start(f32[4,4,128]{2,1,0:T(4,128)S(1)} %get-tuple-element.207.refs_6_), channel_id=1, source_target_pairs={{0,4},{4,0},{8,12},{12,8},{16,20},{20,16},{24,28},{28,24},{1,5},{5... | collective-permute-start | bytes 24584 | tf_op jit(solution)/shard_map/ppermute | solution.py:652
  72.3 3.7 %collective-permute-start.32 = (f32[4,4,128]{2,1,0:T(4,128)S(1)}, f32[4,4,128]{2,1,0:T(4,128)S(1)}, u32[]{:S(2)}, u32[]{:S(2)}) collective-permute-start(f32[4,4,128]{2,1,0:T(4,128)S(1)} %get-tuple-element.229.refs_4_), channel_id=1, source_target_pairs={{0,4},{4,0},{8,12},{12,8},{16,20},{20,16},{24,28},{28,24},{1,5},{5... | collective-permute-start | bytes 24584 | tf_op jit(solution)/shard_map/ppermute | solution.py:652
  77.8 3.7 %collective-permute-start.36 = (f32[4,4,128]{2,1,0:T(4,128)S(1)}, f32[4,4,128]{2,1,0:T(4,128)S(1)}, u32[]{:S(2)}, u32[]{:S(2)}) collective-permute-start(f32[4,4,128]{2,1,0:T(4,128)S(1)} %get-tuple-element.238.refs_4_), channel_id=1, source_target_pairs={{0,4},{4,0},{8,12},{12,8},{16,20},{20,16},{24,28},{28,24},{1,5},{5... | collective-permute-start | bytes 24584 | tf_op jit(solution)/shard_map/ppermute | solution.py:652
  83.4 3.9 %collective-permute-start.40 = (f32[4,4,128]{2,1,0:T(4,128)S(1)}, f32[4,4,128]{2,1,0:T(4,128)S(1)}, u32[]{:S(2)}, u32[]{:S(2)}) collective-permute-start(f32[4,4,128]{2,1,0:T(4,128)S(1)} %get-tuple-element.247.refs_6_), channel_id=1, source_target_pairs={{0,4},{4,0},{8,12},{12,8},{16,20},{20,16},{24,28},{28,24},{1,5},{5... | collective-permute-start | bytes 24584 | tf_op jit(solution)/shard_map/ppermute | solution.py:652
  90.5 3.9 %collective-permute-start.43 = (f32[16,4,128]{2,1,0:T(4,128)S(1)}, f32[16,4,128]{2,1,0:T(4,128)S(1)}, u32[]{:S(2)}, u32[]{:S(2)}) collective-permute-start(f32[16,4,128]{2,1,0:T(4,128)S(1)} %get-tuple-element.253.refs_2_.refs_5_), channel_id=1, source_target_pairs={{4,8},{5,9},{6,10},{7,11},{8,4},{9,5},{10,6},{11,7},{12,16},{13,17... | collective-permute-start | bytes 98312 | tf_op jit(solution)/shard_map/ppermute | solution.py:651
  90.5 4.5 %collective-permute-start.44 = (f32[16,4,128]{2,1,0:T(4,128)S(1)}, f32[16,4,128]{2,1,0:T(4,128)S(1)}, u32[]{:S(2)}, u32[]{:S(2)}) collective-permute-start(f32[16,4,128]{2,1,0:T(4,128)S(1)} %get-tuple-element.253.refs_2_.refs_5_), channel_id=1, source_target_pairs={{0,4},{4,0},{8,12},{12,8},{16,20},{20,16},{24,28},{28,24},{1,5},{5... | collective-permute-start | bytes 98312 | tf_op jit(solution)/shard_map/ppermute | solution.py:652
  93.2 3.3 %collective-permute-start.45 = (f32[16,4,128]{2,1,0:T(4,128)S(1)}, f32[16,4,128]{2,1,0:T(4,128)S(1)}, u32[]{:S(2)}, u32[]{:S(2)}) collective-permute-start(f32[16,4,128]{2,1,0:T(4,128)S(1)} %get-tuple-element.253.refs_2_.refs_5_), channel_id=1, source_target_pairs={{1,2},{2,1},{0,3},{3,0},{5,6},{6,5},{4,7},{7,4},{9,10},{10,9},{8,1... | collective-permute-start | bytes 98312 | tf_op jit(solution)/shard_map/ppermute | solution.py:646
  93.2 3.3 %collective-permute-start.46 = (f32[16,4,128]{2,1,0:T(4,128)S(1)}, f32[16,4,128]{2,1,0:T(4,128)S(1)}, u32[]{:S(2)}, u32[]{:S(2)}) collective-permute-start(f32[16,4,128]{2,1,0:T(4,128)S(1)} %get-tuple-element.253.refs_2_.refs_5_), channel_id=1, source_target_pairs={{0,1},{1,0},{2,3},{3,2},{4,5},{5,4},{6,7},{7,6},{8,9},{9,8},{10,11... | collective-permute-start | bytes 98312 | tf_op jit(solution)/shard_map/ppermute | solution.py:647
  97.5 3.6 %collective-permute-start.47 = (f32[16,4,128]{2,1,0:T(4,128)S(1)}, f32[16,4,128]{2,1,0:T(4,128)S(1)}, u32[]{:S(2)}, u32[]{:S(2)}) collective-permute-start(f32[16,4,128]{2,1,0:T(4,128)S(1)} %get-tuple-element.258.refs_2_.refs_7_), channel_id=1, source_target_pairs={{4,8},{5,9},{6,10},{7,11},{8,4},{9,5},{10,6},{11,7},{12,16},{13,17... | collective-permute-start | bytes 98312 | tf_op jit(solution)/shard_map/ppermute | solution.py:651
  97.5 4.0 %collective-permute-start.48 = (f32[16,4,128]{2,1,0:T(4,128)S(1)}, f32[16,4,128]{2,1,0:T(4,128)S(1)}, u32[]{:S(2)}, u32[]{:S(2)}) collective-permute-start(f32[16,4,128]{2,1,0:T(4,128)S(1)} %get-tuple-element.258.refs_2_.refs_7_), channel_id=1, source_target_pairs={{0,4},{4,0},{8,12},{12,8},{16,20},{20,16},{24,28},{28,24},{1,5},{5... | collective-permute-start | bytes 98312 | tf_op jit(solution)/shard_map/ppermute | solution.py:652
  99.6 3.3 %collective-permute-start.49 = (f32[16,4,128]{2,1,0:T(4,128)S(1)}, f32[16,4,128]{2,1,0:T(4,128)S(1)}, u32[]{:S(2)}, u32[]{:S(2)}) collective-permute-start(f32[16,4,128]{2,1,0:T(4,128)S(1)} %get-tuple-element.258.refs_2_.refs_7_), channel_id=1, source_target_pairs={{1,2},{2,1},{0,3},{3,0},{5,6},{6,5},{4,7},{7,4},{9,10},{10,9},{8,1... | collective-permute-start | bytes 98312 | tf_op jit(solution)/shard_map/ppermute | solution.py:646
  99.6 3.3 %collective-permute-start.50 = (f32[16,4,128]{2,1,0:T(4,128)S(1)}, f32[16,4,128]{2,1,0:T(4,128)S(1)}, u32[]{:S(2)}, u32[]{:S(2)}) collective-permute-start(f32[16,4,128]{2,1,0:T(4,128)S(1)} %get-tuple-element.258.refs_2_.refs_7_), channel_id=1, source_target_pairs={{0,1},{1,0},{2,3},{3,2},{4,5},{5,4},{6,7},{7,6},{8,9},{9,8},{10,11... | collective-permute-start | bytes 98312 | tf_op jit(solution)/shard_map/ppermute | solution.py:647
  108.0 4.6 %collective-permute-start.54 = (f32[4,4,256]{2,1,0:T(4,128)S(1)}, f32[4,4,256]{2,1,0:T(4,128)S(1)}, u32[]{:S(2)}, u32[]{:S(2)}) collective-permute-start(f32[4,4,256]{2,1,0:T(4,128)S(1)} %get-tuple-element.264), channel_id=1, source_target_pairs={{0,4},{4,0},{8,12},{12,8},{16,20},{20,16},{24,28},{28,24},{1,5},{5... | collective-permute-start | bytes 49160 | tf_op jit(solution)/shard_map/ppermute | solution.py:652
  (30 other events, 127.0 us)

commit v9 on v8

--- a/solution.py
+++ b/solution.py
@@ -700,9 +700,10 @@
     def gather_step(anchor):
         step = alone[len(done)]
         merged = held if len(held) == 1 else [jnp.concatenate(held, axis=0)]
-        merged, _ = lax.optimization_barrier((merged, anchor))
+        merged, anchor = lax.optimization_barrier((merged, anchor))
         held[:] = merged + [swap(m, *step) for m in merged]
         done.append(step)
+        return anchor
 
     rim = sds((cols + 2, RIM, LANES))
     flags = sds((LEVEL3 + 1,), jnp.int32)
@@ -761,7 +762,7 @@
         specs=[SMEM] + [VMEM] * 3,
     )
     if alone:
-        gather_step(first)
+        first, second = gather_step((first, second))
     o2, o1 = exchange_wide(first, second, route)
 
     def split_half(i, after):

time: 115 us -> 115 us (level)
  no operation moved by 1% of the time
where the time goes in v9:
time: 115 us
  starting transfers between devices  47.7 us (41%)
  waiting for transfers between devices  28.3 us (25%)
  Pallas kernels  28.1 us (24%)
  blocking collectives  10.2 us (9%)
    ppermute x13, starting transfers between devices, exchange_wide(): return (second, lax.ppermute(first, 'wide', route[2]))  29.9 us
    pallas_call x28, Pallas kernels, call(): pl.pallas_call(inner, out_shape=shapes, in_specs=specs[::ORDER], out_spec...  28.1 us
    ppermute x13, waiting for transfers between devices, exchange_narrow(): second = lax.ppermute(second, 'narrow', route[1])  15.2 us
    ppermute x13, waiting for transfers between devices, exchange_wide(): return (second, lax.ppermute(first, 'wide', route[2]))  11.5 us
    all_to_all x1, blocking collectives, body(): pieces = lax.all_to_all(out3, ('wide', 'narrow'), 0, 0)  10.2 us
    ppermute x13, starting transfers between devices, exchange_narrow(): return (second, lax.ppermute(first, 'narrow', route[0]))  9.26 us
    ppermute x2, starting transfers between devices, swap(): lax.ppermute(x, axis, [(i, i ^ step) for i in range(lax.axis_size(axis))])  4.21 us
    ppermute x13, starting transfers between devices, exchange_wide(): second = lax.ppermute(second, ('wide', 'narrow'), route[3])  2.89 us
  transfers between devices with their start and end apart: 55, of which 26 were waited for; matrix products, arithmetic and copies ran while one was open for 0% of the time, Pallas kernels for 11%

profile of v9, /device:TPU:0, one launch (start us, length us, event | category | flops | bytes accessed | tf_op | source)
XLA Modules:
  0.0 115.1 jit_solution(16392120100370562235)
XLA Ops:
  1.2 4.1 %collective-permute-start.2 = (f32[16,4,128]{2,1,0:T(4,128)S(1)}, f32[16,4,128]{2,1,0:T(4,128)S(1)}, u32[]{:S(2)}, u32[]{:S(2)}) collective-permute-start(f32[16,4,128]{2,1,0:T(4,128)S(1)} %get-tuple-element.149), channel_id=1, source_target_pairs={{0,16},{4,20},{8,24},{12,28},{16,0},{20,4},{24,8},{28,12},{1,17},{... | collective-permute-start | bytes 98312 | tf_op jit(solution)/shard_map/ppermute | solution.py:698
  6.9 2.2 %shard_map.146 = (s32[4,16]{1,0:T(4,128)S(4)}, s32[4,4]{1,0:T(4,128)S(4)}, f32[16,1,128]{2,1,0:T(1,128)S(1)}, bf16[4,256,512]{2,1,0:T(8,128)(2,1)S(1)}, f32[4,1,128]{2,1,0:T(1,128)S(1)}) custom-call(s32[9]{0:T(128)S(4)} %get-tuple-element.137.refs_0_, s32[3,16]{1,0:T(4,128)} %bitcast.8, s32[3,16]{1,0:T(4,128)} %bitcast.9, s32[4,3]{1,0:T(4,128)} %refs_3_.3, ...), custom_call_target="tpu_custom_call" | custom-call | bytes 7000000 | tf_op jit(solution)/shard_map/pallas_call | solution.py:63
  9.5 3.0 %collective-permute-start.4 = (f32[6,4,256]{2,1,0:T(4,128)S(1)}, f32[6,4,256]{2,1,0:T(4,128)S(1)}, u32[]{:S(2)}, u32[]{:S(2)}) collective-permute-start(f32[6,4,256]{2,1,0:T(4,128)S(1)} %get-tuple-element.153.refs_1_), channel_id=1, source_target_pairs={{0,4},{4,0},{8,12},{12,8},{16,20},{20,16},{24,28},{28,24},{1,5},{5... | collective-permute-start | bytes 73736 | tf_op jit(solution)/shard_map/ppermute | solution.py:652
  12.6 1.6 %shard_map.148.refs_8_ = bf16[8,256,512]{2,1,0:T(8,128)(2,1)S(1)} custom-call(f32[16,4,128,128]{3,2,1,0:T(8,128)} %refs_0_.5, f32[6,4,256]{2,1,0:T(4,128)S(1)} %get-tuple-element.153.refs_1_), custom_call_target="tpu_custom_call" | custom-call | bytes 7000000 | tf_op jit(solution)/shard_map/pallas_call | solution.py:63
  14.3 2.6 %shard_map.149 = (f32[11,136,256]{2,1,0:T(8,128)}, f32[16,4,128]{2,1,0:T(4,128)S(1)}, f32[21,4,128]{2,1,0:T(4,128)S(1)}, bf16[8,256,512]{2,1,0:T(8,128)(2,1)S(1)}, f32[16,1,128]{2,1,0:T(1,128)S(1)}) custom-call(s32[9]{0:T(128)S(4)} %get-tuple-element.137.refs_0_, ...), custom_call_target="tpu_custom_call", output_to_operand_aliasing={{3}: (8, {}), {4}: (5, {})} | custom-call | bytes 24500000 | tf_op jit(solution)/shard_map/pallas_call | solution.py:63
  17.1 3.4 %collective-permute-start.6 = (f32[21,4,128]{2,1,0:T(4,128)S(1)}, f32[21,4,128]{2,1,0:T(4,128)S(1)}, u32[]{:S(2)}, u32[]{:S(2)}) collective-permute-start(f32[21,4,128]{2,1,0:T(4,128)S(1)} %get-tuple-element.160.refs_5_.refs_1_), channel_id=1, source_target_pairs={{0,4},{4,0},{8,12},{12,8},{16,20},{20,16},{24,28},{28,24},{1,5},{5... | collective-permute-start | bytes 129032 | tf_op jit(solution)/shard_map/ppermute | solution.py:652
  21.3 1.6 %shard_map.150.refs_2_ = bf16[8,256,512]{2,1,0:T(8,128)(2,1)S(1)} custom-call(f32[16,4,128,128]{3,2,1,0:T(8,128)} %refs_0_.5, f32[16,4,128]{2,1,0:T(4,128)S(1)} %get-tuple-element.158.refs_1_.refs_4_), custom_call_target="tpu_custom_call" | custom-call | bytes 7000000 | tf_op jit(solution)/shard_map/pallas_call | solution.py:63
  27.9 2.0 %collective-permute-done.11.refs_7_ = f32[48,4,128]{2,1,0:T(4,128)S(1)} collective-permute-done((f32[48,4,128]{2,1,0:T(4,128)S(1)}, f32[48,4,128]{2,1,0:T(4,128)S(1)}, u32[]{:S(2)}, u32[]{:S(2)}) %collective-permute-start.11) | collective-permute-done | bytes 98336 | tf_op jit(solution)/shard_map/ppermute | solution.py:652
  31.1 2.5 %collective-permute-start.15 = (f32[80,4,128]{2,1,0:T(4,128)S(1)}, f32[80,4,128]{2,1,0:T(4,128)S(1)}, u32[]{:S(2)}, u32[]{:S(2)}) collective-permute-start(f32[80,4,128]{2,1,0:T(4,128)S(1)} %get-tuple-element.175.refs_3_), channel_id=1, source_target_pairs={{0,4},{4,0},{8,12},{12,8},{16,20},{20,16},{24,28},{28,24},{1,5},{5... | collective-permute-start | bytes 491528 | tf_op jit(solution)/shard_map/ppermute | solution.py:652
  35.7 2.3 %collective-permute-done.15.refs_8_.refs_4_ = f32[80,4,128]{2,1,0:T(4,128)S(1)} collective-permute-done((f32[80,4,128]{2,1,0:T(4,128)S(1)}, f32[80,4,128]{2,1,0:T(4,128)S(1)}, u32[]{:S(2)}, u32[]{:S(2)}) %collective-permute-start.15) | collective-permute-done | bytes 163872 | tf_op jit(solution)/shard_map/ppermute | solution.py:652
  38.0 2.0 %collective-permute-done.16.refs_9_.refs_2_ = f32[80,4,128]{2,1,0:T(4,128)S(1)} collective-permute-done((f32[80,4,128]{2,1,0:T(4,128)S(1)}, f32[80,4,128]{2,1,0:T(4,128)S(1)}, u32[]{:S(2)}, u32[]{:S(2)}) %collective-permute-start.16) | collective-permute-done | bytes 163872 | tf_op jit(solution)/shard_map/ppermute | solution.py:646
  42.1 2.6 %collective-permute-start.19 = (f32[4,4,128]{2,1,0:T(4,128)S(1)}, f32[4,4,128]{2,1,0:T(4,128)S(1)}, u32[]{:S(2)}, u32[]{:S(2)}) collective-permute-start(f32[4,4,128]{2,1,0:T(4,128)S(1)} %get-tuple-element.183.refs_2_.refs_4_.refs_0_), channel_id=1, source_target_pairs={{0,4},{4,0},{8,12},{12,8},{16,20},{20,16},{24,28},{28,24},{1,5},{5... | collective-permute-start | bytes 24584 | tf_op jit(solution)/shard_map/ppermute | solution.py:652
  45.7 2.0 %shard_map.157 = (bf16[8,256,512]{2,1,0:T(8,128)(2,1)}, bf16[8,256,512]{2,1,0:T(8,128)(2,1)}, bf16[8,256,512]{2,1,0:T(8,128)(2,1)S(1)}, f32[16,1,128]{2,1,0:T(1,...) custom-call(bf16[8,256,512]{2,1,0:T(8,128)(2,1)S(1)} %get-tuple-elem, ...), custom_call_target="tpu_custom_call", output_to_operand_aliasing={{2}: (0, {}), {3}: (3, {}), {4}: (4, {}), {5}: (1, {}), {6}... | custom-call | bytes 7000000 | tf_op jit(solution)/shard_map/pallas_call | solution.py:63
  48.3 1.8 %collective-permute-start.23 = (f32[4,4,128]{2,1,0:T(4,128)S(1)}, f32[4,4,128]{2,1,0:T(4,128)S(1)}, u32[]{:S(2)}, u32[]{:S(2)}) collective-permute-start(f32[4,4,128]{2,1,0:T(4,128)S(1)} %get-tuple-element.202.refs_4_), channel_id=1, source_target_pairs={{0,4},{4,0},{8,12},{12,8},{16,20},{20,16},{24,28},{28,24},{1,5},{5... | collective-permute-start | bytes 24584 | tf_op jit(solution)/shard_map/ppermute | solution.py:652
  53.7 2.1 %collective-permute-start.28 = (f32[4,4,128]{2,1,0:T(4,128)S(1)}, f32[4,4,128]{2,1,0:T(4,128)S(1)}, u32[]{:S(2)}, u32[]{:S(2)}) collective-permute-start(f32[4,4,128]{2,1,0:T(4,128)S(1)} %get-tuple-element.211.refs_6_), channel_id=1, source_target_pairs={{0,4},{4,0},{8,12},{12,8},{16,20},{20,16},{24,28},{28,24},{1,5},{5... | collective-permute-start | bytes 24584 | tf_op jit(solution)/shard_map/ppermute | solution.py:652
  57.5 1.4 %collective-permute-done.29.refs_9_ = f32[4,4,128]{2,1,0:T(4,128)S(1)} collective-permute-done((f32[4,4,128]{2,1,0:T(4,128)S(1)}, f32[4,4,128]{2,1,0:T(4,128)S(1)}, u32[]{:S(2)}, u32[]{:S(2)}) %collective-permute-start.29) | collective-permute-done | bytes 8224 | tf_op jit(solution)/shard_map/ppermute | solution.py:646
  59.6 10.2 %all_to_all.5.refs_2_ = f32[32,4,128]{2,1,0:T(4,128)S(1)} all-to-all(f32[32,4,128]{2,1,0:T(4,128)S(1)} %get-tuple-element.221), channel_id=1, replica_groups=mesh['wide'=8,'narrow'=4] {'wide','narrow'}, dimensions={0} | all-to-all | bytes 131072 | tf_op jit(solution)/shard_map/all_to_all | solution.py:918
  69.9 2.2 %shard_map.163 = (f32[4,4,128]{2,1,0:T(4,128)S(1)}, f32[16,1,128]{2,1,0:T(1,128)S(1)}, f32[16,4,128]{2,1,0:T(4,128)S(1)}, f32[16,4,128]{2,1,0:T(4,128)S(1)}, s32...) custom-call(s32[9]{0:T(128)S(4)} %get-tuple-element.137.refs_0_, ...), custom_call_target="tpu_custom_call", output_to_operand_aliasing={{1}: (8, {}), {2}: (9, {}), {3}: (10, {}), {4}: (7, {}), {5... | custom-call | bytes 10500000 | tf_op jit(solution)/shard_map/pallas_call | solution.py:63
  72.3 2.0 %collective-permute-start.32 = (f32[4,4,128]{2,1,0:T(4,128)S(1)}, f32[4,4,128]{2,1,0:T(4,128)S(1)}, u32[]{:S(2)}, u32[]{:S(2)}) collective-permute-start(f32[4,4,128]{2,1,0:T(4,128)S(1)} %get-tuple-element.233.refs_4_), channel_id=1, source_target_pairs={{0,4},{4,0},{8,12},{12,8},{16,20},{20,16},{24,28},{28,24},{1,5},{5... | collective-permute-start | bytes 24584 | tf_op jit(solution)/shard_map/ppermute | solution.py:652
  77.8 2.1 %collective-permute-start.36 = (f32[4,4,128]{2,1,0:T(4,128)S(1)}, f32[4,4,128]{2,1,0:T(4,128)S(1)}, u32[]{:S(2)}, u32[]{:S(2)}) collective-permute-start(f32[4,4,128]{2,1,0:T(4,128)S(1)} %get-tuple-element.242.refs_4_), channel_id=1, source_target_pairs={{0,4},{4,0},{8,12},{12,8},{16,20},{20,16},{24,28},{28,24},{1,5},{5... | collective-permute-start | bytes 24584 | tf_op jit(solution)/shard_map/ppermute | solution.py:652
  81.5 1.4 %collective-permute-done.37.refs_7_ = f32[4,4,128]{2,1,0:T(4,128)S(1)} collective-permute-done((f32[4,4,128]{2,1,0:T(4,128)S(1)}, f32[4,4,128]{2,1,0:T(4,128)S(1)}, u32[]{:S(2)}, u32[]{:S(2)}) %collective-permute-start.37) | collective-permute-done | bytes 8224 | tf_op jit(solution)/shard_map/ppermute | solution.py:646
  83.4 2.3 %collective-permute-start.40 = (f32[4,4,128]{2,1,0:T(4,128)S(1)}, f32[4,4,128]{2,1,0:T(4,128)S(1)}, u32[]{:S(2)}, u32[]{:S(2)}) collective-permute-start(f32[4,4,128]{2,1,0:T(4,128)S(1)} %get-tuple-element.251.refs_6_), channel_id=1, source_target_pairs={{0,4},{4,0},{8,12},{12,8},{16,20},{20,16},{24,28},{28,24},{1,5},{5... | collective-permute-start | bytes 24584 | tf_op jit(solution)/shard_map/ppermute | solution.py:652
  87.3 1.4 %collective-permute-done.41.refs_9_ = f32[4,4,128]{2,1,0:T(4,128)S(1)} collective-permute-done((f32[4,4,128]{2,1,0:T(4,128)S(1)}, f32[4,4,128]{2,1,0:T(4,128)S(1)}, u32[]{:S(2)}, u32[]{:S(2)}) %collective-permute-start.41) | collective-permute-done | bytes 8224 | tf_op jit(solution)/shard_map/ppermute | solution.py:646
  88.8 1.7 %shard_map.166 = (f32[16,4,128]{2,1,0:T(4,128)S(1)}, f32[16,1,128]{2,1,0:T(1,128)S(1)}, f32[16,4,128]{2,1,0:T(4,128)S(1)}, f32[16,4,128]{2,1,0:T(4,128)S(1)}, s3...) custom-call(s32[4,16]{1,0:T(4,128)S(4)} %get-tuple-element.156.refs_, ...), custom_call_target="tpu_custom_call", output_to_operand_aliasing={{1}: (3, {}), {2}: (11, {}), {3}: (4, {}), {4}: (5, {}), {5... | custom-call | bytes 7000000 | tf_op jit(solution)/shard_map/pallas_call | solution.py:63
  90.6 2.6 %collective-permute-start.44 = (f32[16,4,128]{2,1,0:T(4,128)S(1)}, f32[16,4,128]{2,1,0:T(4,128)S(1)}, u32[]{:S(2)}, u32[]{:S(2)}) collective-permute-start(f32[16,4,128]{2,1,0:T(4,128)S(1)} %get-tuple-element.257.refs_2_.refs_5_), channel_id=1, source_target_pairs={{0,4},{4,0},{8,12},{12,8},{16,20},{20,16},{24,28},{28,24},{1,5},{5... | collective-permute-start | bytes 98312 | tf_op jit(solution)/shard_map/ppermute | solution.py:652
  95.1 1.4 %collective-permute-done.45.refs_8_ = f32[16,4,128]{2,1,0:T(4,128)S(1)} collective-permute-done((f32[16,4,128]{2,1,0:T(4,128)S(1)}, f32[16,4,128]{2,1,0:T(4,128)S(1)}, u32[]{:S(2)}, u32[]{:S(2)}) %collective-permute-start.45) | collective-permute-done | bytes 32800 | tf_op jit(solution)/shard_map/ppermute | solution.py:646
  97.6 2.1 %collective-permute-start.48 = (f32[16,4,128]{2,1,0:T(4,128)S(1)}, f32[16,4,128]{2,1,0:T(4,128)S(1)}, u32[]{:S(2)}, u32[]{:S(2)}) collective-permute-start(f32[16,4,128]{2,1,0:T(4,128)S(1)} %get-tuple-element.262.refs_2_.refs_7_), channel_id=1, source_target_pairs={{0,4},{4,0},{8,12},{12,8},{16,20},{20,16},{24,28},{28,24},{1,5},{5... | collective-permute-start | bytes 98312 | tf_op jit(solution)/shard_map/ppermute | solution.py:652
  103.0 1.7 %shard_map.170 = (f32[4,128,128]{2,1,0:T(8,128)S(1)}, f32[4,4,128]{2,1,0:T(4,128)S(1)}, f32[4,4,128]{2,1,0:T(4,128)S(1)}, f32[16,1,128]{2,1,0:T(1,128)S(1)}, f32...) custom-call(s32[9]{0:T(128)S(4)} %get-tuple-element.137.refs_0_, ...), custom_call_target="tpu_custom_call", output_to_operand_aliasing={{3}: (4, {}), {4}: (5, {}), {5}: (1, {}), {6}: (2, {})} | custom-call | bytes 10500000 | tf_op jit(solution)/shard_map/pallas_call | solution.py:63
  105.8 2.0 %collective-permute-done.51.refs_2_ = f32[4,4,128]{2,1,0:T(4,128)S(1)} collective-permute-done((f32[4,4,128]{2,1,0:T(4,128)S(1)}, f32[4,4,128]{2,1,0:T(4,128)S(1)}, u32[]{:S(2)}, u32[]{:S(2)}) %collective-permute-start.51) | collective-permute-done | bytes 8224 | tf_op jit(solution)/shard_map/ppermute | solution.py:646
  108.1 2.9 %collective-permute-start.54 = (f32[4,4,256]{2,1,0:T(4,128)S(1)}, f32[4,4,256]{2,1,0:T(4,128)S(1)}, u32[]{:S(2)}, u32[]{:S(2)}) collective-permute-start(f32[4,4,256]{2,1,0:T(4,128)S(1)} %get-tuple-element.268), channel_id=1, source_target_pairs={{0,4},{4,0},{8,12},{12,8},{16,20},{20,16},{24,28},{28,24},{1,5},{5... | collective-permute-start | bytes 49160 | tf_op jit(solution)/shard_map/ppermute | solution.py:652
  110.9 1.7 %collective-permute-done.54.refs_4_ = f32[4,4,256]{2,1,0:T(4,128)S(1)} collective-permute-done((f32[4,4,256]{2,1,0:T(4,128)S(1)}, f32[4,4,256]{2,1,0:T(4,128)S(1)}, u32[]{:S(2)}, u32[]{:S(2)}) %collective-permute-start.54) | collective-permute-done | bytes 16416 | tf_op jit(solution)/shard_map/ppermute | solution.py:652
  112.7 2.3 %shard_map.172 = f32[4,128,128]{2,1,0:T(8,128)} custom-call(s32[9]{0:T(128)S(4)} %get-tuple-element.137.refs_0_, f32[11,136,256]{2,1,0:T(8,128)S(1)} %copy-done.2, f32[4,128,256]{2,1,0:T(8,128)S(1)} %get-tuple-element.266.refs_2_, f32[4,4,256]{2,1,0:T(4,128)S(1)} %collective-permute-done.53.refs_3_, f32[4,4,256]{2,1,0:T(4,128)S(1)} %collective-permute-done.54.refs_4_), custom_call_target="tpu_custom_call" | custom-call | bytes 7000000 | tf_op jit(solution)/shard_map/pallas_call | solution.py:63
  (122 shorter events, 37.0 us)
Async XLA Ops:
  1.2 8.2 %collective-permute-start.2 = (f32[16,4,128]{2,1,0:T(4,128)S(1)}, f32[16,4,128]{2,1,0:T(4,128)S(1)}, u32[]{:S(2)}, u32[]{:S(2)}) collective-permute-start(f32[16,4,128]{2,1,0:T(4,128)S(1)} %get-tuple-element.149), channel_id=1, source_target_pairs={{0,16},{4,20},{8,24},{12,28},{16,0},{20,4},{24,8},{28,12},{1,17},{... | collective-permute-start | bytes 98312 | tf_op jit(solution)/shard_map/ppermute | solution.py:698
  5.3 3.9 %collective-permute-start = (f32[6,4,128]{2,1,0:T(4,128)S(1)}, f32[6,4,128]{2,1,0:T(4,128)S(1)}, u32[]{:S(2)}, u32[]{:S(2)}) collective-permute-start(f32[6,4,128]{2,1,0:T(4,128)S(1)} %get-tuple-element.139), channel_id=1, source_target_pairs={{1,2},{2,1},{0,3},{3,0},{5,6},{6,5},{4,7},{7,4},{9,10},{10,9},{8,1... | collective-permute-start | bytes 36872 | tf_op jit(solution)/shard_map/ppermute | solution.py:646
  6.0 3.2 %collective-permute-start.1 = (f32[6,4,128]{2,1,0:T(4,128)S(1)}, f32[6,4,128]{2,1,0:T(4,128)S(1)}, u32[]{:S(2)}, u32[]{:S(2)}) collective-permute-start(f32[6,4,128]{2,1,0:T(4,128)S(1)} %get-tuple-element.146), channel_id=1, source_target_pairs={{0,1},{1,0},{2,3},{3,2},{4,5},{5,4},{6,7},{7,6},{8,9},{9,8},{10,11... | collective-permute-start | bytes 36872 | tf_op jit(solution)/shard_map/ppermute | solution.py:647
  9.4 4.9 %collective-permute-start.3 = (f32[6,4,256]{2,1,0:T(4,128)S(1)}, f32[6,4,256]{2,1,0:T(4,128)S(1)}, u32[]{:S(2)}, u32[]{:S(2)}) collective-permute-start(f32[6,4,256]{2,1,0:T(4,128)S(1)} %get-tuple-element.152), channel_id=1, source_target_pairs={{4,8},{5,9},{6,10},{7,11},{8,4},{9,5},{10,6},{11,7},{12,16},{13,17... | collective-permute-start | bytes 73736 | tf_op jit(solution)/shard_map/ppermute | solution.py:651
  9.5 4.8 %collective-permute-start.4 = (f32[6,4,256]{2,1,0:T(4,128)S(1)}, f32[6,4,256]{2,1,0:T(4,128)S(1)}, u32[]{:S(2)}, u32[]{:S(2)}) collective-permute-start(f32[6,4,256]{2,1,0:T(4,128)S(1)} %get-tuple-element.153.refs_1_), channel_id=1, source_target_pairs={{0,4},{4,0},{8,12},{12,8},{16,20},{20,16},{24,28},{28,24},{1,5},{5... | collective-permute-start | bytes 73736 | tf_op jit(solution)/shard_map/ppermute | solution.py:652
  12.5 10.4 %collective-permute-start.9 = (f32[32,4,128]{2,1,0:T(4,128)S(1)}, f32[32,4,128]{2,1,0:T(4,128)S(1)}, u32[]{:S(2)}, u32[]{:S(2)}) collective-permute-start(f32[32,4,128]{2,1,0:T(4,128)S(1)} %pad_maximum_fusion.refs_10_), channel_id=1, source_target_pairs={{0,8},{4,12},{8,0},{12,4},{16,24},{20,28},{24,16},{28,20},{1,9},{5... | collective-permute-start | bytes 196616 | tf_op jit(solution)/shard_map/ppermute | solution.py:698
  17.0 6.0 %collective-permute-start.5 = (f32[21,4,128]{2,1,0:T(4,128)S(1)}, f32[21,4,128]{2,1,0:T(4,128)S(1)}, u32[]{:S(2)}, u32[]{:S(2)}) collective-permute-start(f32[21,4,128]{2,1,0:T(4,128)S(1)} %get-tuple-element.160.refs_5_.refs_1_), channel_id=1, source_target_pairs={{4,8},{5,9},{6,10},{7,11},{8,4},{9,5},{10,6},{11,7},{12,16},{13,17... | collective-permute-start | bytes 129032 | tf_op jit(solution)/shard_map/ppermute | solution.py:651
  17.1 5.9 %collective-permute-start.6 = (f32[21,4,128]{2,1,0:T(4,128)S(1)}, f32[21,4,128]{2,1,0:T(4,128)S(1)}, u32[]{:S(2)}, u32[]{:S(2)}) collective-permute-start(f32[21,4,128]{2,1,0:T(4,128)S(1)} %get-tuple-element.160.refs_5_.refs_1_), channel_id=1, source_target_pairs={{0,4},{4,0},{8,12},{12,8},{16,20},{20,16},{24,28},{28,24},{1,5},{5... | collective-permute-start | bytes 129032 | tf_op jit(solution)/shard_map/ppermute | solution.py:652
  20.5 3.4 %collective-permute-start.7 = (f32[21,4,128]{2,1,0:T(4,128)S(1)}, f32[21,4,128]{2,1,0:T(4,128)S(1)}, u32[]{:S(2)}, u32[]{:S(2)}) collective-permute-start(f32[21,4,128]{2,1,0:T(4,128)S(1)} %get-tuple-element.160.refs_5_.refs_1_), channel_id=1, source_target_pairs={{1,2},{2,1},{0,3},{3,0},{5,6},{6,5},{4,7},{7,4},{9,10},{10,9},{8,1... | collective-permute-start | bytes 129032 | tf_op jit(solution)/shard_map/ppermute | solution.py:646
  20.5 3.4 %collective-permute-start.8 = (f32[21,4,128]{2,1,0:T(4,128)S(1)}, f32[21,4,128]{2,1,0:T(4,128)S(1)}, u32[]{:S(2)}, u32[]{:S(2)}) collective-permute-start(f32[21,4,128]{2,1,0:T(4,128)S(1)} %get-tuple-element.160.refs_5_.refs_1_), channel_id=1, source_target_pairs={{0,1},{1,0},{2,3},{3,2},{4,5},{5,4},{6,7},{7,6},{8,9},{9,8},{10,11... | collective-permute-start | bytes 129032 | tf_op jit(solution)/shard_map/ppermute | solution.py:647
  25.1 4.7 %collective-permute-start.11 = (f32[48,4,128]{2,1,0:T(4,128)S(1)}, f32[48,4,128]{2,1,0:T(4,128)S(1)}, u32[]{:S(2)}, u32[]{:S(2)}) collective-permute-start(f32[48,4,128]{2,1,0:T(4,128)S(1)} %get-tuple-element.167.refs_11_), channel_id=1, source_target_pairs={{0,4},{4,0},{8,12},{12,8},{16,20},{20,16},{24,28},{28,24},{1,5},{5... | collective-permute-start | bytes 294920 | tf_op jit(solution)/shard_map/ppermute | solution.py:652
  25.8 4.4 %collective-permute-start.12 = (f32[48,4,128]{2,1,0:T(4,128)S(1)}, f32[48,4,128]{2,1,0:T(4,128)S(1)}, u32[]{:S(2)}, u32[]{:S(2)}) collective-permute-start(f32[48,4,128]{2,1,0:T(4,128)S(1)} %get-tuple-element.168.refs_12_), channel_id=1, source_target_pairs={{1,2},{2,1},{0,3},{3,0},{5,6},{6,5},{4,7},{7,4},{9,10},{10,9},{8,1... | collective-permute-start | bytes 294920 | tf_op jit(solution)/shard_map/ppermute | solution.py:646
  31.1 6.8 %collective-permute-start.15 = (f32[80,4,128]{2,1,0:T(4,128)S(1)}, f32[80,4,128]{2,1,0:T(4,128)S(1)}, u32[]{:S(2)}, u32[]{:S(2)}) collective-permute-start(f32[80,4,128]{2,1,0:T(4,128)S(1)} %get-tuple-element.175.refs_3_), channel_id=1, source_target_pairs={{0,4},{4,0},{8,12},{12,8},{16,20},{20,16},{24,28},{28,24},{1,5},{5... | collective-permute-start | bytes 491528 | tf_op jit(solution)/shard_map/ppermute | solution.py:652
  33.6 6.4 %collective-permute-start.16 = (f32[80,4,128]{2,1,0:T(4,128)S(1)}, f32[80,4,128]{2,1,0:T(4,128)S(1)}, u32[]{:S(2)}, u32[]{:S(2)}) collective-permute-start(f32[80,4,128]{2,1,0:T(4,128)S(1)} %get-tuple-element.176.refs_1_), channel_id=1, source_target_pairs={{1,2},{2,1},{0,3},{3,0},{5,6},{6,5},{4,7},{7,4},{9,10},{10,9},{8,1... | collective-permute-start | bytes 491528 | tf_op jit(solution)/shard_map/ppermute | solution.py:646
  41.5 12.2 %collective-permute-start.26 = (f32[256,4,128]{2,1,0:T(4,128)S(1)}, f32[256,4,128]{2,1,0:T(4,128)S(1)}, u32[]{:S(2)}, u32[]{:S(2)}) collective-permute-start(f32[256,4,128]{2,1,0:T(4,128)S(1)} %shard_map.160.refs_1_), channel_id=1, source_target_pairs={{0,1},{1,0},{2,3},{3,2},{4,5},{5,4},{6,7},{7,6},{8,9},{9,8},{10,11... | collective-permute-start | bytes 1572872 | tf_op jit(solution)/shard_map/ppermute | solution.py:869
  41.6 6.1 %collective-permute-start.18 = (f32[4,4,128]{2,1,0:T(4,128)S(1)}, f32[4,4,128]{2,1,0:T(4,128)S(1)}, u32[]{:S(2)}, u32[]{:S(2)}) collective-permute-start(f32[4,4,128]{2,1,0:T(4,128)S(1)} %get-tuple-element.183.refs_2_.refs_4_.refs_0_), channel_id=1, source_target_pairs={{4,8},{5,9},{6,10},{7,11},{8,4},{9,5},{10,6},{11,7},{12,16},{13,17... | collective-permute-start | bytes 24584 | tf_op jit(solution)/shard_map/ppermute | solution.py:651
  42.1 5.6 %collective-permute-start.19 = (f32[4,4,128]{2,1,0:T(4,128)S(1)}, f32[4,4,128]{2,1,0:T(4,128)S(1)}, u32[]{:S(2)}, u32[]{:S(2)}) collective-permute-start(f32[4,4,128]{2,1,0:T(4,128)S(1)} %get-tuple-element.183.refs_2_.refs_4_.refs_0_), channel_id=1, source_target_pairs={{0,4},{4,0},{8,12},{12,8},{16,20},{20,16},{24,28},{28,24},{1,5},{5... | collective-permute-start | bytes 24584 | tf_op jit(solution)/shard_map/ppermute | solution.py:652
  48.3 3.7 %collective-permute-start.23 = (f32[4,4,128]{2,1,0:T(4,128)S(1)}, f32[4,4,128]{2,1,0:T(4,128)S(1)}, u32[]{:S(2)}, u32[]{:S(2)}) collective-permute-start(f32[4,4,128]{2,1,0:T(4,128)S(1)} %get-tuple-element.202.refs_4_), channel_id=1, source_target_pairs={{0,4},{4,0},{8,12},{12,8},{16,20},{20,16},{24,28},{28,24},{1,5},{5... | collective-permute-start | bytes 24584 | tf_op jit(solution)/shard_map/ppermute | solution.py:652
  53.6 3.5 %collective-permute-start.27 = (f32[4,4,128]{2,1,0:T(4,128)S(1)}, f32[4,4,128]{2,1,0:T(4,128)S(1)}, u32[]{:S(2)}, u32[]{:S(2)}) collective-permute-start(f32[4,4,128]{2,1,0:T(4,128)S(1)} %get-tuple-element.211.refs_6_), channel_id=1, source_target_pairs={{4,8},{5,9},{6,10},{7,11},{8,4},{9,5},{10,6},{11,7},{12,16},{13,17... | collective-permute-start | bytes 24584 | tf_op jit(solution)/shard_map/ppermute | solution.py:651
  53.7 3.8 %collective-permute-start.28 = (f32[4,4,128]{2,1,0:T(4,128)S(1)}, f32[4,4,128]{2,1,0:T(4,128)S(1)}, u32[]{:S(2)}, u32[]{:S(2)}) collective-permute-start(f32[4,4,128]{2,1,0:T(4,128)S(1)} %get-tuple-element.211.refs_6_), channel_id=1, source_target_pairs={{0,4},{4,0},{8,12},{12,8},{16,20},{20,16},{24,28},{28,24},{1,5},{5... | collective-permute-start | bytes 24584 | tf_op jit(solution)/shard_map/ppermute | solution.py:652
  72.3 3.7 %collective-permute-start.32 = (f32[4,4,128]{2,1,0:T(4,128)S(1)}, f32[4,4,128]{2,1,0:T(4,128)S(1)}, u32[]{:S(2)}, u32[]{:S(2)}) collective-permute-start(f32[4,4,128]{2,1,0:T(4,128)S(1)} %get-tuple-element.233.refs_4_), channel_id=1, source_target_pairs={{0,4},{4,0},{8,12},{12,8},{16,20},{20,16},{24,28},{28,24},{1,5},{5... | collective-permute-start | bytes 24584 | tf_op jit(solution)/shard_map/ppermute | solution.py:652
  77.8 3.7 %collective-permute-start.36 = (f32[4,4,128]{2,1,0:T(4,128)S(1)}, f32[4,4,128]{2,1,0:T(4,128)S(1)}, u32[]{:S(2)}, u32[]{:S(2)}) collective-permute-start(f32[4,4,128]{2,1,0:T(4,128)S(1)} %get-tuple-element.242.refs_4_), channel_id=1, source_target_pairs={{0,4},{4,0},{8,12},{12,8},{16,20},{20,16},{24,28},{28,24},{1,5},{5... | collective-permute-start | bytes 24584 | tf_op jit(solution)/shard_map/ppermute | solution.py:652
  83.4 3.9 %collective-permute-start.40 = (f32[4,4,128]{2,1,0:T(4,128)S(1)}, f32[4,4,128]{2,1,0:T(4,128)S(1)}, u32[]{:S(2)}, u32[]{:S(2)}) collective-permute-start(f32[4,4,128]{2,1,0:T(4,128)S(1)} %get-tuple-element.251.refs_6_), channel_id=1, source_target_pairs={{0,4},{4,0},{8,12},{12,8},{16,20},{20,16},{24,28},{28,24},{1,5},{5... | collective-permute-start | bytes 24584 | tf_op jit(solution)/shard_map/ppermute | solution.py:652
  90.5 3.9 %collective-permute-start.43 = (f32[16,4,128]{2,1,0:T(4,128)S(1)}, f32[16,4,128]{2,1,0:T(4,128)S(1)}, u32[]{:S(2)}, u32[]{:S(2)}) collective-permute-start(f32[16,4,128]{2,1,0:T(4,128)S(1)} %get-tuple-element.257.refs_2_.refs_5_), channel_id=1, source_target_pairs={{4,8},{5,9},{6,10},{7,11},{8,4},{9,5},{10,6},{11,7},{12,16},{13,17... | collective-permute-start | bytes 98312 | tf_op jit(solution)/shard_map/ppermute | solution.py:651
  90.6 4.5 %collective-permute-start.44 = (f32[16,4,128]{2,1,0:T(4,128)S(1)}, f32[16,4,128]{2,1,0:T(4,128)S(1)}, u32[]{:S(2)}, u32[]{:S(2)}) collective-permute-start(f32[16,4,128]{2,1,0:T(4,128)S(1)} %get-tuple-element.257.refs_2_.refs_5_), channel_id=1, source_target_pairs={{0,4},{4,0},{8,12},{12,8},{16,20},{20,16},{24,28},{28,24},{1,5},{5... | collective-permute-start | bytes 98312 | tf_op jit(solution)/shard_map/ppermute | solution.py:652
  93.2 3.3 %collective-permute-start.45 = (f32[16,4,128]{2,1,0:T(4,128)S(1)}, f32[16,4,128]{2,1,0:T(4,128)S(1)}, u32[]{:S(2)}, u32[]{:S(2)}) collective-permute-start(f32[16,4,128]{2,1,0:T(4,128)S(1)} %get-tuple-element.257.refs_2_.refs_5_), channel_id=1, source_target_pairs={{1,2},{2,1},{0,3},{3,0},{5,6},{6,5},{4,7},{7,4},{9,10},{10,9},{8,1... | collective-permute-start | bytes 98312 | tf_op jit(solution)/shard_map/ppermute | solution.py:646
  93.2 3.3 %collective-permute-start.46 = (f32[16,4,128]{2,1,0:T(4,128)S(1)}, f32[16,4,128]{2,1,0:T(4,128)S(1)}, u32[]{:S(2)}, u32[]{:S(2)}) collective-permute-start(f32[16,4,128]{2,1,0:T(4,128)S(1)} %get-tuple-element.257.refs_2_.refs_5_), channel_id=1, source_target_pairs={{0,1},{1,0},{2,3},{3,2},{4,5},{5,4},{6,7},{7,6},{8,9},{9,8},{10,11... | collective-permute-start | bytes 98312 | tf_op jit(solution)/shard_map/ppermute | solution.py:647
  97.5 3.6 %collective-permute-start.47 = (f32[16,4,128]{2,1,0:T(4,128)S(1)}, f32[16,4,128]{2,1,0:T(4,128)S(1)}, u32[]{:S(2)}, u32[]{:S(2)}) collective-permute-start(f32[16,4,128]{2,1,0:T(4,128)S(1)} %get-tuple-element.262.refs_2_.refs_7_), channel_id=1, source_target_pairs={{4,8},{5,9},{6,10},{7,11},{8,4},{9,5},{10,6},{11,7},{12,16},{13,17... | collective-permute-start | bytes 98312 | tf_op jit(solution)/shard_map/ppermute | solution.py:651
  97.6 4.0 %collective-permute-start.48 = (f32[16,4,128]{2,1,0:T(4,128)S(1)}, f32[16,4,128]{2,1,0:T(4,128)S(1)}, u32[]{:S(2)}, u32[]{:S(2)}) collective-permute-start(f32[16,4,128]{2,1,0:T(4,128)S(1)} %get-tuple-element.262.refs_2_.refs_7_), channel_id=1, source_target_pairs={{0,4},{4,0},{8,12},{12,8},{16,20},{20,16},{24,28},{28,24},{1,5},{5... | collective-permute-start | bytes 98312 | tf_op jit(solution)/shard_map/ppermute | solution.py:652
  99.6 3.3 %collective-permute-start.49 = (f32[16,4,128]{2,1,0:T(4,128)S(1)}, f32[16,4,128]{2,1,0:T(4,128)S(1)}, u32[]{:S(2)}, u32[]{:S(2)}) collective-permute-start(f32[16,4,128]{2,1,0:T(4,128)S(1)} %get-tuple-element.262.refs_2_.refs_7_), channel_id=1, source_target_pairs={{1,2},{2,1},{0,3},{3,0},{5,6},{6,5},{4,7},{7,4},{9,10},{10,9},{8,1... | collective-permute-start | bytes 98312 | tf_op jit(solution)/shard_map/ppermute | solution.py:646
  99.6 3.3 %collective-permute-start.50 = (f32[16,4,128]{2,1,0:T(4,128)S(1)}, f32[16,4,128]{2,1,0:T(4,128)S(1)}, u32[]{:S(2)}, u32[]{:S(2)}) collective-permute-start(f32[16,4,128]{2,1,0:T(4,128)S(1)} %get-tuple-element.262.refs_2_.refs_7_), channel_id=1, source_target_pairs={{0,1},{1,0},{2,3},{3,2},{4,5},{5,4},{6,7},{7,6},{8,9},{9,8},{10,11... | collective-permute-start | bytes 98312 | tf_op jit(solution)/shard_map/ppermute | solution.py:647
  108.1 4.6 %collective-permute-start.54 = (f32[4,4,256]{2,1,0:T(4,128)S(1)}, f32[4,4,256]{2,1,0:T(4,128)S(1)}, u32[]{:S(2)}, u32[]{:S(2)}) collective-permute-start(f32[4,4,256]{2,1,0:T(4,128)S(1)} %get-tuple-element.268), channel_id=1, source_target_pairs={{0,4},{4,0},{8,12},{12,8},{16,20},{20,16},{24,28},{28,24},{1,5},{5... | collective-permute-start | bytes 49160 | tf_op jit(solution)/shard_map/ppermute | solution.py:652
  (30 other events, 136.4 us)
